TPU v7x, 128 devices: a whole 4x4x4 slice. The times are simulated.
128 devices in a mesh: grp: 8 (over z, core), rep: 16 (over x, y).
Axes of the slice: x: 4, y: 4, z: 4, core: 2. Of those that a mesh axis runs over, the one named last changes fastest.
Arguments:
- queries: bfloat16 [32768, 1024], P(('grp', 'rep')), may hold values from -24 to 24
- passages: bfloat16 [32768, 1024], P(('grp', 'rep')), may hold values from -24 to 24
- neg_device: int32 [32768, 7], P(('grp', 'rep')), may hold values from 0 to 127, as said below
- neg_row: int32 [32768, 7], P(('grp', 'rep')), may hold values from 0 to 255
Outputs:
- losses: float32 [32768], P(('grp', 'rep'))
- grad_queries: bfloat16 [32768, 1024], P(('grp', 'rep'))
- grad_passages: bfloat16 [32768, 1024], P(('grp', 'rep'))
Inputs may be any that keep to these rules, and one draw needn't show every extreme that they name: `neg_device`: the 7 hard negatives of one query lie on different devices. The 256 queries of one device name any one device at most 16 times (some devices not at all); there is one device that the queries of every device name exactly 16 times.
All inputs are finite; a program needn't handle non-finite values.
Results may differ from a plain program's by a relative error of at most 0.015.
Values may be sent and summed in bfloat16 or wider, within the bound.
No kernel may reach another device: no remote copies, remote signals or barrier semaphores. Data moves between devices by JAX's collectives and lax.ppermute only.
A program may use at most 128 MiB of HBM per device.

v0:
```python
import math

import jax
import jax.numpy as jnp
from jax import lax
from jax.sharding import PartitionSpec as P


def shards(queries, passages, neg_device, neg_row):
    tok_rows, emb_width = queries.shape
    neg_count = neg_device.shape[1]
    groups = lax.axis_size("grp")
    replicas = lax.axis_size("rep")
    devices = groups * replicas
    slot_count = max(2, 8 * tok_rows // devices)
    temper = 3.0 / math.sqrt(emb_width)
    requests = tok_rows * neg_count
    target = neg_device.reshape(requests)
    wanted = neg_row.reshape(requests)
    onehot = (target[:, None] == jnp.arange(devices, dtype=jnp.int32)[None, :]).astype(jnp.int32)
    slot_rank = jnp.sum((jnp.cumsum(onehot, axis=0) - onehot) * onehot, axis=1)
    ask_table = jnp.zeros((devices, slot_count), jnp.int32).at[target, slot_rank].set(wanted)
    asked = lax.all_to_all(ask_table, ("grp", "rep"), split_axis=0, concat_axis=0, tiled=True)
    served = jnp.take(passages, asked.reshape(-1), axis=0).reshape(devices, slot_count, emb_width)
    fetched = lax.all_to_all(served, ("grp", "rep"), split_axis=0, concat_axis=0, tiled=True)
    negatives = fetched[target, slot_rank].reshape(tok_rows, neg_count, emb_width)
    gathered = lax.all_gather(passages, "grp", axis=0, tiled=True)
    grp_index = lax.axis_index("grp")
    own_column = grp_index * tok_rows + jnp.arange(tok_rows, dtype=jnp.int32)
    scores = temper * jnp.einsum("qe,pe->qp", queries, gathered, preferred_element_type=jnp.float32)
    hard_scores = temper * jnp.einsum(
        "qe,qke->qk", queries, negatives, preferred_element_type=jnp.float32
    )
    row_top = jnp.maximum(jnp.max(scores, axis=1), jnp.max(hard_scores, axis=1))
    row_total = jnp.sum(jnp.exp(scores - row_top[:, None]), axis=1) + jnp.sum(
        jnp.exp(hard_scores - row_top[:, None]), axis=1
    )
    log_total = row_top + jnp.log(row_total)
    columns = jnp.arange(groups * tok_rows, dtype=jnp.int32)
    positive_mask = (columns[None, :] == own_column[:, None]).astype(jnp.float32)
    losses = log_total - jnp.sum(scores * positive_mask, axis=1)
    d_scores = (jnp.exp(scores - log_total[:, None]) - positive_mask).astype(jnp.bfloat16)
    d_hard = jnp.exp(hard_scores - log_total[:, None]).astype(jnp.bfloat16)
    grad_queries = temper * (
        jnp.dot(d_scores, gathered, preferred_element_type=jnp.float32)
        + jnp.einsum("qk,qke->qe", d_hard, negatives, preferred_element_type=jnp.float32)
    )
    grad_queries = grad_queries.astype(jnp.bfloat16)
    partial_value = temper * jnp.einsum(
        "qp,qe->pe", d_scores, queries, preferred_element_type=jnp.float32
    )
    in_batch = lax.psum_scatter(
        partial_value.astype(jnp.bfloat16), "grp", scatter_dimension=0, tiled=True
    ).astype(jnp.float32)
    hard_terms = (
        temper * d_hard.astype(jnp.float32)[:, :, None] * queries.astype(jnp.float32)[:, None, :]
    ).astype(jnp.bfloat16)
    outgoing = (
        jnp.zeros((devices, slot_count, emb_width), jnp.bfloat16)
        .at[target, slot_rank]
        .set(hard_terms.reshape(requests, emb_width))
    )
    returned = lax.all_to_all(outgoing, ("grp", "rep"), split_axis=0, concat_axis=0, tiled=True)
    hard_sum = (
        jnp.zeros((tok_rows, emb_width), jnp.float32)
        .at[asked.reshape(-1)]
        .add(returned.reshape(devices * slot_count, emb_width).astype(jnp.float32))
    )
    grad_passages = (in_batch + hard_sum).astype(jnp.bfloat16)
    return (losses, grad_queries, grad_passages)


def solution(mesh):
    in_specs = (
        P(("grp", "rep"), None),
        P(("grp", "rep"), None),
        P(("grp", "rep"), None),
        P(("grp", "rep"), None),
    )
    out_specs = (P(("grp", "rep")), P(("grp", "rep"), None), P(("grp", "rep"), None))
    return jax.shard_map(shards, mesh=mesh, in_specs=in_specs, out_specs=out_specs, check_vma=False)
```

profile of v0, /device:TPU:0, one launch (start us, length us, event | category | flops | bytes accessed | tf_op | source)
XLA Modules:
  0.0 275.1 jit_solution(14277663364937065699)
XLA Ops:
  7.2 0.0 all-gather.2.cloned.1.call-start
  7.3 0.7 all-gather.2.cloned.1.call-update
  7.9 0.8 copy.15
  8.8 0.2 eq.42
  9.0 0.1 copy.18
  9.1 0.3 fusion.9
  9.5 0.2 reshape.154
  9.7 0.2 eq.38
  9.9 0.8 copy.20
  10.7 0.2 reshape.193
  10.9 0.1 broadcast_add_fusion
  11.0 0.3 copy.19
  11.3 0.6 fusion.12
  11.9 0.1 or_reduce_fusion
  12.0 0.1 and_reduce_fusion
  12.1 0.1 multiply_reduce_fusion.1
  12.2 7.1 %scatter_custom_fusion.1 = s32[2048]{0:T(1024)S(1)} fusion(s32[1792]{0:T(1024)S(1)} %get-tuple-element.15, s32[1792]{0:T(1024)S(1)} %reshape.193, s32[]{:T(128)} %constant.14.clone.1), kind=kCustom, calls=%fused_computation.50 | custom fusion | bytes 8196
  19.3 0.1 copy.21
  19.4 20.4 %all_to_all.19 = s32[128,1,16]{2,1,0:T(1,128)S(1)} all-to-all(s32[128,1,16]{2,1,0:T(1,128)S(1)} %copy.21), channel_id=1, replica_groups=mesh['grp'=8,'rep'=16] {'grp','rep'}, dimensions={0} | all-to-all | bytes 16384 | tf_op jit(solution)/shard_map/all_to_all | solution.py:23
  39.9 0.5 broadcast.162
  40.4 0.8 reduce.12
  41.2 0.1 reshape.158
  41.3 9.7 %gather_fusion = bf16[2048,1024]{1,0:T(8,128)(2,1)} fusion(bf16[256,1024]{1,0:T(8,128)(2,1)S(1)} %copy-done, s32[2048]{0:T(1024)S(1)} %broadcast_clamp_fusion), kind=kCustom, calls=%fused_computation | custom fusion | bytes 8396800 | tf_op jit(solution)/shard_map/jit(_take)/gather | solution.py:24
  51.0 3.8 %broadcast_select_fusion = bf16[128,16,1024]{2,1,0:T(8,128)(2,1)} fusion(bf16[128,16,1024]{2,1,0:T(8,128)(2,1)} %bitcast.38, pred[128,16]{1,0:T(8,128)(4,1)S(1)} %compare_and_fusion), kind=kLoop, calls=%fused_computation.9 | loop fusion | flops 2097152 | bytes 8390656 | tf_op jit(solution)/shard_map/jit(_take)/select_n | solution.py:24
  54.9 5.8 %all-to-all-start.1 = ((bf16[128,16,1024]{2,1,0:T(8,128)(2,1)}), bf16[128,16,1024]{2,1,0:T(8,128)(2,1)}, u32[]{:S(2)}, u32[]{:S(2)}) async-start(bf16[128,16,1024]{2,1,0:T(8,128)(2,1)} %broadcast_select_fusion), calls=%async_computation.1 | async-start | bytes 8388608 | tf_op jit(solution)/shard_map/all_to_all | solution.py:25
  60.7 0.2 reduce-scatter.2.cloned.1.call-start
  60.9 50.9 %all-to-all-done.1 = bf16[128,16,1024]{2,1,0:T(8,128)(2,1)} async-done(((bf16[128,16,1024]{2,1,0:T(8,128)(2,1)}), bf16[128,16,1024]{2,1,0:T(8,128)(2,1)}, u32[]{:S(2)}, u32[]{:S(2)}) %all-to-all-start.1) | async-done | bytes 4194336 | tf_op jit(solution)/shard_map/all_to_all | solution.py:25
  111.9 26.1 %gather_fusion.1 = bf16[1792,1024]{1,0:T(8,128)(2,1)} fusion(bf16[128,16,1024]{2,1,0:T(8,128)(2,1)} %all-to-all-done.1, s32[1792]{0:T(1024)S(1)} %get-tuple-element.9), kind=kCustom, calls=%fused_computation.1 | custom fusion | bytes 7354368 | tf_op jit(solution)/shard_map/gather | solution.py:26
  138.0 6.5 %reshape.159 = bf16[256,7,1024]{2,1,0:T(8,128)(2,1)} reshape(bf16[1792,1024]{1,0:T(8,128)(2,1)} %gather_fusion.1) | data formatting | bytes 7340032 | tf_op jit(solution)/shard_map/reshape | solution.py:26
  144.5 4.5 %fusion.7 = f32[256,1,7]{2,1,0:T(1,128)S(1)} fusion(bf16[256,7,1024]{2,1,0:T(8,128)(2,1)} %reshape.159, bf16[256,1024,1]{1,0,2:T(8,128)(2,1)S(1)} %bitcast.43), kind=kOutput, calls=%fused_computation.21 | convolution fusion | flops 3670016 | bytes 4201472 | tf_op jit(solution)/shard_map/qe,qke->qk/dot_general | solution.py:31
  149.0 0.1 multiply_reduce_fusion
  149.2 3.6 %fusion.20 = (f32[256]{0:T(256)S(1)}, f32[256,2048]{1,0:T(8,128)S(1)}) fusion(bf16[256,1024]{1,0:T(8,128)(2,1)S(1)} %copy-done.1, bf16[2048,1024]{1,0:T(8,128)(2,1)} %all-gather.2.cloned.1.call-done), kind=kOutput, calls=%fused_computation.58 | convolution fusion | flops 1074790144 | bytes 6816768 | tf_op jit(solution)/shard_map/qe,pe->qp/dot_general | solution.py:30
  152.7 0.2 exponential_reduce_fusion.1
  152.9 0.8 select_reduce_fusion
  153.7 0.6 fusion.19
  154.3 3.7 %multiply_convert_fusion = bf16[2048,1024]{1,0:T(8,128)(2,1)} fusion(bf16[256,1024]{1,0:T(8,128)(2,1)S(1)} %copy-done.1, f32[256,2048]{1,0:T(8,128)S(1)} %get-tuple-element.17, f32[256]{0:T(256)S(1)} %get-tuple-element.8, s32[256]{0:T(256)S(1)} %iota_add_fusion), kind=kOutput, calls=%fused_computation.7 | convolution fusion | flops 1080557568 | bytes 6817792 | tf_op jit(solution)/shard_map/qp,qe->pe/dot_general | solution.py:49
  158.0 4.3 %mul.70 = f32[256,7,1024]{2,1,0:T(8,128)} broadcast(bf16[256,1024]{1,0:T(8,128)(2,1)S(1)} %copy-done.1), dimensions={0,2} | broadcast | bytes 7864320 | tf_op jit(solution)/shard_map/mul | solution.py:56
  162.3 8.8 %mul.71 = f32[1792,1024]{1,0:T(8,128)} reshape(f32[256,7,1024]{2,1,0:T(8,128)} %mul.70) | data formatting | bytes 14680064 | tf_op jit(solution)/shard_map/mul | solution.py:56
  171.1 0.1 convert_multiply_fusion
  171.2 0.2 mul.68
  171.4 20.5 %scatter_custom_fusion.2 = bf16[2048,1024]{1,0:T(8,128)(2,1)} fusion(s32[1792]{0:T(1024)S(1)} %get-tuple-element.14, f32[1792,1024]{1,0:T(8,128)} %mul.71, f32[1792]{0:T(1024)S(1)} %mul.68, bf16[]{:T(256)} %constant.24.clone.1), kind=kCustom, calls=%fused_computation.10 | custom fusion | flops 3670016 | bytes 11542530
  191.9 5.8 %all-to-all-start.2 = ((bf16[128,16,1024]{2,1,0:T(8,128)(2,1)}), bf16[128,16,1024]{2,1,0:T(8,128)(2,1)}, u32[]{:S(2)}, u32[]{:S(2)}) async-start(bf16[128,16,1024]{2,1,0:T(8,128)(2,1)} %bitcast.37), calls=%async_computation.3 | async-start | bytes 8388608 | tf_op jit(solution)/shard_map/all_to_all | solution.py:63
  197.7 3.6 %fusion.14 = f32[256,1,1024]{2,1,0:T(1,128)S(1)} fusion(bf16[256,7,1024]{2,1,0:T(8,128)(2,1)} %reshape.159, bf16[256,7,1]{1,0,2:T(8,128)(2,1)S(1)} %get-tuple-element.12), kind=kOutput, calls=%fused_computation.33 | convolution fusion | flops 3670016 | bytes 4722176 | tf_op jit(solution)/shard_map/qk,qke->qe/dot_general | solution.py:46
  201.3 2.4 fusion.6
  203.7 1.1 convert_element_type.51
  204.8 44.1 %all-to-all-done.2 = bf16[128,16,1024]{2,1,0:T(8,128)(2,1)} async-done(((bf16[128,16,1024]{2,1,0:T(8,128)(2,1)}), bf16[128,16,1024]{2,1,0:T(8,128)(2,1)}, u32[]{:S(2)}, u32[]{:S(2)}) %all-to-all-start.2) | async-done | bytes 4194336 | tf_op jit(solution)/shard_map/all_to_all | solution.py:63
  248.9 18.5 %scatter_custom_fusion = f32[256,1024]{1,0:T(8,128)S(1)} fusion(f32[256,1024]{1,0:T(8,128)S(1)} %convert_element_type.51, s32[2048]{0:T(1024)S(1)} %bitcast.47, bf16[2048,1024]{1,0:T(8,128)(2,1)} %bitcast.19), kind=kCustom, calls=%fused_computation.5 | custom fusion | flops 4194304 | bytes 5242880 | tf_op jit(solution)/shard_map/scatter-add | solution.py:67
  267.4 0.9 convert_element_type.57
  (23 shorter events, 0.2 us)
Async XLA Ops:
  7.2 4.8 %copy-start.4 = (s32[2]{0:T(128)S(1)}, s32[2]{0:T(128)}, u32[]{:S(2)}) copy-start(s32[2]{0:T(128)} %constant.53) | copy-start | bytes 28
  7.2 4.9 %copy-start.2 = (s32[2]{0:T(128)S(1)}, s32[2]{0:T(128)}, u32[]{:S(2)}) copy-start(s32[2]{0:T(128)} %constant.56) | copy-start | bytes 28
  7.2 4.9 %copy-start.3 = (s32[2]{0:T(128)S(1)}, s32[2]{0:T(128)}, u32[]{:S(2)}) copy-start(s32[2]{0:T(128)} %constant.25) | copy-start | bytes 28
  7.2 34.1 %copy-start = (bf16[256,1024]{1,0:T(8,128)(2,1)S(1)}, bf16[256,1024]{1,0:T(8,128)(2,1)}, u32[]{:S(2)}) copy-start(bf16[256,1024]{1,0:T(8,128)(2,1)} %param.5) | copy-start | bytes 1572868
  7.2 141.9 %all-gather.2.cloned.1.call-start = ((), (), s32[]{:S(2)}) async-start(), calls=%async_computation.4 | async-start | bytes 4718592 | tf_op jit(solution)/shard_map/all_gather | solution.py:27
  54.9 57.0 %all-to-all-start.1 = ((bf16[128,16,1024]{2,1,0:T(8,128)(2,1)}), bf16[128,16,1024]{2,1,0:T(8,128)(2,1)}, u32[]{:S(2)}, u32[]{:S(2)}) async-start(bf16[128,16,1024]{2,1,0:T(8,128)(2,1)} %broadcast_select_fusion), calls=%async_computation.1 | async-start | bytes 8388608 | tf_op jit(solution)/shard_map/all_to_all | solution.py:25
  60.7 143.0 %reduce-scatter.2.cloned.1.call-start = ((), (), s32[]{:S(2)}) async-start(), calls=%async_computation.5 | async-start | bytes 4718592 | tf_op jit(solution)/shard_map/reduce_scatter | solution.py:52
  138.0 6.5 %copy-start.1 = (bf16[256,1024]{1,0:T(8,128)(2,1)S(1)}, bf16[256,1024]{1,0:T(8,128)(2,1)}, u32[]{:S(2)}) copy-start(bf16[256,1024]{1,0:T(8,128)(2,1)} %param.4) | copy-start | bytes 1572868
  191.9 57.0 %all-to-all-start.2 = ((bf16[128,16,1024]{2,1,0:T(8,128)(2,1)}), bf16[128,16,1024]{2,1,0:T(8,128)(2,1)}, u32[]{:S(2)}, u32[]{:S(2)}) async-start(bf16[128,16,1024]{2,1,0:T(8,128)(2,1)} %bitcast.37), calls=%async_computation.3 | async-start | bytes 8388608 | tf_op jit(solution)/shard_map/all_to_all | solution.py:63
  197.7 3.6 %copy-start.5 = (bf16[2048,1024]{1,0:T(8,128)(2,1)S(1)}, bf16[2048,1024]{1,0:T(8,128)(2,1)}, u32[]{:S(2)}) copy-start(bf16[2048,1024]{1,0:T(8,128)(2,1)} %all-gather.2.cloned.1.call-done) | copy-start | bytes 12582916
Sparse Core Ops, SparseCore 0:
  9.8 35.4 all-gather.1
  158.1 34.7 reduce-scatter.1
where the time goes:
time: 278 us; the launch traced here: 275 us
  waiting for transfers between devices  95.7 us (34%)
  local copies, waits for them, and re-layouts  66.3 us (24%)
  other arithmetic  48.7 us (18%)
  blocking collectives  20.4 us (7%)
  matrix products  17.7 us (6%)
  between operations  14.3 us (5%)
  starting transfers between devices  11.9 us (4%)
    all_to_all x1, waiting for transfers between devices, shards(): lax.all_to_all(served, ('grp', 'rep'), split_axis=0, concat_axis=0, tiled...  50.9 us
    all_to_all x1, waiting for transfers between devices, shards(): lax.all_to_all(outgoing, ('grp', 'rep'), split_axis=0, concat_axis=0, til...  44.1 us
    gather x1, local copies, waits for them, and re-layouts, shards(): fetched[target, slot_rank].reshape(tok_rows, neg_count, emb_width)  26.1 us
    unnamed x4, other arithmetic  20.7 us
    all_to_all x1, blocking collectives, shards(): lax.all_to_all(ask_table, ('grp', 'rep'), split_axis=0, concat_axis=0, ti...  20.4 us
    scatter-add x1, other arithmetic, shards(): hard_sum = jnp.zeros((tok_rows, emb_width), jnp.float32).at[asked.reshape...  18.5 us
    mul x3, local copies, waits for them, and re-layouts, shards(): temper * d_hard.astype(jnp.float32)[:, :, None]  13.3 us
    gather x1, local copies, waits for them, and re-layouts, shards(): jnp.take(passages, asked.reshape(-1), axis=0)  9.67 us
  transfers between devices with their start and end apart: 4, of which 2 were waited for; matrix products, arithmetic and copies ran while one was open for 38% of the time, Pallas kernels for 0%

commit v1 on v0

v1 whole, which is shorter than its diff:
```python
import functools
import math

import jax
import jax.numpy as jnp
from jax import lax
from jax.experimental import pallas as pl
from jax.experimental.pallas import tpu as pltpu
from jax.sharding import PartitionSpec as P

F32 = jnp.float32
BF16 = jnp.bfloat16
I32 = jnp.int32
LOW = -1e30
NT = (((1,), (1,)), ((), ()))
TN = (((0,), (0,)), ((), ()))
NN = (((1,), (0,)), ((), ()))
VMEM_LIMIT = 48 * 1024 * 1024


def mm(a, b, dims=NN, exact=False):
    return lax.dot_general(
        a, b, dims, precision=lax.Precision.HIGHEST if exact else None, preferred_element_type=F32
    )


def iota(shape, dim):
    return lax.broadcasted_iota(I32, shape, dim)


def slot_hits(v_ref, g, reps, cap, devices, toks):
    rows = reps * cap
    slot = iota((rows, devices), 0)
    pick = (iota((rows, devices), 1) == g * reps + slot // cap).astype(BF16)
    spread = mm(pick, v_ref[...])
    want = (iota((rows, toks), 0) % cap + 1).astype(F32)
    return pick, spread == want


def prep_kernel(reps, cap, nd_ref, nr_ref, q_ref, slots_ref, code_ref, v_ref, row_ref):
    g = pl.program_id(0)
    negs, toks = nd_ref.shape
    devices = v_ref.shape[0]

    @pl.when(g == 0)
    def _():
        dev = iota((devices, toks), 0)
        named = jnp.zeros((devices, toks), F32)
        rows = jnp.zeros((devices, toks), F32)
        for k in range(negs):
            hit = dev == nd_ref[k : k + 1, :]
            named = named + jnp.where(hit, 1.0, 0.0)
            rows = rows + jnp.where(hit, (nr_ref[k : k + 1, :] + 1).astype(F32), 0.0)
        before = (iota((toks, toks), 0) < iota((toks, toks), 1)).astype(BF16)
        rank = mm(named.astype(BF16), before)
        v_ref[...] = (named * (rank + 1.0)).astype(BF16)
        row_ref[...] = rows.astype(BF16)

    pick, hit = slot_hits(v_ref, g, reps, cap, devices, toks)
    wanted = mm(pick, row_ref[...])
    hot = hit.astype(BF16)
    slots_ref[...] = mm(hot, q_ref[...]).astype(BF16).reshape(slots_ref.shape)
    ids = mm(jnp.ones((8, toks), BF16), jnp.where(hit, wanted, 0.0).astype(BF16), NT)
    tok = mm(iota((8, toks), 1).astype(F32).astype(BF16), hot, NT)
    code = tok * 512.0 + ids
    code_ref[pl.ds(g, 1), :] = code[0:1, :].astype(I32)


def slot_codes(code_ref, g, reps, cap):
    code = code_ref[pl.ds(g, 1), :]
    ids = code & 511
    slots = code.shape[1]
    valid = ids > 0
    mine = iota((reps, slots), 1) // cap == iota((reps, slots), 0)
    return ids, code >> 9, valid, mine


def serve_kernel(
    reps, cap, temper, place_ref, code_ref, qr_ref, p_ref, q_ref,
    served_ref, hs_ref, part_ref, top, total, top_in, total_in,
):
    g = pl.program_id(0)
    groups = pl.num_programs(0)
    toks, width = q_ref.shape
    slots = reps * cap

    @pl.when(g == 0)
    def _():
        top[...] = jnp.full(top.shape, LOW, F32)
        total[...] = jnp.zeros(total.shape, F32)
        top_in[...] = jnp.full(top_in.shape, LOW, F32)
        total_in[...] = jnp.zeros(total_in.shape, F32)

    ids, tok, valid, mine = slot_codes(code_ref, g, reps, cap)
    passages = p_ref[...]
    asking = qr_ref[...].reshape(slots, width)
    hit = iota((toks, slots), 0) + 1 == ids
    served = mm(hit.astype(BF16), passages, TN).astype(BF16)
    served_ref[...] = served.reshape(served_ref.shape)
    cross = mm(passages, asking, NT)
    hs = temper * jnp.sum(jnp.where(hit, cross, 0.0), axis=0, keepdims=True)
    hs_ref[pl.ds(g, 1), :] = hs
    token = (iota((toks, slots), 0) == tok) & valid
    live = mine & valid
    value = mm(jnp.where(live, hs, 0.0), jnp.where(token, 1.0, 0.0), NT, exact=True)
    there = mm(live.astype(BF16), token.astype(BF16), NT) > 0.5
    value = jnp.where(there, value, LOW)
    new_top = jnp.maximum(top[...], value)
    total[...] = total[...] * jnp.exp(top[...] - new_top) + jnp.where(
        there, jnp.exp(value - new_top), 0.0
    )
    top[...] = new_top
    scores = temper * mm(passages, q_ref[...], NT)
    new_in = jnp.maximum(top_in[...], jnp.max(scores, axis=0, keepdims=True))
    total_in[...] = total_in[...] * jnp.exp(top_in[...] - new_in) + jnp.sum(
        jnp.exp(scores - new_in), axis=0, keepdims=True
    )
    top_in[...] = new_in

    @pl.when(g == groups - 1)
    def _():
        part = jnp.where(total[...] > 0.0, top[...] + jnp.log(total[...]), LOW)
        inside = top_in[...] + jnp.log(total_in[...])
        high = jnp.maximum(part, inside)
        both = high + jnp.log(jnp.exp(part - high) + jnp.exp(inside - high))
        own = iota(part.shape, 0) == place_ref[1]
        part_ref[...] = jnp.where(own, both, part)


def own_row(lt_ref, place_ref):
    lt = lt_ref[...]
    own = iota(lt.shape, 0) == place_ref[1]
    return jnp.sum(jnp.where(own, lt, 0.0), axis=0, keepdims=True)


def grad_kernel(
    reps, cap, temper, place_ref, code_ref, hs_ref, lt_ref, qr_ref, p_ref, q_ref,
    gp_ref, gq_ref, loss_ref,
):
    g = pl.program_id(0)
    toks, width = q_ref.shape
    slots = reps * cap
    ids, tok, valid, mine = slot_codes(code_ref, g, reps, cap)
    passages = p_ref[...]
    asking = qr_ref[...].reshape(slots, width)
    queries = q_ref[...]
    token = jnp.where((iota((toks, slots), 0) == tok) & valid, 1.0, 0.0)
    found = mm(lt_ref[...], token, exact=True)
    log_slot = jnp.sum(jnp.where(mine, found, 0.0), axis=0, keepdims=True)
    hs = hs_ref[pl.ds(g, 1), :]
    d_hard = jnp.where(valid, jnp.exp(hs - log_slot), 0.0)
    hard = jnp.where(iota((toks, slots), 0) + 1 == ids, d_hard, 0.0).astype(BF16)
    lt_own = own_row(lt_ref, place_ref)
    scores = temper * mm(passages, queries, NT)
    eye = iota((toks, toks), 0) == iota((toks, toks), 1)
    here = g == place_ref[0]
    d_scores = jnp.exp(scores - lt_own) - jnp.where(eye & here, 1.0, 0.0)
    d_scores = d_scores.astype(BF16)
    gp_ref[...] = (temper * (mm(hard, asking) + mm(d_scores, queries))).astype(BF16)
    step = mm(d_scores, passages, TN)

    @pl.when(g == 0)
    def _():
        gq_ref[...] = step

    @pl.when(g > 0)
    def _():
        gq_ref[...] += step

    @pl.when(here)
    def _():
        loss_ref[...] = lt_own - jnp.sum(jnp.where(eye, scores, 0.0), axis=0, keepdims=True)


def final_kernel(reps, cap, temper, place_ref, v_ref, lt_ref, f_ref, q_ref, gq_ref, out_ref, acc):
    g = pl.program_id(0)
    toks, width = q_ref.shape
    slots = reps * cap
    _, hit = slot_hits(v_ref, g, reps, cap, v_ref.shape[0], toks)
    fetched = f_ref[...].reshape(slots, width)
    scores = temper * mm(fetched, q_ref[...], NT)
    d_hard = jnp.where(hit, jnp.exp(scores - own_row(lt_ref, place_ref)), 0.0).astype(BF16)
    step = mm(d_hard, fetched, TN)

    @pl.when(g == 0)
    def _():
        acc[...] = gq_ref[...] + step

    @pl.when(g > 0)
    def _():
        acc[...] += step

    @pl.when(g == pl.num_programs(0) - 1)
    def _():
        out_ref[...] = (temper * acc[...]).astype(BF16)


def full(shape):
    return pl.BlockSpec(shape, lambda g: (0,) * len(shape))


def log_add_over_rep(part, reps):
    step = 1
    while step < reps:
        other = lax.ppermute(part, "rep", [(i, i ^ step) for i in range(reps)])
        part = jnp.maximum(part, other) + jnp.log1p(jnp.exp(-jnp.abs(part - other)))
        step *= 2
    return part


def shards(queries, passages, neg_device, neg_row):
    toks, width = queries.shape
    negs = neg_device.shape[1]
    groups = lax.axis_size("grp")
    reps = lax.axis_size("rep")
    devices = groups * reps
    cap = 8 * toks // devices
    slots = reps * cap
    temper = 3.0 / math.sqrt(width)
    place = jnp.stack([lax.axis_index("grp"), lax.axis_index("rep")]).astype(I32)
    smem = pl.BlockSpec(memory_space=pltpu.SMEM)
    by_group = pl.BlockSpec((reps, cap, width), lambda g: (0, g, 0))
    block = pl.BlockSpec((toks, width), lambda g: (g, 0))
    params = pltpu.CompilerParams(
        dimension_semantics=("arbitrary",), vmem_limit_bytes=VMEM_LIMIT
    )
    unit = 2 * toks * width * groups * slots

    def cost(n, mib):
        return pl.CostEstimate(flops=n * unit, bytes_accessed=mib << 20, transcendentals=0)

    gathered = lax.all_gather(passages, "grp", axis=0, tiled=True)

    slot_queries, code, ranks = pl.pallas_call(
        functools.partial(prep_kernel, reps, cap),
        grid=(groups,),
        in_specs=[full((negs, toks)), full((negs, toks)), full((toks, width))],
        out_specs=[by_group, full((groups, slots)), full((devices, toks))],
        out_shape=[
            jax.ShapeDtypeStruct((reps, groups * cap, width), BF16),
            jax.ShapeDtypeStruct((groups, slots), I32),
            jax.ShapeDtypeStruct((devices, toks), BF16),
        ],
        scratch_shapes=[pltpu.VMEM((devices, toks), BF16)],
        compiler_params=params,
        cost_estimate=cost(1, 5),
        name="prep",
    )(neg_device.T, neg_row.T, queries)

    asked = lax.all_to_all(
        code.reshape(groups, reps, cap).transpose(1, 0, 2).reshape(reps, groups * cap),
        "rep", split_axis=0, concat_axis=0, tiled=True,
    )
    asked = asked.reshape(reps, groups, cap).transpose(1, 0, 2).reshape(groups, slots)
    asking = lax.all_to_all(slot_queries, "rep", split_axis=0, concat_axis=0, tiled=True)

    served, hard_scores, part = pl.pallas_call(
        functools.partial(serve_kernel, reps, cap, temper),
        grid=(groups,),
        in_specs=[smem, full((groups, slots)), by_group, block, full((toks, width))],
        out_specs=[by_group, full((groups, slots)), full((reps, toks))],
        out_shape=[
            jax.ShapeDtypeStruct((reps, groups * cap, width), BF16),
            jax.ShapeDtypeStruct((groups, slots), F32),
            jax.ShapeDtypeStruct((reps, toks), F32),
        ],
        scratch_shapes=[
            pltpu.VMEM((reps, toks), F32),
            pltpu.VMEM((reps, toks), F32),
            pltpu.VMEM((1, toks), F32),
            pltpu.VMEM((1, toks), F32),
        ],
        compiler_params=params,
        cost_estimate=cost(3, 13),
        name="serve",
    )(place, asked, asking, gathered, queries)

    fetched = lax.all_to_all(served, "rep", split_axis=0, concat_axis=0, tiled=True)
    log_total = log_add_over_rep(part, reps)

    partial_sum, inner, losses = pl.pallas_call(
        functools.partial(grad_kernel, reps, cap, temper),
        grid=(groups,),
        in_specs=[
            smem, full((groups, slots)), full((groups, slots)), full((reps, toks)),
            by_group, block, full((toks, width)),
        ],
        out_specs=[block, full((toks, width)), full((1, toks))],
        out_shape=[
            jax.ShapeDtypeStruct((groups * toks, width), BF16),
            jax.ShapeDtypeStruct((toks, width), F32),
            jax.ShapeDtypeStruct((1, toks), F32),
        ],
        compiler_params=params,
        cost_estimate=cost(4, 14),
        name="grads",
    )(place, asked, hard_scores, log_total, asking, gathered, queries)

    grad_passages = lax.psum_scatter(partial_sum, "grp", scatter_dimension=0, tiled=True)

    grad_queries = pl.pallas_call(
        functools.partial(final_kernel, reps, cap, temper),
        grid=(groups,),
        in_specs=[
            smem, full((devices, toks)), full((reps, toks)), by_group,
            full((toks, width)), full((toks, width)),
        ],
        out_specs=full((toks, width)),
        out_shape=jax.ShapeDtypeStruct((toks, width), BF16),
        scratch_shapes=[pltpu.VMEM((toks, width), F32)],
        compiler_params=params,
        cost_estimate=cost(2, 6),
        name="final",
    )(place, ranks, log_total, fetched, queries, inner)
    return (losses.reshape(toks), grad_queries, grad_passages)


def solution(mesh):
    in_specs = (
        P(("grp", "rep"), None),
        P(("grp", "rep"), None),
        P(("grp", "rep"), None),
        P(("grp", "rep"), None),
    )
    out_specs = (P(("grp", "rep")), P(("grp", "rep"), None), P(("grp", "rep"), None))
    return jax.shard_map(shards, mesh=mesh, in_specs=in_specs, out_specs=out_specs, check_vma=False)
```

time: 278 us -> 199 us (0.72)
  local copies, waits for them, and re-layouts: 66.3 us -> 9.21 us
  other arithmetic: 48.7 us -> 0.81 us
  blocking collectives: 20.4 us -> 62.1 us
  Pallas kernels: 0 us -> 35 us
  waiting for transfers between devices: 95.7 us -> 69.1 us
  matrix products: 17.7 us -> 0 us
  starting transfers between devices: 11.9 us -> 7.64 us
    all_to_all x2 -> x1, waiting for transfers between devices: 95 us -> 53.1 us  [shards(): lax.all_to_all(slot_queries, 'rep', split_axis=0, concat_axis=0, tiled=True)]
    all_to_all x1 -> x2, blocking collectives: 20.4 us -> 62.1 us  [the longest x1 47.6 us: shards(): lax.all_to_all(served, 'rep', split_axis=0, concat_axis=0, tiled=True)]
    gather x2 -> x0, local copies, waits for them, and re-layouts: 35.7 us -> none  [the longest x1 26.1 us: shards(): fetched[target, slot_rank].reshape(tok_rows, neg_count, emb_width)]
    pallas_call x0 -> x4, Pallas kernels: none -> 35 us  [the longest x1 11.2 us: shards(): pl.pallas_call(functools.partial(grad_kernel, reps, cap, temper), grid=(g...]
    unnamed x4 -> x0, other arithmetic: 20.7 us -> none
    scatter-add x1 -> x0, other arithmetic: 18.5 us -> none  [shards(): hard_sum = jnp.zeros((tok_rows, emb_width), jnp.float32).at[asked.reshape...]
    dot_general x5 -> x0, matrix products: 17.7 us -> none  [the longest x1 4.53 us: shards(): jnp.einsum('qe,qke->qk', queries, negatives, preferred_element_type=jnp.f...]
    ppermute x0 -> x4, waiting for transfers between devices: none -> 15.3 us  [log_add_over_rep(): other = lax.ppermute(part, 'rep', [(i, i ^ step) for i in range(reps)])]
  transfers between devices with their start and end apart: 4 -> 7, of which waited for: 2 -> 5; matrix products, arithmetic and copies ran while one was open for 38% -> 1% of each run, Pallas kernels for 0% -> 7%
where the time goes in v1:
time: 199 us; the launch traced here: 198 us
  waiting for transfers between devices  69.1 us (35%)
  blocking collectives  62.1 us (31%)
  Pallas kernels  35 us (18%)
  between operations  14.2 us (7%)
  local copies, waits for them, and re-layouts  9.21 us (5%)
  starting transfers between devices  7.64 us (4%)
    all_to_all x1, waiting for transfers between devices, shards(): lax.all_to_all(slot_queries, 'rep', split_axis=0, concat_axis=0, tiled=True)  53.1 us
    all_to_all x1, blocking collectives, shards(): lax.all_to_all(served, 'rep', split_axis=0, concat_axis=0, tiled=True)  47.6 us
    ppermute x4, waiting for transfers between devices, log_add_over_rep(): other = lax.ppermute(part, 'rep', [(i, i ^ step) for i in range(reps)])  15.3 us
    all_to_all x1, blocking collectives, shards(): lax.all_to_all(code.reshape(groups, reps, cap).transpose(1, 0, 2).reshape...  14.5 us
    pallas_call x1, Pallas kernels, shards(): pl.pallas_call(functools.partial(grad_kernel, reps, cap, temper), grid=(g...  11.2 us
    pallas_call x1, Pallas kernels, shards(): pl.pallas_call(functools.partial(serve_kernel, reps, cap, temper), grid=(...  10.1 us
    pallas_call x1, Pallas kernels, shards(): pl.pallas_call(functools.partial(final_kernel, reps, cap, temper), grid=(...  9.73 us
    unnamed x14, local copies, waits for them, and re-layouts  8.33 us
  transfers between devices with their start and end apart: 7, of which 5 were waited for; matrix products, arithmetic and copies ran while one was open for 1% of the time, Pallas kernels for 7%

profile of v1, /device:TPU:0, one launch (start us, length us, event | category | flops | bytes accessed | tf_op | source)
XLA Modules:
  0.0 198.0 jit_solution(15746157700168627226)
XLA Ops:
  7.2 0.0 all-gather.2.cloned.1.call-start
  7.2 0.7 all-gather.2.cloned.1.call-update
  7.9 0.0 copy-start.3
  7.9 1.0 copy-done.3
  8.9 0.0 copy-start.5
  8.9 0.7 copy-done.5
  9.6 0.0 copy-start.6
  9.6 0.7 copy-done.6
  10.3 3.9 %prep.1 = (bf16[16,128,1024]{2,1,0:T(8,128)(2,1)S(1)}, s32[8,256]{1,0:T(8,128)S(1)}, bf16[128,256]{1,0:T(8,128)(2,1)S(1)}) custom-call(s32[7,256]{1,0:T(8,128)S(1)} %bitcast.10, s32[7,256]{1,0:T(8,128)S(1)} %bitcast.11, bf16[256,1024]{1,0:T(8,128)(2,1)S(1)} %copy-done.3), custom_call_target="tpu_custom_call" | custom-call | flops 1073741824 | bytes 5242880 | tf_op jit(solution)/shard_map/prep/pallas_call | solution.py:234
  14.3 0.0 copy-start.1
  14.3 2.0 copy-done.1
  16.2 0.1 reshape.23
  16.3 0.1 all_to_all.12
  16.4 14.5 %all_to_all.19 = s32[16,1,128]{2,1,0:T(1,128)S(1)} all-to-all(s32[16,1,128]{2,1,0:T(1,128)S(1)} %bitcast.14), channel_id=1, replica_groups=mesh['grp'=8,'rep'=16] {'rep'}, dimensions={0} | all-to-all | bytes 16384 | tf_op jit(solution)/shard_map/all_to_all | solution.py:250
  30.9 0.0 copy-start.4
  30.9 4.7 %all-to-all-start.1 = ((bf16[16,128,1024]{2,1,0:T(8,128)(2,1)}), bf16[16,128,1024]{2,1,0:T(8,128)(2,1)}, u32[]{:S(2)}, u32[]{:S(2)}) async-start(bf16[16,128,1024]{2,1,0:T(8,128)(2,1)} %copy-done.1), calls=%async_computation.1 | async-start | bytes 8388608 | tf_op jit(solution)/shard_map/all_to_all | solution.py:255
  35.6 0.0 reduce-scatter.2.cloned.1.call-start
  35.6 0.1 pad_add_fusion.place_ref
  35.7 0.5 broadcast.3
  36.2 0.7 reduce.3
  36.9 0.1 reshape.24
  37.0 0.1 reshape.25.code_ref
  37.1 53.1 %all-to-all-done.1.qr_ref = bf16[16,128,1024]{2,1,0:T(8,128)(2,1)} async-done(((bf16[16,128,1024]{2,1,0:T(8,128)(2,1)}), bf16[16,128,1024]{2,1,0:T(8,128)(2,1)}, u32[]{:S(2)}, u32[]{:S(2)}) %all-to-all-start.1) | async-done | bytes 4194336 | tf_op jit(solution)/shard_map/all_to_all | solution.py:255
  90.2 0.0 all-gather.2.cloned.1.call-done.p_ref
  90.2 0.0 copy-done.4
  90.2 10.1 %serve.1 = (bf16[16,128,1024]{2,1,0:T(8,128)(2,1)S(1)}, f32[8,256]{1,0:T(8,128)S(1)}, f32[16,256]{1,0:T(8,128)S(1)}) custom-call(s32[2]{0:T(128)S(1)} %pad_add_fusion.place_ref, s32[8,256]{1,0:T(8,128)S(1)} %reshape.25.code_ref, bf16[16,128,1024]{2,1,0:T(8,128)(2,1)} %all-to-all-done.1.qr_ref, bf16[2048,1024]{1,0:T(8,128)(2,1)} %all-gather.2.cloned.1.call-done.p_ref, ...), custom_call_target="tpu_custom_call" | custom-call | flops 3221225472 | bytes 13631488 | tf_op jit(solution)/shard_map/serve/pallas_call | solution.py:257
  100.3 0.0 copy-start
  100.3 2.0 copy-done
  102.3 0.7 collective-permute-start
  103.0 3.0 %collective-permute-done = f32[16,256]{1,0:T(8,128)S(1)} collective-permute-done((f32[16,256]{1,0:T(8,128)S(1)}, f32[16,256]{1,0:T(8,128)S(1)}, u32[]{:S(2)}, u32[]{:S(2)}) %collective-permute-start) | collective-permute-done | bytes 16416 | tf_op jit(solution)/shard_map/ppermute | solution.py:205
  106.0 1.3 collective-permute-start.1
  107.4 4.0 %collective-permute-done.1 = f32[16,256]{1,0:T(8,128)S(1)} collective-permute-done((f32[16,256]{1,0:T(8,128)S(1)}, f32[16,256]{1,0:T(8,128)S(1)}, u32[]{:S(2)}, u32[]{:S(2)}) %collective-permute-start.1) | collective-permute-done | bytes 16416 | tf_op jit(solution)/shard_map/ppermute | solution.py:205
  111.4 0.1 collective-permute-start.2
  111.5 3.7 %collective-permute-done.2 = f32[16,256]{1,0:T(8,128)S(1)} collective-permute-done((f32[16,256]{1,0:T(8,128)S(1)}, f32[16,256]{1,0:T(8,128)S(1)}, u32[]{:S(2)}, u32[]{:S(2)}) %collective-permute-start.2) | collective-permute-done | bytes 16416 | tf_op jit(solution)/shard_map/ppermute | solution.py:205
  115.2 0.7 collective-permute-start.3
  116.0 4.6 %collective-permute-done.3 = f32[16,256]{1,0:T(8,128)S(1)} collective-permute-done((f32[16,256]{1,0:T(8,128)S(1)}, f32[16,256]{1,0:T(8,128)S(1)}, u32[]{:S(2)}, u32[]{:S(2)}) %collective-permute-start.3) | collective-permute-done | bytes 16416 | tf_op jit(solution)/shard_map/ppermute | solution.py:205
  120.6 11.2 %grads.1 = (bf16[2048,1024]{1,0:T(8,128)(2,1)S(1)}, f32[256,1024]{1,0:T(8,128)S(1)}, f32[1,256]{1,0:T(1,128)}) custom-call(s32[2]{0:T(128)S(1)} %pad_add_fusion.place_ref, s32[8,256]{1,0:T(8,128)S(1)} %reshape.25.code_ref, f32[8,256]{1,0:T(8,128)S(1)} %get-tuple-element.14.hs_ref, f32[16,256]{1,0:T(8,128)S(1)} %log-plus-one_add_fusion.lt_ref, ...), custom_call_target="tpu_custom_call" | custom-call | flops 4294967296 | bytes 14680064 | tf_op jit(solution)/shard_map/grads/pallas_call | solution.py:281
  131.8 0.0 copy-start.2
  131.8 2.0 copy-done.2
  133.8 0.0 reduce-scatter.2.cloned.1.call-update
  133.8 47.6 %all_to_all.20.f_ref = bf16[16,128,1024]{2,1,0:T(8,128)(2,1)S(1)} all-to-all(bf16[16,128,1024]{2,1,0:T(8,128)(2,1)} %copy-done), channel_id=1, replica_groups=mesh['grp'=8,'rep'=16] {'rep'}, dimensions={0} | all-to-all | bytes 8388608 | tf_op jit(solution)/shard_map/all_to_all | solution.py:278
  181.4 9.7 %final.1 = bf16[256,1024]{1,0:T(8,128)(2,1)} custom-call(s32[2]{0:T(128)S(1)} %pad_add_fusion.place_ref, bf16[128,256]{1,0:T(8,128)(2,1)S(1)} %get-tuple-element.17.v_ref, f32[16,256]{1,0:T(8,128)S(1)} %log-plus-one_add_fusion.lt_ref, bf16[16,128,1024]{2,1,0:T(8,128)(2,1)S(1)} %all_to_all.20.f_ref, bf16[256,1024]{1,0:T(8,128)(2,1)S(1)} %copy-done.4, ...), custom_call_target="tpu_custom_call" | custom-call | flops 2147483648 | bytes 6291456 | tf_op jit(solution)/shard_map/final/pallas_call | solution.py:301
  191.1 0.0 reduce-scatter.2.cloned.1.call-done
  (6 shorter events, 0.1 us)
Async XLA Ops:
  7.2 83.0 %all-gather.2.cloned.1.call-start = ((), (), s32[]{:S(2)}) async-start(), calls=%async_computation.4 | async-start | bytes 4718592 | tf_op jit(solution)/shard_map/all_gather | solution.py:232
  7.9 1.0 copy-start.3
  8.9 0.7 copy-start.5
  9.6 0.7 copy-start.6
  14.3 2.0 copy-start.1
  30.9 59.3 %copy-start.4 = (bf16[256,1024]{1,0:T(8,128)(2,1)S(1)}, bf16[256,1024]{1,0:T(8,128)(2,1)}, u32[]{:S(2)}) copy-start(bf16[256,1024]{1,0:T(8,128)(2,1)} %q_ref.7) | copy-start | bytes 1572868
  30.9 59.3 %all-to-all-start.1 = ((bf16[16,128,1024]{2,1,0:T(8,128)(2,1)}), bf16[16,128,1024]{2,1,0:T(8,128)(2,1)}, u32[]{:S(2)}, u32[]{:S(2)}) async-start(bf16[16,128,1024]{2,1,0:T(8,128)(2,1)} %copy-done.1), calls=%async_computation.1 | async-start | bytes 8388608 | tf_op jit(solution)/shard_map/all_to_all | solution.py:255
  35.6 155.5 %reduce-scatter.2.cloned.1.call-start = ((), (), s32[]{:S(2)}) async-start(), calls=%async_computation.5 | async-start | bytes 4718592 | tf_op jit(solution)/shard_map/reduce_scatter | solution.py:299
  100.3 2.0 copy-start
  102.3 3.7 %collective-permute-start = (f32[16,256]{1,0:T(8,128)S(1)}, f32[16,256]{1,0:T(8,128)S(1)}, u32[]{:S(2)}, u32[]{:S(2)}) collective-permute-start(f32[16,256]{1,0:T(8,128)S(1)} %get-tuple-element.15), channel_id=1, source_target_pairs={{0,1},{1,0},{2,3},{3,2},{4,5},{5,4},{6,7},{7,6},{8,9},{9,8},{10,11... | collective-permute-start | bytes 49160 | tf_op jit(solution)/shard_map/ppermute | solution.py:205
  106.0 5.3 %collective-permute-start.1 = (f32[16,256]{1,0:T(8,128)S(1)}, f32[16,256]{1,0:T(8,128)S(1)}, u32[]{:S(2)}, u32[]{:S(2)}) collective-permute-start(f32[16,256]{1,0:T(8,128)S(1)} %log-plus-one_add_fusion.3), channel_id=1, source_target_pairs={{0,2},{1,3},{2,0},{3,1},{4,6},{5,7},{6,4},{7,5},{8,10},{9,11},{10,... | collective-permute-start | bytes 49160 | tf_op jit(solution)/shard_map/ppermute | solution.py:205
  111.4 3.8 %collective-permute-start.2 = (f32[16,256]{1,0:T(8,128)S(1)}, f32[16,256]{1,0:T(8,128)S(1)}, u32[]{:S(2)}, u32[]{:S(2)}) collective-permute-start(f32[16,256]{1,0:T(8,128)S(1)} %log-plus-one_add_fusion.2), channel_id=1, source_target_pairs={{0,4},{1,5},{2,6},{3,7},{4,0},{5,1},{6,2},{7,3},{8,12},{9,13},{10,... | collective-permute-start | bytes 49160 | tf_op jit(solution)/shard_map/ppermute | solution.py:205
  115.2 5.3 %collective-permute-start.3 = (f32[16,256]{1,0:T(8,128)S(1)}, f32[16,256]{1,0:T(8,128)S(1)}, u32[]{:S(2)}, u32[]{:S(2)}) collective-permute-start(f32[16,256]{1,0:T(8,128)S(1)} %log-plus-one_add_fusion.1), channel_id=1, source_target_pairs={{0,8},{1,9},{2,10},{3,11},{4,12},{5,13},{6,14},{7,15},{8,0},{9,1},... | collective-permute-start | bytes 49160 | tf_op jit(solution)/shard_map/ppermute | solution.py:205
  131.8 2.0 copy-start.2
Sparse Core Ops, SparseCore 0:
  9.7 34.7 all-gather.1
  133.9 38.8 reduce-scatter.1

commit v2 on v0

v2 whole, which is shorter than its diff:
```python
import functools
import math

import jax
import jax.numpy as jnp
from jax import lax
from jax.experimental import pallas as pl
from jax.experimental.pallas import tpu as pltpu
from jax.sharding import PartitionSpec as P

F32 = jnp.float32
BF16 = jnp.bfloat16
I32 = jnp.int32
LOW = -1e30
NT = (((1,), (1,)), ((), ()))
TN = (((0,), (0,)), ((), ()))
NN = (((1,), (0,)), ((), ()))
VMEM_LIMIT = 60 * 1024 * 1024


def mm(a, b, dims=NN):
    return lax.dot_general(a, b, dims, preferred_element_type=F32)


def iota(shape, dim):
    return lax.broadcasted_iota(I32, shape, dim)


def split3(x):
    a = x.astype(BF16)
    rest = x - a.astype(F32)
    b = rest.astype(BF16)
    c = (rest - b.astype(F32)).astype(BF16)
    return jnp.concatenate([a, b, c], axis=0)


def slot_hits(v_ref, step, reps, cap, toks):
    rows = reps * 2 * cap
    devices = v_ref.shape[0]
    slot = iota((rows, devices), 0)
    owner = (2 * step + slot // cap % 2) * reps + slot // (2 * cap)
    pick = (iota((rows, devices), 1) == owner).astype(BF16)
    spread = mm(pick, v_ref[...])
    want = (iota((rows, toks), 0) % cap + 1).astype(F32)
    return pick, spread == want


def prep_kernel(reps, cap, nd_ref, nr_ref, q_ref, slots_ref, code_ref, v_ref, row_ref):
    step = pl.program_id(0)
    negs, toks = nd_ref.shape
    devices = v_ref.shape[0]

    @pl.when(step == 0)
    def _():
        dev = iota((devices, toks), 0)
        named = jnp.zeros((devices, toks), F32)
        rows = jnp.zeros((devices, toks), F32)
        for k in range(negs):
            hit = dev == nd_ref[k : k + 1, :]
            named = named + jnp.where(hit, 1.0, 0.0)
            rows = rows + jnp.where(hit, (nr_ref[k : k + 1, :] + 1).astype(F32), 0.0)
        before = (iota((toks, toks), 0) < iota((toks, toks), 1)).astype(BF16)
        rank = mm(named.astype(BF16), before)
        v_ref[...] = (named * (rank + 1.0)).astype(BF16)
        row_ref[...] = rows.astype(BF16)

    pick, hit = slot_hits(v_ref, step, reps, cap, toks)
    wanted = mm(pick, row_ref[...])
    hot = hit.astype(BF16)
    slots_ref[...] = mm(hot, q_ref[...]).astype(BF16).reshape(slots_ref.shape)
    ids = mm(jnp.ones((8, toks), BF16), jnp.where(hit, wanted, 0.0).astype(BF16), NT)
    tok = mm(iota((8, toks), 1).astype(F32).astype(BF16), hot, NT)
    code = tok * 512.0 + ids
    code_ref[pl.ds(step, 1), :] = code[0:1, :].astype(I32)


def serve_kernel(reps, cap, place_ref, code_ref, p_ref, served_ref):
    toks, width = p_ref.shape[1:]
    level = (place_ref[0] + pl.program_id(0)) % pl.num_programs(0)
    for core in range(2):
        ids = code_ref[pl.ds(2 * level + core, 1), :] & 511
        hot = (iota((toks, reps * cap), 0) + 1 == ids).astype(BF16)
        rows = mm(hot, p_ref[core], TN).astype(BF16).reshape(reps, cap, width)
        served_ref[:, core * cap : (core + 1) * cap, :] = rows


def inside_kernel(temper, p_ref, q_ref, out_ref, top, total):
    step = pl.program_id(0)

    @pl.when(step == 0)
    def _():
        top[...] = jnp.full(top.shape, LOW, F32)
        total[...] = jnp.zeros(total.shape, F32)

    scores = temper * mm(p_ref[...], q_ref[...], NT)
    high = jnp.maximum(top[...], jnp.max(scores, axis=0, keepdims=True))
    total[...] = total[...] * jnp.exp(top[...] - high) + jnp.sum(
        jnp.exp(scores - high), axis=0, keepdims=True
    )
    top[...] = high

    @pl.when(step == pl.num_programs(0) - 1)
    def _():
        out_ref[...] = top[...] + jnp.log(total[...])


def hard_kernel(
    reps, cap, temper, place_ref, code_ref, qr_ref, p_ref, inside_ref,
    hs_ref, part_ref, top, total,
):
    step = pl.program_id(0)
    toks, width = p_ref.shape[1:]
    slots = reps * cap
    level = (place_ref[0] + step) % pl.num_programs(0)
    mine = iota((reps, slots), 1) // cap == iota((reps, slots), 0)

    @pl.when(step == 0)
    def _():
        top[...] = jnp.full(top.shape, LOW, F32)
        total[...] = jnp.zeros(total.shape, F32)

    for core in range(2):
        code = code_ref[pl.ds(2 * level + core, 1), :]
        ids = code & 511
        valid = ids > 0
        asking = qr_ref[:, core * cap : (core + 1) * cap, :].reshape(slots, width)
        cross = mm(p_ref[core], asking, NT)
        hit = iota((toks, slots), 0) + 1 == ids
        hs = temper * jnp.sum(jnp.where(hit, cross, 0.0), axis=0, keepdims=True)
        hs_ref[pl.ds(2 * level + core, 1), :] = hs
        token = ((iota((toks, slots), 0) == code >> 9) & valid).astype(BF16)
        live = mine & valid
        parts = jnp.concatenate([split3(jnp.where(live, hs, 0.0)), live.astype(BF16)], axis=0)
        laid = mm(parts, token, NT)
        there = laid[3 * reps :] > 0.5
        value = laid[:reps] + laid[reps : 2 * reps] + laid[2 * reps : 3 * reps]
        value = jnp.where(there, value, LOW)
        high = jnp.maximum(top[...], value)
        total[...] = total[...] * jnp.exp(top[...] - high) + jnp.where(
            there, jnp.exp(value - high), 0.0
        )
        top[...] = high

    @pl.when(step == pl.num_programs(0) - 1)
    def _():
        part = jnp.where(total[...] > 0.0, top[...] + jnp.log(total[...]), LOW)
        inside = inside_ref[...]
        high = jnp.maximum(part, inside)
        both = high + jnp.log(jnp.exp(part - high) + jnp.exp(inside - high))
        own = iota(part.shape, 0) == place_ref[2]
        part_ref[...] = jnp.where(own, both, part)


def own_row(lt_ref, place_ref):
    lt = lt_ref[...]
    own = iota(lt.shape, 0) == place_ref[2]
    return jnp.sum(jnp.where(own, lt, 0.0), axis=0, keepdims=True)


def grad_kernel(
    reps, cap, temper, own_core, place_ref, code_ref, hs_ref, lt_ref, qr_ref, p_ref, q_ref, gp_ref,
):
    step = pl.program_id(0)
    toks, width = q_ref.shape
    slots = reps * cap
    level = (place_ref[0] + step) % pl.num_programs(0)
    core = place_ref[1] if own_core else 1 - place_ref[1]
    code = code_ref[pl.ds(2 * level + core, 1), :]
    ids = code & 511
    valid = ids > 0
    mine = iota((reps, slots), 1) // cap == iota((reps, slots), 0)
    token = ((iota((toks, slots), 0) == code >> 9) & valid).astype(BF16)
    found = mm(split3(lt_ref[...]), token)
    found = found[:reps] + found[reps : 2 * reps] + found[2 * reps :]
    log_slot = jnp.sum(jnp.where(mine, found, 0.0), axis=0, keepdims=True)
    hs = hs_ref[pl.ds(2 * level + core, 1), :]
    d_hard = jnp.where(valid, jnp.exp(hs - log_slot), 0.0)
    hard = jnp.where(iota((toks, slots), 0) + 1 == ids, d_hard, 0.0).astype(BF16)
    queries = q_ref[...]
    scores = temper * mm(p_ref[0], queries, NT)
    d_scores = jnp.exp(scores - own_row(lt_ref, place_ref))
    if own_core:
        eye = (iota((toks, toks), 0) == iota((toks, toks), 1)) & (step == 0)
        d_scores = d_scores - jnp.where(eye, 1.0, 0.0)
    d_scores = d_scores.astype(BF16)
    asking = qr_ref[...].reshape(slots, width)
    gp_ref[0] = (temper * (mm(hard, asking) + mm(d_scores, queries))).astype(BF16)


def inner_kernel(temper, place_ref, lt_ref, p_ref, q_ref, gq_ref, loss_ref, acc):
    step = pl.program_id(0)
    toks, width = q_ref.shape
    lt_own = own_row(lt_ref, place_ref)
    passages = p_ref[...]
    scores = temper * mm(passages, q_ref[...], NT)
    row = iota(scores.shape, 0) - toks * place_ref[1]
    eye = (row == iota(scores.shape, 1)) & (step == 0)
    d_scores = (jnp.exp(scores - lt_own) - jnp.where(eye, 1.0, 0.0)).astype(BF16)
    new = mm(d_scores, passages, TN)

    @pl.when(step == 0)
    def _():
        acc[...] = new
        loss_ref[...] = lt_own - jnp.sum(jnp.where(eye, scores, 0.0), axis=0, keepdims=True)

    @pl.when(step > 0)
    def _():
        acc[...] += new

    @pl.when(step == pl.num_programs(0) - 1)
    def _():
        gq_ref[...] = acc[...]


def final_kernel(reps, cap, temper, place_ref, v_ref, lt_ref, f_ref, q_ref, gq_ref, out_ref, acc):
    step = pl.program_id(0)
    toks, width = q_ref.shape
    _, hit = slot_hits(v_ref, step, reps, cap, toks)
    fetched = f_ref[...].reshape(2 * reps * cap, width)
    scores = temper * mm(fetched, q_ref[...], NT)
    d_hard = jnp.where(hit, jnp.exp(scores - own_row(lt_ref, place_ref)), 0.0).astype(BF16)
    new = mm(d_hard, fetched, TN)

    @pl.when(step == 0)
    def _():
        acc[...] = gq_ref[...] + new

    @pl.when(step > 0)
    def _():
        acc[...] += new

    @pl.when(step == pl.num_programs(0) - 1)
    def _():
        out_ref[...] = (temper * acc[...]).astype(BF16)


def full(shape):
    return pl.BlockSpec(shape, lambda *_: (0,) * len(shape))


def log_add_over_rep(part, reps):
    step = 1
    while step < reps:
        other = lax.ppermute(part, "rep", [(i, i ^ step) for i in range(reps)])
        part = jnp.maximum(part, other) + jnp.log1p(jnp.exp(-jnp.abs(part - other)))
        step *= 2
    return part


def codes_over_rep(code, reps, me):
    table = code[None]
    step = 1
    while step < reps:
        other = lax.ppermute(table, "rep", [(i, i ^ step) for i in range(reps)])
        table = jnp.concatenate([table, other], axis=0)
        step *= 2
    meant = jnp.sum(jnp.where((jnp.arange(reps) == me)[None, :, None], table, 0), axis=1)
    order = (jnp.arange(reps)[None, :] ^ me) == jnp.arange(reps)[:, None]
    return jnp.sum(jnp.where(order[:, :, None], meant[None], 0), axis=1)


def along_z(x, shift, groups):
    return lax.ppermute(
        x, "grp", [(i, (i + 2 * shift) % groups) for i in range(groups)]
    )


def other_core(x, groups):
    return lax.ppermute(x, "grp", [(i, i ^ 1) for i in range(groups)])


def gather_group(block, core, groups):
    half = block.shape[0] // 2
    below = along_z(block, 1, groups)
    above = along_z(block, -1, groups)
    far = jnp.concatenate(
        [along_z(below[:half], 1, groups), along_z(above[half:], -1, groups)], axis=0
    )
    own = jnp.stack([block, above, far, below])
    theirs = other_core(own, groups)
    first = core == 0
    return jnp.stack([jnp.where(first, own, theirs), jnp.where(first, theirs, own)], axis=1)


def scatter_group(own, other, groups):
    half = own.shape[1] // 2
    whole = own.astype(F32) + other_core(other, groups).astype(F32)
    up = along_z(whole[2, :half].astype(BF16), 1, groups).astype(F32)
    down = along_z(whole[2, half:].astype(BF16), -1, groups).astype(F32)
    to_above = jnp.concatenate([whole[1, :half] + up, whole[1, half:]], axis=0)
    to_below = jnp.concatenate([whole[3, :half], whole[3, half:] + down], axis=0)
    from_below = along_z(to_above.astype(BF16), 1, groups).astype(F32)
    from_above = along_z(to_below.astype(BF16), -1, groups).astype(F32)
    return (whole[0] + from_below + from_above).astype(BF16)


def shards(queries, passages, neg_device, neg_row):
    toks, width = queries.shape
    negs = neg_device.shape[1]
    groups = lax.axis_size("grp")
    reps = lax.axis_size("rep")
    devices = groups * reps
    levels = groups // 2
    cap = 8 * toks // devices
    slots = reps * cap
    temper = 3.0 / math.sqrt(width)
    me = lax.axis_index("rep")
    core = lax.axis_index("grp") % 2
    place = jnp.stack([lax.axis_index("grp") // 2, core, me]).astype(I32)
    block = jax.ShapeDtypeStruct((toks, width), BF16)
    slot_shape = jax.ShapeDtypeStruct((reps, groups * cap, width), BF16)
    pair = (reps, 2 * cap, width)

    def rows(*shape):
        return jax.ShapeDtypeStruct(shape, F32)

    def call(kernel, name, ins, outs, shapes, scratch, weight, prefetch):
        return pl.pallas_call(
            kernel,
            grid_spec=pltpu.PrefetchScalarGridSpec(
                num_scalar_prefetch=int(prefetch),
                grid=(levels,),
                in_specs=ins,
                out_specs=outs,
                scratch_shapes=scratch,
            ),
            out_shape=shapes,
            compiler_params=pltpu.CompilerParams(
                dimension_semantics=("arbitrary",), vmem_limit_bytes=VMEM_LIMIT
            ),
            cost_estimate=pl.CostEstimate(
                flops=weight, bytes_accessed=1 << 16, transcendentals=0
            ),
            name=name,
        )

    light, heavy = 1 << 20, 1 << 39

    slot_queries, code, ranks = call(
        functools.partial(prep_kernel, reps, cap), "prep",
        [full((negs, toks)), full((negs, toks)), full((toks, width))],
        [pl.BlockSpec(pair, lambda s: (0, s, 0)), full((levels, 2 * slots)), full((devices, toks))],
        [slot_shape, jax.ShapeDtypeStruct((levels, 2 * slots), I32),
         jax.ShapeDtypeStruct((devices, toks), BF16)],
        [pltpu.VMEM((devices, toks), BF16)], light, False,
    )(neg_device.T, neg_row.T, queries)

    asking = lax.all_to_all(slot_queries, "rep", split_axis=0, concat_axis=0, tiled=True)

    code = code.reshape(levels, reps, 2 * cap).transpose(1, 0, 2).reshape(reps, groups * cap)
    asked = codes_over_rep(code, reps, me)
    asked = asked.reshape(reps, groups, cap).transpose(1, 0, 2).reshape(groups, slots)
    gathered = gather_group(passages, core, groups)

    by_level = pl.BlockSpec((1, 2, toks, width), lambda s, *_: (s, 0, 0, 0))
    pair_block = pl.BlockSpec((None, 2, toks, width), lambda s, *_: (s, 0, 0, 0))
    flat_pair = pl.BlockSpec((2 * toks, width), lambda s, *_: (s, 0))
    slot_pair = pl.BlockSpec(pair, lambda s, place: (0, (place[0] + s) % levels, 0))
    flat = gathered.reshape(groups * toks, width)

    served = call(
        functools.partial(serve_kernel, reps, cap), "serve",
        [full((groups, slots)), pair_block], slot_pair, slot_shape, [], light, True,
    )(place, asked, gathered)

    inside = call(
        functools.partial(inside_kernel, temper), "inside",
        [flat_pair, full((toks, width))], full((1, toks)), rows(1, toks),
        [pltpu.VMEM((1, toks), F32), pltpu.VMEM((1, toks), F32)], light, False,
    )(flat, queries)

    fetched = lax.all_to_all(served, "rep", split_axis=0, concat_axis=0, tiled=True)

    hard_scores, part = call(
        functools.partial(hard_kernel, reps, cap, temper), "hard",
        [full((groups, slots)), slot_pair, pair_block, full((1, toks))],
        [full((groups, slots)), full((reps, toks))],
        [rows(groups, slots), rows(reps, toks)],
        [pltpu.VMEM((reps, toks), F32), pltpu.VMEM((reps, toks), F32)], light, True,
    )(place, asked, asking, gathered, inside)

    log_total = log_add_over_rep(part, reps)

    def column(own_core):
        def which(place):
            return place[1] if own_core else 1 - place[1]

        return call(
            functools.partial(grad_kernel, reps, cap, temper, own_core),
            "own" if own_core else "other",
            [full((groups, slots)), full((groups, slots)), full((reps, toks)),
             pl.BlockSpec((reps, cap, width),
                          lambda s, place: (0, 2 * ((place[0] + s) % levels) + which(place), 0)),
             pl.BlockSpec((None, 1, toks, width), lambda s, place: (s, which(place), 0, 0)),
             full((toks, width))],
            pl.BlockSpec((1, toks, width), lambda s, place: (s, 0, 0)),
            jax.ShapeDtypeStruct((levels, toks, width), BF16), [], light, True,
        )(place, asked, hard_scores, log_total, asking, gathered, queries)

    other = column(False)
    own = column(True)
    grad_passages = scatter_group(own, other, groups)

    inner, losses = call(
        functools.partial(inner_kernel, temper), "inner",
        [full((reps, toks)), flat_pair, full((toks, width))],
        [full((toks, width)), full((1, toks))], [rows(toks, width), rows(1, toks)],
        [pltpu.VMEM((toks, width), F32)], light, True,
    )(place, log_total, flat, queries)

    grad_queries = call(
        functools.partial(final_kernel, reps, cap, temper), "final",
        [full((devices, toks)), full((reps, toks)),
         pl.BlockSpec(pair, lambda s, place: (0, s, 0)),
         full((toks, width)), full((toks, width))],
        full((toks, width)), block, [pltpu.VMEM((toks, width), F32)], heavy, True,
    )(place, ranks, log_total, fetched, queries, inner)
    return (losses.reshape(toks), grad_queries, grad_passages)


def solution(mesh):
    in_specs = (
        P(("grp", "rep"), None),
        P(("grp", "rep"), None),
        P(("grp", "rep"), None),
        P(("grp", "rep"), None),
    )
    out_specs = (P(("grp", "rep")), P(("grp", "rep"), None), P(("grp", "rep"), None))
    return jax.shard_map(shards, mesh=mesh, in_specs=in_specs, out_specs=out_specs, check_vma=False)
```

time: 278 us -> 234 us (0.84)
  the two profiles are of different devices: /device:TPU:0 before, /device:TPU:12 now
where the time goes in v2:
time: 234 us; the launch traced here: 233 us
  waiting for transfers between devices  116 us (50%)
  Pallas kernels  57.8 us (25%)
  starting transfers between devices  39.2 us (17%)
  other arithmetic  18.1 us (8%)
    ppermute x4, waiting for transfers between devices, log_add_over_rep(): other = lax.ppermute(part, 'rep', [(i, i ^ step) for i in range(reps)])  59.3 us
    ppermute x4, waiting for transfers between devices, codes_over_rep(): other = lax.ppermute(table, 'rep', [(i, i ^ step) for i in range(reps)])  37.8 us
    ppermute x8, waiting for transfers between devices, along_z(): lax.ppermute(x, 'grp', [(i, (i + 2 * shift) % groups) for i in range(grou...  18.4 us
    ppermute x8, starting transfers between devices, along_z(): lax.ppermute(x, 'grp', [(i, (i + 2 * shift) % groups) for i in range(grou...  15.1 us
    pallas_call x2, Pallas kernels, column(): call(functools.partial(grad_kernel, reps, cap, temper, own_core), 'own' i...  14.7 us
    pallas_call x1, Pallas kernels, shards(): call(functools.partial(final_kernel, reps, cap, temper), 'final', [full((...  9.34 us
    pallas_call x1, Pallas kernels, shards(): call(functools.partial(inner_kernel, temper), 'inner', [full((reps, toks)...  9.19 us
    pallas_call x1, Pallas kernels, shards(): call(functools.partial(hard_kernel, reps, cap, temper), 'hard', [full((gr...  7.84 us
  transfers between devices with their start and end apart: 20, of which 11 were waited for; matrix products, arithmetic and copies ran while one was open for 7% of the time, Pallas kernels for 19%

profile of v2, /device:TPU:12, one launch (start us, length us, event | category | flops | bytes accessed | tf_op | source)
XLA Modules:
  0.0 232.6 jit_solution(1260874332528660743)
XLA Ops:
  0.6 5.3 %prep.1 = (bf16[16,128,1024]{2,1,0:T(8,128)(2,1)}, s32[4,512]{1,0:T(4,128)}, bf16[128,256]{1,0:T(8,128)(2,1)}) custom-call(s32[7,256]{1,0:T(8,128)} %bitcast.60, s32[7,256]{1,0:T(8,128)} %bitcast.61, bf16[256,1024]{1,0:T(8,128)(2,1)} %q_ref.11), custom_call_target="tpu_custom_call" | custom-call | flops 1048576 | bytes 65536 | tf_op jit(solution)/shard_map/prep/pallas_call | solution.py:339
  6.0 7.5 %all-to-all-start = ((bf16[16,128,1024]{2,1,0:T(8,128)(2,1)}), bf16[16,128,1024]{2,1,0:T(8,128)(2,1)}, u32[]{:S(2)}, u32[]{:S(2)}) async-start(bf16[16,128,1024]{2,1,0:T(8,128)(2,1)} %get-tuple-element.11), calls=%async_computation | async-start | bytes 8388608 | tf_op jit(solution)/shard_map/all_to_all | solution.py:348
  13.5 2.0 collective-permute-start.5
  15.4 2.2 collective-permute-start.4
  17.6 11.3 %collective-permute-done.5 = bf16[256,1024]{1,0:T(8,128)(2,1)S(1)} collective-permute-done((bf16[256,1024]{1,0:T(8,128)(2,1)S(1)}, bf16[256,1024]{1,0:T(8,128)(2,1)S(1)}, u32[]{:S(2)}, u32[]{:S(2)}) %collective-permute-start.5) | collective-permute-done | bytes 524320 | tf_op jit(solution)/shard_map/ppermute | solution.py:263
  29.1 3.3 %collective-permute-start.7 = (bf16[128,1024]{1,0:T(8,128)(2,1)S(1)}, bf16[128,1024]{1,0:T(8,128)(2,1)S(1)}, u32[]{:S(2)}, u32[]{:S(2)}) collective-permute-start(bf16[128,1024]{1,0:T(8,128)(2,1)S(1)} %slice.41), channel_id=1, source_target_pairs={{0,96},{16,112},{32,0},{48,16},{64,32},{80,48},{96,64},{112,80},{1... | collective-permute-start | bytes 786440 | tf_op jit(solution)/shard_map/ppermute | solution.py:263
  32.4 4.8 %collective-permute-done.6 = bf16[128,1024]{1,0:T(8,128)(2,1)S(1)} collective-permute-done((bf16[128,1024]{1,0:T(8,128)(2,1)S(1)}, bf16[128,1024]{1,0:T(8,128)(2,1)S(1)}, u32[]{:S(2)}, u32[]{:S(2)}) %collective-permute-start.6) | collective-permute-done | bytes 262176 | tf_op jit(solution)/shard_map/ppermute | solution.py:263
  37.2 1.6 pad_maximum_fusion.1
  39.1 0.6 collective-permute-start
  39.7 0.7 pad_add_fusion.3.place_ref
  40.3 8.3 %collective-permute-done = s32[1,16,128]{2,1,0:T(8,128)S(1)} collective-permute-done((s32[1,16,128]{2,1,0:T(8,128)S(1)}, s32[1,16,128]{2,1,0:T(8,128)S(1)}, u32[]{:S(2)}, u32[]{:S(2)}) %collective-permute-start) | collective-permute-done | bytes 8224 | tf_op jit(solution)/shard_map/ppermute | solution.py:254
  48.6 18.7 %collective-permute-done.1 = s32[2,16,128]{2,1,0:T(8,128)S(1)} collective-permute-done((s32[2,16,128]{2,1,0:T(8,128)S(1)}, s32[2,16,128]{2,1,0:T(8,128)S(1)}, u32[]{:S(2)}, u32[]{:S(2)}) %collective-permute-start.1) | collective-permute-done | bytes 16416 | tf_op jit(solution)/shard_map/ppermute | solution.py:254
  67.4 5.2 %collective-permute-start.2 = (s32[4,16,128]{2,1,0:T(8,128)S(1)}, s32[4,16,128]{2,1,0:T(8,128)S(1)}, u32[]{:S(2)}, u32[]{:S(2)}) collective-permute-start(s32[4,16,128]{2,1,0:T(8,128)S(1)} %pad_add_fusion.1), channel_id=1, source_target_pairs={{0,4},{1,5},{2,6},{3,7},{4,0},{5,1},{6,2},{7,3},{8,12},{9,13},{10,... | collective-permute-start | bytes 98312 | tf_op jit(solution)/shard_map/ppermute | solution.py:254
  72.6 5.3 %collective-permute-done.2 = s32[4,16,128]{2,1,0:T(8,128)S(1)} collective-permute-done((s32[4,16,128]{2,1,0:T(8,128)S(1)}, s32[4,16,128]{2,1,0:T(8,128)S(1)}, u32[]{:S(2)}, u32[]{:S(2)}) %collective-permute-start.2) | collective-permute-done | bytes 32800 | tf_op jit(solution)/shard_map/ppermute | solution.py:254
  77.9 0.3 collective-permute-start.3
  78.2 5.5 %collective-permute-done.3 = s32[8,16,128]{2,1,0:T(8,128)S(1)} collective-permute-done((s32[8,16,128]{2,1,0:T(8,128)S(1)}, s32[8,16,128]{2,1,0:T(8,128)S(1)}, u32[]{:S(2)}, u32[]{:S(2)}) %collective-permute-start.3) | collective-permute-done | bytes 65568 | tf_op jit(solution)/shard_map/ppermute | solution.py:254
  83.7 0.1 select_reduce_fusion.1
  83.8 0.1 select_reduce_fusion
  84.0 0.7 reshape.54.code_ref
  84.7 1.8 select_bitcast_fusion.1
  86.5 2.3 pad_maximum_fusion.p_ref
  88.8 5.0 %inside.1.inside_ref = f32[1,256]{1,0:T(1,128)} custom-call(bf16[2048,1024]{1,0:T(8,128)(2,1)} %bitcast.50, bf16[256,1024]{1,0:T(8,128)(2,1)} %q_ref.11), custom_call_target="tpu_custom_call" | custom-call | flops 1048576 | bytes 65536 | tf_op jit(solution)/shard_map/inside/pallas_call | solution.py:366
  93.8 7.8 %hard.1 = (f32[8,256]{1,0:T(8,128)}, f32[16,256]{1,0:T(8,128)}) custom-call(s32[3]{0:T(128)} %pad_add_fusion.3.place_ref, s32[8,256]{1,0:T(8,128)} %reshape.54.code_ref, bf16[16,128,1024]{2,1,0:T(8,128)(2,1)} %all-to-all-done.qr_ref, bf16[4,2,256,1024]{3,2,1,0:T(8,128)(2,1)} %pad_maximum_fusion.p_ref, f32[1,256]{1,0:T(1,128)} %inside.1.inside_ref), custom_call_target="tpu_custom_call" | custom-call | flops 1048576 | bytes 65536 | tf_op jit(solution)/shard_map/hard/pallas_call | solution.py:374
  101.6 2.9 %collective-permute-start.9 = (f32[16,256]{1,0:T(8,128)}, f32[16,256]{1,0:T(8,128)S(1)}, u32[]{:S(2)}, u32[]{:S(2)}) collective-permute-start(f32[16,256]{1,0:T(8,128)} %get-tuple-element.12), channel_id=1, source_target_pairs={{0,1},{1,0},{2,3},{3,2},{4,5},{5,4},{6,7},{7,6},{8,9},{9,8},{10,11... | collective-permute-start | bytes 49160 | tf_op jit(solution)/shard_map/ppermute | solution.py:244
  104.5 1.9 collective-permute-done.9
  106.5 0.7 log-plus-one_add_fusion.3
  107.2 0.1 collective-permute-start.10
  107.3 5.2 %collective-permute-done.10 = f32[16,256]{1,0:T(8,128)S(1)} collective-permute-done((f32[16,256]{1,0:T(8,128)S(1)}, f32[16,256]{1,0:T(8,128)S(1)}, u32[]{:S(2)}, u32[]{:S(2)}) %collective-permute-start.10) | collective-permute-done | bytes 16416 | tf_op jit(solution)/shard_map/ppermute | solution.py:244
  112.6 0.1 collective-permute-start.11
  112.7 6.4 %serve.1 = bf16[16,128,1024]{2,1,0:T(8,128)(2,1)} custom-call(s32[3]{0:T(128)} %pad_add_fusion.3.place_ref, s32[8,256]{1,0:T(8,128)} %reshape.54.code_ref, bf16[4,2,256,1024]{3,2,1,0:T(8,128)(2,1)} %pad_maximum_fusion.p_ref), custom_call_target="tpu_custom_call" | custom-call | flops 1048576 | bytes 65536 | tf_op jit(solution)/shard_map/serve/pallas_call | solution.py:361
  119.0 6.8 %all-to-all-start.1 = ((bf16[16,128,1024]{2,1,0:T(8,128)(2,1)}), bf16[16,128,1024]{2,1,0:T(8,128)(2,1)}, u32[]{:S(2)}, u32[]{:S(2)}) async-start(bf16[16,128,1024]{2,1,0:T(8,128)(2,1)} %serve.1), calls=%async_computation.1 | async-start | bytes 8388608 | tf_op jit(solution)/shard_map/all_to_all | solution.py:372
  125.9 0.6 collective-permute-start.12
  126.5 52.2 %collective-permute-done.12 = f32[16,256]{1,0:T(8,128)S(1)} collective-permute-done((f32[16,256]{1,0:T(8,128)S(1)}, f32[16,256]{1,0:T(8,128)S(1)}, u32[]{:S(2)}, u32[]{:S(2)}) %collective-permute-start.12) | collective-permute-done | bytes 16416 | tf_op jit(solution)/shard_map/ppermute | solution.py:244
  178.7 0.6 log-plus-one_add_fusion.lt_ref
  179.3 7.3 %other.1 = bf16[4,256,1024]{2,1,0:T(8,128)(2,1)} custom-call(s32[3]{0:T(128)} %pad_add_fusion.3.place_ref, s32[8,256]{1,0:T(8,128)} %reshape.54.code_ref, f32[8,256]{1,0:T(8,128)} %get-tuple-element.16.hs_ref, f32[16,256]{1,0:T(8,128)} %log-plus-one_add_fusion.lt_ref, bf16[16,128,1024]{2,1,0:T(8,128)(2,1)} %all-to-all-done.qr_ref, ...), custom_call_target="tpu_custom_call" | custom-call | flops 1048576 | bytes 65536 | tf_op jit(solution)/shard_map/other/pallas_call | solution.py:388
  186.7 7.4 %own.1 = bf16[4,256,1024]{2,1,0:T(8,128)(2,1)} custom-call(s32[3]{0:T(128)} %pad_add_fusion.3.place_ref, s32[8,256]{1,0:T(8,128)} %reshape.54.code_ref, f32[8,256]{1,0:T(8,128)} %get-tuple-element.16.hs_ref, f32[16,256]{1,0:T(8,128)} %log-plus-one_add_fusion.lt_ref, bf16[16,128,1024]{2,1,0:T(8,128)(2,1)} %all-to-all-done.qr_ref, ...), custom_call_target="tpu_custom_call" | custom-call | flops 1048576 | bytes 65536 | tf_op jit(solution)/shard_map/own/pallas_call | solution.py:388
  194.0 4.6 %fusion.7 = (bf16[4,256,1024]{2,1,0:T(8,128)(2,1)S(1)}, f32[4,256,1024]{2,1,0:T(8,128)}) fusion(bf16[4,256,1024]{2,1,0:T(8,128)(2,1)S(1)} %collective-permute-done.13, bf16[4,256,1024]{2,1,0:T(8,128)(2,1)} %own.1), kind=kLoop, calls=%fused_computation.41 | loop fusion | flops 4194304 | bytes 10485760 | tf_op jit(solution)/shard_map/convert.9
  198.7 1.7 collective-permute-start.14
  200.4 2.6 %collective-permute-start.16 = (bf16[128,1024]{1,0:T(8,128)(2,1)S(1)}, bf16[128,1024]{1,0:T(8,128)(2,1)S(1)}, u32[]{:S(2)}, u32[]{:S(2)}) collective-permute-start(bf16[128,1024]{1,0:T(8,128)(2,1)S(1)} %get-tuple-element.24), channel_id=1, source_target_pairs={{0,96},{16,112},{32,0},{48,16},{64,32},{80,48},{96,64},{112,80},{1... | collective-permute-start | bytes 786440 | tf_op jit(solution)/shard_map/ppermute | solution.py:263
  203.0 9.2 %inner.1 = (f32[256,1024]{1,0:T(8,128)}, f32[1,256]{1,0:T(1,128)}) custom-call(s32[3]{0:T(128)} %pad_add_fusion.3.place_ref, f32[16,256]{1,0:T(8,128)} %log-plus-one_add_fusion.lt_ref, bf16[2048,1024]{1,0:T(8,128)(2,1)} %bitcast.51, bf16[256,1024]{1,0:T(8,128)(2,1)} %q_ref.11), custom_call_target="tpu_custom_call" | custom-call | flops 1048576 | bytes 65536 | tf_op jit(solution)/shard_map/inner/pallas_call | solution.py:404
  212.2 1.3 fusion.6
  213.5 0.8 pad_maximum_fusion.2
  214.4 0.8 pad_maximum_fusion.3
  215.2 3.2 %collective-permute-start.17 = (bf16[256,1024]{1,0:T(8,128)(2,1)}, bf16[256,1024]{1,0:T(8,128)(2,1)}, u32[]{:S(2)}, u32[]{:S(2)}) collective-permute-start(bf16[256,1024]{1,0:T(8,128)(2,1)} %pad_maximum_fusion.3), channel_id=1, source_target_pairs={{0,96},{16,112},{32,0},{48,16},{64,32},{80,48},{96,64},{112,80},{1... | collective-permute-start | bytes 1572872 | tf_op jit(solution)/shard_map/ppermute | solution.py:263
  218.4 9.3 %final.1 = bf16[256,1024]{1,0:T(8,128)(2,1)} custom-call(s32[3]{0:T(128)} %pad_add_fusion.3.place_ref, bf16[128,256]{1,0:T(8,128)(2,1)} %get-tuple-element.14.v_ref, f32[16,256]{1,0:T(8,128)} %log-plus-one_add_fusion.lt_ref, bf16[16,128,1024]{2,1,0:T(8,128)(2,1)} %all-to-all-done.1.f_ref, bf16[256,1024]{1,0:T(8,128)(2,1)} %q_ref.11, ...), custom_call_target="tpu_custom_call" | custom-call | flops 549755813888 | bytes 65536 | tf_op jit(solution)/shard_map/final/pallas_call | solution.py:411
  227.8 2.2 collective-permute-done.15
  230.0 0.1 collective-permute-done.17
  230.1 2.5 %fusion.2 = bf16[256,1024]{1,0:T(8,128)(2,1)} fusion(f32[4,256,1024]{2,1,0:T(8,128)} %get-tuple-element.20, bf16[256,1024]{1,0:T(8,128)(2,1)} %collective-permute-done.17, bf16[256,1024]{1,0:T(8,128)(2,1)} %collective-permute-done.15), kind=kLoop, calls=%fused_computation.8 | loop fusion | flops 1310720 | bytes 2621440 | tf_op jit(solution)/shard_map/convert_element_type | solution.py:294
  (40 shorter events, 0.6 us)
Async XLA Ops:
  6.0 7.5 %copy-start = (bf16[256,1024]{1,0:T(8,128)(2,1)S(1)}, bf16[256,1024]{1,0:T(8,128)(2,1)}, u32[]{:S(2)}) copy-start(bf16[256,1024]{1,0:T(8,128)(2,1)} %param.5) | copy-start | bytes 1572868
  6.0 87.8 %all-to-all-start = ((bf16[16,128,1024]{2,1,0:T(8,128)(2,1)}), bf16[16,128,1024]{2,1,0:T(8,128)(2,1)}, u32[]{:S(2)}, u32[]{:S(2)}) async-start(bf16[16,128,1024]{2,1,0:T(8,128)(2,1)} %get-tuple-element.11), calls=%async_computation | async-start | bytes 8388608 | tf_op jit(solution)/shard_map/all_to_all | solution.py:348
  13.5 15.5 %collective-permute-start.5 = (bf16[256,1024]{1,0:T(8,128)(2,1)S(1)}, bf16[256,1024]{1,0:T(8,128)(2,1)S(1)}, u32[]{:S(2)}, u32[]{:S(2)}) collective-permute-start(bf16[256,1024]{1,0:T(8,128)(2,1)S(1)} %copy-done), channel_id=1, source_target_pairs={{0,32},{16,48},{32,64},{48,80},{64,96},{80,112},{96,0},{112,16},{1... | collective-permute-start | bytes 1572872 | tf_op jit(solution)/shard_map/ppermute | solution.py:263
  15.4 13.6 %collective-permute-start.4 = (bf16[256,1024]{1,0:T(8,128)(2,1)S(1)}, bf16[256,1024]{1,0:T(8,128)(2,1)S(1)}, u32[]{:S(2)}, u32[]{:S(2)}) collective-permute-start(bf16[256,1024]{1,0:T(8,128)(2,1)S(1)} %copy-done), channel_id=1, source_target_pairs={{0,96},{16,112},{32,0},{48,16},{64,32},{80,48},{96,64},{112,80},{1... | collective-permute-start | bytes 1572872 | tf_op jit(solution)/shard_map/ppermute | solution.py:263
  29.0 8.2 %collective-permute-start.6 = (bf16[128,1024]{1,0:T(8,128)(2,1)S(1)}, bf16[128,1024]{1,0:T(8,128)(2,1)S(1)}, u32[]{:S(2)}, u32[]{:S(2)}) collective-permute-start(bf16[128,1024]{1,0:T(8,128)(2,1)S(1)} %slice.40), channel_id=1, source_target_pairs={{0,32},{16,48},{32,64},{48,80},{64,96},{80,112},{96,0},{112,16},{1... | collective-permute-start | bytes 786440 | tf_op jit(solution)/shard_map/ppermute | solution.py:263
  29.1 8.1 %collective-permute-start.7 = (bf16[128,1024]{1,0:T(8,128)(2,1)S(1)}, bf16[128,1024]{1,0:T(8,128)(2,1)S(1)}, u32[]{:S(2)}, u32[]{:S(2)}) collective-permute-start(bf16[128,1024]{1,0:T(8,128)(2,1)S(1)} %slice.41), channel_id=1, source_target_pairs={{0,96},{16,112},{32,0},{48,16},{64,32},{80,48},{96,64},{112,80},{1... | collective-permute-start | bytes 786440 | tf_op jit(solution)/shard_map/ppermute | solution.py:263
  37.2 1.6 copy-start.1
  38.9 45.8 %collective-permute-start.8 = (bf16[4,256,1024]{2,1,0:T(8,128)(2,1)}, bf16[4,256,1024]{2,1,0:T(8,128)(2,1)}, u32[]{:S(2)}, u32[]{:S(2)}) collective-permute-start(bf16[4,256,1024]{2,1,0:T(8,128)(2,1)} %pad_maximum_fusion.1), channel_id=1, source_target_pairs={{0,16},{16,0},{32,48},{48,32},{64,80},{80,64},{96,112},{112,96},{1... | collective-permute-start | bytes 6291464 | tf_op jit(solution)/shard_map/ppermute | solution.py:269
  39.1 9.6 %collective-permute-start = (s32[1,16,128]{2,1,0:T(8,128)S(1)}, s32[1,16,128]{2,1,0:T(8,128)S(1)}, u32[]{:S(2)}, u32[]{:S(2)}) collective-permute-start(s32[1,16,128]{2,1,0:T(8,128)S(1)} %broadcast_in_dim_reshape.3), channel_id=1, source_target_pairs={{0,1},{1,0},{2,3},{3,2},{4,5},{5,4},{6,7},{7,6},{8,9},{9,8},{10,11... | collective-permute-start | bytes 24584 | tf_op jit(solution)/shard_map/ppermute | solution.py:254
  48.6 18.7 %collective-permute-start.1 = (s32[2,16,128]{2,1,0:T(8,128)S(1)}, s32[2,16,128]{2,1,0:T(8,128)S(1)}, u32[]{:S(2)}, u32[]{:S(2)}) collective-permute-start(s32[2,16,128]{2,1,0:T(8,128)S(1)} %pad_add_fusion.2), channel_id=1, source_target_pairs={{0,2},{1,3},{2,0},{3,1},{4,6},{5,7},{6,4},{7,5},{8,10},{9,11},{10,... | collective-permute-start | bytes 49160 | tf_op jit(solution)/shard_map/ppermute | solution.py:254
  67.4 10.5 %collective-permute-start.2 = (s32[4,16,128]{2,1,0:T(8,128)S(1)}, s32[4,16,128]{2,1,0:T(8,128)S(1)}, u32[]{:S(2)}, u32[]{:S(2)}) collective-permute-start(s32[4,16,128]{2,1,0:T(8,128)S(1)} %pad_add_fusion.1), channel_id=1, source_target_pairs={{0,4},{1,5},{2,6},{3,7},{4,0},{5,1},{6,2},{7,3},{8,12},{9,13},{10,... | collective-permute-start | bytes 98312 | tf_op jit(solution)/shard_map/ppermute | solution.py:254
  77.9 5.8 %collective-permute-start.3 = (s32[8,16,128]{2,1,0:T(8,128)S(1)}, s32[8,16,128]{2,1,0:T(8,128)S(1)}, u32[]{:S(2)}, u32[]{:S(2)}) collective-permute-start(s32[8,16,128]{2,1,0:T(8,128)S(1)} %pad_add_fusion), channel_id=1, source_target_pairs={{0,8},{1,9},{2,10},{3,11},{4,12},{5,13},{6,14},{7,15},{8,0},{9,1},... | collective-permute-start | bytes 196616 | tf_op jit(solution)/shard_map/ppermute | solution.py:254
  101.6 4.8 %collective-permute-start.9 = (f32[16,256]{1,0:T(8,128)}, f32[16,256]{1,0:T(8,128)S(1)}, u32[]{:S(2)}, u32[]{:S(2)}) collective-permute-start(f32[16,256]{1,0:T(8,128)} %get-tuple-element.12), channel_id=1, source_target_pairs={{0,1},{1,0},{2,3},{3,2},{4,5},{5,4},{6,7},{7,6},{8,9},{9,8},{10,11... | collective-permute-start | bytes 49160 | tf_op jit(solution)/shard_map/ppermute | solution.py:244
  107.2 5.3 %collective-permute-start.10 = (f32[16,256]{1,0:T(8,128)S(1)}, f32[16,256]{1,0:T(8,128)S(1)}, u32[]{:S(2)}, u32[]{:S(2)}) collective-permute-start(f32[16,256]{1,0:T(8,128)S(1)} %log-plus-one_add_fusion.3), channel_id=1, source_target_pairs={{0,2},{1,3},{2,0},{3,1},{4,6},{5,7},{6,4},{7,5},{8,10},{9,11},{10,... | collective-permute-start | bytes 49160 | tf_op jit(solution)/shard_map/ppermute | solution.py:244
  112.6 13.3 %collective-permute-start.11 = (f32[16,256]{1,0:T(8,128)S(1)}, f32[16,256]{1,0:T(8,128)S(1)}, u32[]{:S(2)}, u32[]{:S(2)}) collective-permute-start(f32[16,256]{1,0:T(8,128)S(1)} %log-plus-one_add_fusion.2), channel_id=1, source_target_pairs={{0,4},{1,5},{2,6},{3,7},{4,0},{5,1},{6,2},{7,3},{8,12},{9,13},{10,... | collective-permute-start | bytes 49160 | tf_op jit(solution)/shard_map/ppermute | solution.py:244
  119.0 99.4 %all-to-all-start.1 = ((bf16[16,128,1024]{2,1,0:T(8,128)(2,1)}), bf16[16,128,1024]{2,1,0:T(8,128)(2,1)}, u32[]{:S(2)}, u32[]{:S(2)}) async-start(bf16[16,128,1024]{2,1,0:T(8,128)(2,1)} %serve.1), calls=%async_computation.1 | async-start | bytes 8388608 | tf_op jit(solution)/shard_map/all_to_all | solution.py:372
  125.9 52.8 %collective-permute-start.12 = (f32[16,256]{1,0:T(8,128)S(1)}, f32[16,256]{1,0:T(8,128)S(1)}, u32[]{:S(2)}, u32[]{:S(2)}) collective-permute-start(f32[16,256]{1,0:T(8,128)S(1)} %log-plus-one_add_fusion.1), channel_id=1, source_target_pairs={{0,8},{1,9},{2,10},{3,11},{4,12},{5,13},{6,14},{7,15},{8,0},{9,1},... | collective-permute-start | bytes 49160 | tf_op jit(solution)/shard_map/ppermute | solution.py:244
  186.7 7.4 %collective-permute-start.13 = (bf16[4,256,1024]{2,1,0:T(8,128)(2,1)}, bf16[4,256,1024]{2,1,0:T(8,128)(2,1)S(1)}, u32[]{:S(2)}, u32[]{:S(2)}) collective-permute-start(bf16[4,256,1024]{2,1,0:T(8,128)(2,1)} %other.1), channel_id=1, source_target_pairs={{0,16},{16,0},{32,48},{48,32},{64,80},{80,64},{96,112},{112,96},{1... | collective-permute-start | bytes 6291464 | tf_op jit(solution)/shard_map/ppermute | solution.py:269
  198.7 13.5 %collective-permute-start.14 = (bf16[128,1024]{1,0:T(8,128)(2,1)S(1)}, bf16[128,1024]{1,0:T(8,128)(2,1)S(1)}, u32[]{:S(2)}, u32[]{:S(2)}) collective-permute-start(bf16[128,1024]{1,0:T(8,128)(2,1)S(1)} %get-tuple-element.23), channel_id=1, source_target_pairs={{0,32},{16,48},{32,64},{48,80},{64,96},{80,112},{96,0},{112,16},{1... | collective-permute-start | bytes 786440 | tf_op jit(solution)/shard_map/ppermute | solution.py:263
  200.4 11.8 %collective-permute-start.16 = (bf16[128,1024]{1,0:T(8,128)(2,1)S(1)}, bf16[128,1024]{1,0:T(8,128)(2,1)S(1)}, u32[]{:S(2)}, u32[]{:S(2)}) collective-permute-start(bf16[128,1024]{1,0:T(8,128)(2,1)S(1)} %get-tuple-element.24), channel_id=1, source_target_pairs={{0,96},{16,112},{32,0},{48,16},{64,32},{80,48},{96,64},{112,80},{1... | collective-permute-start | bytes 786440 | tf_op jit(solution)/shard_map/ppermute | solution.py:263
  214.4 15.6 %collective-permute-start.15 = (bf16[256,1024]{1,0:T(8,128)(2,1)}, bf16[256,1024]{1,0:T(8,128)(2,1)}, u32[]{:S(2)}, u32[]{:S(2)}) collective-permute-start(bf16[256,1024]{1,0:T(8,128)(2,1)} %pad_maximum_fusion.2), channel_id=1, source_target_pairs={{0,32},{16,48},{32,64},{48,80},{64,96},{80,112},{96,0},{112,16},{1... | collective-permute-start | bytes 1572872 | tf_op jit(solution)/shard_map/ppermute | solution.py:263
  215.2 14.9 %collective-permute-start.17 = (bf16[256,1024]{1,0:T(8,128)(2,1)}, bf16[256,1024]{1,0:T(8,128)(2,1)}, u32[]{:S(2)}, u32[]{:S(2)}) collective-permute-start(bf16[256,1024]{1,0:T(8,128)(2,1)} %pad_maximum_fusion.3), channel_id=1, source_target_pairs={{0,96},{16,112},{32,0},{48,16},{64,32},{80,48},{96,64},{112,80},{1... | collective-permute-start | bytes 1572872 | tf_op jit(solution)/shard_map/ppermute | solution.py:263

commit v3 on v2

--- a/solution.py
+++ b/solution.py
@@ -34,21 +34,21 @@
     return jnp.concatenate([a, b, c], axis=0)
 
 
-def slot_hits(v_ref, step, reps, cap, toks):
-    rows = reps * 2 * cap
+def slot_hits(v_ref, group, reps, cap, toks):
+    rows = reps * cap
     devices = v_ref.shape[0]
-    slot = iota((rows, devices), 0)
-    owner = (2 * step + slot // cap % 2) * reps + slot // (2 * cap)
+    owner = group * reps + iota((rows, devices), 0) // cap
     pick = (iota((rows, devices), 1) == owner).astype(BF16)
     spread = mm(pick, v_ref[...])
     want = (iota((rows, toks), 0) % cap + 1).astype(F32)
     return pick, spread == want
 
 
-def prep_kernel(reps, cap, nd_ref, nr_ref, q_ref, slots_ref, code_ref, v_ref, row_ref):
+def prep_kernel(reps, cap, groups, nd_ref, nr_ref, q_ref, slots_ref, v_ref, row_ref, code_ref):
     step = pl.program_id(0)
     negs, toks = nd_ref.shape
     devices = v_ref.shape[0]
+    slots = reps * cap
 
     @pl.when(step == 0)
     def _():
@@ -63,15 +63,42 @@
         rank = mm(named.astype(BF16), before)
         v_ref[...] = (named * (rank + 1.0)).astype(BF16)
         row_ref[...] = rows.astype(BF16)
-
-    pick, hit = slot_hits(v_ref, step, reps, cap, toks)
-    wanted = mm(pick, row_ref[...])
-    hot = hit.astype(BF16)
-    slots_ref[...] = mm(hot, q_ref[...]).astype(BF16).reshape(slots_ref.shape)
-    ids = mm(jnp.ones((8, toks), BF16), jnp.where(hit, wanted, 0.0).astype(BF16), NT)
-    tok = mm(iota((8, toks), 1).astype(F32).astype(BF16), hot, NT)
-    code = tok * 512.0 + ids
-    code_ref[pl.ds(step, 1), :] = code[0:1, :].astype(I32)
+        code_ref[...] = jnp.zeros(code_ref.shape, F32)
+
+    @pl.when(step < groups)
+    def _():
+        pick, hit = slot_hits(v_ref, step, reps, cap, toks)
+        hot = hit.astype(BF16)
+        slots_ref[...] = mm(hot, q_ref[...]).astype(BF16).reshape(slots_ref.shape)
+        wanted = mm(pick, row_ref[...])
+        row = mm(jnp.ones((8, toks), BF16), jnp.where(hit, wanted, 0.0).astype(BF16), NT)
+        tok = mm(iota((8, toks), 1).astype(F32).astype(BF16), hot, NT)
+        place = iota((slots, slots), 0)
+        same = place // cap == iota((slots, slots), 1) // cap
+        spread = jnp.where(same & (place % cap == 0), row[0:1], 0.0)
+        spread = spread + jnp.where(same & (place % cap == 1), tok[0:1], 0.0)
+        lane = iota((slots, groups * cap), 1)
+        to_lane = lane == step * cap + iota((slots, groups * cap), 0) % cap
+        code_ref[...] += mm(spread.astype(BF16), to_lane.astype(BF16))
+
+    @pl.when(step == groups)
+    def _():
+        rest = jnp.zeros((slots, slots_ref.shape[2] - groups * cap), F32)
+        wide = jnp.concatenate([code_ref[...], rest], axis=1)
+        slots_ref[...] = wide.astype(BF16).reshape(slots_ref.shape)
+
+
+def read_codes(ext_ref, group, reps, cap):
+    slots = reps * cap
+    lanes = ext_ref.shape[2]
+    ext = ext_ref[...].reshape(slots, lanes)
+    to_slot = iota((lanes, slots), 0) == group * cap + iota((lanes, slots), 1) % cap
+    laid = mm(ext, to_slot.astype(BF16))
+    place = iota((slots, slots), 0)
+    same = place // cap == iota((slots, slots), 1) // cap
+    ids = jnp.sum(jnp.where(same & (place % cap == 0), laid, 0.0), axis=0, keepdims=True)
+    tok = jnp.sum(jnp.where(same & (place % cap == 1), laid, 0.0), axis=0, keepdims=True)
+    return ids.astype(I32), tok.astype(I32)
 
 
 def serve_kernel(reps, cap, place_ref, code_ref, p_ref, served_ref):
@@ -105,8 +132,8 @@
 
 
 def hard_kernel(
-    reps, cap, temper, place_ref, code_ref, qr_ref, p_ref, inside_ref,
-    hs_ref, part_ref, top, total,
+    reps, cap, temper, place_ref, ext_ref, qr_ref, p_ref, inside_ref,
+    hs_ref, code_ref, part_ref, top, total,
 ):
     step = pl.program_id(0)
     toks, width = p_ref.shape[1:]
@@ -120,15 +147,15 @@
         total[...] = jnp.zeros(total.shape, F32)
 
     for core in range(2):
-        code = code_ref[pl.ds(2 * level + core, 1), :]
-        ids = code & 511
+        ids, tok = read_codes(ext_ref, 2 * level + core, reps, cap)
+        code_ref[pl.ds(2 * level + core, 1), :] = tok * 512 + ids
         valid = ids > 0
         asking = qr_ref[:, core * cap : (core + 1) * cap, :].reshape(slots, width)
         cross = mm(p_ref[core], asking, NT)
         hit = iota((toks, slots), 0) + 1 == ids
         hs = temper * jnp.sum(jnp.where(hit, cross, 0.0), axis=0, keepdims=True)
         hs_ref[pl.ds(2 * level + core, 1), :] = hs
-        token = ((iota((toks, slots), 0) == code >> 9) & valid).astype(BF16)
+        token = ((iota((toks, slots), 0) == tok) & valid).astype(BF16)
         live = mine & valid
         parts = jnp.concatenate([split3(jnp.where(live, hs, 0.0)), live.astype(BF16)], axis=0)
         laid = mm(parts, token, NT)
@@ -148,7 +175,7 @@
         high = jnp.maximum(part, inside)
         both = high + jnp.log(jnp.exp(part - high) + jnp.exp(inside - high))
         own = iota(part.shape, 0) == place_ref[2]
-        part_ref[...] = jnp.where(own, both, part)
+        part_ref[...] = jnp.broadcast_to(jnp.where(own, both, part)[None], part_ref.shape)
 
 
 def own_row(lt_ref, place_ref):
@@ -215,11 +242,13 @@
 def final_kernel(reps, cap, temper, place_ref, v_ref, lt_ref, f_ref, q_ref, gq_ref, out_ref, acc):
     step = pl.program_id(0)
     toks, width = q_ref.shape
-    _, hit = slot_hits(v_ref, step, reps, cap, toks)
-    fetched = f_ref[...].reshape(2 * reps * cap, width)
-    scores = temper * mm(fetched, q_ref[...], NT)
-    d_hard = jnp.where(hit, jnp.exp(scores - own_row(lt_ref, place_ref)), 0.0).astype(BF16)
-    new = mm(d_hard, fetched, TN)
+    new = jnp.zeros((toks, width), F32)
+    for core in range(2):
+        _, hit = slot_hits(v_ref, 2 * step + core, reps, cap, toks)
+        fetched = f_ref[:, core * cap : (core + 1) * cap, :].reshape(reps * cap, width)
+        scores = temper * mm(fetched, q_ref[...], NT)
+        d_hard = jnp.where(hit, jnp.exp(scores - own_row(lt_ref, place_ref)), 0.0).astype(BF16)
+        new = new + mm(d_hard, fetched, TN)
 
     @pl.when(step == 0)
     def _():
@@ -236,27 +265,6 @@
 
 def full(shape):
     return pl.BlockSpec(shape, lambda *_: (0,) * len(shape))
-
-
-def log_add_over_rep(part, reps):
-    step = 1
-    while step < reps:
-        other = lax.ppermute(part, "rep", [(i, i ^ step) for i in range(reps)])
-        part = jnp.maximum(part, other) + jnp.log1p(jnp.exp(-jnp.abs(part - other)))
-        step *= 2
-    return part
-
-
-def codes_over_rep(code, reps, me):
-    table = code[None]
-    step = 1
-    while step < reps:
-        other = lax.ppermute(table, "rep", [(i, i ^ step) for i in range(reps)])
-        table = jnp.concatenate([table, other], axis=0)
-        step *= 2
-    meant = jnp.sum(jnp.where((jnp.arange(reps) == me)[None, :, None], table, 0), axis=1)
-    order = (jnp.arange(reps)[None, :] ^ me) == jnp.arange(reps)[:, None]
-    return jnp.sum(jnp.where(order[:, :, None], meant[None], 0), axis=1)
 
 
 def along_z(x, shift, groups):
@@ -314,12 +322,12 @@
     def rows(*shape):
         return jax.ShapeDtypeStruct(shape, F32)
 
-    def call(kernel, name, ins, outs, shapes, scratch, weight, prefetch):
+    def call(kernel, name, ins, outs, shapes, scratch, weight, prefetch, steps=levels):
         return pl.pallas_call(
             kernel,
             grid_spec=pltpu.PrefetchScalarGridSpec(
                 num_scalar_prefetch=int(prefetch),
-                grid=(levels,),
+                grid=(steps,),
                 in_specs=ins,
                 out_specs=outs,
                 scratch_shapes=scratch,
@@ -336,20 +344,17 @@
 
     light, heavy = 1 << 20, 1 << 39
 
-    slot_queries, code, ranks = call(
-        functools.partial(prep_kernel, reps, cap), "prep",
+    sent, ranks = call(
+        functools.partial(prep_kernel, reps, cap, groups), "prep",
         [full((negs, toks)), full((negs, toks)), full((toks, width))],
-        [pl.BlockSpec(pair, lambda s: (0, s, 0)), full((levels, 2 * slots)), full((devices, toks))],
-        [slot_shape, jax.ShapeDtypeStruct((levels, 2 * slots), I32),
+        [pl.BlockSpec((reps, cap, width), lambda s: (0, s, 0)), full((devices, toks))],
+        [jax.ShapeDtypeStruct((reps, (groups + 1) * cap, width), BF16),
          jax.ShapeDtypeStruct((devices, toks), BF16)],
-        [pltpu.VMEM((devices, toks), BF16)], light, False,
+        [pltpu.VMEM((devices, toks), BF16), pltpu.VMEM((slots, groups * cap), F32)],
+        light, False, groups + 1,
     )(neg_device.T, neg_row.T, queries)
 
-    asking = lax.all_to_all(slot_queries, "rep", split_axis=0, concat_axis=0, tiled=True)
-
-    code = code.reshape(levels, reps, 2 * cap).transpose(1, 0, 2).reshape(reps, groups * cap)
-    asked = codes_over_rep(code, reps, me)
-    asked = asked.reshape(reps, groups, cap).transpose(1, 0, 2).reshape(groups, slots)
+    asking = lax.all_to_all(sent, "rep", split_axis=0, concat_axis=0, tiled=True)
     gathered = gather_group(passages, core, groups)
 
     by_level = pl.BlockSpec((1, 2, toks, width), lambda s, *_: (s, 0, 0, 0))
@@ -358,28 +363,31 @@
     slot_pair = pl.BlockSpec(pair, lambda s, place: (0, (place[0] + s) % levels, 0))
     flat = gathered.reshape(groups * toks, width)
 
-    served = call(
-        functools.partial(serve_kernel, reps, cap), "serve",
-        [full((groups, slots)), pair_block], slot_pair, slot_shape, [], light, True,
-    )(place, asked, gathered)
-
     inside = call(
         functools.partial(inside_kernel, temper), "inside",
         [flat_pair, full((toks, width))], full((1, toks)), rows(1, toks),
         [pltpu.VMEM((1, toks), F32), pltpu.VMEM((1, toks), F32)], light, False,
     )(flat, queries)
 
+    hard_scores, asked, part = call(
+        functools.partial(hard_kernel, reps, cap, temper), "hard",
+        [pl.BlockSpec((reps, cap, groups * cap), lambda s, place: (0, groups, 0)),
+         slot_pair, pair_block, full((1, toks))],
+        [full((groups, slots)), full((groups, slots)), full((reps, reps, toks))],
+        [rows(groups, slots), jax.ShapeDtypeStruct((groups, slots), I32), rows(reps, reps, toks)],
+        [pltpu.VMEM((reps, toks), F32), pltpu.VMEM((reps, toks), F32)], light, True,
+    )(place, asking, asking, gathered, inside)
+
+    parts = lax.all_to_all(part, "rep", split_axis=0, concat_axis=0, tiled=True)
+    high = jnp.max(parts, axis=0)
+    log_total = high + jnp.log(jnp.sum(jnp.exp(parts - high), axis=0))
+
+    served = call(
+        functools.partial(serve_kernel, reps, cap), "serve",
+        [full((groups, slots)), pair_block], slot_pair, slot_shape, [], light, True,
+    )(place, asked, gathered)
+
     fetched = lax.all_to_all(served, "rep", split_axis=0, concat_axis=0, tiled=True)
-
-    hard_scores, part = call(
-        functools.partial(hard_kernel, reps, cap, temper), "hard",
-        [full((groups, slots)), slot_pair, pair_block, full((1, toks))],
-        [full((groups, slots)), full((reps, toks))],
-        [rows(groups, slots), rows(reps, toks)],
-        [pltpu.VMEM((reps, toks), F32), pltpu.VMEM((reps, toks), F32)], light, True,
-    )(place, asked, asking, gathered, inside)
-
-    log_total = log_add_over_rep(part, reps)
 
     def column(own_core):
         def which(place):

time: 234 us -> 207 us (0.88)
  the two profiles are of different devices: /device:TPU:12 before, /device:TPU:52 now
where the time goes in v3:
time: 207 us; the launch traced here: 206 us
  waiting for transfers between devices  94.2 us (46%)
  Pallas kernels  61 us (29%)
  starting transfers between devices  24.4 us (12%)
  blocking collectives  13 us (6%)
  other arithmetic  12.3 us (6%)
    all_to_all x1, waiting for transfers between devices, shards(): lax.all_to_all(sent, 'rep', split_axis=0, concat_axis=0, tiled=True)  37.8 us
    ppermute x8, waiting for transfers between devices, along_z(): lax.ppermute(x, 'grp', [(i, (i + 2 * shift) % groups) for i in range(grou...  27.9 us
    all_to_all x1, waiting for transfers between devices, shards(): lax.all_to_all(served, 'rep', split_axis=0, concat_axis=0, tiled=True)  24.5 us
    pallas_call x2, Pallas kernels, column(): call(functools.partial(grad_kernel, reps, cap, temper, own_core), 'own' i...  14.7 us
    all_to_all x1, blocking collectives, shards(): parts = lax.all_to_all(part, 'rep', split_axis=0, concat_axis=0, tiled=True)  13 us
    pallas_call x1, Pallas kernels, shards(): call(functools.partial(inner_kernel, temper), 'inner', [full((reps, toks)...  9.18 us
    ppermute x8, starting transfers between devices, along_z(): lax.ppermute(x, 'grp', [(i, (i + 2 * shift) % groups) for i in range(grou...  9.03 us
    pallas_call x1, Pallas kernels, shards(): call(functools.partial(prep_kernel, reps, cap, groups), 'prep', [full((ne...  8.99 us
  transfers between devices with their start and end apart: 12, of which 10 were waited for; matrix products, arithmetic and copies ran while one was open for 6% of the time, Pallas kernels for 14%

profile of v3, /device:TPU:52, one launch (start us, length us, event | category | flops | bytes accessed | tf_op | source)
XLA Modules:
  0.0 205.7 jit_solution(2604262874933312367)
XLA Ops:
  0.6 9.0 %prep.1 = (bf16[16,144,1024]{2,1,0:T(8,128)(2,1)}, bf16[128,256]{1,0:T(8,128)(2,1)}) custom-call(s32[7,256]{1,0:T(8,128)} %bitcast.54, s32[7,256]{1,0:T(8,128)} %bitcast.55, bf16[256,1024]{1,0:T(8,128)(2,1)} %q_ref.11), custom_call_target="tpu_custom_call" | custom-call | flops 1048576 | bytes 65536 | tf_op jit(solution)/shard_map/prep/pallas_call | solution.py:347
  9.6 0.0 copy-start.1
  9.6 7.4 %all-to-all-start = ((bf16[16,144,1024]{2,1,0:T(8,128)(2,1)}), bf16[16,144,1024]{2,1,0:T(8,128)(2,1)}, u32[]{:S(2)}, u32[]{:S(2)}) async-start(bf16[16,144,1024]{2,1,0:T(8,128)(2,1)} %get-tuple-element.10), calls=%async_computation | async-start | bytes 9437184 | tf_op jit(solution)/shard_map/all_to_all | solution.py:357
  17.0 0.0 copy-done.1
  17.0 1.9 collective-permute-start.1
  18.9 0.2 collective-permute-start
  19.1 11.1 %collective-permute-done.1 = bf16[256,1024]{1,0:T(8,128)(2,1)S(1)} collective-permute-done((bf16[256,1024]{1,0:T(8,128)(2,1)S(1)}, bf16[256,1024]{1,0:T(8,128)(2,1)S(1)}, u32[]{:S(2)}, u32[]{:S(2)}) %collective-permute-start.1) | collective-permute-done | bytes 524320 | tf_op jit(solution)/shard_map/ppermute | solution.py:271
  30.2 1.9 collective-permute-start.2
  32.1 0.0 collective-permute-done
  32.1 0.6 collective-permute-start.3
  32.7 5.0 %collective-permute-done.2 = bf16[128,1024]{1,0:T(8,128)(2,1)S(1)} collective-permute-done((bf16[128,1024]{1,0:T(8,128)(2,1)S(1)}, bf16[128,1024]{1,0:T(8,128)(2,1)S(1)}, u32[]{:S(2)}, u32[]{:S(2)}) %collective-permute-start.2) | collective-permute-done | bytes 262176 | tf_op jit(solution)/shard_map/ppermute | solution.py:271
  37.7 0.9 collective-permute-done.3
  38.6 1.6 pad_maximum_fusion.1
  40.3 0.0 collective-permute-start.4
  40.3 0.6 pad_add_fusion.place_ref
  40.9 3.9 %collective-permute-done.4 = bf16[4,256,1024]{2,1,0:T(8,128)(2,1)} collective-permute-done((bf16[4,256,1024]{2,1,0:T(8,128)(2,1)}, bf16[4,256,1024]{2,1,0:T(8,128)(2,1)}, u32[]{:S(2)}, u32[]{:S(2)}) %collective-permute-start.4) | collective-permute-done | bytes 2097184 | tf_op jit(solution)/shard_map/ppermute | solution.py:277
  44.8 1.8 select_bitcast_fusion.1
  46.5 2.4 %pad_maximum_fusion.p_ref = bf16[4,2,256,1024]{3,2,1,0:T(8,128)(2,1)} fusion(bf16[4,1,256,1024]{3,2,1,0:T(8,128)(2,1)S(1)} %get-tuple-element.22, bf16[4,1,256,1024]{3,2,1,0:T(8,128)(2,1)S(1)} %get-tuple-element.21), kind=kLoop, calls=%fused_computation | loop fusion | flops 2097152 | bytes 8388608 | tf_op jit(solution)/shard_map/stack | solution.py:290
  48.9 5.0 %inside.1.inside_ref = f32[1,256]{1,0:T(1,128)} custom-call(bf16[2048,1024]{1,0:T(8,128)(2,1)} %bitcast.46, bf16[256,1024]{1,0:T(8,128)(2,1)} %q_ref.11), custom_call_target="tpu_custom_call" | custom-call | flops 1048576 | bytes 65536 | tf_op jit(solution)/shard_map/inside/pallas_call | solution.py:366
  54.0 37.8 %all-to-all-done.ext_ref.qr_ref = bf16[16,144,1024]{2,1,0:T(8,128)(2,1)} async-done(((bf16[16,144,1024]{2,1,0:T(8,128)(2,1)}), bf16[16,144,1024]{2,1,0:T(8,128)(2,1)}, u32[]{:S(2)}, u32[]{:S(2)}) %all-to-all-start) | async-done | bytes 4718624 | tf_op jit(solution)/shard_map/all_to_all | solution.py:357
  91.8 8.1 %hard.1 = (f32[8,256]{1,0:T(8,128)}, s32[8,256]{1,0:T(8,128)}, f32[16,16,256]{2,1,0:T(8,128)}) custom-call(s32[3]{0:T(128)} %pad_add_fusion.place_ref, bf16[16,144,1024]{2,1,0:T(8,128)(2,1)} %all-to-all-done.ext_ref.qr_ref, bf16[16,144,1024]{2,1,0:T(8,128)(2,1)} %all-to-all-done.ext_ref.qr_ref, bf16[4,2,256,1024]{3,2,1,0:T(8,128)(2,1)} %pad_maximum_fusion.p_ref, ...), custom_call_target="tpu_custom_call" | custom-call | flops 1048576 | bytes 65536 | tf_op jit(solution)/shard_map/hard/pallas_call | solution.py:372
  99.9 13.0 %all_to_all.15 = f32[16,16,256]{2,1,0:T(8,128)S(1)} all-to-all(f32[16,16,256]{2,1,0:T(8,128)} %get-tuple-element.11), channel_id=1, replica_groups=mesh['grp'=8,'rep'=16] {'rep'}, dimensions={0} | all-to-all | bytes 524288 | tf_op jit(solution)/shard_map/all_to_all | solution.py:381
  113.0 0.1 exponential_reduce_fusion
  113.0 0.6 log_add_fusion.lt_ref
  113.6 7.3 %other.1 = bf16[4,256,1024]{2,1,0:T(8,128)(2,1)} custom-call(s32[3]{0:T(128)} %pad_add_fusion.place_ref, s32[8,256]{1,0:T(8,128)} %get-tuple-element.14.code_ref, f32[8,256]{1,0:T(8,128)} %get-tuple-element.16.hs_ref, f32[16,256]{1,0:T(8,128)} %log_add_fusion.lt_ref, bf16[16,144,1024]{2,1,0:T(8,128)(2,1)} %all-to-all-done.ext_ref.qr_ref, ...), custom_call_target="tpu_custom_call" | custom-call | flops 1048576 | bytes 65536 | tf_op jit(solution)/shard_map/other/pallas_call | solution.py:396
  121.0 0.0 collective-permute-start.5
  121.0 6.3 %serve.1 = bf16[16,128,1024]{2,1,0:T(8,128)(2,1)} custom-call(s32[3]{0:T(128)} %pad_add_fusion.place_ref, s32[8,256]{1,0:T(8,128)} %get-tuple-element.14.code_ref, bf16[4,2,256,1024]{3,2,1,0:T(8,128)(2,1)} %pad_maximum_fusion.p_ref), custom_call_target="tpu_custom_call" | custom-call | flops 1048576 | bytes 65536 | tf_op jit(solution)/shard_map/serve/pallas_call | solution.py:385
  127.3 8.0 %all-to-all-start.2 = ((bf16[16,128,1024]{2,1,0:T(8,128)(2,1)}), bf16[16,128,1024]{2,1,0:T(8,128)(2,1)}, u32[]{:S(2)}, u32[]{:S(2)}) async-start(bf16[16,128,1024]{2,1,0:T(8,128)(2,1)} %serve.1), calls=%async_computation.2 | async-start | bytes 8388608 | tf_op jit(solution)/shard_map/all_to_all | solution.py:390
  135.3 7.4 %own.1 = bf16[4,256,1024]{2,1,0:T(8,128)(2,1)} custom-call(s32[3]{0:T(128)} %pad_add_fusion.place_ref, s32[8,256]{1,0:T(8,128)} %get-tuple-element.14.code_ref, f32[8,256]{1,0:T(8,128)} %get-tuple-element.16.hs_ref, f32[16,256]{1,0:T(8,128)} %log_add_fusion.lt_ref, bf16[16,144,1024]{2,1,0:T(8,128)(2,1)} %all-to-all-done.ext_ref.qr_ref, ...), custom_call_target="tpu_custom_call" | custom-call | flops 1048576 | bytes 65536 | tf_op jit(solution)/shard_map/own/pallas_call | solution.py:396
  142.6 0.0 collective-permute-done.5
  142.6 2.7 %fusion.7 = (bf16[4,256,1024]{2,1,0:T(8,128)(2,1)S(1)}, f32[4,256,1024]{2,1,0:T(8,128)S(1)}) fusion(bf16[4,256,1024]{2,1,0:T(8,128)(2,1)S(1)} %collective-permute-done.5, bf16[4,256,1024]{2,1,0:T(8,128)(2,1)} %own.1), kind=kLoop, calls=%fused_computation.25 | loop fusion | flops 4194304 | bytes 10485760 | tf_op jit(solution)/shard_map/convert.9
  145.3 0.0 copy-start
  145.3 0.1 slice_bitcast_fusion.6
  145.4 1.9 collective-permute-start.6
  147.3 0.2 collective-permute-start.8
  147.5 6.4 %collective-permute-done.6 = bf16[128,1024]{1,0:T(8,128)(2,1)S(1)} collective-permute-done((bf16[128,1024]{1,0:T(8,128)(2,1)S(1)}, bf16[128,1024]{1,0:T(8,128)(2,1)S(1)}, u32[]{:S(2)}, u32[]{:S(2)}) %collective-permute-start.6) | collective-permute-done | bytes 262176 | tf_op jit(solution)/shard_map/ppermute | solution.py:271
  153.9 1.6 collective-permute-done.8
  155.5 0.2 fusion.6
  155.7 0.0 copy-done
  155.7 1.4 collective-permute-start.7
  157.2 0.9 collective-permute-start.9
  158.1 9.2 %inner.1 = (f32[256,1024]{1,0:T(8,128)}, f32[1,256]{1,0:T(1,128)}) custom-call(s32[3]{0:T(128)} %pad_add_fusion.place_ref, f32[16,256]{1,0:T(8,128)} %log_add_fusion.lt_ref, bf16[2048,1024]{1,0:T(8,128)(2,1)} %bitcast.47, bf16[256,1024]{1,0:T(8,128)(2,1)} %q_ref.11), custom_call_target="tpu_custom_call" | custom-call | flops 1048576 | bytes 65536 | tf_op jit(solution)/shard_map/inner/pallas_call | solution.py:412
  167.3 1.5 collective-permute-done.7
  168.8 1.4 collective-permute-done.9
  170.2 2.3 %fusion.2 = bf16[256,1024]{1,0:T(8,128)(2,1)} fusion(f32[4,256,1024]{2,1,0:T(8,128)} %copy-done, bf16[256,1024]{1,0:T(8,128)(2,1)S(1)} %collective-permute-done.9, bf16[256,1024]{1,0:T(8,128)(2,1)S(1)} %collective-permute-done.7), kind=kLoop, calls=%fused_computation.8 | loop fusion | flops 1310720 | bytes 2621440 | tf_op jit(solution)/shard_map/convert_element_type | solution.py:302
  172.5 24.5 %all-to-all-done.2.f_ref = bf16[16,128,1024]{2,1,0:T(8,128)(2,1)} async-done(((bf16[16,128,1024]{2,1,0:T(8,128)(2,1)}), bf16[16,128,1024]{2,1,0:T(8,128)(2,1)}, u32[]{:S(2)}, u32[]{:S(2)}) %all-to-all-start.2) | async-done | bytes 4194336 | tf_op jit(solution)/shard_map/all_to_all | solution.py:390
  197.0 8.7 %final.1 = bf16[256,1024]{1,0:T(8,128)(2,1)} custom-call(s32[3]{0:T(128)} %pad_add_fusion.place_ref, bf16[128,256]{1,0:T(8,128)(2,1)} %get-tuple-element.13.v_ref, f32[16,256]{1,0:T(8,128)} %log_add_fusion.lt_ref, bf16[16,128,1024]{2,1,0:T(8,128)(2,1)} %all-to-all-done.2.f_ref, bf16[256,1024]{1,0:T(8,128)(2,1)} %q_ref.11, f32[256,1024]{1,0:T(8,128)} %get-tuple-element.15.gq_ref), custom_call_target="tpu_custom_call" | custom-call | flops 549755813888 | bytes 65536 | tf_op jit(solution)/shard_map/final/pallas_call | solution.py:419
  (6 shorter events, 0.2 us)
Async XLA Ops:
  9.6 7.4 %copy-start.1 = (bf16[256,1024]{1,0:T(8,128)(2,1)S(1)}, bf16[256,1024]{1,0:T(8,128)(2,1)}, u32[]{:S(2)}) copy-start(bf16[256,1024]{1,0:T(8,128)(2,1)} %param.5) | copy-start | bytes 1572868
  9.6 82.2 %all-to-all-start = ((bf16[16,144,1024]{2,1,0:T(8,128)(2,1)}), bf16[16,144,1024]{2,1,0:T(8,128)(2,1)}, u32[]{:S(2)}, u32[]{:S(2)}) async-start(bf16[16,144,1024]{2,1,0:T(8,128)(2,1)} %get-tuple-element.10), calls=%async_computation | async-start | bytes 9437184 | tf_op jit(solution)/shard_map/all_to_all | solution.py:357
  17.0 13.2 %collective-permute-start.1 = (bf16[256,1024]{1,0:T(8,128)(2,1)S(1)}, bf16[256,1024]{1,0:T(8,128)(2,1)S(1)}, u32[]{:S(2)}, u32[]{:S(2)}) collective-permute-start(bf16[256,1024]{1,0:T(8,128)(2,1)S(1)} %copy-done.1), channel_id=1, source_target_pairs={{0,32},{16,48},{32,64},{48,80},{64,96},{80,112},{96,0},{112,16},{1... | collective-permute-start | bytes 1572872 | tf_op jit(solution)/shard_map/ppermute | solution.py:271
  18.9 13.2 %collective-permute-start = (bf16[256,1024]{1,0:T(8,128)(2,1)S(1)}, bf16[256,1024]{1,0:T(8,128)(2,1)S(1)}, u32[]{:S(2)}, u32[]{:S(2)}) collective-permute-start(bf16[256,1024]{1,0:T(8,128)(2,1)S(1)} %copy-done.1), channel_id=1, source_target_pairs={{0,96},{16,112},{32,0},{48,16},{64,32},{80,48},{96,64},{112,80},{1... | collective-permute-start | bytes 1572872 | tf_op jit(solution)/shard_map/ppermute | solution.py:271
  30.2 7.5 %collective-permute-start.2 = (bf16[128,1024]{1,0:T(8,128)(2,1)S(1)}, bf16[128,1024]{1,0:T(8,128)(2,1)S(1)}, u32[]{:S(2)}, u32[]{:S(2)}) collective-permute-start(bf16[128,1024]{1,0:T(8,128)(2,1)S(1)} %slice.40), channel_id=1, source_target_pairs={{0,32},{16,48},{32,64},{48,80},{64,96},{80,112},{96,0},{112,16},{1... | collective-permute-start | bytes 786440 | tf_op jit(solution)/shard_map/ppermute | solution.py:271
  32.1 6.5 %collective-permute-start.3 = (bf16[128,1024]{1,0:T(8,128)(2,1)S(1)}, bf16[128,1024]{1,0:T(8,128)(2,1)S(1)}, u32[]{:S(2)}, u32[]{:S(2)}) collective-permute-start(bf16[128,1024]{1,0:T(8,128)(2,1)S(1)} %slice.41), channel_id=1, source_target_pairs={{0,96},{16,112},{32,0},{48,16},{64,32},{80,48},{96,64},{112,80},{1... | collective-permute-start | bytes 786440 | tf_op jit(solution)/shard_map/ppermute | solution.py:271
  40.3 4.5 %collective-permute-start.4 = (bf16[4,256,1024]{2,1,0:T(8,128)(2,1)}, bf16[4,256,1024]{2,1,0:T(8,128)(2,1)}, u32[]{:S(2)}, u32[]{:S(2)}) collective-permute-start(bf16[4,256,1024]{2,1,0:T(8,128)(2,1)} %pad_maximum_fusion.1), channel_id=1, source_target_pairs={{0,16},{16,0},{32,48},{48,32},{64,80},{80,64},{96,112},{112,96},{1... | collective-permute-start | bytes 6291464 | tf_op jit(solution)/shard_map/ppermute | solution.py:277
  121.0 21.7 %collective-permute-start.5 = (bf16[4,256,1024]{2,1,0:T(8,128)(2,1)}, bf16[4,256,1024]{2,1,0:T(8,128)(2,1)S(1)}, u32[]{:S(2)}, u32[]{:S(2)}) collective-permute-start(bf16[4,256,1024]{2,1,0:T(8,128)(2,1)} %other.1), channel_id=1, source_target_pairs={{0,16},{16,0},{32,48},{48,32},{64,80},{80,64},{96,112},{112,96},{1... | collective-permute-start | bytes 6291464 | tf_op jit(solution)/shard_map/ppermute | solution.py:277
  127.3 69.7 %all-to-all-start.2 = ((bf16[16,128,1024]{2,1,0:T(8,128)(2,1)}), bf16[16,128,1024]{2,1,0:T(8,128)(2,1)}, u32[]{:S(2)}, u32[]{:S(2)}) async-start(bf16[16,128,1024]{2,1,0:T(8,128)(2,1)} %serve.1), calls=%async_computation.2 | async-start | bytes 8388608 | tf_op jit(solution)/shard_map/all_to_all | solution.py:390
  145.3 10.4 %copy-start = (f32[4,256,1024]{2,1,0:T(8,128)}, f32[4,256,1024]{2,1,0:T(8,128)S(1)}, u32[]{:S(2)}) copy-start(f32[4,256,1024]{2,1,0:T(8,128)S(1)} %get-tuple-element.20) | copy-start | bytes 12582916
  145.4 8.5 %collective-permute-start.6 = (bf16[128,1024]{1,0:T(8,128)(2,1)S(1)}, bf16[128,1024]{1,0:T(8,128)(2,1)S(1)}, u32[]{:S(2)}, u32[]{:S(2)}) collective-permute-start(bf16[128,1024]{1,0:T(8,128)(2,1)S(1)} %get-tuple-element.23), channel_id=1, source_target_pairs={{0,32},{16,48},{32,64},{48,80},{64,96},{80,112},{96,0},{112,16},{1... | collective-permute-start | bytes 786440 | tf_op jit(solution)/shard_map/ppermute | solution.py:271
  147.3 8.2 %collective-permute-start.8 = (bf16[128,1024]{1,0:T(8,128)(2,1)S(1)}, bf16[128,1024]{1,0:T(8,128)(2,1)S(1)}, u32[]{:S(2)}, u32[]{:S(2)}) collective-permute-start(bf16[128,1024]{1,0:T(8,128)(2,1)S(1)} %get-tuple-element.24), channel_id=1, source_target_pairs={{0,96},{16,112},{32,0},{48,16},{64,32},{80,48},{96,64},{112,80},{1... | collective-permute-start | bytes 786440 | tf_op jit(solution)/shard_map/ppermute | solution.py:271
  155.7 13.1 %collective-permute-start.7 = (bf16[256,1024]{1,0:T(8,128)(2,1)S(1)}, bf16[256,1024]{1,0:T(8,128)(2,1)S(1)}, u32[]{:S(2)}, u32[]{:S(2)}) collective-permute-start(bf16[256,1024]{1,0:T(8,128)(2,1)S(1)} %pad_maximum_fusion.2), channel_id=1, source_target_pairs={{0,32},{16,48},{32,64},{48,80},{64,96},{80,112},{96,0},{112,16},{1... | collective-permute-start | bytes 1572872 | tf_op jit(solution)/shard_map/ppermute | solution.py:271
  157.2 13.0 %collective-permute-start.9 = (bf16[256,1024]{1,0:T(8,128)(2,1)S(1)}, bf16[256,1024]{1,0:T(8,128)(2,1)S(1)}, u32[]{:S(2)}, u32[]{:S(2)}) collective-permute-start(bf16[256,1024]{1,0:T(8,128)(2,1)S(1)} %pad_maximum_fusion.3), channel_id=1, source_target_pairs={{0,96},{16,112},{32,0},{48,16},{64,32},{80,48},{96,64},{112,80},{1... | collective-permute-start | bytes 1572872 | tf_op jit(solution)/shard_map/ppermute | solution.py:271

commit v4 on v0

v4 whole, which is shorter than its diff:
```python
import functools
import math

import jax
import jax.numpy as jnp
from jax import lax
from jax.experimental import pallas as pl
from jax.experimental.pallas import tpu as pltpu
from jax.sharding import PartitionSpec as P

F32 = jnp.float32
BF16 = jnp.bfloat16
I32 = jnp.int32
LOW = -1e30
NT = (((1,), (1,)), ((), ()))
TN = (((0,), (0,)), ((), ()))
NN = (((1,), (0,)), ((), ()))
VMEM_LIMIT = 60 * 1024 * 1024


def mm(a, b, dims=NN):
    return lax.dot_general(a, b, dims, preferred_element_type=F32)


def iota(shape, dim):
    return lax.broadcasted_iota(I32, shape, dim)


def split3(x):
    a = x.astype(BF16)
    rest = x - a.astype(F32)
    b = rest.astype(BF16)
    c = (rest - b.astype(F32)).astype(BF16)
    return jnp.concatenate([a, b, c], axis=0)


def full(shape):
    return pl.BlockSpec(shape, lambda *_: (0,) * len(shape))


def call(kernel, name, steps, ins, outs, shapes, scratch, weight):
    return pl.pallas_call(
        kernel,
        grid_spec=pltpu.PrefetchScalarGridSpec(
            num_scalar_prefetch=1, grid=(steps,), in_specs=ins, out_specs=outs,
            scratch_shapes=scratch,
        ),
        out_shape=shapes,
        compiler_params=pltpu.CompilerParams(
            dimension_semantics=("arbitrary",), vmem_limit_bytes=VMEM_LIMIT
        ),
        cost_estimate=pl.CostEstimate(flops=weight, bytes_accessed=1 << 16, transcendentals=0),
        name=name,
    )


LIGHT, MIDDLE, HEAVY = 1 << 20, 1 << 32, 1 << 39
SIDE = 4
CORES = 2


def rep_of(x, y):
    return x % SIDE * SIDE + y % SIDE


def columns_of(place_ref, half, shift):
    x, y = place_ref[2], place_ref[3]
    return rep_of(x, y + shift) if half == 0 else rep_of(x + shift, y)


def source_of(place_ref, half, shift):
    x, y = place_ref[2], place_ref[3]
    return rep_of(x + SIDE - shift, y) if half == 0 else rep_of(x, y + SIDE - shift)


def pick_of(source, groups, cap):
    shape = (groups * cap, SIDE * groups)
    return (iota(shape, 1) == source * groups + iota(shape, 0) // cap).astype(BF16)


def hits_of(pick, ranks, cap):
    spread = mm(pick, ranks)
    return spread == (iota(spread.shape, 0) % cap + 1).astype(F32)


def mid_kernel(shift, cap, groups, reps, negs, place_ref, *refs):
    sources = (refs[0:SIDE], refs[SIDE : 2 * SIDE])
    outs, ranks_out = refs[2 * SIDE : 2 * SIDE + 2], refs[2 * SIDE + 2 :]
    rows, half_width = sources[0][0].shape
    toks = rows - 16
    before = (iota((toks, toks), 0) < iota((toks, toks), 1)).astype(BF16)
    for half in range(2):
        col = columns_of(place_ref, half, shift)
        dev = (iota((groups, toks), 0) * reps + col).astype(F32)
        named_all, rows_all = [], []
        for source in sources[half]:
            table = source[toks:, :toks].astype(F32)
            named = jnp.zeros((groups, toks), F32)
            wanted = jnp.zeros((groups, toks), F32)
            for k in range(negs):
                hit = dev == table[k : k + 1]
                named = named + jnp.where(hit, 1.0, 0.0)
                wanted = wanted + jnp.where(hit, table[8 + k : 9 + k] + 1.0, 0.0)
            named_all.append(named)
            rows_all.append(wanted)
        named = jnp.concatenate(named_all, axis=0)
        wanted = jnp.concatenate(rows_all, axis=0).astype(BF16)
        ranks = (named * (mm(named.astype(BF16), before) + 1.0)).astype(BF16)
        ranks_out[half][...] = ranks
        ids, tok = [], []
        index = iota((8, toks), 1).astype(F32).astype(BF16)
        for s, source in enumerate(sources[half]):
            pick = pick_of(s, groups, cap)
            hit = hits_of(pick, ranks, cap)
            hot = hit.astype(BF16)
            moved = mm(hot, source[:toks, :]).astype(BF16)
            for g in range(groups):
                first = (g * SIDE + s) * cap
                outs[half][first : first + cap, :] = moved[g * cap : (g + 1) * cap]
            row = jnp.where(hit, mm(pick, wanted), 0.0).astype(BF16)
            ids.append(mm(jnp.ones((8, toks), BF16), row, NT)[0:1])
            tok.append(mm(index, hot, NT)[0:1])
        codes = jnp.concatenate(ids + tok, axis=0)
        codes = jnp.concatenate([codes, jnp.zeros_like(codes)], axis=0)
        codes = jnp.concatenate(
            [codes, jnp.zeros((16, half_width - codes.shape[1]), F32)], axis=1
        )
        outs[half][groups * SIDE * cap :, :] = codes.astype(BF16)


def mid(place, shift, first, second, groups, reps, cap, negs):
    rows, half_width = first[0].shape
    slots = jax.ShapeDtypeStruct((groups * SIDE * cap + 16, half_width), BF16)
    ranks = jax.ShapeDtypeStruct((SIDE * groups, rows - 16), BF16)
    return call(
        functools.partial(mid_kernel, shift, cap, groups, reps, negs), "mid", 1,
        [full((rows, half_width))] * (2 * SIDE),
        [full(slots.shape)] * 2 + [full(ranks.shape)] * 2,
        [slots, slots, ranks, ranks], [], LIGHT,
    )(place, *first, *second)


def inside_kernel(temper, place_ref, p_ref, q_ref, out_ref, top, total):
    step = pl.program_id(0)

    @pl.when(step == 0)
    def _():
        top[...] = jnp.full(top.shape, LOW, F32)
        total[...] = jnp.zeros(total.shape, F32)

    scores = temper * mm(p_ref[...], q_ref[...], NT)
    high = jnp.maximum(top[...], jnp.max(scores, axis=0, keepdims=True))
    total[...] = total[...] * jnp.exp(top[...] - high) + jnp.sum(
        jnp.exp(scores - high), axis=0, keepdims=True
    )
    top[...] = high

    @pl.when(step == pl.num_programs(0) - 1)
    def _():
        out_ref[...] = top[...] + jnp.log(total[...])


def inside(place, gathered, queries, temper):
    toks, width = queries.shape
    steps = gathered.shape[0] // (CORES * toks)
    return call(
        functools.partial(inside_kernel, temper), "inside", steps,
        [pl.BlockSpec((CORES * toks, width), lambda s, _: (s, 0)), full((toks, width))],
        full((1, toks)), jax.ShapeDtypeStruct((1, toks), F32),
        [pltpu.VMEM((1, toks), F32), pltpu.VMEM((1, toks), F32)], MIDDLE,
    )(place, gathered, queries)


def asking_rows(first, second, base, cap):
    def piece(ref, s):
        return ref[base + s * cap : base + (s + 1) * cap, :]

    pairs = [(dx, dy) for dx in range(SIDE) for dy in range(SIDE)]
    one = jnp.concatenate([piece(first[dy], dx) for dx, dy in pairs], axis=0)
    two = jnp.concatenate([piece(second[dx], dy) for dx, dy in pairs], axis=0)
    return one, two


def source_mask(place_ref, reps, cap):
    shape = (reps, reps * cap)
    dx = iota(shape, 1) // (SIDE * cap)
    dy = iota(shape, 1) // cap % SIDE
    x = (place_ref[2] + SIDE - dx) % SIDE
    y = (place_ref[3] + SIDE - dy) % SIDE
    return iota(shape, 0) == x * SIDE + y


def hard_kernel(
    reps, cap, temper, place_ref, *refs
):
    first, second, exts = refs[0:4], refs[4:8], refs[8:12]
    p_ref, inside_ref = refs[12:14]
    out_first, out_second = refs[14:18], refs[18:22]
    hs_ref, code_ref, part_ref, top, total = refs[22:]
    step = pl.program_id(0)
    levels = pl.num_programs(0) - 1
    toks = inside_ref.shape[1]
    half_width = p_ref.shape[1] // 2
    slots = reps * cap
    groups = code_ref.shape[0] // 2
    source = source_mask(place_ref, reps, cap)

    @pl.when(step == 0)
    def _():
        top[...] = jnp.full(top.shape, LOW, F32)
        total[...] = jnp.zeros(total.shape, F32)
        table = jnp.concatenate([ext[...] for ext in exts], axis=0)[:, : groups * cap]
        shape = (table.shape[0], slots)
        row = iota(shape, 0)
        dx, dy = iota(shape, 1) // (SIDE * cap), iota(shape, 1) // cap % SIDE
        here = row // 16 == dy
        is_id = here & (row % 16 == dx)
        is_tok = here & (row % 16 == SIDE + dx)
        lane = iota((groups * cap, slots), 0)
        for g in range(groups):
            to_slot = lane == g * cap + iota((groups * cap, slots), 1) % cap
            laid = mm(table, to_slot.astype(BF16))
            ids = jnp.sum(jnp.where(is_id, laid, 0.0), axis=0, keepdims=True)
            tok = jnp.sum(jnp.where(is_tok, laid, 0.0), axis=0, keepdims=True)
            code_ref[g : g + 1, :] = ids.astype(I32)
            code_ref[groups + g : groups + g + 1, :] = tok.astype(I32)

    @pl.when(step < levels)
    def _():
        level = (place_ref[0] + step) % levels
        for core in range(CORES):
            group = CORES * level + core
            ids = code_ref[pl.ds(group, 1), :]
            tok = code_ref[pl.ds(groups + group, 1), :]
            valid = ids > 0
            base = core * SIDE * cap
            one, two = asking_rows(first, second, base, cap)
            passages = p_ref[core * toks : (core + 1) * toks, :]
            cross = mm(passages[:, :half_width], one, NT) + mm(passages[:, half_width:], two, NT)
            hit = iota((toks, slots), 0) + 1 == ids
            hs = temper * jnp.sum(jnp.where(hit, cross, 0.0), axis=0, keepdims=True)
            hs_ref[pl.ds(group, 1), :] = hs
            served = mm(hit.astype(BF16), passages, TN).astype(BF16)
            for dx in range(SIDE):
                for dy in range(SIDE):
                    at = (dx * SIDE + dy) * cap
                    out_first[dy][base + dx * cap : base + (dx + 1) * cap, :] = served[
                        at : at + cap, :half_width
                    ]
                    out_second[dx][base + dy * cap : base + (dy + 1) * cap, :] = served[
                        at : at + cap, half_width:
                    ]
            token = ((iota((toks, slots), 0) == tok) & valid).astype(BF16)
            live = source & valid
            parts = jnp.concatenate(
                [split3(jnp.where(live, hs, 0.0)), live.astype(BF16)], axis=0
            )
            laid = mm(parts, token, NT)
            there = laid[3 * reps :] > 0.5
            value = laid[:reps] + laid[reps : 2 * reps] + laid[2 * reps : 3 * reps]
            value = jnp.where(there, value, LOW)
            high = jnp.maximum(top[...], value)
            total[...] = total[...] * jnp.exp(top[...] - high) + jnp.where(
                there, jnp.exp(value - high), 0.0
            )
            top[...] = high

    @pl.when(step == levels)
    def _():
        part = jnp.where(total[...] > 0.0, top[...] + jnp.log(total[...]), LOW)
        within = inside_ref[...]
        high = jnp.maximum(part, within)
        both = high + jnp.log(jnp.exp(part - high) + jnp.exp(within - high))
        own = iota(part.shape, 0) == rep_of(place_ref[2], place_ref[3])
        part_ref[...] = jnp.broadcast_to(jnp.where(own, both, part)[None], part_ref.shape)
        pieces = split3(hs_ref[...])
        which = pieces.shape[0]
        lanes = groups * cap
        for line in range(SIDE):
            for half, out in ((0, out_first[line]), (1, out_second[line])):
                table = jnp.zeros((16, lanes), F32)
                for s in range(SIDE):
                    dx, dy = (s, line) if half == 0 else (line, s)
                    at = (dx * SIDE + dy) * cap
                    to_lane = (
                        iota((slots, lanes), 0) == at + iota((slots, lanes), 1) % cap
                    ).astype(BF16)
                    laid = mm(pieces, to_lane)
                    keep = iota((which, lanes), 0) % groups == iota((which, lanes), 1) // cap
                    laid = jnp.where(keep, laid, 0.0)
                    to_row = (
                        iota((16, which), 0) == SIDE * (iota((16, which), 1) // groups) + s
                    ).astype(BF16)
                    table = table + mm(to_row, laid.astype(BF16))
                table = jnp.concatenate(
                    [table, jnp.zeros((16, half_width - lanes), F32)], axis=1
                )
                out[0:16, :] = table.astype(BF16)


def hard(place, first, second, gathered, within, temper, reps, cap):
    rows, half_width = first[0].shape
    toks = within.shape[1]
    groups = gathered.shape[0] // toks
    levels = groups // CORES
    slots = reps * cap
    per = CORES * SIDE * cap

    def level(s, place):
        return lax.select(s < levels, (place[0] + s) % levels, (place[0] + levels - 1) % levels)

    ins = pl.BlockSpec((per, half_width), lambda s, place: (level(s, place), 0))
    outs = pl.BlockSpec(
        (per, half_width),
        lambda s, place: (lax.select(s < levels, (place[0] + s) % levels, levels), 0),
    )
    ext = pl.BlockSpec((16, half_width), lambda s, place: (groups * SIDE * cap // 16, 0))
    made = call(
        functools.partial(hard_kernel, reps, cap, temper), "hard", levels + 1,
        [ins] * 8 + [ext] * 4
        + [pl.BlockSpec((CORES * toks, CORES * half_width),
                        lambda s, _: (lax.min(s, levels - 1), 0)), full((1, toks))],
        [outs] * 8 + [full((groups, slots)), full((2 * groups, slots)), full((reps, reps, toks))],
        [jax.ShapeDtypeStruct((rows, half_width), BF16)] * 8
        + [jax.ShapeDtypeStruct((groups, slots), F32),
           jax.ShapeDtypeStruct((2 * groups, slots), I32),
           jax.ShapeDtypeStruct((reps, reps, toks), F32)],
        [pltpu.VMEM((reps, toks), F32), pltpu.VMEM((reps, toks), F32)], LIGHT,
    )(place, *first, *second, *first, gathered, within)
    return made[0:4], made[4:8], made[8], made[9], made[10]


def own_row(lt_ref, rep):
    lt = lt_ref[...]
    return jnp.sum(jnp.where(iota(lt.shape, 0) == rep, lt, 0.0), axis=0, keepdims=True)


def column_kernel(reps, cap, temper, own_core, place_ref, code_ref, hs_ref, lt_ref, *refs):
    first, second = refs[0:4], refs[4:8]
    p_ref, q_ref, gp_ref = refs[8:]
    step = pl.program_id(0)
    toks, width = q_ref.shape
    half_width = width // 2
    slots = reps * cap
    groups = code_ref.shape[0] // 2
    core = place_ref[1] if own_core else 1 - place_ref[1]
    group = CORES * ((place_ref[0] + step) % pl.num_programs(0)) + core
    ids = code_ref[pl.ds(group, 1), :]
    tok = code_ref[pl.ds(groups + group, 1), :]
    valid = ids > 0
    token = ((iota((toks, slots), 0) == tok) & valid).astype(BF16)
    found = mm(split3(lt_ref[...]), token)
    found = found[:reps] + found[reps : 2 * reps] + found[2 * reps :]
    source = source_mask(place_ref, reps, cap)
    log_slot = jnp.sum(jnp.where(source, found, 0.0), axis=0, keepdims=True)
    d_hard = jnp.where(valid, jnp.exp(hs_ref[pl.ds(group, 1), :] - log_slot), 0.0)
    hot = jnp.where(iota((toks, slots), 0) + 1 == ids, d_hard, 0.0).astype(BF16)
    queries = q_ref[...]
    scores = temper * mm(p_ref[...], queries, NT)
    d_scores = jnp.exp(scores - own_row(lt_ref, rep_of(place_ref[2], place_ref[3])))
    if own_core:
        eye = (iota((toks, toks), 0) == iota((toks, toks), 1)) & (step == 0)
        d_scores = d_scores - jnp.where(eye, 1.0, 0.0)
    both = jnp.concatenate([hot, d_scores.astype(BF16)], axis=1)
    one, two = asking_rows(first, second, 0, cap)
    one = jnp.concatenate([one, queries[:, :half_width]], axis=0)
    two = jnp.concatenate([two, queries[:, half_width:]], axis=0)
    gp_ref[0, :, :half_width] = (temper * mm(both, one)).astype(BF16)
    gp_ref[0, :, half_width:] = (temper * mm(both, two)).astype(BF16)


def column(own_core, place, codes, hard_scores, log_total, first, second, gathered, queries,
           temper, cap):
    reps = log_total.shape[0]
    toks, width = queries.shape
    levels = gathered.shape[0] // (CORES * toks)

    def core(place):
        return place[1] if own_core else 1 - place[1]

    slots = pl.BlockSpec(
        (SIDE * cap, width // 2),
        lambda s, place: (CORES * ((place[0] + s) % levels) + core(place), 0),
    )
    return call(
        functools.partial(column_kernel, reps, cap, temper, own_core),
        "own" if own_core else "other", levels,
        [full(codes.shape), full(hard_scores.shape), full(log_total.shape)] + [slots] * 8
        + [pl.BlockSpec((toks, width), lambda s, place: (CORES * s + core(place), 0)),
           full((toks, width))],
        pl.BlockSpec((1, toks, width), lambda s, _: (s, 0, 0)),
        jax.ShapeDtypeStruct((levels, toks, width), BF16), [], LIGHT,
    )(place, codes, hard_scores, log_total, *first, *second, gathered, queries)


def inner_kernel(temper, place_ref, lt_ref, p_ref, q_ref, gq_ref, loss_ref, acc):
    step = pl.program_id(0)
    toks, width = q_ref.shape
    lt_own = own_row(lt_ref, rep_of(place_ref[2], place_ref[3]))
    passages = p_ref[...]
    scores = temper * mm(passages, q_ref[...], NT)
    row = iota(scores.shape, 0) - toks * place_ref[1]
    eye = (row == iota(scores.shape, 1)) & (step == 0)
    d_scores = (jnp.exp(scores - lt_own) - jnp.where(eye, 1.0, 0.0)).astype(BF16)
    new = mm(d_scores, passages, TN)

    @pl.when(step == 0)
    def _():
        acc[...] = new
        loss_ref[...] = lt_own - jnp.sum(jnp.where(eye, scores, 0.0), axis=0, keepdims=True)

    @pl.when(step > 0)
    def _():
        acc[...] += new

    @pl.when(step == pl.num_programs(0) - 1)
    def _():
        gq_ref[...] = acc[...]


def inner(place, log_total, gathered, queries, temper):
    toks, width = queries.shape
    return call(
        functools.partial(inner_kernel, temper), "inner", gathered.shape[0] // (CORES * toks),
        [full(log_total.shape), pl.BlockSpec((CORES * toks, width), lambda s, _: (s, 0)),
         full((toks, width))],
        [full((toks, width)), full((1, toks))],
        [jax.ShapeDtypeStruct((toks, width), F32), jax.ShapeDtypeStruct((1, toks), F32)],
        [pltpu.VMEM((toks, width), F32)], LIGHT,
    )(place, log_total, gathered, queries)


def reduce_kernel(half, cap, groups, place_ref, lt_ref, *refs):
    ranks, rows, outs = refs[0:4], refs[4:8], refs[8:12]
    toks = lt_ref.shape[1]
    slots = groups * cap
    for s in range(SIDE):
        lt = own_row(lt_ref, source_of(place_ref, half, s))
        pick = pick_of(s, groups, cap)
        part = (iota((16, toks), 0) % SIDE == s) & (iota((16, toks), 0) < 3 * SIDE)
        weights, values = [], []
        for line in range(SIDE):
            ext = rows[line][slots * SIDE :, :slots]
            hs = mm(ext, part.astype(BF16), TN)
            hit = hits_of(pick, ranks[line][...], cap)
            weights.append(jnp.where(hit, jnp.exp(hs - lt), 0.0).astype(BF16))
            for g in range(groups):
                at = (g * SIDE + s) * cap
                values.append(rows[line][at : at + cap, :])
        total = mm(jnp.concatenate(weights, axis=0), jnp.concatenate(values, axis=0), TN)
        outs[s][...] = total.astype(outs[s].dtype)


def reduce(place, half, log_total, ranks, rows, groups, cap):
    toks = log_total.shape[1]
    shape = (toks, rows[0].shape[1])
    return call(
        functools.partial(reduce_kernel, half, cap, groups), "reduce", 1,
        [full(log_total.shape)] + [full(ranks[0].shape)] * 4 + [full(rows[0].shape)] * 4,
        [full(shape)] * 4,
        [jax.ShapeDtypeStruct(shape, F32)] + [jax.ShapeDtypeStruct(shape, BF16)] * 3, [], LIGHT,
    )(place, log_total, *ranks, *rows)


def final_kernel(temper, place_ref, gq_ref, *refs):
    out_ref = refs[8]
    half_width = out_ref.shape[1] // 2
    for half in range(2):
        lanes = slice(half * half_width, (half + 1) * half_width)
        total = gq_ref[:, lanes]
        for ref in refs[4 * half : 4 * half + 4]:
            total = total + ref[...].astype(F32)
        out_ref[:, lanes] = (temper * total).astype(BF16)


def final(place, within, first, second, temper):
    shape = within.shape
    return call(
        functools.partial(final_kernel, temper), "final", 1,
        [full(shape)] + [full(first[0].shape)] * 8,
        full(shape), jax.ShapeDtypeStruct(shape, BF16), [], HEAVY,
    )(place, within, *first, *second)


def along_z(x, shift, groups):
    return lax.ppermute(x, "grp", [(i, (i + CORES * shift) % groups) for i in range(groups)])


def other_core(x, groups):
    return lax.ppermute(x, "grp", [(i, i ^ 1) for i in range(groups)])


def along(x, half, shift):
    pairs = []
    for i in range(SIDE * SIDE):
        a, b = i // SIDE, i % SIDE
        pairs.append((i, rep_of(a + shift, b) if half == 0 else rep_of(a, b + shift)))
    return lax.ppermute(x, "rep", pairs)


def gather_group(block, core, groups):
    half = block.shape[0] // 2
    below = along_z(block, 1, groups)
    above = along_z(block, -1, groups)
    far = jnp.concatenate(
        [along_z(below[:half], 1, groups), along_z(above[half:], -1, groups)], axis=0
    )
    own = jnp.stack([block, above, far, below])
    theirs = other_core(own, groups)
    first = core == 0
    return jnp.stack([jnp.where(first, own, theirs), jnp.where(first, theirs, own)], axis=1)


def scatter_group(own, other, groups):
    half = own.shape[1] // 2
    whole = own.astype(F32) + other_core(other, groups).astype(F32)
    up = along_z(whole[2, :half].astype(BF16), 1, groups).astype(F32)
    down = along_z(whole[2, half:].astype(BF16), -1, groups).astype(F32)
    to_above = jnp.concatenate([whole[1, :half] + up, whole[1, half:]], axis=0)
    to_below = jnp.concatenate([whole[3, :half], whole[3, half:] + down], axis=0)
    from_below = along_z(to_above.astype(BF16), 1, groups).astype(F32)
    from_above = along_z(to_below.astype(BF16), -1, groups).astype(F32)
    return (whole[0] + from_below + from_above).astype(BF16)


def shards(queries, passages, neg_device, neg_row):
    toks, width = queries.shape
    negs = neg_device.shape[1]
    groups = lax.axis_size("grp")
    reps = lax.axis_size("rep")
    cap = 8 * toks // (groups * reps)
    half_width = width // 2
    temper = 3.0 / math.sqrt(width)
    grp, rep = lax.axis_index("grp"), lax.axis_index("rep")
    place = jnp.stack([grp // CORES, grp % CORES, rep // SIDE, rep % SIDE]).astype(I32)

    lines = jnp.pad(jnp.stack([neg_device.T, neg_row.T]), ((0, 0), (0, 8 - negs), (0, 0)))
    lines = jnp.pad(lines.reshape(16, toks), ((0, 0), (0, half_width - toks))).astype(BF16)
    sources = []
    for half in range(2):
        block = queries[:, half * half_width : (half + 1) * half_width]
        block = jnp.concatenate([block, lines], axis=0)
        sources.append([block] + [along(block, half, s) for s in range(1, SIDE)])
    gathered = gather_group(passages, grp % CORES, groups).reshape(groups * toks, width)

    first, second, ranks_first, ranks_second = [], [], [], []
    for shift in range(SIDE):
        one, two, rank_one, rank_two = mid(place, shift, *sources, groups, reps, cap, negs)
        first.append(along(one, 1, shift) if shift else one)
        second.append(along(two, 0, shift) if shift else two)
        ranks_first.append(rank_one)
        ranks_second.append(rank_two)

    within = inside(place, gathered, queries, temper)
    back_first, back_second, hard_scores, codes, part = hard(
        place, first, second, gathered, within, temper, reps, cap
    )
    parts = lax.all_to_all(part, "rep", split_axis=0, concat_axis=0, tiled=True)
    parts, back_first, back_second = lax.optimization_barrier((parts, back_first, back_second))
    high = jnp.max(parts, axis=0)
    log_total = high + jnp.log(jnp.sum(jnp.exp(parts - high), axis=0))

    back_first = [along(v, 1, -s) if s else v for s, v in enumerate(back_first)]
    back_second = [along(v, 0, -s) if s else v for s, v in enumerate(back_second)]

    def column_of(own_core):
        return column(own_core, place, codes, hard_scores, log_total, first, second, gathered,
                      queries, temper, cap)

    other = column_of(False)
    grad_passages = scatter_group(column_of(True), other, groups)
    grad_inner, losses = inner(place, log_total, gathered, queries, temper)

    sums = []
    for half, ranks, rows in ((0, ranks_first, back_first), (1, ranks_second, back_second)):
        made = reduce(place, half, log_total, ranks, rows, groups, cap)
        sums.append([along(v, half, -s) if s else v for s, v in enumerate(made)])
    grad_queries = final(place, grad_inner, *sums, temper)
    return (losses.reshape(toks), grad_queries, grad_passages)


def solution(mesh):
    in_specs = (
        P(("grp", "rep"), None),
        P(("grp", "rep"), None),
        P(("grp", "rep"), None),
        P(("grp", "rep"), None),
    )
    out_specs = (P(("grp", "rep")), P(("grp", "rep"), None), P(("grp", "rep"), None))
    return jax.shard_map(shards, mesh=mesh, in_specs=in_specs, out_specs=out_specs, check_vma=False)
```

time: 278 us -> 226 us (0.81)
  Pallas kernels: 0 us -> 77.8 us
  local copies, waits for them, and re-layouts: 66.3 us -> 4.99 us
  other arithmetic: 48.7 us -> 15.7 us
  starting transfers between devices: 11.9 us -> 44.3 us
  waiting for transfers between devices: 95.7 us -> 67.6 us
  matrix products: 17.7 us -> 0 us
  between operations: 14.3 us -> 1.09 us
  blocking collectives: 20.4 us -> 13.6 us
    all_to_all x2 -> x0, waiting for transfers between devices: 95 us -> none  [the longest x1 50.9 us: shards(): lax.all_to_all(served, ('grp', 'rep'), split_axis=0, concat_axis=0, tiled...]
    pallas_call x0 -> x12, Pallas kernels: none -> 77.8 us  [the longest x4 23.8 us: mid(): call(functools.partial(mid_kernel, shift, cap, groups, reps, negs), 'mid'...]
    ppermute x0 -> x34, waiting for transfers between devices: none -> 67.6 us  [the longest x24 47 us: along(): return lax.ppermute(x, 'rep', pairs)]
    ppermute x0 -> x34, starting transfers between devices: none -> 44.3 us  [the longest x24 31 us: along(): return lax.ppermute(x, 'rep', pairs)]
    gather x2 -> x0, local copies, waits for them, and re-layouts: 35.7 us -> none  [the longest x1 26.1 us: shards(): fetched[target, slot_rank].reshape(tok_rows, neg_count, emb_width)]
    unnamed x4 -> x0, other arithmetic: 20.7 us -> none
    scatter-add x1 -> x0, other arithmetic: 18.5 us -> none  [shards(): hard_sum = jnp.zeros((tok_rows, emb_width), jnp.float32).at[asked.reshape...]
    dot_general x5 -> x0, matrix products: 17.7 us -> none  [the longest x1 4.53 us: shards(): jnp.einsum('qe,qke->qk', queries, negatives, preferred_element_type=jnp.f...]
  transfers between devices with their start and end apart: 4 -> 34, of which waited for: 2 -> 14; matrix products, arithmetic and copies ran while one was open for 38% -> 6% of each run, Pallas kernels for 0% -> 26%
where the time goes in v4:
time: 226 us; the launch traced here: 225 us
  Pallas kernels  77.8 us (34%)
  waiting for transfers between devices  67.6 us (30%)
  starting transfers between devices  44.3 us (20%)
  other arithmetic  15.7 us (7%)
  blocking collectives  13.6 us (6%)
  local copies, waits for them, and re-layouts  4.99 us (2%)
    ppermute x24, waiting for transfers between devices, along(): return lax.ppermute(x, 'rep', pairs)  47 us
    ppermute x24, starting transfers between devices, along(): return lax.ppermute(x, 'rep', pairs)  31 us
    pallas_call x4, Pallas kernels, mid(): call(functools.partial(mid_kernel, shift, cap, groups, reps, negs), 'mid'...  23.8 us
    ppermute x8, waiting for transfers between devices, along_z(): lax.ppermute(x, 'grp', [(i, (i + CORES * shift) % groups) for i in range(...  20.5 us
    pallas_call x2, Pallas kernels, column(): call(functools.partial(column_kernel, reps, cap, temper, own_core), 'own'...  15 us
    all_to_all x1, blocking collectives, shards(): parts = lax.all_to_all(part, 'rep', split_axis=0, concat_axis=0, tiled=True)  13.6 us
    ppermute x8, starting transfers between devices, along_z(): lax.ppermute(x, 'grp', [(i, (i + CORES * shift) % groups) for i in range(...  13.3 us
    pallas_call x1, Pallas kernels, hard(): call(functools.partial(hard_kernel, reps, cap, temper), 'hard', levels +...  10.9 us
  transfers between devices with their start and end apart: 34, of which 14 were waited for; matrix products, arithmetic and copies ran while one was open for 6% of the time, Pallas kernels for 26%

profile of v4, /device:TPU:0, one launch (start us, length us, event | category | flops | bytes accessed | tf_op | source)
XLA Modules:
  0.0 225.1 jit_solution(6978153912084593608)
XLA Ops:
  0.6 2.1 collective-permute-start.13
  2.7 2.2 collective-permute-start.12
  4.9 12.1 %collective-permute-done.13 = bf16[256,1024]{1,0:T(8,128)(2,1)S(1)} collective-permute-done((bf16[256,1024]{1,0:T(8,128)(2,1)}, bf16[256,1024]{1,0:T(8,128)(2,1)S(1)}, u32[]{:S(2)}, u32[]{:S(2)}) %collective-permute-start.13) | collective-permute-done | bytes 524320 | tf_op jit(solution)/shard_map/ppermute | solution.py:486
  17.1 3.3 %collective-permute-start.15 = (bf16[128,1024]{1,0:T(8,128)(2,1)S(1)}, bf16[128,1024]{1,0:T(8,128)(2,1)S(1)}, u32[]{:S(2)}, u32[]{:S(2)}) collective-permute-start(bf16[128,1024]{1,0:T(8,128)(2,1)S(1)} %slice.49), channel_id=1, source_target_pairs={{0,96},{16,112},{32,0},{48,16},{64,32},{80,48},{96,64},{112,80},{1... | collective-permute-start | bytes 786440 | tf_op jit(solution)/shard_map/ppermute | solution.py:486
  20.4 5.4 %collective-permute-done.14 = bf16[128,1024]{1,0:T(8,128)(2,1)S(1)} collective-permute-done((bf16[128,1024]{1,0:T(8,128)(2,1)S(1)}, bf16[128,1024]{1,0:T(8,128)(2,1)S(1)}, u32[]{:S(2)}, u32[]{:S(2)}) %collective-permute-start.14) | collective-permute-done | bytes 262176 | tf_op jit(solution)/shard_map/ppermute | solution.py:486
  25.9 1.6 pad_maximum_fusion.1
  27.6 3.1 %collective-permute-start.5 = (bf16[272,512]{1,0:T(8,128)(2,1)S(1)}, bf16[272,512]{1,0:T(8,128)(2,1)S(1)}, u32[]{:S(2)}, u32[]{:S(2)}) collective-permute-start(bf16[272,512]{1,0:T(8,128)(2,1)S(1)} %get-tuple-element.107.refs_4_), channel_id=1, source_target_pairs={{0,3},{1,0},{2,1},{3,2},{4,7},{5,4},{6,5},{7,6},{8,11},{9,8},{10,9... | collective-permute-start | bytes 835592 | tf_op jit(solution)/shard_map/ppermute | solution.py:498
  32.3 2.8 %collective-permute-start.2 = (bf16[272,512]{1,0:T(8,128)(2,1)S(1)}, bf16[272,512]{1,0:T(8,128)(2,1)S(1)}, u32[]{:S(2)}, u32[]{:S(2)}) collective-permute-start(bf16[272,512]{1,0:T(8,128)(2,1)S(1)} %get-tuple-element.108.refs_0_), channel_id=1, source_target_pairs={{0,12},{1,13},{2,14},{3,15},{4,0},{5,1},{6,2},{7,3},{8,4},{9,5},{1... | collective-permute-start | bytes 835592 | tf_op jit(solution)/shard_map/ppermute | solution.py:498
  35.1 8.2 %collective-permute-done.5.refs_7_ = bf16[272,512]{1,0:T(8,128)(2,1)S(1)} collective-permute-done((bf16[272,512]{1,0:T(8,128)(2,1)S(1)}, bf16[272,512]{1,0:T(8,128)(2,1)S(1)}, u32[]{:S(2)}, u32[]{:S(2)}) %collective-permute-start.5) | collective-permute-done | bytes 278560 | tf_op jit(solution)/shard_map/ppermute | solution.py:498
  43.2 3.0 %collective-permute-start.1 = (bf16[272,512]{1,0:T(8,128)(2,1)S(1)}, bf16[272,512]{1,0:T(8,128)(2,1)S(1)}, u32[]{:S(2)}, u32[]{:S(2)}) collective-permute-start(bf16[272,512]{1,0:T(8,128)(2,1)S(1)} %get-tuple-element.108.refs_0_), channel_id=1, source_target_pairs={{0,8},{1,9},{2,10},{3,11},{4,12},{5,13},{6,14},{7,15},{8,0},{9,1},... | collective-permute-start | bytes 835592 | tf_op jit(solution)/shard_map/ppermute | solution.py:498
  47.5 6.8 %collective-permute-done.1.refs_2_ = bf16[272,512]{1,0:T(8,128)(2,1)S(1)} collective-permute-done((bf16[272,512]{1,0:T(8,128)(2,1)S(1)}, bf16[272,512]{1,0:T(8,128)(2,1)S(1)}, u32[]{:S(2)}, u32[]{:S(2)}) %collective-permute-start.1) | collective-permute-done | bytes 278560 | tf_op jit(solution)/shard_map/ppermute | solution.py:498
  54.4 4.6 %collective-permute-done.refs_1_ = bf16[272,512]{1,0:T(8,128)(2,1)} collective-permute-done((bf16[272,512]{1,0:T(8,128)(2,1)S(1)}, bf16[272,512]{1,0:T(8,128)(2,1)}, u32[]{:S(2)}, u32[]{:S(2)}) %collective-permute-start) | collective-permute-done | bytes 278560 | tf_op jit(solution)/shard_map/ppermute | solution.py:498
  59.0 6.0 %mid.7 = (bf16[528,512]{1,0:T(8,128)(2,1)}, bf16[528,512]{1,0:T(8,128)(2,1)}, bf16[32,256]{1,0:T(8,128)(2,1)}, bf16[32,256]{1,0:T(8,128)(2,1)}) custom-call(s32[4]{0:T(128)} %pad_add_fusion.place_ref, bf16[272,512]{1,0:T(8,128)(2,1)} %copy-done.6, bf16[272,512]{1,0:T(8,128)(2,1)} %collective-permute-done.refs_1_, bf16[272,512]{1,0:T(8,128)(2,1)} %copy-done.14, ...), custom_call_target="tpu_custom_call" | custom-call | flops 1048576 | bytes 65536 | tf_op jit(solution)/shard_map/mid/pallas_call | solution.py:135
  64.9 3.8 %collective-permute-start.8 = (bf16[528,512]{1,0:T(8,128)(2,1)}, bf16[528,512]{1,0:T(8,128)(2,1)S(1)}, u32[]{:S(2)}, u32[]{:S(2)}) collective-permute-start(bf16[528,512]{1,0:T(8,128)(2,1)} %get-tuple-element.52), channel_id=1, source_target_pairs={{0,3},{1,0},{2,1},{3,2},{4,7},{5,4},{6,5},{7,6},{8,11},{9,8},{10,9... | collective-permute-start | bytes 1622024 | tf_op jit(solution)/shard_map/ppermute | solution.py:498
  69.4 6.0 %mid.6 = (bf16[528,512]{1,0:T(8,128)(2,1)}, bf16[528,512]{1,0:T(8,128)(2,1)}, bf16[32,256]{1,0:T(8,128)(2,1)}, bf16[32,256]{1,0:T(8,128)(2,1)}) custom-call(s32[4]{0:T(128)} %pad_add_fusion.place_ref, bf16[272,512]{1,0:T(8,128)(2,1)} %copy-done.6, bf16[272,512]{1,0:T(8,128)(2,1)} %collective-permute-done.refs_1_, bf16[272,512]{1,0:T(8,128)(2,1)} %copy-done.14, ...), custom_call_target="tpu_custom_call" | custom-call | flops 1048576 | bytes 65536 | tf_op jit(solution)/shard_map/mid/pallas_call | solution.py:135
  75.4 3.1 %collective-permute-start.10 = (bf16[528,512]{1,0:T(8,128)(2,1)}, bf16[528,512]{1,0:T(8,128)(2,1)S(1)}, u32[]{:S(2)}, u32[]{:S(2)}) collective-permute-start(bf16[528,512]{1,0:T(8,128)(2,1)} %get-tuple-element.55), channel_id=1, source_target_pairs={{0,8},{1,9},{2,10},{3,11},{4,12},{5,13},{6,14},{7,15},{8,0},{9,1},... | collective-permute-start | bytes 1622024 | tf_op jit(solution)/shard_map/ppermute | solution.py:498
  78.5 5.9 %mid.5 = (bf16[528,512]{1,0:T(8,128)(2,1)}, bf16[528,512]{1,0:T(8,128)(2,1)}, bf16[32,256]{1,0:T(8,128)(2,1)}, bf16[32,256]{1,0:T(8,128)(2,1)}) custom-call(s32[4]{0:T(128)} %pad_add_fusion.place_ref, bf16[272,512]{1,0:T(8,128)(2,1)} %copy-done.6, bf16[272,512]{1,0:T(8,128)(2,1)} %collective-permute-done.refs_1_, bf16[272,512]{1,0:T(8,128)(2,1)} %copy-done.14, ...), custom_call_target="tpu_custom_call" | custom-call | flops 1048576 | bytes 65536 | tf_op jit(solution)/shard_map/mid/pallas_call | solution.py:135
  84.4 6.0 %mid.4 = (bf16[528,512]{1,0:T(8,128)(2,1)}, bf16[528,512]{1,0:T(8,128)(2,1)}, bf16[32,256]{1,0:T(8,128)(2,1)}, bf16[32,256]{1,0:T(8,128)(2,1)}) custom-call(s32[4]{0:T(128)} %pad_add_fusion.place_ref, bf16[272,512]{1,0:T(8,128)(2,1)} %copy-done.6, bf16[272,512]{1,0:T(8,128)(2,1)} %collective-permute-done.refs_1_, bf16[272,512]{1,0:T(8,128)(2,1)} %copy-done.14, ...), custom_call_target="tpu_custom_call" | custom-call | flops 1048576 | bytes 65536 | tf_op jit(solution)/shard_map/mid/pallas_call | solution.py:135
  91.5 2.0 select_bitcast_fusion.1
  94.3 2.4 %copy.7 = bf16[4,2,256,1024]{3,2,1,0:T(8,128)(2,1)} copy(bf16[4,2,256,1024]{3,2,0,1:T(8,128)(2,1)S(1)} %pad_maximum_fusion) | data formatting | bytes 8388608 | tf_op jit(solution)/shard_map/stack | solution.py:511
  96.7 5.7 %inside.1.refs_13_ = f32[1,256]{1,0:T(1,128)} custom-call(s32[4]{0:T(128)} %pad_add_fusion.place_ref, bf16[2048,1024]{1,0:T(8,128)(2,1)} %bitcast.53, bf16[256,1024]{1,0:T(8,128)(2,1)} %refs_9_.3), custom_call_target="tpu_custom_call" | custom-call | flops 4294967296 | bytes 65536 | tf_op jit(solution)/shard_map/inside/pallas_call | solution.py:166
  102.5 1.8 collective-permute-done.6.refs_1_.refs_9_
  104.2 2.8 %collective-permute-done.9.refs_5_ = bf16[528,512]{1,0:T(8,128)(2,1)S(1)} collective-permute-done((bf16[528,512]{1,0:T(8,128)(2,1)}, bf16[528,512]{1,0:T(8,128)(2,1)S(1)}, u32[]{:S(2)}, u32[]{:S(2)}) %collective-permute-start.9) | collective-permute-done | bytes 540704 | tf_op jit(solution)/shard_map/ppermute | solution.py:498
  107.9 10.9 %hard.1 = (bf16[528,512]{1,0:T(8,128)(2,1)}, bf16[528,512]{1,0:T(8,128)(2,1)}, bf16[528,512]{1,0:T(8,128)(2,1)}, bf16[528,512]{1,0:T(8,128)(2,1)}, bf16[528,512]...) custom-call(s32[4]{0:T(128)} %pad_add_fusion.place_ref, ...), custom_call_target="tpu_custom_call" | custom-call | flops 1048576 | bytes 65536 | tf_op jit(solution)/shard_map/hard/pallas_call | solution.py:318
  118.8 13.6 %all_to_all.5 = f32[16,16,256]{2,1,0:T(8,128)S(1)} all-to-all(f32[16,16,256]{2,1,0:T(8,128)} %get-tuple-element.57), channel_id=1, replica_groups=mesh['grp'=8,'rep'=16] {'rep'}, dimensions={0} | all-to-all | bytes 524288 | tf_op jit(solution)/shard_map/all_to_all | solution.py:558
  133.1 7.6 %other.1 = bf16[4,256,1024]{2,1,0:T(8,128)(2,1)} custom-call(s32[4]{0:T(128)} %pad_add_fusion.place_ref, s32[16,256]{1,0:T(8,128)} %get-tuple-element.93.code_ref, f32[8,256]{1,0:T(8,128)} %get-tuple-element.94.hs_ref, f32[16,256]{1,0:T(8,128)} %log_add_fusion.lt_ref, bf16[528,512]{1,0:T(8,128)(2,1)} %get-tuple-element.49.refs_0_.refs_8_, ...), custom_call_target="tpu_custom_call" | custom-call | flops 1048576 | bytes 65536 | tf_op jit(solution)/shard_map/other/pallas_call | solution.py:385
  140.6 1.1 collective-permute-start.17
  141.7 1.5 collective-permute-start.18
  144.6 7.5 %own.1 = bf16[4,256,1024]{2,1,0:T(8,128)(2,1)} custom-call(s32[4]{0:T(128)} %pad_add_fusion.place_ref, s32[16,256]{1,0:T(8,128)} %get-tuple-element.93.code_ref, f32[8,256]{1,0:T(8,128)} %get-tuple-element.94.hs_ref, f32[16,256]{1,0:T(8,128)} %log_add_fusion.lt_ref, bf16[528,512]{1,0:T(8,128)(2,1)} %get-tuple-element.49.refs_0_.refs_8_, ...), custom_call_target="tpu_custom_call" | custom-call | flops 1048576 | bytes 65536 | tf_op jit(solution)/shard_map/own/pallas_call | solution.py:385
  152.1 3.8 %collective-permute-done.17.refs_5_ = bf16[528,512]{1,0:T(8,128)(2,1)} collective-permute-done((bf16[528,512]{1,0:T(8,128)(2,1)S(1)}, bf16[528,512]{1,0:T(8,128)(2,1)}, u32[]{:S(2)}, u32[]{:S(2)}) %collective-permute-start.17) | collective-permute-done | bytes 540704 | tf_op jit(solution)/shard_map/ppermute | solution.py:498
  155.9 1.3 collective-permute-start.24
  157.2 1.3 collective-permute-done.18.refs_6_
  158.8 10.5 %collective-permute-done.19.refs_7_ = bf16[528,512]{1,0:T(8,128)(2,1)} collective-permute-done((bf16[528,512]{1,0:T(8,128)(2,1)}, bf16[528,512]{1,0:T(8,128)(2,1)}, u32[]{:S(2)}, u32[]{:S(2)}) %collective-permute-start.19) | collective-permute-done | bytes 540704 | tf_op jit(solution)/shard_map/ppermute | solution.py:498
  169.3 4.7 %reduce.2 = (f32[256,512]{1,0:T(8,128)}, bf16[256,512]{1,0:T(8,128)(2,1)}, bf16[256,512]{1,0:T(8,128)(2,1)}, bf16[256,512]{1,0:T(8,128)(2,1)}) custom-call(s32[4]{0:T(128)} %pad_add_fusion.place_ref, f32[16,256]{1,0:T(8,128)} %log_add_fusion.lt_ref, bf16[32,256]{1,0:T(8,128)(2,1)} %get-tuple-element.69.refs_0_, bf16[32,256]{1,0:T(8,128)(2,1)} %get-tuple-element.70.refs_1_, ...), custom_call_target="tpu_custom_call" | custom-call | flops 1048576 | bytes 65536 | tf_op jit(solution)/shard_map/reduce/pallas_call | solution.py:457
  174.9 4.7 %fusion.14 = (bf16[4,256,1024]{2,1,0:T(8,128)(2,1)S(1)}, f32[4,256,1024]{2,1,0:T(8,128)}) fusion(bf16[4,256,1024]{2,1,0:T(8,128)(2,1)} %collective-permute-done.29, bf16[4,256,1024]{2,1,0:T(8,128)(2,1)S(1)} %copy-done.3), kind=kLoop, calls=%fused_computation.36 | loop fusion | flops 4194304 | bytes 10485760 | tf_op jit(solution)/shard_map/convert.9
  179.7 3.5 %collective-permute-start.32 = (bf16[128,1024]{1,0:T(8,128)(2,1)S(1)}, bf16[128,1024]{1,0:T(8,128)(2,1)S(1)}, u32[]{:S(2)}, u32[]{:S(2)}) collective-permute-start(bf16[128,1024]{1,0:T(8,128)(2,1)S(1)} %get-tuple-element.102), channel_id=1, source_target_pairs={{0,96},{16,112},{32,0},{48,16},{64,32},{80,48},{96,64},{112,80},{1... | collective-permute-start | bytes 786440 | tf_op jit(solution)/shard_map/ppermute | solution.py:486
  183.2 9.1 %inner.1 = (f32[256,1024]{1,0:T(8,128)}, f32[1,256]{1,0:T(1,128)}) custom-call(s32[4]{0:T(128)} %pad_add_fusion.place_ref, f32[16,256]{1,0:T(8,128)} %log_add_fusion.lt_ref, bf16[2048,1024]{1,0:T(8,128)(2,1)} %bitcast.57, bf16[256,1024]{1,0:T(8,128)(2,1)} %refs_9_.3), custom_call_target="tpu_custom_call" | custom-call | flops 1048576 | bytes 65536 | tf_op jit(solution)/shard_map/inner/pallas_call | solution.py:423
  192.4 1.5 collective-permute-start.21
  194.8 4.7 %reduce.3 = (f32[256,512]{1,0:T(8,128)}, bf16[256,512]{1,0:T(8,128)(2,1)}, bf16[256,512]{1,0:T(8,128)(2,1)}, bf16[256,512]{1,0:T(8,128)(2,1)}) custom-call(s32[4]{0:T(128)} %pad_add_fusion.place_ref, f32[16,256]{1,0:T(8,128)} %log_add_fusion.lt_ref, bf16[32,256]{1,0:T(8,128)(2,1)} %get-tuple-element.81.refs_0_, bf16[32,256]{1,0:T(8,128)(2,1)} %get-tuple-element.82.refs_1_, ...), custom_call_target="tpu_custom_call" | custom-call | flops 1048576 | bytes 65536 | tf_op jit(solution)/shard_map/reduce/pallas_call | solution.py:457
  199.5 1.5 collective-permute-start.26
  202.5 1.3 fusion.7
  205.6 1.9 collective-permute-start.33
  207.7 1.4 collective-permute-done.26.refs_5_
  209.1 3.0 %collective-permute-done.27.refs_6_ = bf16[256,512]{1,0:T(8,128)(2,1)S(1)} collective-permute-done((bf16[256,512]{1,0:T(8,128)(2,1)}, bf16[256,512]{1,0:T(8,128)(2,1)S(1)}, u32[]{:S(2)}, u32[]{:S(2)}) %collective-permute-start.27) | collective-permute-done | bytes 262176 | tf_op jit(solution)/shard_map/ppermute | solution.py:498
  212.0 2.9 %collective-permute-done.28.refs_7_ = bf16[256,512]{1,0:T(8,128)(2,1)S(1)} collective-permute-done((bf16[256,512]{1,0:T(8,128)(2,1)}, bf16[256,512]{1,0:T(8,128)(2,1)S(1)}, u32[]{:S(2)}, u32[]{:S(2)}) %collective-permute-start.28) | collective-permute-done | bytes 262176 | tf_op jit(solution)/shard_map/ppermute | solution.py:498
  215.7 3.7 %final.1 = bf16[256,1024]{1,0:T(8,128)(2,1)} custom-call(s32[4]{0:T(128)} %pad_add_fusion.place_ref, f32[256,1024]{1,0:T(8,128)} %get-tuple-element.68.gq_ref, f32[256,512]{1,0:T(8,128)} %get-tuple-element.77.refs_0_, bf16[256,512]{1,0:T(8,128)(2,1)} %copy-done.26, bf16[256,512]{1,0:T(8,128)(2,1)} %copy-done.29, bf16[256,512]{1,0:T(8,128)(2,1)} %copy-done.30, ...), custom_call_target="tpu_custom_call" | custom-call | flops 549755813888 | bytes 65536 | tf_op jit(solution)/shard_map/final/pallas_call | solution.py:478
  219.4 3.1 %collective-permute-done.31 = bf16[256,1024]{1,0:T(8,128)(2,1)} collective-permute-done((bf16[256,1024]{1,0:T(8,128)(2,1)}, bf16[256,1024]{1,0:T(8,128)(2,1)}, u32[]{:S(2)}, u32[]{:S(2)}) %collective-permute-start.31) | collective-permute-done | bytes 524320 | tf_op jit(solution)/shard_map/ppermute | solution.py:486
  222.5 2.5 %fusion.2 = bf16[256,1024]{1,0:T(8,128)(2,1)} fusion(f32[4,256,1024]{2,1,0:T(8,128)} %get-tuple-element.98, bf16[256,1024]{1,0:T(8,128)(2,1)} %collective-permute-done.33, bf16[256,1024]{1,0:T(8,128)(2,1)} %collective-permute-done.31), kind=kLoop, calls=%fused_computation.8 | loop fusion | flops 1310720 | bytes 2621440 | tf_op jit(solution)/shard_map/convert_element_type | solution.py:523
  (122 shorter events, 14.8 us)
Async XLA Ops:
  0.6 25.2 %copy-start.18 = (bf16[256,1024]{1,0:T(8,128)(2,1)S(1)}, bf16[256,1024]{1,0:T(8,128)(2,1)}, u32[]{:S(2)}) copy-start(bf16[256,1024]{1,0:T(8,128)(2,1)} %param.5) | copy-start | bytes 1572868
  0.6 16.3 %collective-permute-start.13 = (bf16[256,1024]{1,0:T(8,128)(2,1)}, bf16[256,1024]{1,0:T(8,128)(2,1)S(1)}, u32[]{:S(2)}, u32[]{:S(2)}) collective-permute-start(bf16[256,1024]{1,0:T(8,128)(2,1)} %param.5), channel_id=1, source_target_pairs={{0,32},{16,48},{32,64},{48,80},{64,96},{80,112},{96,0},{112,16},{1... | collective-permute-start | bytes 1572872 | tf_op jit(solution)/shard_map/ppermute | solution.py:486
  2.7 14.4 %collective-permute-start.12 = (bf16[256,1024]{1,0:T(8,128)(2,1)}, bf16[256,1024]{1,0:T(8,128)(2,1)S(1)}, u32[]{:S(2)}, u32[]{:S(2)}) collective-permute-start(bf16[256,1024]{1,0:T(8,128)(2,1)} %param.5), channel_id=1, source_target_pairs={{0,96},{16,112},{32,0},{48,16},{64,32},{80,48},{96,64},{112,80},{1... | collective-permute-start | bytes 1572872 | tf_op jit(solution)/shard_map/ppermute | solution.py:486
  17.0 10.5 %copy-start.15 = (bf16[256,1024]{1,0:T(8,128)(2,1)}, bf16[256,1024]{1,0:T(8,128)(2,1)S(1)}, u32[]{:S(2)}) copy-start(bf16[256,1024]{1,0:T(8,128)(2,1)S(1)} %collective-permute-done.13) | copy-start | bytes 1572868
  17.0 8.8 %collective-permute-start.14 = (bf16[128,1024]{1,0:T(8,128)(2,1)S(1)}, bf16[128,1024]{1,0:T(8,128)(2,1)S(1)}, u32[]{:S(2)}, u32[]{:S(2)}) collective-permute-start(bf16[128,1024]{1,0:T(8,128)(2,1)S(1)} %slice.48), channel_id=1, source_target_pairs={{0,32},{16,48},{32,64},{48,80},{64,96},{80,112},{96,0},{112,16},{1... | collective-permute-start | bytes 786440 | tf_op jit(solution)/shard_map/ppermute | solution.py:486
  17.1 10.3 %copy-start.17 = (bf16[256,1024]{1,0:T(8,128)(2,1)}, bf16[256,1024]{1,0:T(8,128)(2,1)S(1)}, u32[]{:S(2)}) copy-start(bf16[256,1024]{1,0:T(8,128)(2,1)S(1)} %collective-permute-done.12) | copy-start | bytes 1572868
  17.1 8.6 %collective-permute-start.15 = (bf16[128,1024]{1,0:T(8,128)(2,1)S(1)}, bf16[128,1024]{1,0:T(8,128)(2,1)S(1)}, u32[]{:S(2)}, u32[]{:S(2)}) collective-permute-start(bf16[128,1024]{1,0:T(8,128)(2,1)S(1)} %slice.49), channel_id=1, source_target_pairs={{0,96},{16,112},{32,0},{48,16},{64,32},{80,48},{96,64},{112,80},{1... | collective-permute-start | bytes 786440 | tf_op jit(solution)/shard_map/ppermute | solution.py:486
  27.4 62.9 %collective-permute-start.16 = (bf16[4,256,1024]{2,1,0:T(8,128)(2,1)}, bf16[4,256,1024]{2,1,0:T(8,128)(2,1)}, u32[]{:S(2)}, u32[]{:S(2)}) collective-permute-start(bf16[4,256,1024]{2,1,0:T(8,128)(2,1)} %pad_maximum_fusion.1), channel_id=1, source_target_pairs={{0,16},{16,0},{32,48},{48,32},{64,80},{80,64},{96,112},{112,96},{1... | collective-permute-start | bytes 6291464 | tf_op jit(solution)/shard_map/ppermute | solution.py:490
  27.6 31.3 %copy-start.5 = (bf16[272,512]{1,0:T(8,128)(2,1)}, bf16[272,512]{1,0:T(8,128)(2,1)S(1)}, u32[]{:S(2)}) copy-start(bf16[272,512]{1,0:T(8,128)(2,1)S(1)} %get-tuple-element.107.refs_4_) | copy-start | bytes 835588
  27.6 31.3 %copy-start.6 = (bf16[272,512]{1,0:T(8,128)(2,1)}, bf16[272,512]{1,0:T(8,128)(2,1)S(1)}, u32[]{:S(2)}) copy-start(bf16[272,512]{1,0:T(8,128)(2,1)S(1)} %get-tuple-element.108.refs_0_) | copy-start | bytes 835588
  27.6 15.6 %collective-permute-start.5 = (bf16[272,512]{1,0:T(8,128)(2,1)S(1)}, bf16[272,512]{1,0:T(8,128)(2,1)S(1)}, u32[]{:S(2)}, u32[]{:S(2)}) collective-permute-start(bf16[272,512]{1,0:T(8,128)(2,1)S(1)} %get-tuple-element.107.refs_4_), channel_id=1, source_target_pairs={{0,3},{1,0},{2,1},{3,2},{4,7},{5,4},{6,5},{7,6},{8,11},{9,8},{10,9... | collective-permute-start | bytes 835592 | tf_op jit(solution)/shard_map/ppermute | solution.py:498
  30.7 15.6 %collective-permute-start.4 = (bf16[272,512]{1,0:T(8,128)(2,1)S(1)}, bf16[272,512]{1,0:T(8,128)(2,1)S(1)}, u32[]{:S(2)}, u32[]{:S(2)}) collective-permute-start(bf16[272,512]{1,0:T(8,128)(2,1)S(1)} %get-tuple-element.107.refs_4_), channel_id=1, source_target_pairs={{0,2},{1,3},{2,0},{3,1},{4,6},{5,7},{6,4},{7,5},{8,10},{9,11},{10,... | collective-permute-start | bytes 835592 | tf_op jit(solution)/shard_map/ppermute | solution.py:498
  31.3 16.2 %collective-permute-start.3 = (bf16[272,512]{1,0:T(8,128)(2,1)S(1)}, bf16[272,512]{1,0:T(8,128)(2,1)S(1)}, u32[]{:S(2)}, u32[]{:S(2)}) collective-permute-start(bf16[272,512]{1,0:T(8,128)(2,1)S(1)} %get-tuple-element.107.refs_4_), channel_id=1, source_target_pairs={{0,1},{1,2},{2,3},{3,0},{4,5},{5,6},{6,7},{7,4},{8,9},{9,10},{10,1... | collective-permute-start | bytes 835592 | tf_op jit(solution)/shard_map/ppermute | solution.py:498
  32.3 15.2 %collective-permute-start.2 = (bf16[272,512]{1,0:T(8,128)(2,1)S(1)}, bf16[272,512]{1,0:T(8,128)(2,1)S(1)}, u32[]{:S(2)}, u32[]{:S(2)}) collective-permute-start(bf16[272,512]{1,0:T(8,128)(2,1)S(1)} %get-tuple-element.108.refs_0_), channel_id=1, source_target_pairs={{0,12},{1,13},{2,14},{3,15},{4,0},{5,1},{6,2},{7,3},{8,4},{9,5},{1... | collective-permute-start | bytes 835592 | tf_op jit(solution)/shard_map/ppermute | solution.py:498
  43.2 15.7 %copy-start.10 = (bf16[272,512]{1,0:T(8,128)(2,1)}, bf16[272,512]{1,0:T(8,128)(2,1)S(1)}, u32[]{:S(2)}) copy-start(bf16[272,512]{1,0:T(8,128)(2,1)S(1)} %collective-permute-done.5.refs_7_) | copy-start | bytes 835588
  43.2 11.1 %collective-permute-start.1 = (bf16[272,512]{1,0:T(8,128)(2,1)S(1)}, bf16[272,512]{1,0:T(8,128)(2,1)S(1)}, u32[]{:S(2)}, u32[]{:S(2)}) collective-permute-start(bf16[272,512]{1,0:T(8,128)(2,1)S(1)} %get-tuple-element.108.refs_0_), channel_id=1, source_target_pairs={{0,8},{1,9},{2,10},{3,11},{4,12},{5,13},{6,14},{7,15},{8,0},{9,1},... | collective-permute-start | bytes 835592 | tf_op jit(solution)/shard_map/ppermute | solution.py:498
  46.3 12.7 %copy-start.11 = (bf16[272,512]{1,0:T(8,128)(2,1)}, bf16[272,512]{1,0:T(8,128)(2,1)S(1)}, u32[]{:S(2)}) copy-start(bf16[272,512]{1,0:T(8,128)(2,1)S(1)} %collective-permute-done.4.refs_6_) | copy-start | bytes 835588
  46.3 12.7 %collective-permute-start = (bf16[272,512]{1,0:T(8,128)(2,1)S(1)}, bf16[272,512]{1,0:T(8,128)(2,1)}, u32[]{:S(2)}, u32[]{:S(2)}) collective-permute-start(bf16[272,512]{1,0:T(8,128)(2,1)S(1)} %get-tuple-element.108.refs_0_), channel_id=1, source_target_pairs={{0,4},{1,5},{2,6},{3,7},{4,8},{5,9},{6,10},{7,11},{8,12},{9,13},{1... | collective-permute-start | bytes 835592 | tf_op jit(solution)/shard_map/ppermute | solution.py:498
  47.5 11.4 %copy-start.12 = (bf16[272,512]{1,0:T(8,128)(2,1)}, bf16[272,512]{1,0:T(8,128)(2,1)S(1)}, u32[]{:S(2)}) copy-start(bf16[272,512]{1,0:T(8,128)(2,1)S(1)} %collective-permute-done.3.refs_5_) | copy-start | bytes 835588
  47.5 11.4 %copy-start.13 = (bf16[272,512]{1,0:T(8,128)(2,1)}, bf16[272,512]{1,0:T(8,128)(2,1)S(1)}, u32[]{:S(2)}) copy-start(bf16[272,512]{1,0:T(8,128)(2,1)S(1)} %collective-permute-done.2.refs_3_) | copy-start | bytes 835588
  64.9 28.6 %collective-permute-start.8 = (bf16[528,512]{1,0:T(8,128)(2,1)}, bf16[528,512]{1,0:T(8,128)(2,1)S(1)}, u32[]{:S(2)}, u32[]{:S(2)}) collective-permute-start(bf16[528,512]{1,0:T(8,128)(2,1)} %get-tuple-element.52), channel_id=1, source_target_pairs={{0,3},{1,0},{2,1},{3,2},{4,7},{5,4},{6,5},{7,6},{8,11},{9,8},{10,9... | collective-permute-start | bytes 1622024 | tf_op jit(solution)/shard_map/ppermute | solution.py:498
  68.8 33.7 %collective-permute-start.11 = (bf16[528,512]{1,0:T(8,128)(2,1)}, bf16[528,512]{1,0:T(8,128)(2,1)S(1)}, u32[]{:S(2)}, u32[]{:S(2)}) collective-permute-start(bf16[528,512]{1,0:T(8,128)(2,1)} %get-tuple-element.56), channel_id=1, source_target_pairs={{0,12},{1,13},{2,14},{3,15},{4,0},{5,1},{6,2},{7,3},{8,4},{9,5},{1... | collective-permute-start | bytes 1622024 | tf_op jit(solution)/shard_map/ppermute | solution.py:498
  75.4 27.1 %collective-permute-start.7 = (bf16[528,512]{1,0:T(8,128)(2,1)}, bf16[528,512]{1,0:T(8,128)(2,1)S(1)}, u32[]{:S(2)}, u32[]{:S(2)}) collective-permute-start(bf16[528,512]{1,0:T(8,128)(2,1)} %get-tuple-element.51), channel_id=1, source_target_pairs={{0,2},{1,3},{2,0},{3,1},{4,6},{5,7},{6,4},{7,5},{8,10},{9,11},{10,... | collective-permute-start | bytes 1622024 | tf_op jit(solution)/shard_map/ppermute | solution.py:498
  75.4 16.1 %copy-start.16 = (bf16[256,1024]{1,0:T(8,128)(2,1)S(1)}, bf16[256,1024]{1,0:T(8,128)(2,1)}, u32[]{:S(2)}) copy-start(bf16[256,1024]{1,0:T(8,128)(2,1)} %copy-done.15) | copy-start | bytes 1572868
  75.4 27.1 %collective-permute-start.10 = (bf16[528,512]{1,0:T(8,128)(2,1)}, bf16[528,512]{1,0:T(8,128)(2,1)S(1)}, u32[]{:S(2)}, u32[]{:S(2)}) collective-permute-start(bf16[528,512]{1,0:T(8,128)(2,1)} %get-tuple-element.55), channel_id=1, source_target_pairs={{0,8},{1,9},{2,10},{3,11},{4,12},{5,13},{6,14},{7,15},{8,0},{9,1},... | collective-permute-start | bytes 1622024 | tf_op jit(solution)/shard_map/ppermute | solution.py:498
  90.4 13.9 %collective-permute-start.6 = (bf16[528,512]{1,0:T(8,128)(2,1)}, bf16[528,512]{1,0:T(8,128)(2,1)S(1)}, u32[]{:S(2)}, u32[]{:S(2)}) collective-permute-start(bf16[528,512]{1,0:T(8,128)(2,1)} %get-tuple-element.50), channel_id=1, source_target_pairs={{0,1},{1,2},{2,3},{3,0},{4,5},{5,6},{6,7},{7,4},{8,9},{9,10},{10,1... | collective-permute-start | bytes 1622024 | tf_op jit(solution)/shard_map/ppermute | solution.py:498
  93.5 13.5 %collective-permute-start.9 = (bf16[528,512]{1,0:T(8,128)(2,1)}, bf16[528,512]{1,0:T(8,128)(2,1)S(1)}, u32[]{:S(2)}, u32[]{:S(2)}) collective-permute-start(bf16[528,512]{1,0:T(8,128)(2,1)} %get-tuple-element.54), channel_id=1, source_target_pairs={{0,4},{1,5},{2,6},{3,7},{4,8},{5,9},{6,10},{7,11},{8,12},{9,13},{1... | collective-permute-start | bytes 1622024 | tf_op jit(solution)/shard_map/ppermute | solution.py:498
  140.6 34.3 %collective-permute-start.29 = (bf16[4,256,1024]{2,1,0:T(8,128)(2,1)}, bf16[4,256,1024]{2,1,0:T(8,128)(2,1)}, u32[]{:S(2)}, u32[]{:S(2)}) collective-permute-start(bf16[4,256,1024]{2,1,0:T(8,128)(2,1)} %other.1), channel_id=1, source_target_pairs={{0,16},{16,0},{32,48},{48,32},{64,80},{80,64},{96,112},{112,96},{1... | collective-permute-start | bytes 6291464 | tf_op jit(solution)/shard_map/ppermute | solution.py:490
  140.6 15.3 %collective-permute-start.17 = (bf16[528,512]{1,0:T(8,128)(2,1)S(1)}, bf16[528,512]{1,0:T(8,128)(2,1)}, u32[]{:S(2)}, u32[]{:S(2)}) collective-permute-start(bf16[528,512]{1,0:T(8,128)(2,1)S(1)} %copy-done.25), channel_id=1, source_target_pairs={{0,3},{1,0},{2,1},{3,2},{4,7},{5,4},{6,5},{7,6},{8,11},{9,8},{10,9... | collective-permute-start | bytes 1622024 | tf_op jit(solution)/shard_map/ppermute | solution.py:498
  141.7 16.8 %collective-permute-start.18 = (bf16[528,512]{1,0:T(8,128)(2,1)S(1)}, bf16[528,512]{1,0:T(8,128)(2,1)}, u32[]{:S(2)}, u32[]{:S(2)}) collective-permute-start(bf16[528,512]{1,0:T(8,128)(2,1)S(1)} %copy-done.24), channel_id=1, source_target_pairs={{0,2},{1,3},{2,0},{3,1},{4,6},{5,7},{6,4},{7,5},{8,10},{9,11},{10,... | collective-permute-start | bytes 1622024 | tf_op jit(solution)/shard_map/ppermute | solution.py:498
  143.2 26.1 %collective-permute-start.19 = (bf16[528,512]{1,0:T(8,128)(2,1)}, bf16[528,512]{1,0:T(8,128)(2,1)}, u32[]{:S(2)}, u32[]{:S(2)}) collective-permute-start(bf16[528,512]{1,0:T(8,128)(2,1)} %get-tuple-element.76), channel_id=1, source_target_pairs={{0,1},{1,2},{2,3},{3,0},{4,5},{5,6},{6,7},{7,4},{8,9},{9,10},{10,1... | collective-permute-start | bytes 1622024 | tf_op jit(solution)/shard_map/ppermute | solution.py:498
  143.6 36.1 %collective-permute-start.23 = (bf16[528,512]{1,0:T(8,128)(2,1)}, bf16[528,512]{1,0:T(8,128)(2,1)S(1)}, u32[]{:S(2)}, u32[]{:S(2)}) collective-permute-start(bf16[528,512]{1,0:T(8,128)(2,1)} %get-tuple-element.86), channel_id=1, source_target_pairs={{0,12},{1,13},{2,14},{3,15},{4,0},{5,1},{6,2},{7,3},{8,4},{9,5},{1... | collective-permute-start | bytes 1622024 | tf_op jit(solution)/shard_map/ppermute | solution.py:498
  152.1 22.8 %copy-start.3 = (bf16[4,256,1024]{2,1,0:T(8,128)(2,1)S(1)}, bf16[4,256,1024]{2,1,0:T(8,128)(2,1)}, u32[]{:S(2)}) copy-start(bf16[4,256,1024]{2,1,0:T(8,128)(2,1)} %own.1) | copy-start | bytes 6291460
  155.9 36.5 %collective-permute-start.24 = (bf16[528,512]{1,0:T(8,128)(2,1)}, bf16[528,512]{1,0:T(8,128)(2,1)S(1)}, u32[]{:S(2)}, u32[]{:S(2)}) collective-permute-start(bf16[528,512]{1,0:T(8,128)(2,1)} %get-tuple-element.87), channel_id=1, source_target_pairs={{0,8},{1,9},{2,10},{3,11},{4,12},{5,13},{6,14},{7,15},{8,0},{9,1},... | collective-permute-start | bytes 1622024 | tf_op jit(solution)/shard_map/ppermute | solution.py:498
  158.5 35.4 %collective-permute-start.25 = (bf16[528,512]{1,0:T(8,128)(2,1)}, bf16[528,512]{1,0:T(8,128)(2,1)S(1)}, u32[]{:S(2)}, u32[]{:S(2)}) collective-permute-start(bf16[528,512]{1,0:T(8,128)(2,1)} %get-tuple-element.88), channel_id=1, source_target_pairs={{0,4},{1,5},{2,6},{3,7},{4,8},{5,9},{6,10},{7,11},{8,12},{9,13},{1... | collective-permute-start | bytes 1622024 | tf_op jit(solution)/shard_map/ppermute | solution.py:498
  174.0 25.5 %collective-permute-start.20 = (bf16[256,512]{1,0:T(8,128)(2,1)}, bf16[256,512]{1,0:T(8,128)(2,1)S(1)}, u32[]{:S(2)}, u32[]{:S(2)}) collective-permute-start(bf16[256,512]{1,0:T(8,128)(2,1)} %get-tuple-element.78), channel_id=1, source_target_pairs={{0,12},{1,13},{2,14},{3,15},{4,0},{5,1},{6,2},{7,3},{8,4},{9,5},{1... | collective-permute-start | bytes 786440 | tf_op jit(solution)/shard_map/ppermute | solution.py:498
  179.6 21.4 %collective-permute-start.30 = (bf16[128,1024]{1,0:T(8,128)(2,1)S(1)}, bf16[128,1024]{1,0:T(8,128)(2,1)S(1)}, u32[]{:S(2)}, u32[]{:S(2)}) collective-permute-start(bf16[128,1024]{1,0:T(8,128)(2,1)S(1)} %get-tuple-element.101), channel_id=1, source_target_pairs={{0,32},{16,48},{32,64},{48,80},{64,96},{80,112},{96,0},{112,16},{1... | collective-permute-start | bytes 786440 | tf_op jit(solution)/shard_map/ppermute | solution.py:486
  179.7 12.7 %copy-start.19 = (bf16[528,512]{1,0:T(8,128)(2,1)}, bf16[528,512]{1,0:T(8,128)(2,1)S(1)}, u32[]{:S(2)}) copy-start(bf16[528,512]{1,0:T(8,128)(2,1)S(1)} %collective-permute-done.23.refs_5_) | copy-start | bytes 1622020
  179.7 12.7 %copy-start.28 = (bf16[256,512]{1,0:T(8,128)(2,1)S(1)}, bf16[256,512]{1,0:T(8,128)(2,1)}, u32[]{:S(2)}) copy-start(bf16[256,512]{1,0:T(8,128)(2,1)} %get-tuple-element.79) | copy-start | bytes 786436
  179.7 14.2 %copy-start.27 = (bf16[256,512]{1,0:T(8,128)(2,1)S(1)}, bf16[256,512]{1,0:T(8,128)(2,1)}, u32[]{:S(2)}) copy-start(bf16[256,512]{1,0:T(8,128)(2,1)} %get-tuple-element.80) | copy-start | bytes 786436
  179.7 21.9 %collective-permute-start.32 = (bf16[128,1024]{1,0:T(8,128)(2,1)S(1)}, bf16[128,1024]{1,0:T(8,128)(2,1)S(1)}, u32[]{:S(2)}, u32[]{:S(2)}) collective-permute-start(bf16[128,1024]{1,0:T(8,128)(2,1)S(1)} %get-tuple-element.102), channel_id=1, source_target_pairs={{0,96},{16,112},{32,0},{48,16},{64,32},{80,48},{96,64},{112,80},{1... | collective-permute-start | bytes 786440 | tf_op jit(solution)/shard_map/ppermute | solution.py:486
  192.4 13.1 %collective-permute-start.21 = (bf16[256,512]{1,0:T(8,128)(2,1)S(1)}, bf16[256,512]{1,0:T(8,128)(2,1)S(1)}, u32[]{:S(2)}, u32[]{:S(2)}) collective-permute-start(bf16[256,512]{1,0:T(8,128)(2,1)S(1)} %copy-done.28), channel_id=1, source_target_pairs={{0,8},{1,9},{2,10},{3,11},{4,12},{5,13},{6,14},{7,15},{8,0},{9,1},... | collective-permute-start | bytes 786440 | tf_op jit(solution)/shard_map/ppermute | solution.py:498
  194.0 13.5 %collective-permute-start.22 = (bf16[256,512]{1,0:T(8,128)(2,1)S(1)}, bf16[256,512]{1,0:T(8,128)(2,1)S(1)}, u32[]{:S(2)}, u32[]{:S(2)}) collective-permute-start(bf16[256,512]{1,0:T(8,128)(2,1)S(1)} %copy-done.27), channel_id=1, source_target_pairs={{0,4},{1,5},{2,6},{3,7},{4,8},{5,9},{6,10},{7,11},{8,12},{9,13},{1... | collective-permute-start | bytes 786440 | tf_op jit(solution)/shard_map/ppermute | solution.py:498
  199.5 9.5 %collective-permute-start.26 = (bf16[256,512]{1,0:T(8,128)(2,1)}, bf16[256,512]{1,0:T(8,128)(2,1)S(1)}, u32[]{:S(2)}, u32[]{:S(2)}) collective-permute-start(bf16[256,512]{1,0:T(8,128)(2,1)} %get-tuple-element.90), channel_id=1, source_target_pairs={{0,3},{1,0},{2,1},{3,2},{4,7},{5,4},{6,5},{7,6},{8,11},{9,8},{10,9... | collective-permute-start | bytes 786440 | tf_op jit(solution)/shard_map/ppermute | solution.py:498
  201.1 11.0 %collective-permute-start.27 = (bf16[256,512]{1,0:T(8,128)(2,1)}, bf16[256,512]{1,0:T(8,128)(2,1)S(1)}, u32[]{:S(2)}, u32[]{:S(2)}) collective-permute-start(bf16[256,512]{1,0:T(8,128)(2,1)} %get-tuple-element.91), channel_id=1, source_target_pairs={{0,2},{1,3},{2,0},{3,1},{4,6},{5,7},{6,4},{7,5},{8,10},{9,11},{10,... | collective-permute-start | bytes 786440 | tf_op jit(solution)/shard_map/ppermute | solution.py:498
  201.7 13.3 %collective-permute-start.28 = (bf16[256,512]{1,0:T(8,128)(2,1)}, bf16[256,512]{1,0:T(8,128)(2,1)S(1)}, u32[]{:S(2)}, u32[]{:S(2)}) collective-permute-start(bf16[256,512]{1,0:T(8,128)(2,1)} %get-tuple-element.92), channel_id=1, source_target_pairs={{0,1},{1,2},{2,3},{3,0},{4,5},{5,6},{6,7},{7,4},{8,9},{9,10},{10,1... | collective-permute-start | bytes 786440 | tf_op jit(solution)/shard_map/ppermute | solution.py:498
  205.6 13.8 %collective-permute-start.33 = (bf16[256,1024]{1,0:T(8,128)(2,1)}, bf16[256,1024]{1,0:T(8,128)(2,1)}, u32[]{:S(2)}, u32[]{:S(2)}) collective-permute-start(bf16[256,1024]{1,0:T(8,128)(2,1)} %pad_maximum_fusion.3), channel_id=1, source_target_pairs={{0,96},{16,112},{32,0},{48,16},{64,32},{80,48},{96,64},{112,80},{1... | collective-permute-start | bytes 1572872 | tf_op jit(solution)/shard_map/ppermute | solution.py:486
  207.5 15.0 %collective-permute-start.31 = (bf16[256,1024]{1,0:T(8,128)(2,1)}, bf16[256,1024]{1,0:T(8,128)(2,1)}, u32[]{:S(2)}, u32[]{:S(2)}) collective-permute-start(bf16[256,1024]{1,0:T(8,128)(2,1)} %pad_maximum_fusion.2), channel_id=1, source_target_pairs={{0,32},{16,48},{32,64},{48,80},{64,96},{80,112},{96,0},{112,16},{1... | collective-permute-start | bytes 1572872 | tf_op jit(solution)/shard_map/ppermute | solution.py:486
  (20 other events, 79.2 us)

commit v5 on v4

v5 whole, which is shorter than its diff:
```python
import functools
import math

import jax
import jax.numpy as jnp
from jax import lax
from jax.experimental import pallas as pl
from jax.experimental.pallas import tpu as pltpu
from jax.sharding import PartitionSpec as P

F32 = jnp.float32
BF16 = jnp.bfloat16
I32 = jnp.int32
LOW = -1e30
NT = (((1,), (1,)), ((), ()))
TN = (((0,), (0,)), ((), ()))
NN = (((1,), (0,)), ((), ()))
VMEM_LIMIT = 60 * 1024 * 1024


def mm(a, b, dims=NN):
    return lax.dot_general(a, b, dims, preferred_element_type=F32)


def iota(shape, dim):
    return lax.broadcasted_iota(I32, shape, dim)


def split3(x):
    a = x.astype(BF16)
    rest = x - a.astype(F32)
    b = rest.astype(BF16)
    c = (rest - b.astype(F32)).astype(BF16)
    return jnp.concatenate([a, b, c], axis=0)


def full(shape):
    return pl.BlockSpec(shape, lambda *_: (0,) * len(shape))


def call(kernel, name, steps, ins, outs, shapes, scratch, weight):
    return pl.pallas_call(
        kernel,
        grid_spec=pltpu.PrefetchScalarGridSpec(
            num_scalar_prefetch=1, grid=(steps,), in_specs=ins, out_specs=outs,
            scratch_shapes=scratch,
        ),
        out_shape=shapes,
        compiler_params=pltpu.CompilerParams(
            dimension_semantics=("arbitrary",), vmem_limit_bytes=VMEM_LIMIT
        ),
        cost_estimate=pl.CostEstimate(flops=weight, bytes_accessed=1 << 16, transcendentals=0),
        name=name,
    )


LIGHT, MIDDLE, HEAVY = 1 << 20, 1 << 32, 1 << 39
SIDE = 4
CORES = 2


def rep_of(x, y):
    return x % SIDE * SIDE + y % SIDE


def columns_of(place_ref, half, shift):
    x, y = place_ref[1], place_ref[2]
    return rep_of(x, y + shift) if half == 0 else rep_of(x + shift, y)


def source_of(place_ref, half, shift):
    x, y = place_ref[1], place_ref[2]
    return rep_of(x + SIDE - shift, y) if half == 0 else rep_of(x, y + SIDE - shift)


def hits_of(ranks, groups, cap):
    shape = (ranks.shape[0] * cap, ranks.shape[0])
    pick = (iota(shape, 1) == iota(shape, 0) // cap).astype(BF16)
    spread = mm(pick, ranks)
    return pick, spread == (iota(spread.shape, 0) % cap + 1).astype(F32)


def mid_kernel(shift, cap, groups, reps, negs, place_ref, *refs):
    sources = (refs[0:SIDE], refs[SIDE : 2 * SIDE])
    outs, ranks_out = refs[2 * SIDE : 2 * SIDE + 2], refs[2 * SIDE + 2 :]
    rows, half_width = sources[0][0].shape
    toks = rows - 16
    slots = groups * cap
    before = (iota((toks, toks), 0) < iota((toks, toks), 1)).astype(BF16)
    for half in range(2):
        col = columns_of(place_ref, half, shift)
        dev = (iota((groups, toks), 0) * reps + col).astype(F32)
        named_all, rows_all = [], []
        for source in sources[half]:
            table = source[toks:, :toks].astype(F32)
            named = jnp.zeros((groups, toks), F32)
            wanted = jnp.zeros((groups, toks), F32)
            for k in range(negs):
                hit = dev == table[k : k + 1]
                named = named + jnp.where(hit, 1.0, 0.0)
                wanted = wanted + jnp.where(hit, table[8 + k : 9 + k] + 1.0, 0.0)
            named_all.append(named)
            rows_all.append(wanted)
        named = jnp.concatenate(named_all, axis=0)
        wanted = jnp.concatenate(rows_all, axis=0).astype(BF16)
        ranks = (named * (mm(named.astype(BF16), before) + 1.0)).astype(BF16)
        ranks_out[half][...] = ranks
        pick, hit = hits_of(ranks, groups, cap)
        hot = hit.astype(BF16)
        row = jnp.where(hit, mm(pick, wanted), 0.0).astype(BF16)
        ids = mm(jnp.ones((8, toks), BF16), row, NT)[0:1]
        tok = mm(iota((8, toks), 1).astype(F32).astype(BF16), hot, NT)[0:1]
        for s, source in enumerate(sources[half]):
            moved = mm(hot[s * slots : (s + 1) * slots], source[:toks, :]).astype(BF16)
            for g in range(groups):
                first = (g * SIDE + s) * cap
                outs[half][first : first + cap, :] = moved[g * cap : (g + 1) * cap]
        codes = [v[:, s * slots : (s + 1) * slots] for v in (ids, tok) for s in range(SIDE)]
        codes = jnp.concatenate(codes + [jnp.zeros((8, slots), F32)], axis=0)
        codes = jnp.concatenate([codes, jnp.zeros((16, half_width - slots), F32)], axis=1)
        outs[half][groups * SIDE * cap :, :] = codes.astype(BF16)


def mid(place, shift, first, second, groups, reps, cap, negs):
    rows, half_width = first[0].shape
    slots = jax.ShapeDtypeStruct((groups * SIDE * cap + 16, half_width), BF16)
    ranks = jax.ShapeDtypeStruct((SIDE * groups, rows - 16), BF16)
    return call(
        functools.partial(mid_kernel, shift, cap, groups, reps, negs), "mid", 1,
        [full((rows, half_width))] * (2 * SIDE),
        [full(slots.shape)] * 2 + [full(ranks.shape)] * 2,
        [slots, slots, ranks, ranks], [], LIGHT,
    )(place, *first, *second)


def inside_kernel(temper, place_ref, p_ref, q_ref, out_ref, top, total):
    step = pl.program_id(0)

    @pl.when(step == 0)
    def _():
        top[...] = jnp.full(top.shape, LOW, F32)
        total[...] = jnp.zeros(total.shape, F32)

    scores = temper * mm(p_ref[...], q_ref[...], NT)
    high = jnp.maximum(top[...], jnp.max(scores, axis=0, keepdims=True))
    total[...] = total[...] * jnp.exp(top[...] - high) + jnp.sum(
        jnp.exp(scores - high), axis=0, keepdims=True
    )
    top[...] = high

    @pl.when(step == pl.num_programs(0) - 1)
    def _():
        out_ref[...] = top[...] + jnp.log(total[...])


def inside(place, gathered, queries, temper):
    toks, width = queries.shape
    return call(
        functools.partial(inside_kernel, temper), "inside", 2,
        [pl.BlockSpec((gathered.shape[0] // 2, width), lambda s, _: (s, 0)), full((toks, width))],
        full((1, toks)), jax.ShapeDtypeStruct((1, toks), F32),
        [pltpu.VMEM((1, toks), F32), pltpu.VMEM((1, toks), F32)], MIDDLE,
    )(place, gathered, queries)


def asking_rows(first, second, base, cap):
    def piece(ref, s):
        return ref[base + s * cap : base + (s + 1) * cap, :]

    pairs = [(dx, dy) for dx in range(SIDE) for dy in range(SIDE)]
    one = jnp.concatenate([piece(first[dy], dx) for dx, dy in pairs], axis=0)
    two = jnp.concatenate([piece(second[dx], dy) for dx, dy in pairs], axis=0)
    return one, two


def source_mask(place_ref, reps, cap):
    shape = (reps, reps * cap)
    dx = iota(shape, 1) // (SIDE * cap)
    dy = iota(shape, 1) // cap % SIDE
    x = (place_ref[1] + SIDE - dx) % SIDE
    y = (place_ref[2] + SIDE - dy) % SIDE
    return iota(shape, 0) == x * SIDE + y


def hard_kernel(reps, cap, temper, place_ref, *refs):
    first, second, exts = refs[0:4], refs[4:8], refs[8:12]
    p_ref, inside_ref = refs[12:14]
    out_first, out_second = refs[14:18], refs[18:22]
    hs_ref, code_ref, part_ref, top, total = refs[22:]
    step = pl.program_id(0)
    levels = pl.num_programs(0) - 1
    toks = inside_ref.shape[1]
    half_width = p_ref.shape[1] // 2
    slots = reps * cap
    groups = code_ref.shape[0] // 2
    source = source_mask(place_ref, reps, cap)

    @pl.when(step == 0)
    def _():
        top[...] = jnp.full(top.shape, LOW, F32)
        total[...] = jnp.zeros(total.shape, F32)
        table = jnp.concatenate([ext[...] for ext in exts], axis=0)[:, : groups * cap]
        shape = (groups * cap, groups * slots)
        lane, slot = iota(shape, 0), iota(shape, 1)
        to_slot = (lane == slot // slots * cap + slot % cap).astype(BF16)
        laid = mm(table, to_slot)
        row, slot = iota(laid.shape, 0), iota(laid.shape, 1) % slots
        dx, dy = slot // (SIDE * cap), slot // cap % SIDE
        want = dy * 16 + dx
        ids = jnp.sum(jnp.where(row == want, laid, 0.0), axis=0, keepdims=True).astype(I32)
        tok = jnp.sum(jnp.where(row == want + SIDE, laid, 0.0), axis=0, keepdims=True).astype(I32)
        for g in range(groups):
            code_ref[g : g + 1, :] = ids[:, g * slots : (g + 1) * slots]
            code_ref[groups + g : groups + g + 1, :] = tok[:, g * slots : (g + 1) * slots]

    @pl.when(step < levels)
    def _():
        values = []
        for core in range(CORES):
            group = CORES * step + core
            ids = code_ref[pl.ds(group, 1), :]
            tok = code_ref[pl.ds(groups + group, 1), :]
            valid = ids > 0
            base = core * SIDE * cap
            one, two = asking_rows(first, second, base, cap)
            passages = p_ref[core * toks : (core + 1) * toks, :]
            cross = mm(passages, jnp.concatenate([one, two], axis=1), NT)
            hit = iota((toks, slots), 0) + 1 == ids
            hs = temper * jnp.sum(jnp.where(hit, cross, 0.0), axis=0, keepdims=True)
            hs_ref[pl.ds(group, 1), :] = hs
            served = mm(hit.astype(BF16), passages, TN).astype(BF16)
            for dx in range(SIDE):
                for dy in range(SIDE):
                    at = (dx * SIDE + dy) * cap
                    out_first[dy][base + dx * cap : base + (dx + 1) * cap, :] = served[
                        at : at + cap, :half_width
                    ]
                    out_second[dx][base + dy * cap : base + (dy + 1) * cap, :] = served[
                        at : at + cap, half_width:
                    ]
            token = ((iota((toks, slots), 0) == tok) & valid).astype(BF16)
            live = source & valid
            parts = jnp.concatenate(
                [split3(jnp.where(live, hs, 0.0)), live.astype(BF16)], axis=0
            )
            laid = mm(parts, token, NT)
            there = laid[3 * reps :] > 0.5
            value = laid[:reps] + laid[reps : 2 * reps] + laid[2 * reps : 3 * reps]
            values.append((there, jnp.where(there, value, LOW)))
        high = top[...]
        for there, value in values:
            high = jnp.maximum(high, value)
        new = total[...] * jnp.exp(top[...] - high)
        for there, value in values:
            new = new + jnp.where(there, jnp.exp(value - high), 0.0)
        total[...] = new
        top[...] = high

    @pl.when(step == levels)
    def _():
        part = jnp.where(total[...] > 0.0, top[...] + jnp.log(total[...]), LOW)
        within = inside_ref[...]
        high = jnp.maximum(part, within)
        both = high + jnp.log(jnp.exp(part - high) + jnp.exp(within - high))
        own = iota(part.shape, 0) == rep_of(place_ref[1], place_ref[2])
        part_ref[...] = jnp.broadcast_to(jnp.where(own, both, part)[None], part_ref.shape)
        pieces = split3(hs_ref[...]).astype(F32)
        pieces = jnp.concatenate([pieces, jnp.zeros((groups, slots), F32)], axis=0)
        pieces = jnp.concatenate(
            [pieces, jnp.zeros((4 * groups, half_width - slots), F32)], axis=1
        ).astype(BF16)
        for out in (*out_first, *out_second):
            out[: 4 * groups, :] = pieces


def hard(place, first, second, gathered, within, temper, reps, cap):
    rows, half_width = first[0].shape
    toks = within.shape[1]
    groups = gathered.shape[0] // toks
    levels = groups // CORES
    slots = reps * cap
    per = CORES * SIDE * cap
    ins = pl.BlockSpec((per, half_width), lambda s, _: (lax.min(s, levels - 1), 0))
    outs = pl.BlockSpec((per, half_width), lambda s, _: (s, 0))
    ext = pl.BlockSpec((16, half_width), lambda s, _: (groups * SIDE * cap // 16, 0))
    made = call(
        functools.partial(hard_kernel, reps, cap, temper), "hard", levels + 1,
        [ins] * 8 + [ext] * 4
        + [pl.BlockSpec((CORES * toks, CORES * half_width),
                        lambda s, _: (lax.min(s, levels - 1), 0)), full((1, toks))],
        [outs] * 8 + [full((groups, slots)), full((2 * groups, slots)), full((reps, reps, toks))],
        [jax.ShapeDtypeStruct((groups * SIDE * cap + 4 * groups, half_width), BF16)] * 8
        + [jax.ShapeDtypeStruct((groups, slots), F32),
           jax.ShapeDtypeStruct((2 * groups, slots), I32),
           jax.ShapeDtypeStruct((reps, reps, toks), F32)],
        [pltpu.VMEM((reps, toks), F32), pltpu.VMEM((reps, toks), F32)], LIGHT,
    )(place, *first, *second, *first, gathered, within)
    return made[0:4], made[4:8], made[8], made[9], made[10]


def own_row(lt_ref, rep):
    lt = lt_ref[...]
    return jnp.sum(jnp.where(iota(lt.shape, 0) == rep, lt, 0.0), axis=0, keepdims=True)


def column_kernel(reps, cap, temper, place_ref, code_ref, hs_ref, lt_ref, *refs):
    first, second = refs[0:4], refs[4:8]
    p_ref, q_ref, gp_ref, d_ref = refs[8:]
    step = pl.program_id(0)
    toks, width = q_ref.shape
    half_width = width // 2
    slots = reps * cap
    groups = code_ref.shape[0] // 2

    @pl.when(step == 0)
    def _():
        log_parts = split3(lt_ref[...])
        source = source_mask(place_ref, reps, cap)
        rows = []
        for g in range(groups):
            valid = code_ref[g : g + 1, :] > 0
            tok = code_ref[groups + g : groups + g + 1, :]
            token = ((iota((toks, slots), 0) == tok) & valid).astype(BF16)
            found = mm(log_parts, token)
            found = found[:reps] + found[reps : 2 * reps] + found[2 * reps :]
            log_slot = jnp.sum(jnp.where(source, found, 0.0), axis=0, keepdims=True)
            rows.append(jnp.where(valid, jnp.exp(hs_ref[g : g + 1, :] - log_slot), 0.0))
        d_ref[...] = jnp.concatenate(rows, axis=0)

    queries = q_ref[...]
    lt_own = own_row(lt_ref, rep_of(place_ref[1], place_ref[2]))
    for core in range(CORES):
        group = CORES * step + core
        here = pl.ds(core * toks, toks)
        ids = code_ref[pl.ds(group, 1), :]
        d_hard = d_ref[pl.ds(group, 1), :]
        hot = jnp.where(iota((toks, slots), 0) + 1 == ids, d_hard, 0.0).astype(BF16)
        scores = temper * mm(p_ref[here, :], queries, NT)
        eye = (iota((toks, toks), 0) == iota((toks, toks), 1)) & (group == place_ref[0])
        d_scores = (jnp.exp(scores - lt_own) - jnp.where(eye, 1.0, 0.0)).astype(BF16)
        both = jnp.concatenate([hot, d_scores], axis=1)
        one, two = asking_rows(first, second, core * SIDE * cap, cap)
        rows = jnp.concatenate([jnp.concatenate([one, two], axis=1), queries], axis=0)
        gp_ref[here, :] = (temper * mm(both, rows)).astype(BF16)


def column(place, codes, hard_scores, log_total, first, second, gathered, queries, temper, cap):
    reps = log_total.shape[0]
    toks, width = queries.shape
    slots = pl.BlockSpec((CORES * SIDE * cap, width // 2), lambda s, _: (s, 0))
    block = pl.BlockSpec((CORES * toks, width), lambda s, _: (s, 0))
    return call(
        functools.partial(column_kernel, reps, cap, temper), "column",
        gathered.shape[0] // (CORES * toks),
        [full(codes.shape), full(hard_scores.shape), full(log_total.shape)] + [slots] * 8
        + [block, full((toks, width))],
        block, jax.ShapeDtypeStruct(gathered.shape, BF16),
        [pltpu.VMEM(hard_scores.shape, F32)], LIGHT,
    )(place, codes, hard_scores, log_total, *first, *second, gathered, queries)


def inner_kernel(temper, place_ref, lt_ref, p_ref, q_ref, gq_ref, loss_ref):
    step = pl.program_id(0)
    toks, width = q_ref.shape
    lt_own = own_row(lt_ref, rep_of(place_ref[1], place_ref[2]))
    passages = p_ref[...]
    scores = temper * mm(passages, q_ref[...], NT)
    row = iota(scores.shape, 0) + passages.shape[0] * step - toks * place_ref[0]
    eye = row == iota(scores.shape, 1)
    d_scores = (jnp.exp(scores - lt_own) - jnp.where(eye, 1.0, 0.0)).astype(BF16)
    new = mm(d_scores, passages, TN)
    own = jnp.sum(jnp.where(eye, scores, 0.0), axis=0, keepdims=True)

    @pl.when(step == 0)
    def _():
        gq_ref[...] = new
        loss_ref[...] = lt_own - own

    @pl.when(step > 0)
    def _():
        gq_ref[...] += new
        loss_ref[...] -= own


def inner(place, log_total, gathered, queries, temper):
    toks, width = queries.shape
    return call(
        functools.partial(inner_kernel, temper), "inner", 2,
        [full(log_total.shape), pl.BlockSpec((gathered.shape[0] // 2, width), lambda s, _: (s, 0)),
         full((toks, width))],
        [full((toks, width)), full((1, toks))],
        [jax.ShapeDtypeStruct((toks, width), F32), jax.ShapeDtypeStruct((1, toks), F32)],
        [], LIGHT,
    )(place, log_total, gathered, queries)


def reduce_kernel(half, cap, groups, place_ref, lt_ref, *refs):
    ranks, rows, outs = refs[0:4], refs[4:8], refs[8:12]
    toks = lt_ref.shape[1]
    slots = groups * cap
    reps = lt_ref.shape[0]
    shape = (SIDE * slots, 4 * groups)
    group = iota(shape, 0) // cap % groups
    parts = (iota(shape, 1) % groups == group) & (iota(shape, 1) < 3 * groups)
    parts = parts.astype(BF16)
    log_rows = jnp.concatenate(
        [jnp.broadcast_to(own_row(lt_ref, source_of(place_ref, half, s)), (slots, toks))
         for s in range(SIDE)], axis=0
    )
    weights = []
    for line in range(SIDE):
        scores = mm(parts, rows[line][slots * SIDE :, : reps * cap])
        slot, lane = iota(scores.shape, 0), iota(scores.shape, 1)
        s = slot // slots
        block = s * SIDE + line if half == 0 else line * SIDE + s
        hs = jnp.sum(
            jnp.where(lane == block * cap + slot % cap, scores, 0.0), axis=1, keepdims=True
        )
        _, hit = hits_of(ranks[line][...], groups, cap)
        weights.append(jnp.where(hit, jnp.exp(hs - log_rows), 0.0).astype(BF16))
    for s in range(SIDE):
        values = [
            rows[line][(g * SIDE + s) * cap : (g * SIDE + s + 1) * cap, :]
            for line in range(SIDE) for g in range(groups)
        ]
        weight = jnp.concatenate([w[s * slots : (s + 1) * slots] for w in weights], axis=0)
        outs[s][...] = mm(weight, jnp.concatenate(values, axis=0), TN).astype(outs[s].dtype)


def reduce(place, half, log_total, ranks, rows, groups, cap):
    toks = log_total.shape[1]
    shape = (toks, rows[0].shape[1])
    return call(
        functools.partial(reduce_kernel, half, cap, groups), "reduce", 1,
        [full(log_total.shape)] + [full(ranks[0].shape)] * 4 + [full(rows[0].shape)] * 4,
        [full(shape)] * 4,
        [jax.ShapeDtypeStruct(shape, F32)] + [jax.ShapeDtypeStruct(shape, BF16)] * 3, [], LIGHT,
    )(place, log_total, *ranks, *rows)


def final_kernel(temper, place_ref, gq_ref, *refs):
    out_ref = refs[8]
    half_width = out_ref.shape[1] // 2
    for half in range(2):
        lanes = slice(half * half_width, (half + 1) * half_width)
        total = gq_ref[:, lanes]
        for ref in refs[4 * half : 4 * half + 4]:
            total = total + ref[...].astype(F32)
        out_ref[:, lanes] = (temper * total).astype(BF16)


def final(place, within, first, second, temper):
    rows, width = within.shape
    wide = pl.BlockSpec((rows // 4, width), lambda s, _: (s, 0))
    narrow = pl.BlockSpec((rows // 4, width // 2), lambda s, _: (s, 0))
    return call(
        functools.partial(final_kernel, temper), "final", 4, [wide] + [narrow] * 8, wide,
        jax.ShapeDtypeStruct((rows, width), BF16), [], HEAVY,
    )(place, within, *first, *second)


def along(x, half, shift):
    pairs = []
    for i in range(SIDE * SIDE):
        a, b = i // SIDE, i % SIDE
        pairs.append((i, rep_of(a + shift, b) if half == 0 else rep_of(a, b + shift)))
    return lax.ppermute(x, "rep", pairs)


def shards(queries, passages, neg_device, neg_row):
    toks, width = queries.shape
    negs = neg_device.shape[1]
    groups = lax.axis_size("grp")
    reps = lax.axis_size("rep")
    cap = 8 * toks // (groups * reps)
    half_width = width // 2
    temper = 3.0 / math.sqrt(width)
    grp, rep = lax.axis_index("grp"), lax.axis_index("rep")
    place = jnp.stack([grp, rep // SIDE, rep % SIDE]).astype(I32)

    lines = jnp.pad(jnp.stack([neg_device.T, neg_row.T]), ((0, 0), (0, 8 - negs), (0, 0)))
    lines = jnp.pad(lines.reshape(16, toks), ((0, 0), (0, half_width - toks))).astype(BF16)
    sources = []
    for half in range(2):
        block = queries[:, half * half_width : (half + 1) * half_width]
        block = jnp.concatenate([block, lines], axis=0)
        sources.append([block] + [along(block, half, s) for s in range(1, SIDE)])
    gathered = lax.all_gather(passages, "grp", axis=0, tiled=True)

    first, second, ranks_first, ranks_second = [], [], [], []
    for shift in range(SIDE):
        one, two, rank_one, rank_two = mid(place, shift, *sources, groups, reps, cap, negs)
        first.append(along(one, 1, shift) if shift else one)
        second.append(along(two, 0, shift) if shift else two)
        ranks_first.append(rank_one)
        ranks_second.append(rank_two)

    within = inside(place, gathered, queries, temper)
    back_first, back_second, hard_scores, codes, part = hard(
        place, first, second, gathered, within, temper, reps, cap
    )
    parts = lax.all_to_all(part, "rep", split_axis=0, concat_axis=0, tiled=True)
    parts, back_first, back_second = lax.optimization_barrier((parts, back_first, back_second))
    high = jnp.max(parts, axis=0)
    log_total = high + jnp.log(jnp.sum(jnp.exp(parts - high), axis=0))

    back_first = [along(v, 1, -s) if s else v for s, v in enumerate(back_first)]
    back_second = [along(v, 0, -s) if s else v for s, v in enumerate(back_second)]

    partial_sum = column(
        place, codes, hard_scores, log_total, first, second, gathered, queries, temper, cap
    )
    grad_passages = lax.psum_scatter(partial_sum, "grp", scatter_dimension=0, tiled=True)
    grad_inner, losses = inner(place, log_total, gathered, queries, temper)

    sums = []
    for half, ranks, rows in ((0, ranks_first, back_first), (1, ranks_second, back_second)):
        made = reduce(place, half, log_total, ranks, rows, groups, cap)
        sums.append([along(v, half, -s) if s else v for s, v in enumerate(made)])
    grad_queries = final(place, grad_inner, *sums, temper)
    return (losses.reshape(toks), grad_queries, grad_passages)


def solution(mesh):
    in_specs = (
        P(("grp", "rep"), None),
        P(("grp", "rep"), None),
        P(("grp", "rep"), None),
        P(("grp", "rep"), None),
    )
    out_specs = (P(("grp", "rep")), P(("grp", "rep"), None), P(("grp", "rep"), None))
    return jax.shard_map(shards, mesh=mesh, in_specs=in_specs, out_specs=out_specs, check_vma=False)
```

time: 226 us -> 204 us (0.903)
  other arithmetic: 15.7 us -> 2.07 us
  Pallas kernels: 77.8 us -> 64.3 us
  between operations: 1.09 us -> 14.3 us
  starting transfers between devices: 44.3 us -> 32 us
  waiting for transfers between devices: 67.6 us -> 71.4 us
    reduce_scatter x0 -> x1, waiting for transfers between devices: none -> 27.3 us  [shards(): lax.psum_scatter(partial_sum, 'grp', scatter_dimension=0, tiled=True)]
    ppermute x10 -> x0, waiting for transfers between devices: 20.6 us -> none  [the longest x8 20.5 us: along_z(): lax.ppermute(x, 'grp', [(i, (i + CORES * shift) % groups) for i in range(...]
    ppermute x10 -> x0, starting transfers between devices: 13.3 us -> none  [the longest x8 13.3 us: along_z(): lax.ppermute(x, 'grp', [(i, (i + CORES * shift) % groups) for i in range(...]
    another operation x7 -> x1, other arithmetic: 10.7 us -> 0.61 us  [shards(): place = jnp.stack([grp, rep // SIDE, rep % SIDE]).astype(I32)]
    pallas_call x4, Pallas kernels: 23.8 us -> 18 us  [mid(): call(functools.partial(mid_kernel, shift, cap, groups, reps, negs), 'mid'...]
    pallas_call x5 -> x4, Pallas kernels: 33.6 us -> 28.3 us  [the longest x1 10.5 us: column(): call(functools.partial(column_kernel, reps, cap, temper), 'column', gathe...]
    ppermute x24, waiting for transfers between devices: 47 us -> 43.4 us  [along(): return lax.ppermute(x, 'rep', pairs)]
    unnamed x68 -> x52, local copies, waits for them, and re-layouts: 2.42 us -> 5.04 us
  transfers between devices with their start and end apart: 34 -> 26, of which waited for: 14 -> 9; matrix products, arithmetic and copies ran while one was open for 6% -> 2% of each run, Pallas kernels for 26% -> 27%
where the time goes in v5:
time: 204 us; the launch traced here: 203 us
  waiting for transfers between devices  71.4 us (35%)
  Pallas kernels  64.3 us (32%)
  starting transfers between devices  32 us (16%)
  between operations  14.3 us (7%)
  blocking collectives  12.9 us (6%)
  local copies, waits for them, and re-layouts  6.11 us (3%)
  other arithmetic  2.07 us (1%)
    ppermute x24, waiting for transfers between devices, along(): return lax.ppermute(x, 'rep', pairs)  43.4 us
    ppermute x24, starting transfers between devices, along(): return lax.ppermute(x, 'rep', pairs)  32 us
    reduce_scatter x1, waiting for transfers between devices, shards(): lax.psum_scatter(partial_sum, 'grp', scatter_dimension=0, tiled=True)  27.3 us
    pallas_call x4, Pallas kernels, mid(): call(functools.partial(mid_kernel, shift, cap, groups, reps, negs), 'mid'...  18 us
    all_to_all x1, blocking collectives, shards(): parts = lax.all_to_all(part, 'rep', split_axis=0, concat_axis=0, tiled=True)  12.9 us
    pallas_call x1, Pallas kernels, column(): call(functools.partial(column_kernel, reps, cap, temper), 'column', gathe...  10.5 us
    pallas_call x2, Pallas kernels, reduce(): call(functools.partial(reduce_kernel, half, cap, groups), 'reduce', 1, [f...  9.09 us
    pallas_call x1, Pallas kernels, hard(): call(functools.partial(hard_kernel, reps, cap, temper), 'hard', levels +...  9.02 us
  transfers between devices with their start and end apart: 26, of which 9 were waited for; matrix products, arithmetic and copies ran while one was open for 2% of the time, Pallas kernels for 27%

profile of v5, /device:TPU:0, one launch (start us, length us, event | category | flops | bytes accessed | tf_op | source)
XLA Modules:
  0.0 203.1 jit_solution(1765268642053557224)
XLA Ops:
  7.2 0.7 all-gather.2.cloned.1.call-update
  7.9 0.7 convert_bitcast_fusion
  8.7 1.1 fusion.7
  9.8 1.6 collective-permute-start
  11.5 2.7 %collective-permute-start.1 = (bf16[272,512]{1,0:T(8,128)(2,1)S(1)}, bf16[272,512]{1,0:T(8,128)(2,1)S(1)}, u32[]{:S(2)}, u32[]{:S(2)}) collective-permute-start(bf16[272,512]{1,0:T(8,128)(2,1)S(1)} %get-tuple-element.98.refs_0_), channel_id=1, source_target_pairs={{0,8},{1,9},{2,10},{3,11},{4,12},{5,13},{6,14},{7,15},{8,0},{9,1},... | collective-permute-start | bytes 835592 | tf_op jit(solution)/shard_map/ppermute | solution.py:467
  14.2 1.4 collective-permute-start.2
  15.6 1.6 collective-permute-start.3
  17.2 2.9 %collective-permute-start.4 = (bf16[272,512]{1,0:T(8,128)(2,1)S(1)}, bf16[272,512]{1,0:T(8,128)(2,1)S(1)}, u32[]{:S(2)}, u32[]{:S(2)}) collective-permute-start(bf16[272,512]{1,0:T(8,128)(2,1)S(1)} %get-tuple-element.97.refs_4_), channel_id=1, source_target_pairs={{0,2},{1,3},{2,0},{3,1},{4,6},{5,7},{6,4},{7,5},{8,10},{9,11},{10,... | collective-permute-start | bytes 835592 | tf_op jit(solution)/shard_map/ppermute | solution.py:467
  20.1 2.6 %collective-permute-start.5 = (bf16[272,512]{1,0:T(8,128)(2,1)S(1)}, bf16[272,512]{1,0:T(8,128)(2,1)S(1)}, u32[]{:S(2)}, u32[]{:S(2)}) collective-permute-start(bf16[272,512]{1,0:T(8,128)(2,1)S(1)} %get-tuple-element.97.refs_4_), channel_id=1, source_target_pairs={{0,3},{1,0},{2,1},{3,2},{4,7},{5,4},{6,5},{7,6},{8,11},{9,8},{10,9... | collective-permute-start | bytes 835592 | tf_op jit(solution)/shard_map/ppermute | solution.py:467
  23.4 3.2 %collective-permute-done.1.refs_2_ = bf16[272,512]{1,0:T(8,128)(2,1)S(1)} collective-permute-done((bf16[272,512]{1,0:T(8,128)(2,1)S(1)}, bf16[272,512]{1,0:T(8,128)(2,1)S(1)}, u32[]{:S(2)}, u32[]{:S(2)}) %collective-permute-start.1) | collective-permute-done | bytes 278560 | tf_op jit(solution)/shard_map/ppermute | solution.py:467
  26.6 5.0 %collective-permute-done.4.refs_6_ = bf16[272,512]{1,0:T(8,128)(2,1)S(1)} collective-permute-done((bf16[272,512]{1,0:T(8,128)(2,1)S(1)}, bf16[272,512]{1,0:T(8,128)(2,1)S(1)}, u32[]{:S(2)}, u32[]{:S(2)}) %collective-permute-start.4) | collective-permute-done | bytes 278560 | tf_op jit(solution)/shard_map/ppermute | solution.py:467
  31.7 0.6 copy-done.9
  32.3 0.7 copy-done.10
  33.0 4.6 %mid.5 = (bf16[528,512]{1,0:T(8,128)(2,1)}, bf16[528,512]{1,0:T(8,128)(2,1)}, bf16[32,256]{1,0:T(8,128)(2,1)}, bf16[32,256]{1,0:T(8,128)(2,1)}) custom-call(s32[3]{0:T(128)} %pad_add_fusion.place_ref, bf16[272,512]{1,0:T(8,128)(2,1)} %copy-done.1, bf16[272,512]{1,0:T(8,128)(2,1)} %copy-done.5, bf16[272,512]{1,0:T(8,128)(2,1)} %copy-done.6, ...), custom_call_target="tpu_custom_call" | custom-call | flops 1048576 | bytes 65536 | tf_op jit(solution)/shard_map/mid/pallas_call | solution.py:128
  37.6 1.3 collective-permute-start.6
  38.9 4.5 %mid.6 = (bf16[528,512]{1,0:T(8,128)(2,1)}, bf16[528,512]{1,0:T(8,128)(2,1)}, bf16[32,256]{1,0:T(8,128)(2,1)}, bf16[32,256]{1,0:T(8,128)(2,1)}) custom-call(s32[3]{0:T(128)} %pad_add_fusion.place_ref, bf16[272,512]{1,0:T(8,128)(2,1)} %copy-done.1, bf16[272,512]{1,0:T(8,128)(2,1)} %copy-done.5, bf16[272,512]{1,0:T(8,128)(2,1)} %copy-done.6, ...), custom_call_target="tpu_custom_call" | custom-call | flops 1048576 | bytes 65536 | tf_op jit(solution)/shard_map/mid/pallas_call | solution.py:128
  43.4 1.6 collective-permute-start.7
  45.0 4.5 %mid.7 = (bf16[528,512]{1,0:T(8,128)(2,1)}, bf16[528,512]{1,0:T(8,128)(2,1)}, bf16[32,256]{1,0:T(8,128)(2,1)}, bf16[32,256]{1,0:T(8,128)(2,1)}) custom-call(s32[3]{0:T(128)} %pad_add_fusion.place_ref, bf16[272,512]{1,0:T(8,128)(2,1)} %copy-done.1, bf16[272,512]{1,0:T(8,128)(2,1)} %copy-done.5, bf16[272,512]{1,0:T(8,128)(2,1)} %copy-done.6, ...), custom_call_target="tpu_custom_call" | custom-call | flops 1048576 | bytes 65536 | tf_op jit(solution)/shard_map/mid/pallas_call | solution.py:128
  49.4 1.6 collective-permute-start.8
  51.0 0.7 collective-permute-start.9
  51.7 1.1 collective-permute-start.10
  52.8 1.6 collective-permute-start.11
  54.4 4.5 %mid.4 = (bf16[528,512]{1,0:T(8,128)(2,1)}, bf16[528,512]{1,0:T(8,128)(2,1)}, bf16[32,256]{1,0:T(8,128)(2,1)}, bf16[32,256]{1,0:T(8,128)(2,1)}) custom-call(s32[3]{0:T(128)} %pad_add_fusion.place_ref, bf16[272,512]{1,0:T(8,128)(2,1)} %copy-done.1, bf16[272,512]{1,0:T(8,128)(2,1)} %copy-done.5, bf16[272,512]{1,0:T(8,128)(2,1)} %copy-done.6, ...), custom_call_target="tpu_custom_call" | custom-call | flops 1048576 | bytes 65536 | tf_op jit(solution)/shard_map/mid/pallas_call | solution.py:128
  58.9 5.0 %inside.1.refs_13_ = f32[1,256]{1,0:T(1,128)} custom-call(s32[3]{0:T(128)} %pad_add_fusion.place_ref, bf16[2048,1024]{1,0:T(8,128)(2,1)} %all-gather.2.cloned.1.call-done.p_ref.refs_12_.refs_8_, bf16[256,1024]{1,0:T(8,128)(2,1)} %refs_9_.1), custom_call_target="tpu_custom_call" | custom-call | flops 4294967296 | bytes 65536 | tf_op jit(solution)/shard_map/inside/pallas_call | solution.py:158
  63.8 4.1 %collective-permute-done.8.refs_3_.refs_11_ = bf16[528,512]{1,0:T(8,128)(2,1)S(1)} collective-permute-done((bf16[528,512]{1,0:T(8,128)(2,1)}, bf16[528,512]{1,0:T(8,128)(2,1)S(1)}, u32[]{:S(2)}, u32[]{:S(2)}) %collective-permute-start.8) | collective-permute-done | bytes 540704 | tf_op jit(solution)/shard_map/ppermute | solution.py:467
  67.9 9.3 %collective-permute-done.9.refs_5_ = bf16[528,512]{1,0:T(8,128)(2,1)S(1)} collective-permute-done((bf16[528,512]{1,0:T(8,128)(2,1)}, bf16[528,512]{1,0:T(8,128)(2,1)S(1)}, u32[]{:S(2)}, u32[]{:S(2)}) %collective-permute-start.9) | collective-permute-done | bytes 540704 | tf_op jit(solution)/shard_map/ppermute | solution.py:467
  78.6 9.0 %hard.1 = (bf16[544,512]{1,0:T(8,128)(2,1)}, bf16[544,512]{1,0:T(8,128)(2,1)}, bf16[544,512]{1,0:T(8,128)(2,1)}, bf16[544,512]{1,0:T(8,128)(2,1)}, bf16[544,512]...) custom-call(s32[3]{0:T(128)} %pad_add_fusion.place_ref, ...), custom_call_target="tpu_custom_call" | custom-call | flops 1048576 | bytes 65536 | tf_op jit(solution)/shard_map/hard/pallas_call | solution.py:286
  87.7 12.9 %all_to_all.5 = f32[16,16,256]{2,1,0:T(8,128)S(1)} all-to-all(f32[16,16,256]{2,1,0:T(8,128)} %get-tuple-element.57), channel_id=1, replica_groups=mesh['grp'=8,'rep'=16] {'rep'}, dimensions={0} | all-to-all | bytes 524288 | tf_op jit(solution)/shard_map/all_to_all | solution.py:502
  100.6 0.9 collective-permute-start.12
  101.5 1.6 collective-permute-start.13
  103.5 1.0 collective-permute-start.18
  104.4 1.5 collective-permute-start.19
  105.9 10.4 %collective-permute-done.12.refs_5_ = bf16[544,512]{1,0:T(8,128)(2,1)S(1)} collective-permute-done((bf16[544,512]{1,0:T(8,128)(2,1)}, bf16[544,512]{1,0:T(8,128)(2,1)S(1)}, u32[]{:S(2)}, u32[]{:S(2)}) %collective-permute-start.12) | collective-permute-done | bytes 557088 | tf_op jit(solution)/shard_map/ppermute | solution.py:467
  116.6 0.6 log_add_fusion.lt_ref
  117.2 1.6 collective-permute-done.13.refs_6_
  118.8 9.2 %collective-permute-done.14.refs_7_ = bf16[544,512]{1,0:T(8,128)(2,1)S(1)} collective-permute-done((bf16[544,512]{1,0:T(8,128)(2,1)}, bf16[544,512]{1,0:T(8,128)(2,1)S(1)}, u32[]{:S(2)}, u32[]{:S(2)}) %collective-permute-start.14) | collective-permute-done | bytes 557088 | tf_op jit(solution)/shard_map/ppermute | solution.py:467
  128.1 0.8 copy-done.19
  128.9 4.6 %reduce.2 = (f32[256,512]{1,0:T(8,128)}, bf16[256,512]{1,0:T(8,128)(2,1)}, bf16[256,512]{1,0:T(8,128)(2,1)}, bf16[256,512]{1,0:T(8,128)(2,1)}) custom-call(s32[3]{0:T(128)} %pad_add_fusion.place_ref, f32[16,256]{1,0:T(8,128)} %log_add_fusion.lt_ref, bf16[32,256]{1,0:T(8,128)(2,1)} %get-tuple-element.69.refs_0_, bf16[32,256]{1,0:T(8,128)(2,1)} %get-tuple-element.70.refs_1_, ...), custom_call_target="tpu_custom_call" | custom-call | flops 1048576 | bytes 65536 | tf_op jit(solution)/shard_map/reduce/pallas_call | solution.py:433
  133.4 1.0 collective-permute-start.15
  134.4 1.3 collective-permute-start.16
  137.1 4.5 %reduce.3 = (f32[256,512]{1,0:T(8,128)}, bf16[256,512]{1,0:T(8,128)(2,1)}, bf16[256,512]{1,0:T(8,128)(2,1)}, bf16[256,512]{1,0:T(8,128)(2,1)}) custom-call(s32[3]{0:T(128)} %pad_add_fusion.place_ref, f32[16,256]{1,0:T(8,128)} %log_add_fusion.lt_ref, bf16[32,256]{1,0:T(8,128)(2,1)} %get-tuple-element.81.refs_0_, bf16[32,256]{1,0:T(8,128)(2,1)} %get-tuple-element.82.refs_1_, ...), custom_call_target="tpu_custom_call" | custom-call | flops 1048576 | bytes 65536 | tf_op jit(solution)/shard_map/reduce/pallas_call | solution.py:433
  141.7 0.6 collective-permute-start.21
  142.3 1.5 collective-permute-start.22
  143.8 0.8 collective-permute-start.23
  144.6 10.5 %column.1 = bf16[2048,1024]{1,0:T(8,128)(2,1)} custom-call(s32[3]{0:T(128)} %pad_add_fusion.place_ref, s32[16,256]{1,0:T(8,128)} %get-tuple-element.93.code_ref, f32[8,256]{1,0:T(8,128)} %get-tuple-element.94.hs_ref, f32[16,256]{1,0:T(8,128)} %log_add_fusion.lt_ref, bf16[528,512]{1,0:T(8,128)(2,1)} %get-tuple-element.49.refs_0_.refs_8_, ...), custom_call_target="tpu_custom_call" | custom-call | flops 1048576 | bytes 65536 | tf_op jit(solution)/shard_map/column/pallas_call | solution.py:352
  155.1 8.4 %inner.1 = (f32[256,1024]{1,0:T(8,128)}, f32[1,256]{1,0:T(1,128)}) custom-call(s32[3]{0:T(128)} %pad_add_fusion.place_ref, f32[16,256]{1,0:T(8,128)} %log_add_fusion.lt_ref, bf16[2048,1024]{1,0:T(8,128)(2,1)} %all-gather.2.cloned.1.call-done.p_ref.refs_12_.refs_8_, bf16[256,1024]{1,0:T(8,128)(2,1)} %refs_9_.1), custom_call_target="tpu_custom_call" | custom-call | flops 1048576 | bytes 65536 | tf_op jit(solution)/shard_map/inner/pallas_call | solution.py:387
  164.5 4.5 %final.1 = bf16[256,1024]{1,0:T(8,128)(2,1)} custom-call(s32[3]{0:T(128)} %pad_add_fusion.place_ref, f32[256,1024]{1,0:T(8,128)} %get-tuple-element.68.gq_ref, f32[256,512]{1,0:T(8,128)} %get-tuple-element.77.refs_0_, bf16[256,512]{1,0:T(8,128)(2,1)} %copy-done.20, bf16[256,512]{1,0:T(8,128)(2,1)} %copy-done.21, bf16[256,512]{1,0:T(8,128)(2,1)} %copy-done.22, ...), custom_call_target="tpu_custom_call" | custom-call | flops 549755813888 | bytes 65536 | tf_op jit(solution)/shard_map/final/pallas_call | solution.py:456
  169.0 27.3 %reduce-scatter.2.cloned.1.call-done = bf16[256,1024]{1,0:T(8,128)(2,1)} async-done(((bf16[2048,1024]{1,0:T(8,128)(2,1)}), bf16[256,1024]{1,0:T(8,128)(2,1)}) %reduce-scatter.2.cloned.1.call-update) | async-done | bytes 524304 | tf_op jit(solution)/shard_map/reduce_scatter | solution.py:513
  (78 shorter events, 5.4 us)
Async XLA Ops:
  7.2 51.7 %all-gather.2.cloned.1.call-start = ((), (), s32[]{:S(2)}) async-start(), calls=%async_computation.2 | async-start | bytes 4718592 | tf_op jit(solution)/shard_map/all_gather | solution.py:488
  7.9 188.4 %reduce-scatter.2.cloned.1.call-start = ((), (), s32[]{:S(2)}) async-start(), calls=%async_computation.3 | async-start | bytes 4718592 | tf_op jit(solution)/shard_map/reduce_scatter | solution.py:513
  9.8 21.8 %copy-start = (bf16[272,512]{1,0:T(8,128)(2,1)}, bf16[272,512]{1,0:T(8,128)(2,1)S(1)}, u32[]{:S(2)}) copy-start(bf16[272,512]{1,0:T(8,128)(2,1)S(1)} %get-tuple-element.97.refs_4_) | copy-start | bytes 835588
  9.8 21.8 %copy-start.1 = (bf16[272,512]{1,0:T(8,128)(2,1)}, bf16[272,512]{1,0:T(8,128)(2,1)S(1)}, u32[]{:S(2)}) copy-start(bf16[272,512]{1,0:T(8,128)(2,1)S(1)} %get-tuple-element.98.refs_0_) | copy-start | bytes 835588
  9.8 10.3 %collective-permute-start = (bf16[272,512]{1,0:T(8,128)(2,1)S(1)}, bf16[272,512]{1,0:T(8,128)(2,1)S(1)}, u32[]{:S(2)}, u32[]{:S(2)}) collective-permute-start(bf16[272,512]{1,0:T(8,128)(2,1)S(1)} %get-tuple-element.98.refs_0_), channel_id=1, source_target_pairs={{0,4},{1,5},{2,6},{3,7},{4,8},{5,9},{6,10},{7,11},{8,12},{9,13},{1... | collective-permute-start | bytes 835592 | tf_op jit(solution)/shard_map/ppermute | solution.py:467
  11.5 15.1 %collective-permute-start.1 = (bf16[272,512]{1,0:T(8,128)(2,1)S(1)}, bf16[272,512]{1,0:T(8,128)(2,1)S(1)}, u32[]{:S(2)}, u32[]{:S(2)}) collective-permute-start(bf16[272,512]{1,0:T(8,128)(2,1)S(1)} %get-tuple-element.98.refs_0_), channel_id=1, source_target_pairs={{0,8},{1,9},{2,10},{3,11},{4,12},{5,13},{6,14},{7,15},{8,0},{9,1},... | collective-permute-start | bytes 835592 | tf_op jit(solution)/shard_map/ppermute | solution.py:467
  14.2 12.3 %collective-permute-start.2 = (bf16[272,512]{1,0:T(8,128)(2,1)S(1)}, bf16[272,512]{1,0:T(8,128)(2,1)S(1)}, u32[]{:S(2)}, u32[]{:S(2)}) collective-permute-start(bf16[272,512]{1,0:T(8,128)(2,1)S(1)} %get-tuple-element.98.refs_0_), channel_id=1, source_target_pairs={{0,12},{1,13},{2,14},{3,15},{4,0},{5,1},{6,2},{7,3},{8,4},{9,5},{1... | collective-permute-start | bytes 835592 | tf_op jit(solution)/shard_map/ppermute | solution.py:467
  15.6 10.9 %collective-permute-start.3 = (bf16[272,512]{1,0:T(8,128)(2,1)S(1)}, bf16[272,512]{1,0:T(8,128)(2,1)S(1)}, u32[]{:S(2)}, u32[]{:S(2)}) collective-permute-start(bf16[272,512]{1,0:T(8,128)(2,1)S(1)} %get-tuple-element.97.refs_4_), channel_id=1, source_target_pairs={{0,1},{1,2},{2,3},{3,0},{4,5},{5,6},{6,7},{7,4},{8,9},{9,10},{10,1... | collective-permute-start | bytes 835592 | tf_op jit(solution)/shard_map/ppermute | solution.py:467
  17.2 14.4 %collective-permute-start.4 = (bf16[272,512]{1,0:T(8,128)(2,1)S(1)}, bf16[272,512]{1,0:T(8,128)(2,1)S(1)}, u32[]{:S(2)}, u32[]{:S(2)}) collective-permute-start(bf16[272,512]{1,0:T(8,128)(2,1)S(1)} %get-tuple-element.97.refs_4_), channel_id=1, source_target_pairs={{0,2},{1,3},{2,0},{3,1},{4,6},{5,7},{6,4},{7,5},{8,10},{9,11},{10,... | collective-permute-start | bytes 835592 | tf_op jit(solution)/shard_map/ppermute | solution.py:467
  20.1 11.5 %copy-start.5 = (bf16[272,512]{1,0:T(8,128)(2,1)}, bf16[272,512]{1,0:T(8,128)(2,1)S(1)}, u32[]{:S(2)}) copy-start(bf16[272,512]{1,0:T(8,128)(2,1)S(1)} %collective-permute-done.refs_1_) | copy-start | bytes 835588
  20.1 11.5 %collective-permute-start.5 = (bf16[272,512]{1,0:T(8,128)(2,1)S(1)}, bf16[272,512]{1,0:T(8,128)(2,1)S(1)}, u32[]{:S(2)}, u32[]{:S(2)}) collective-permute-start(bf16[272,512]{1,0:T(8,128)(2,1)S(1)} %get-tuple-element.97.refs_4_), channel_id=1, source_target_pairs={{0,3},{1,0},{2,1},{3,2},{4,7},{5,4},{6,5},{7,6},{8,11},{9,8},{10,9... | collective-permute-start | bytes 835592 | tf_op jit(solution)/shard_map/ppermute | solution.py:467
  26.5 5.1 %copy-start.6 = (bf16[272,512]{1,0:T(8,128)(2,1)}, bf16[272,512]{1,0:T(8,128)(2,1)S(1)}, u32[]{:S(2)}) copy-start(bf16[272,512]{1,0:T(8,128)(2,1)S(1)} %collective-permute-done.1.refs_2_) | copy-start | bytes 835588
  26.5 5.1 %copy-start.7 = (bf16[272,512]{1,0:T(8,128)(2,1)}, bf16[272,512]{1,0:T(8,128)(2,1)S(1)}, u32[]{:S(2)}) copy-start(bf16[272,512]{1,0:T(8,128)(2,1)S(1)} %collective-permute-done.2.refs_3_) | copy-start | bytes 835588
  26.5 5.1 %copy-start.8 = (bf16[272,512]{1,0:T(8,128)(2,1)}, bf16[272,512]{1,0:T(8,128)(2,1)S(1)}, u32[]{:S(2)}) copy-start(bf16[272,512]{1,0:T(8,128)(2,1)S(1)} %collective-permute-done.3.refs_5_) | copy-start | bytes 835588
  37.6 15.2 %collective-permute-start.6 = (bf16[528,512]{1,0:T(8,128)(2,1)}, bf16[528,512]{1,0:T(8,128)(2,1)S(1)}, u32[]{:S(2)}, u32[]{:S(2)}) collective-permute-start(bf16[528,512]{1,0:T(8,128)(2,1)} %get-tuple-element.50), channel_id=1, source_target_pairs={{0,1},{1,2},{2,3},{3,0},{4,5},{5,6},{6,7},{7,4},{8,9},{9,10},{10,1... | collective-permute-start | bytes 1622024 | tf_op jit(solution)/shard_map/ppermute | solution.py:467
  43.4 20.5 %collective-permute-start.7 = (bf16[528,512]{1,0:T(8,128)(2,1)}, bf16[528,512]{1,0:T(8,128)(2,1)S(1)}, u32[]{:S(2)}, u32[]{:S(2)}) collective-permute-start(bf16[528,512]{1,0:T(8,128)(2,1)} %get-tuple-element.51), channel_id=1, source_target_pairs={{0,2},{1,3},{2,0},{3,1},{4,6},{5,7},{6,4},{7,5},{8,10},{9,11},{10,... | collective-permute-start | bytes 1622024 | tf_op jit(solution)/shard_map/ppermute | solution.py:467
  49.4 18.5 %collective-permute-start.8 = (bf16[528,512]{1,0:T(8,128)(2,1)}, bf16[528,512]{1,0:T(8,128)(2,1)S(1)}, u32[]{:S(2)}, u32[]{:S(2)}) collective-permute-start(bf16[528,512]{1,0:T(8,128)(2,1)} %get-tuple-element.52), channel_id=1, source_target_pairs={{0,3},{1,0},{2,1},{3,2},{4,7},{5,4},{6,5},{7,6},{8,11},{9,8},{10,9... | collective-permute-start | bytes 1622024 | tf_op jit(solution)/shard_map/ppermute | solution.py:467
  51.0 26.1 %collective-permute-start.9 = (bf16[528,512]{1,0:T(8,128)(2,1)}, bf16[528,512]{1,0:T(8,128)(2,1)S(1)}, u32[]{:S(2)}, u32[]{:S(2)}) collective-permute-start(bf16[528,512]{1,0:T(8,128)(2,1)} %get-tuple-element.54), channel_id=1, source_target_pairs={{0,4},{1,5},{2,6},{3,7},{4,8},{5,9},{6,10},{7,11},{8,12},{9,13},{1... | collective-permute-start | bytes 1622024 | tf_op jit(solution)/shard_map/ppermute | solution.py:467
  51.7 25.5 %collective-permute-start.10 = (bf16[528,512]{1,0:T(8,128)(2,1)}, bf16[528,512]{1,0:T(8,128)(2,1)S(1)}, u32[]{:S(2)}, u32[]{:S(2)}) collective-permute-start(bf16[528,512]{1,0:T(8,128)(2,1)} %get-tuple-element.55), channel_id=1, source_target_pairs={{0,8},{1,9},{2,10},{3,11},{4,12},{5,13},{6,14},{7,15},{8,0},{9,1},... | collective-permute-start | bytes 1622024 | tf_op jit(solution)/shard_map/ppermute | solution.py:467
  52.8 11.0 %copy-start.2 = (bf16[528,512]{1,0:T(8,128)(2,1)}, bf16[528,512]{1,0:T(8,128)(2,1)S(1)}, u32[]{:S(2)}) copy-start(bf16[528,512]{1,0:T(8,128)(2,1)S(1)} %collective-permute-done.6.refs_1_.refs_9_) | copy-start | bytes 1622020
  52.8 25.0 %collective-permute-start.11 = (bf16[528,512]{1,0:T(8,128)(2,1)}, bf16[528,512]{1,0:T(8,128)(2,1)S(1)}, u32[]{:S(2)}, u32[]{:S(2)}) collective-permute-start(bf16[528,512]{1,0:T(8,128)(2,1)} %get-tuple-element.56), channel_id=1, source_target_pairs={{0,12},{1,13},{2,14},{3,15},{4,0},{5,1},{6,2},{7,3},{8,4},{9,5},{1... | collective-permute-start | bytes 1622024 | tf_op jit(solution)/shard_map/ppermute | solution.py:467
  63.8 14.0 %copy-start.3 = (bf16[528,512]{1,0:T(8,128)(2,1)}, bf16[528,512]{1,0:T(8,128)(2,1)S(1)}, u32[]{:S(2)}) copy-start(bf16[528,512]{1,0:T(8,128)(2,1)S(1)} %collective-permute-done.7.refs_2_.refs_10_) | copy-start | bytes 1622020
  67.9 9.9 %copy-start.4 = (bf16[528,512]{1,0:T(8,128)(2,1)}, bf16[528,512]{1,0:T(8,128)(2,1)S(1)}, u32[]{:S(2)}) copy-start(bf16[528,512]{1,0:T(8,128)(2,1)S(1)} %collective-permute-done.8.refs_3_.refs_11_) | copy-start | bytes 1622020
  77.2 0.8 copy-start.11
  77.2 1.1 copy-start.12
  77.8 0.8 copy-start.13
  100.6 15.8 %collective-permute-start.12 = (bf16[544,512]{1,0:T(8,128)(2,1)}, bf16[544,512]{1,0:T(8,128)(2,1)S(1)}, u32[]{:S(2)}, u32[]{:S(2)}) collective-permute-start(bf16[544,512]{1,0:T(8,128)(2,1)} %get-tuple-element.74), channel_id=1, source_target_pairs={{0,3},{1,0},{2,1},{3,2},{4,7},{5,4},{6,5},{7,6},{8,11},{9,8},{10,9... | collective-permute-start | bytes 1671176 | tf_op jit(solution)/shard_map/ppermute | solution.py:467
  101.5 17.3 %collective-permute-start.13 = (bf16[544,512]{1,0:T(8,128)(2,1)}, bf16[544,512]{1,0:T(8,128)(2,1)S(1)}, u32[]{:S(2)}, u32[]{:S(2)}) collective-permute-start(bf16[544,512]{1,0:T(8,128)(2,1)} %get-tuple-element.75), channel_id=1, source_target_pairs={{0,2},{1,3},{2,0},{3,1},{4,6},{5,7},{6,4},{7,5},{8,10},{9,11},{10,... | collective-permute-start | bytes 1671176 | tf_op jit(solution)/shard_map/ppermute | solution.py:467
  103.1 25.0 %collective-permute-start.14 = (bf16[544,512]{1,0:T(8,128)(2,1)}, bf16[544,512]{1,0:T(8,128)(2,1)S(1)}, u32[]{:S(2)}, u32[]{:S(2)}) collective-permute-start(bf16[544,512]{1,0:T(8,128)(2,1)} %get-tuple-element.76), channel_id=1, source_target_pairs={{0,1},{1,2},{2,3},{3,0},{4,5},{5,6},{6,7},{7,4},{8,9},{9,10},{10,1... | collective-permute-start | bytes 1671176 | tf_op jit(solution)/shard_map/ppermute | solution.py:467
  103.5 32.2 %collective-permute-start.18 = (bf16[544,512]{1,0:T(8,128)(2,1)}, bf16[544,512]{1,0:T(8,128)(2,1)S(1)}, u32[]{:S(2)}, u32[]{:S(2)}) collective-permute-start(bf16[544,512]{1,0:T(8,128)(2,1)} %get-tuple-element.86), channel_id=1, source_target_pairs={{0,12},{1,13},{2,14},{3,15},{4,0},{5,1},{6,2},{7,3},{8,4},{9,5},{1... | collective-permute-start | bytes 1671176 | tf_op jit(solution)/shard_map/ppermute | solution.py:467
  104.4 31.7 %collective-permute-start.19 = (bf16[544,512]{1,0:T(8,128)(2,1)}, bf16[544,512]{1,0:T(8,128)(2,1)S(1)}, u32[]{:S(2)}, u32[]{:S(2)}) collective-permute-start(bf16[544,512]{1,0:T(8,128)(2,1)} %get-tuple-element.87), channel_id=1, source_target_pairs={{0,8},{1,9},{2,10},{3,11},{4,12},{5,13},{6,14},{7,15},{8,0},{9,1},... | collective-permute-start | bytes 1671176 | tf_op jit(solution)/shard_map/ppermute | solution.py:467
  116.3 11.7 %copy-start.17 = (bf16[544,512]{1,0:T(8,128)(2,1)}, bf16[544,512]{1,0:T(8,128)(2,1)S(1)}, u32[]{:S(2)}) copy-start(bf16[544,512]{1,0:T(8,128)(2,1)S(1)} %collective-permute-done.12.refs_5_) | copy-start | bytes 1671172
  116.3 19.8 %collective-permute-start.20 = (bf16[544,512]{1,0:T(8,128)(2,1)}, bf16[544,512]{1,0:T(8,128)(2,1)S(1)}, u32[]{:S(2)}, u32[]{:S(2)}) collective-permute-start(bf16[544,512]{1,0:T(8,128)(2,1)} %get-tuple-element.88), channel_id=1, source_target_pairs={{0,4},{1,5},{2,6},{3,7},{4,8},{5,9},{6,10},{7,11},{8,12},{9,13},{1... | collective-permute-start | bytes 1671176 | tf_op jit(solution)/shard_map/ppermute | solution.py:467
  118.8 9.2 %copy-start.18 = (bf16[544,512]{1,0:T(8,128)(2,1)}, bf16[544,512]{1,0:T(8,128)(2,1)S(1)}, u32[]{:S(2)}) copy-start(bf16[544,512]{1,0:T(8,128)(2,1)S(1)} %collective-permute-done.13.refs_6_) | copy-start | bytes 1671172
  128.1 0.8 copy-start.19
  133.4 10.3 %collective-permute-start.15 = (bf16[256,512]{1,0:T(8,128)(2,1)}, bf16[256,512]{1,0:T(8,128)(2,1)S(1)}, u32[]{:S(2)}, u32[]{:S(2)}) collective-permute-start(bf16[256,512]{1,0:T(8,128)(2,1)} %get-tuple-element.78), channel_id=1, source_target_pairs={{0,12},{1,13},{2,14},{3,15},{4,0},{5,1},{6,2},{7,3},{8,4},{9,5},{1... | collective-permute-start | bytes 786440 | tf_op jit(solution)/shard_map/ppermute | solution.py:467
  134.4 29.1 %collective-permute-start.16 = (bf16[256,512]{1,0:T(8,128)(2,1)}, bf16[256,512]{1,0:T(8,128)(2,1)S(1)}, u32[]{:S(2)}, u32[]{:S(2)}) collective-permute-start(bf16[256,512]{1,0:T(8,128)(2,1)} %get-tuple-element.79), channel_id=1, source_target_pairs={{0,8},{1,9},{2,10},{3,11},{4,12},{5,13},{6,14},{7,15},{8,0},{9,1},... | collective-permute-start | bytes 786440 | tf_op jit(solution)/shard_map/ppermute | solution.py:467
  135.7 0.8 copy-start.14
  135.7 27.8 %collective-permute-start.17 = (bf16[256,512]{1,0:T(8,128)(2,1)}, bf16[256,512]{1,0:T(8,128)(2,1)S(1)}, u32[]{:S(2)}, u32[]{:S(2)}) collective-permute-start(bf16[256,512]{1,0:T(8,128)(2,1)} %get-tuple-element.80), channel_id=1, source_target_pairs={{0,4},{1,5},{2,6},{3,7},{4,8},{5,9},{6,10},{7,11},{8,12},{9,13},{1... | collective-permute-start | bytes 786440 | tf_op jit(solution)/shard_map/ppermute | solution.py:467
  136.1 0.8 copy-start.15
  136.2 1.0 copy-start.16
  141.7 21.8 %collective-permute-start.21 = (bf16[256,512]{1,0:T(8,128)(2,1)}, bf16[256,512]{1,0:T(8,128)(2,1)S(1)}, u32[]{:S(2)}, u32[]{:S(2)}) collective-permute-start(bf16[256,512]{1,0:T(8,128)(2,1)} %get-tuple-element.90), channel_id=1, source_target_pairs={{0,3},{1,0},{2,1},{3,2},{4,7},{5,4},{6,5},{7,6},{8,11},{9,8},{10,9... | collective-permute-start | bytes 786440 | tf_op jit(solution)/shard_map/ppermute | solution.py:467
  142.3 21.2 %collective-permute-start.22 = (bf16[256,512]{1,0:T(8,128)(2,1)}, bf16[256,512]{1,0:T(8,128)(2,1)S(1)}, u32[]{:S(2)}, u32[]{:S(2)}) collective-permute-start(bf16[256,512]{1,0:T(8,128)(2,1)} %get-tuple-element.91), channel_id=1, source_target_pairs={{0,2},{1,3},{2,0},{3,1},{4,6},{5,7},{6,4},{7,5},{8,10},{9,11},{10,... | collective-permute-start | bytes 786440 | tf_op jit(solution)/shard_map/ppermute | solution.py:467
  143.8 11.3 %copy-start.20 = (bf16[256,512]{1,0:T(8,128)(2,1)}, bf16[256,512]{1,0:T(8,128)(2,1)S(1)}, u32[]{:S(2)}) copy-start(bf16[256,512]{1,0:T(8,128)(2,1)S(1)} %collective-permute-done.15.refs_1_) | copy-start | bytes 786436
  143.8 19.8 %collective-permute-start.23 = (bf16[256,512]{1,0:T(8,128)(2,1)}, bf16[256,512]{1,0:T(8,128)(2,1)S(1)}, u32[]{:S(2)}, u32[]{:S(2)}) collective-permute-start(bf16[256,512]{1,0:T(8,128)(2,1)} %get-tuple-element.92), channel_id=1, source_target_pairs={{0,1},{1,2},{2,3},{3,0},{4,5},{5,6},{6,7},{7,4},{8,9},{9,10},{10,1... | collective-permute-start | bytes 786440 | tf_op jit(solution)/shard_map/ppermute | solution.py:467
  163.5 0.8 copy-start.23
  163.5 0.9 copy-start.24
  163.5 1.0 copy-start.25
  (4 other events, 2.9 us)
Sparse Core Ops, SparseCore 0:
  9.7 34.7 all-gather.1
  155.2 41.0 reduce-scatter.1

commit v6 on v5

--- a/solution.py
+++ b/solution.py
@@ -54,7 +54,7 @@
     )
 
 
-LIGHT, MIDDLE, HEAVY = 1 << 20, 1 << 32, 1 << 39
+LIGHT, MIDDLE, HEAVY = 1 << 20, 1 << 20, 1 << 39
 SIDE = 4
 CORES = 2
 
@@ -305,7 +305,7 @@
 
 def column_kernel(reps, cap, temper, place_ref, code_ref, hs_ref, lt_ref, *refs):
     first, second = refs[0:4], refs[4:8]
-    p_ref, q_ref, gp_ref, d_ref = refs[8:]
+    p_ref, q_ref, gp_ref, mark_ref, d_ref = refs[8:]
     step = pl.program_id(0)
     toks, width = q_ref.shape
     half_width = width // 2
@@ -326,6 +326,7 @@
             log_slot = jnp.sum(jnp.where(source, found, 0.0), axis=0, keepdims=True)
             rows.append(jnp.where(valid, jnp.exp(hs_ref[g : g + 1, :] - log_slot), 0.0))
         d_ref[...] = jnp.concatenate(rows, axis=0)
+        mark_ref[...] = jnp.zeros(mark_ref.shape, F32)
 
     queries = q_ref[...]
     lt_own = own_row(lt_ref, rep_of(place_ref[1], place_ref[2]))
@@ -354,7 +355,8 @@
         gathered.shape[0] // (CORES * toks),
         [full(codes.shape), full(hard_scores.shape), full(log_total.shape)] + [slots] * 8
         + [block, full((toks, width))],
-        block, jax.ShapeDtypeStruct(gathered.shape, BF16),
+        [block, full((8, 128))],
+        [jax.ShapeDtypeStruct(gathered.shape, BF16), jax.ShapeDtypeStruct((8, 128), F32)],
         [pltpu.VMEM(hard_scores.shape, F32)], LIGHT,
     )(place, codes, hard_scores, log_total, *first, *second, gathered, queries)
 
@@ -395,7 +397,7 @@
 
 
 def reduce_kernel(half, cap, groups, place_ref, lt_ref, *refs):
-    ranks, rows, outs = refs[0:4], refs[4:8], refs[8:12]
+    ranks, rows, outs = refs[0:4], refs[4:8], refs[9:13]
     toks = lt_ref.shape[1]
     slots = groups * cap
     reps = lt_ref.shape[0]
@@ -427,15 +429,16 @@
         outs[s][...] = mm(weight, jnp.concatenate(values, axis=0), TN).astype(outs[s].dtype)
 
 
-def reduce(place, half, log_total, ranks, rows, groups, cap):
+def reduce(place, half, log_total, ranks, rows, mark, groups, cap):
     toks = log_total.shape[1]
     shape = (toks, rows[0].shape[1])
     return call(
         functools.partial(reduce_kernel, half, cap, groups), "reduce", 1,
-        [full(log_total.shape)] + [full(ranks[0].shape)] * 4 + [full(rows[0].shape)] * 4,
+        [full(log_total.shape)] + [full(ranks[0].shape)] * 4 + [full(rows[0].shape)] * 4
+        + [full(mark.shape)],
         [full(shape)] * 4,
-        [jax.ShapeDtypeStruct(shape, F32)] + [jax.ShapeDtypeStruct(shape, BF16)] * 3, [], LIGHT,
-    )(place, log_total, *ranks, *rows)
+        [jax.ShapeDtypeStruct(shape, F32)] + [jax.ShapeDtypeStruct(shape, BF16)] * 3, [], HEAVY,
+    )(place, log_total, *ranks, *rows, mark)
 
 
 def final_kernel(temper, place_ref, gq_ref, *refs):
@@ -455,7 +458,7 @@
     narrow = pl.BlockSpec((rows // 4, width // 2), lambda s, _: (s, 0))
     return call(
         functools.partial(final_kernel, temper), "final", 4, [wide] + [narrow] * 8, wide,
-        jax.ShapeDtypeStruct((rows, width), BF16), [], HEAVY,
+        jax.ShapeDtypeStruct((rows, width), BF16), [], LIGHT,
     )(place, within, *first, *second)
 
 
@@ -500,22 +503,20 @@
         place, first, second, gathered, within, temper, reps, cap
     )
     parts = lax.all_to_all(part, "rep", split_axis=0, concat_axis=0, tiled=True)
-    parts, back_first, back_second = lax.optimization_barrier((parts, back_first, back_second))
     high = jnp.max(parts, axis=0)
     log_total = high + jnp.log(jnp.sum(jnp.exp(parts - high), axis=0))
 
-    back_first = [along(v, 1, -s) if s else v for s, v in enumerate(back_first)]
-    back_second = [along(v, 0, -s) if s else v for s, v in enumerate(back_second)]
-
-    partial_sum = column(
+    partial_sum, mark = column(
         place, codes, hard_scores, log_total, first, second, gathered, queries, temper, cap
     )
     grad_passages = lax.psum_scatter(partial_sum, "grp", scatter_dimension=0, tiled=True)
+    back_first = [along(v, 1, -s) if s else v for s, v in enumerate(back_first)]
+    back_second = [along(v, 0, -s) if s else v for s, v in enumerate(back_second)]
     grad_inner, losses = inner(place, log_total, gathered, queries, temper)
 
     sums = []
     for half, ranks, rows in ((0, ranks_first, back_first), (1, ranks_second, back_second)):
-        made = reduce(place, half, log_total, ranks, rows, groups, cap)
+        made = reduce(place, half, log_total, ranks, rows, mark, groups, cap)
         sums.append([along(v, half, -s) if s else v for s, v in enumerate(made)])
     grad_queries = final(place, grad_inner, *sums, temper)
     return (losses.reshape(toks), grad_queries, grad_passages)

time: 204 us -> 163 us (0.80)
  waiting for transfers between devices: 71.4 us -> 38 us
  blocking collectives: 12.9 us -> 0 us
  starting transfers between devices: 32 us -> 39.4 us
    reduce_scatter x1, waiting for transfers between devices: 27.3 us -> 0.59 us  [shards(): lax.psum_scatter(partial_sum, 'grp', scatter_dimension=0, tiled=True)]
    all_to_all x1 -> x0, blocking collectives: 12.9 us -> none  [shards(): parts = lax.all_to_all(part, 'rep', split_axis=0, concat_axis=0, tiled=True)]
    ppermute x24, waiting for transfers between devices: 43.4 us -> 31.2 us  [along(): return lax.ppermute(x, 'rep', pairs)]
    all_to_all x0 -> x1, starting transfers between devices: none -> 7.03 us  [shards(): parts = lax.all_to_all(part, 'rep', split_axis=0, concat_axis=0, tiled=True)]
    all_to_all x0 -> x1, waiting for transfers between devices: none -> 5.54 us  [shards(): parts = lax.all_to_all(part, 'rep', split_axis=0, concat_axis=0, tiled=True)]
    unnamed x52 -> x40, local copies, waits for them, and re-layouts: 5.04 us -> 3.07 us
  transfers between devices with their start and end apart: 26 -> 27, of which waited for: 9 -> 11; matrix products, arithmetic and copies ran while one was open for 2% -> 2% of each run, Pallas kernels for 27% -> 34%
where the time goes in v6:
time: 163 us; the launch traced here: 162 us
  Pallas kernels  64.4 us (40%)
  starting transfers between devices  39.4 us (24%)
  waiting for transfers between devices  38 us (23%)
  between operations  14.3 us (9%)
  local copies, waits for them, and re-layouts  4.14 us (3%)
  other arithmetic  2.04 us (1%)
    ppermute x24, starting transfers between devices, along(): return lax.ppermute(x, 'rep', pairs)  32.3 us
    ppermute x24, waiting for transfers between devices, along(): return lax.ppermute(x, 'rep', pairs)  31.2 us
    pallas_call x4, Pallas kernels, mid(): call(functools.partial(mid_kernel, shift, cap, groups, reps, negs), 'mid'...  17.8 us
    pallas_call x1, Pallas kernels, column(): call(functools.partial(column_kernel, reps, cap, temper), 'column', gathe...  10.5 us
    pallas_call x2, Pallas kernels, reduce(): call(functools.partial(reduce_kernel, half, cap, groups), 'reduce', 1, [f...  9.2 us
    pallas_call x1, Pallas kernels, hard(): call(functools.partial(hard_kernel, reps, cap, temper), 'hard', levels +...  9.02 us
    pallas_call x1, Pallas kernels, inner(): call(functools.partial(inner_kernel, temper), 'inner', 2, [full(log_total...  8.37 us
    all_to_all x1, starting transfers between devices, shards(): parts = lax.all_to_all(part, 'rep', split_axis=0, concat_axis=0, tiled=True)  7.03 us
  transfers between devices with their start and end apart: 27, of which 11 were waited for; matrix products, arithmetic and copies ran while one was open for 2% of the time, Pallas kernels for 34%

profile of v6, /device:TPU:0, one launch (start us, length us, event | category | flops | bytes accessed | tf_op | source)
XLA Modules:
  0.0 162.2 jit_solution(3376491262951284265)
XLA Ops:
  7.2 0.7 all-gather.2.cloned.1.call-update
  7.9 0.7 convert_bitcast_fusion
  8.6 1.1 fusion.7
  9.8 3.2 %collective-permute-start.5 = (bf16[272,512]{1,0:T(8,128)(2,1)S(1)}, bf16[272,512]{1,0:T(8,128)(2,1)S(1)}, u32[]{:S(2)}, u32[]{:S(2)}) collective-permute-start(bf16[272,512]{1,0:T(8,128)(2,1)S(1)} %get-tuple-element.83.refs_4_), channel_id=1, source_target_pairs={{0,3},{1,0},{2,1},{3,2},{4,7},{5,4},{6,5},{7,6},{8,11},{9,8},{10,9... | collective-permute-start | bytes 835592 | tf_op jit(solution)/shard_map/ppermute | solution.py:470
  12.9 0.6 collective-permute-start.4
  13.6 1.0 collective-permute-start.3
  14.5 2.8 %collective-permute-start.2 = (bf16[272,512]{1,0:T(8,128)(2,1)S(1)}, bf16[272,512]{1,0:T(8,128)(2,1)S(1)}, u32[]{:S(2)}, u32[]{:S(2)}) collective-permute-start(bf16[272,512]{1,0:T(8,128)(2,1)S(1)} %get-tuple-element.84.refs_0_), channel_id=1, source_target_pairs={{0,12},{1,13},{2,14},{3,15},{4,0},{5,1},{6,2},{7,3},{8,4},{9,5},{1... | collective-permute-start | bytes 835592 | tf_op jit(solution)/shard_map/ppermute | solution.py:470
  17.3 0.8 collective-permute-start.1
  18.1 6.7 %collective-permute-done.5.refs_7_ = bf16[272,512]{1,0:T(8,128)(2,1)S(1)} collective-permute-done((bf16[272,512]{1,0:T(8,128)(2,1)S(1)}, bf16[272,512]{1,0:T(8,128)(2,1)S(1)}, u32[]{:S(2)}, u32[]{:S(2)}) %collective-permute-start.5) | collective-permute-done | bytes 278560 | tf_op jit(solution)/shard_map/ppermute | solution.py:470
  24.8 1.5 collective-permute-start
  26.9 1.6 collective-permute-done.3.refs_5_
  28.5 5.3 %collective-permute-done.refs_1_ = bf16[272,512]{1,0:T(8,128)(2,1)S(1)} collective-permute-done((bf16[272,512]{1,0:T(8,128)(2,1)S(1)}, bf16[272,512]{1,0:T(8,128)(2,1)S(1)}, u32[]{:S(2)}, u32[]{:S(2)}) %collective-permute-start) | collective-permute-done | bytes 278560 | tf_op jit(solution)/shard_map/ppermute | solution.py:470
  34.0 0.7 copy-done.10
  34.7 4.5 %mid.7 = (bf16[528,512]{1,0:T(8,128)(2,1)}, bf16[528,512]{1,0:T(8,128)(2,1)}, bf16[32,256]{1,0:T(8,128)(2,1)}, bf16[32,256]{1,0:T(8,128)(2,1)}) custom-call(s32[3]{0:T(128)} %pad_add_fusion.place_ref, bf16[272,512]{1,0:T(8,128)(2,1)} %copy-done.1, bf16[272,512]{1,0:T(8,128)(2,1)} %copy-done.10, bf16[272,512]{1,0:T(8,128)(2,1)} %copy-done.9, ...), custom_call_target="tpu_custom_call" | custom-call | flops 1048576 | bytes 65536 | tf_op jit(solution)/shard_map/mid/pallas_call | solution.py:128
  39.1 3.4 %collective-permute-start.8 = (bf16[528,512]{1,0:T(8,128)(2,1)}, bf16[528,512]{1,0:T(8,128)(2,1)S(1)}, u32[]{:S(2)}, u32[]{:S(2)}) collective-permute-start(bf16[528,512]{1,0:T(8,128)(2,1)} %get-tuple-element.45), channel_id=1, source_target_pairs={{0,3},{1,0},{2,1},{3,2},{4,7},{5,4},{6,5},{7,6},{8,11},{9,8},{10,9... | collective-permute-start | bytes 1622024 | tf_op jit(solution)/shard_map/ppermute | solution.py:470
  42.5 1.6 collective-permute-start.11
  44.1 4.4 %mid.6 = (bf16[528,512]{1,0:T(8,128)(2,1)}, bf16[528,512]{1,0:T(8,128)(2,1)}, bf16[32,256]{1,0:T(8,128)(2,1)}, bf16[32,256]{1,0:T(8,128)(2,1)}) custom-call(s32[3]{0:T(128)} %pad_add_fusion.place_ref, bf16[272,512]{1,0:T(8,128)(2,1)} %copy-done.1, bf16[272,512]{1,0:T(8,128)(2,1)} %copy-done.10, bf16[272,512]{1,0:T(8,128)(2,1)} %copy-done.9, ...), custom_call_target="tpu_custom_call" | custom-call | flops 1048576 | bytes 65536 | tf_op jit(solution)/shard_map/mid/pallas_call | solution.py:128
  48.5 0.9 collective-permute-start.10
  49.4 4.4 %mid.5 = (bf16[528,512]{1,0:T(8,128)(2,1)}, bf16[528,512]{1,0:T(8,128)(2,1)}, bf16[32,256]{1,0:T(8,128)(2,1)}, bf16[32,256]{1,0:T(8,128)(2,1)}) custom-call(s32[3]{0:T(128)} %pad_add_fusion.place_ref, bf16[272,512]{1,0:T(8,128)(2,1)} %copy-done.1, bf16[272,512]{1,0:T(8,128)(2,1)} %copy-done.10, bf16[272,512]{1,0:T(8,128)(2,1)} %copy-done.9, ...), custom_call_target="tpu_custom_call" | custom-call | flops 1048576 | bytes 65536 | tf_op jit(solution)/shard_map/mid/pallas_call | solution.py:128
  53.8 0.8 collective-permute-start.6
  54.7 9.5 %collective-permute-done.8.refs_3_.refs_11_ = bf16[528,512]{1,0:T(8,128)(2,1)S(1)} collective-permute-done((bf16[528,512]{1,0:T(8,128)(2,1)}, bf16[528,512]{1,0:T(8,128)(2,1)S(1)}, u32[]{:S(2)}, u32[]{:S(2)}) %collective-permute-start.8) | collective-permute-done | bytes 540704 | tf_op jit(solution)/shard_map/ppermute | solution.py:470
  64.5 4.5 %mid.4 = (bf16[528,512]{1,0:T(8,128)(2,1)}, bf16[528,512]{1,0:T(8,128)(2,1)}, bf16[32,256]{1,0:T(8,128)(2,1)}, bf16[32,256]{1,0:T(8,128)(2,1)}) custom-call(s32[3]{0:T(128)} %pad_add_fusion.place_ref, bf16[272,512]{1,0:T(8,128)(2,1)} %copy-done.1, bf16[272,512]{1,0:T(8,128)(2,1)} %copy-done.10, bf16[272,512]{1,0:T(8,128)(2,1)} %copy-done.9, ...), custom_call_target="tpu_custom_call" | custom-call | flops 1048576 | bytes 65536 | tf_op jit(solution)/shard_map/mid/pallas_call | solution.py:128
  69.0 5.0 %inside.1.refs_13_ = f32[1,256]{1,0:T(1,128)} custom-call(s32[3]{0:T(128)} %pad_add_fusion.place_ref, bf16[2048,1024]{1,0:T(8,128)(2,1)} %all-gather.2.cloned.1.call-done.p_ref.refs_12_.refs_8_, bf16[256,1024]{1,0:T(8,128)(2,1)} %refs_9_.1), custom_call_target="tpu_custom_call" | custom-call | flops 1048576 | bytes 65536 | tf_op jit(solution)/shard_map/inside/pallas_call | solution.py:158
  74.0 1.0 collective-permute-done.9.refs_5_
  75.8 9.0 %hard.1 = (bf16[544,512]{1,0:T(8,128)(2,1)}, bf16[544,512]{1,0:T(8,128)(2,1)}, bf16[544,512]{1,0:T(8,128)(2,1)}, bf16[544,512]{1,0:T(8,128)(2,1)}, bf16[544,512]...) custom-call(s32[3]{0:T(128)} %pad_add_fusion.place_ref, ...), custom_call_target="tpu_custom_call" | custom-call | flops 1048576 | bytes 65536 | tf_op jit(solution)/shard_map/hard/pallas_call | solution.py:286
  84.8 7.0 %all-to-all-start = ((f32[16,16,256]{2,1,0:T(8,128)}), f32[16,16,256]{2,1,0:T(8,128)S(1)}, u32[]{:S(2)}, u32[]{:S(2)}) async-start(f32[16,16,256]{2,1,0:T(8,128)} %get-tuple-element.50), calls=%async_computation | async-start | bytes 524288 | tf_op jit(solution)/shard_map/all_to_all | solution.py:505
  91.9 3.2 %collective-permute-start.12 = (bf16[544,512]{1,0:T(8,128)(2,1)}, bf16[544,512]{1,0:T(8,128)(2,1)S(1)}, u32[]{:S(2)}, u32[]{:S(2)}) collective-permute-start(bf16[544,512]{1,0:T(8,128)(2,1)} %get-tuple-element.58), channel_id=1, source_target_pairs={{0,3},{1,0},{2,1},{3,2},{4,7},{5,4},{6,5},{7,6},{8,11},{9,8},{10,9... | collective-permute-start | bytes 1671176 | tf_op jit(solution)/shard_map/ppermute | solution.py:470
  95.1 0.9 collective-permute-start.13
  96.0 0.9 collective-permute-start.14
  96.8 2.7 %collective-permute-start.18 = (bf16[544,512]{1,0:T(8,128)(2,1)}, bf16[544,512]{1,0:T(8,128)(2,1)}, u32[]{:S(2)}, u32[]{:S(2)}) collective-permute-start(bf16[544,512]{1,0:T(8,128)(2,1)} %get-tuple-element.73), channel_id=1, source_target_pairs={{0,12},{1,13},{2,14},{3,15},{4,0},{5,1},{6,2},{7,3},{8,4},{9,5},{1... | collective-permute-start | bytes 1671176 | tf_op jit(solution)/shard_map/ppermute | solution.py:470
  99.5 0.9 collective-permute-start.19
  100.4 5.5 %all-to-all-done = f32[16,16,256]{2,1,0:T(8,128)S(1)} async-done(((f32[16,16,256]{2,1,0:T(8,128)}), f32[16,16,256]{2,1,0:T(8,128)S(1)}, u32[]{:S(2)}, u32[]{:S(2)}) %all-to-all-start) | async-done | bytes 262176 | tf_op jit(solution)/shard_map/all_to_all | solution.py:505
  106.6 10.5 %column.1 = (bf16[2048,1024]{1,0:T(8,128)(2,1)}, f32[8,128]{1,0:T(8,128)}) custom-call(s32[3]{0:T(128)} %pad_add_fusion.place_ref, s32[16,256]{1,0:T(8,128)} %get-tuple-element.61.code_ref, f32[8,256]{1,0:T(8,128)} %get-tuple-element.62.hs_ref, f32[16,256]{1,0:T(8,128)} %log_add_fusion.lt_ref, bf16[528,512]{1,0:T(8,128)(2,1)} %get-tuple-element.42.refs_0_.refs_8_, ...), custom_call_target="tpu_custom_call" | custom-call | flops 1048576 | bytes 65536 | tf_op jit(solution)/shard_map/column/pallas_call | solution.py:353
  117.2 0.7 collective-permute-done.12.refs_5_
  117.9 0.9 collective-permute-start.20
  118.8 2.2 %collective-permute-done.14.refs_7_ = bf16[544,512]{1,0:T(8,128)(2,1)S(1)} collective-permute-done((bf16[544,512]{1,0:T(8,128)(2,1)}, bf16[544,512]{1,0:T(8,128)(2,1)S(1)}, u32[]{:S(2)}, u32[]{:S(2)}) %collective-permute-start.14) | collective-permute-done | bytes 557088 | tf_op jit(solution)/shard_map/ppermute | solution.py:470
  121.0 0.8 copy-done.19
  121.8 4.6 %reduce.2 = (f32[256,512]{1,0:T(8,128)}, bf16[256,512]{1,0:T(8,128)(2,1)}, bf16[256,512]{1,0:T(8,128)(2,1)}, bf16[256,512]{1,0:T(8,128)(2,1)}) custom-call(s32[3]{0:T(128)} %pad_add_fusion.place_ref, f32[16,256]{1,0:T(8,128)} %log_add_fusion.lt_ref, bf16[32,256]{1,0:T(8,128)(2,1)} %get-tuple-element.53.refs_0_, bf16[32,256]{1,0:T(8,128)(2,1)} %get-tuple-element.54.refs_1_, ...), custom_call_target="tpu_custom_call" | custom-call | flops 549755813888 | bytes 65536 | tf_op jit(solution)/shard_map/reduce/pallas_call | solution.py:435
  126.4 2.3 %collective-permute-start.15 = (bf16[256,512]{1,0:T(8,128)(2,1)}, bf16[256,512]{1,0:T(8,128)(2,1)}, u32[]{:S(2)}, u32[]{:S(2)}) collective-permute-start(bf16[256,512]{1,0:T(8,128)(2,1)} %get-tuple-element.65), channel_id=1, source_target_pairs={{0,12},{1,13},{2,14},{3,15},{4,0},{5,1},{6,2},{7,3},{8,4},{9,5},{1... | collective-permute-start | bytes 786440 | tf_op jit(solution)/shard_map/ppermute | solution.py:470
  128.7 0.8 collective-permute-start.16
  129.6 0.9 collective-permute-start.17
  130.4 4.6 %reduce.3 = (f32[256,512]{1,0:T(8,128)}, bf16[256,512]{1,0:T(8,128)(2,1)}, bf16[256,512]{1,0:T(8,128)(2,1)}, bf16[256,512]{1,0:T(8,128)(2,1)}) custom-call(s32[3]{0:T(128)} %pad_add_fusion.place_ref, f32[16,256]{1,0:T(8,128)} %log_add_fusion.lt_ref, bf16[32,256]{1,0:T(8,128)(2,1)} %get-tuple-element.68.refs_0_, bf16[32,256]{1,0:T(8,128)(2,1)} %get-tuple-element.69.refs_1_, ...), custom_call_target="tpu_custom_call" | custom-call | flops 549755813888 | bytes 65536 | tf_op jit(solution)/shard_map/reduce/pallas_call | solution.py:435
  135.1 2.1 %collective-permute-start.21 = (bf16[256,512]{1,0:T(8,128)(2,1)}, bf16[256,512]{1,0:T(8,128)(2,1)S(1)}, u32[]{:S(2)}, u32[]{:S(2)}) collective-permute-start(bf16[256,512]{1,0:T(8,128)(2,1)} %get-tuple-element.77), channel_id=1, source_target_pairs={{0,3},{1,0},{2,1},{3,2},{4,7},{5,4},{6,5},{7,6},{8,11},{9,8},{10,9... | collective-permute-start | bytes 786440 | tf_op jit(solution)/shard_map/ppermute | solution.py:470
  137.2 3.2 %collective-permute-done.15.refs_1_ = bf16[256,512]{1,0:T(8,128)(2,1)} collective-permute-done((bf16[256,512]{1,0:T(8,128)(2,1)}, bf16[256,512]{1,0:T(8,128)(2,1)}, u32[]{:S(2)}, u32[]{:S(2)}) %collective-permute-start.15) | collective-permute-done | bytes 262176 | tf_op jit(solution)/shard_map/ppermute | solution.py:470
  140.4 8.4 %inner.1 = (f32[256,1024]{1,0:T(8,128)}, f32[1,256]{1,0:T(1,128)}) custom-call(s32[3]{0:T(128)} %pad_add_fusion.place_ref, f32[16,256]{1,0:T(8,128)} %log_add_fusion.lt_ref, bf16[2048,1024]{1,0:T(8,128)(2,1)} %all-gather.2.cloned.1.call-done.p_ref.refs_12_.refs_8_, bf16[256,1024]{1,0:T(8,128)(2,1)} %refs_9_.1), custom_call_target="tpu_custom_call" | custom-call | flops 1048576 | bytes 65536 | tf_op jit(solution)/shard_map/inner/pallas_call | solution.py:389
  148.8 0.9 collective-permute-done.23.refs_7_
  149.6 0.7 copy-done.16
  150.3 4.5 %final.1 = bf16[256,1024]{1,0:T(8,128)(2,1)} custom-call(s32[3]{0:T(128)} %pad_add_fusion.place_ref, f32[256,1024]{1,0:T(8,128)} %get-tuple-element.52.gq_ref, f32[256,512]{1,0:T(8,128)} %get-tuple-element.64.refs_0_, bf16[256,512]{1,0:T(8,128)(2,1)} %collective-permute-done.15.refs_1_, bf16[256,512]{1,0:T(8,128)(2,1)} %collective-permute-done.16.refs_2_, ...), custom_call_target="tpu_custom_call" | custom-call | flops 1048576 | bytes 65536 | tf_op jit(solution)/shard_map/final/pallas_call | solution.py:459
  (67 shorter events, 3.3 us)
Async XLA Ops:
  7.2 61.9 %all-gather.2.cloned.1.call-start = ((), (), s32[]{:S(2)}) async-start(), calls=%async_computation.2 | async-start | bytes 4718592 | tf_op jit(solution)/shard_map/all_gather | solution.py:491
  9.7 24.1 %copy-start = (bf16[272,512]{1,0:T(8,128)(2,1)}, bf16[272,512]{1,0:T(8,128)(2,1)S(1)}, u32[]{:S(2)}) copy-start(bf16[272,512]{1,0:T(8,128)(2,1)S(1)} %get-tuple-element.83.refs_4_) | copy-start | bytes 835588
  9.8 24.1 %copy-start.1 = (bf16[272,512]{1,0:T(8,128)(2,1)}, bf16[272,512]{1,0:T(8,128)(2,1)S(1)}, u32[]{:S(2)}) copy-start(bf16[272,512]{1,0:T(8,128)(2,1)S(1)} %get-tuple-element.84.refs_0_) | copy-start | bytes 835588
  9.8 15.1 %collective-permute-start.5 = (bf16[272,512]{1,0:T(8,128)(2,1)S(1)}, bf16[272,512]{1,0:T(8,128)(2,1)S(1)}, u32[]{:S(2)}, u32[]{:S(2)}) collective-permute-start(bf16[272,512]{1,0:T(8,128)(2,1)S(1)} %get-tuple-element.83.refs_4_), channel_id=1, source_target_pairs={{0,3},{1,0},{2,1},{3,2},{4,7},{5,4},{6,5},{7,6},{8,11},{9,8},{10,9... | collective-permute-start | bytes 835592 | tf_op jit(solution)/shard_map/ppermute | solution.py:470
  12.9 14.0 %collective-permute-start.4 = (bf16[272,512]{1,0:T(8,128)(2,1)S(1)}, bf16[272,512]{1,0:T(8,128)(2,1)S(1)}, u32[]{:S(2)}, u32[]{:S(2)}) collective-permute-start(bf16[272,512]{1,0:T(8,128)(2,1)S(1)} %get-tuple-element.83.refs_4_), channel_id=1, source_target_pairs={{0,2},{1,3},{2,0},{3,1},{4,6},{5,7},{6,4},{7,5},{8,10},{9,11},{10,... | collective-permute-start | bytes 835592 | tf_op jit(solution)/shard_map/ppermute | solution.py:470
  13.6 15.0 %collective-permute-start.3 = (bf16[272,512]{1,0:T(8,128)(2,1)S(1)}, bf16[272,512]{1,0:T(8,128)(2,1)S(1)}, u32[]{:S(2)}, u32[]{:S(2)}) collective-permute-start(bf16[272,512]{1,0:T(8,128)(2,1)S(1)} %get-tuple-element.83.refs_4_), channel_id=1, source_target_pairs={{0,1},{1,2},{2,3},{3,0},{4,5},{5,6},{6,7},{7,4},{8,9},{9,10},{10,1... | collective-permute-start | bytes 835592 | tf_op jit(solution)/shard_map/ppermute | solution.py:470
  14.5 14.0 %collective-permute-start.2 = (bf16[272,512]{1,0:T(8,128)(2,1)S(1)}, bf16[272,512]{1,0:T(8,128)(2,1)S(1)}, u32[]{:S(2)}, u32[]{:S(2)}) collective-permute-start(bf16[272,512]{1,0:T(8,128)(2,1)S(1)} %get-tuple-element.84.refs_0_), channel_id=1, source_target_pairs={{0,12},{1,13},{2,14},{3,15},{4,0},{5,1},{6,2},{7,3},{8,4},{9,5},{1... | collective-permute-start | bytes 835592 | tf_op jit(solution)/shard_map/ppermute | solution.py:470
  17.3 11.2 %collective-permute-start.1 = (bf16[272,512]{1,0:T(8,128)(2,1)S(1)}, bf16[272,512]{1,0:T(8,128)(2,1)S(1)}, u32[]{:S(2)}, u32[]{:S(2)}) collective-permute-start(bf16[272,512]{1,0:T(8,128)(2,1)S(1)} %get-tuple-element.84.refs_0_), channel_id=1, source_target_pairs={{0,8},{1,9},{2,10},{3,11},{4,12},{5,13},{6,14},{7,15},{8,0},{9,1},... | collective-permute-start | bytes 835592 | tf_op jit(solution)/shard_map/ppermute | solution.py:470
  24.8 9.1 %copy-start.5 = (bf16[272,512]{1,0:T(8,128)(2,1)}, bf16[272,512]{1,0:T(8,128)(2,1)S(1)}, u32[]{:S(2)}) copy-start(bf16[272,512]{1,0:T(8,128)(2,1)S(1)} %collective-permute-done.5.refs_7_) | copy-start | bytes 835588
  24.8 9.1 %collective-permute-start = (bf16[272,512]{1,0:T(8,128)(2,1)S(1)}, bf16[272,512]{1,0:T(8,128)(2,1)S(1)}, u32[]{:S(2)}, u32[]{:S(2)}) collective-permute-start(bf16[272,512]{1,0:T(8,128)(2,1)S(1)} %get-tuple-element.84.refs_0_), channel_id=1, source_target_pairs={{0,4},{1,5},{2,6},{3,7},{4,8},{5,9},{6,10},{7,11},{8,12},{9,13},{1... | collective-permute-start | bytes 835592 | tf_op jit(solution)/shard_map/ppermute | solution.py:470
  26.9 7.0 %copy-start.6 = (bf16[272,512]{1,0:T(8,128)(2,1)}, bf16[272,512]{1,0:T(8,128)(2,1)S(1)}, u32[]{:S(2)}) copy-start(bf16[272,512]{1,0:T(8,128)(2,1)S(1)} %collective-permute-done.4.refs_6_) | copy-start | bytes 835588
  28.5 5.4 %copy-start.7 = (bf16[272,512]{1,0:T(8,128)(2,1)}, bf16[272,512]{1,0:T(8,128)(2,1)S(1)}, u32[]{:S(2)}) copy-start(bf16[272,512]{1,0:T(8,128)(2,1)S(1)} %collective-permute-done.3.refs_5_) | copy-start | bytes 835588
  28.5 5.4 %copy-start.8 = (bf16[272,512]{1,0:T(8,128)(2,1)}, bf16[272,512]{1,0:T(8,128)(2,1)S(1)}, u32[]{:S(2)}) copy-start(bf16[272,512]{1,0:T(8,128)(2,1)S(1)} %collective-permute-done.2.refs_3_) | copy-start | bytes 835588
  28.5 5.4 %copy-start.9 = (bf16[272,512]{1,0:T(8,128)(2,1)}, bf16[272,512]{1,0:T(8,128)(2,1)S(1)}, u32[]{:S(2)}) copy-start(bf16[272,512]{1,0:T(8,128)(2,1)S(1)} %collective-permute-done.1.refs_2_) | copy-start | bytes 835588
  33.9 0.7 copy-start.10
  39.1 25.1 %collective-permute-start.8 = (bf16[528,512]{1,0:T(8,128)(2,1)}, bf16[528,512]{1,0:T(8,128)(2,1)S(1)}, u32[]{:S(2)}, u32[]{:S(2)}) collective-permute-start(bf16[528,512]{1,0:T(8,128)(2,1)} %get-tuple-element.45), channel_id=1, source_target_pairs={{0,3},{1,0},{2,1},{3,2},{4,7},{5,4},{6,5},{7,6},{8,11},{9,8},{10,9... | collective-permute-start | bytes 1622024 | tf_op jit(solution)/shard_map/ppermute | solution.py:470
  42.5 31.5 %collective-permute-start.11 = (bf16[528,512]{1,0:T(8,128)(2,1)}, bf16[528,512]{1,0:T(8,128)(2,1)S(1)}, u32[]{:S(2)}, u32[]{:S(2)}) collective-permute-start(bf16[528,512]{1,0:T(8,128)(2,1)} %get-tuple-element.49), channel_id=1, source_target_pairs={{0,12},{1,13},{2,14},{3,15},{4,0},{5,1},{6,2},{7,3},{8,4},{9,5},{1... | collective-permute-start | bytes 1622024 | tf_op jit(solution)/shard_map/ppermute | solution.py:470
  48.5 25.5 %collective-permute-start.7 = (bf16[528,512]{1,0:T(8,128)(2,1)}, bf16[528,512]{1,0:T(8,128)(2,1)S(1)}, u32[]{:S(2)}, u32[]{:S(2)}) collective-permute-start(bf16[528,512]{1,0:T(8,128)(2,1)} %get-tuple-element.44), channel_id=1, source_target_pairs={{0,2},{1,3},{2,0},{3,1},{4,6},{5,7},{6,4},{7,5},{8,10},{9,11},{10,... | collective-permute-start | bytes 1622024 | tf_op jit(solution)/shard_map/ppermute | solution.py:470
  48.5 25.5 %collective-permute-start.10 = (bf16[528,512]{1,0:T(8,128)(2,1)}, bf16[528,512]{1,0:T(8,128)(2,1)S(1)}, u32[]{:S(2)}, u32[]{:S(2)}) collective-permute-start(bf16[528,512]{1,0:T(8,128)(2,1)} %get-tuple-element.48), channel_id=1, source_target_pairs={{0,8},{1,9},{2,10},{3,11},{4,12},{5,13},{6,14},{7,15},{8,0},{9,1},... | collective-permute-start | bytes 1622024 | tf_op jit(solution)/shard_map/ppermute | solution.py:470
  53.8 20.2 %collective-permute-start.6 = (bf16[528,512]{1,0:T(8,128)(2,1)}, bf16[528,512]{1,0:T(8,128)(2,1)S(1)}, u32[]{:S(2)}, u32[]{:S(2)}) collective-permute-start(bf16[528,512]{1,0:T(8,128)(2,1)} %get-tuple-element.43), channel_id=1, source_target_pairs={{0,1},{1,2},{2,3},{3,0},{4,5},{5,6},{6,7},{7,4},{8,9},{9,10},{10,1... | collective-permute-start | bytes 1622024 | tf_op jit(solution)/shard_map/ppermute | solution.py:470
  64.2 10.8 %copy-start.2 = (bf16[528,512]{1,0:T(8,128)(2,1)}, bf16[528,512]{1,0:T(8,128)(2,1)S(1)}, u32[]{:S(2)}) copy-start(bf16[528,512]{1,0:T(8,128)(2,1)S(1)} %collective-permute-done.8.refs_3_.refs_11_) | copy-start | bytes 1622020
  64.2 10.8 %collective-permute-start.9 = (bf16[528,512]{1,0:T(8,128)(2,1)}, bf16[528,512]{1,0:T(8,128)(2,1)S(1)}, u32[]{:S(2)}, u32[]{:S(2)}) collective-permute-start(bf16[528,512]{1,0:T(8,128)(2,1)} %get-tuple-element.47), channel_id=1, source_target_pairs={{0,4},{1,5},{2,6},{3,7},{4,8},{5,9},{6,10},{7,11},{8,12},{9,13},{1... | collective-permute-start | bytes 1622024 | tf_op jit(solution)/shard_map/ppermute | solution.py:470
  74.0 1.0 copy-start.11
  74.0 1.0 copy-start.3
  74.0 1.1 copy-start.12
  74.0 1.3 copy-start.4
  75.0 0.8 copy-start.13
  84.8 21.1 %all-to-all-start = ((f32[16,16,256]{2,1,0:T(8,128)}), f32[16,16,256]{2,1,0:T(8,128)S(1)}, u32[]{:S(2)}, u32[]{:S(2)}) async-start(f32[16,16,256]{2,1,0:T(8,128)} %get-tuple-element.50), calls=%async_computation | async-start | bytes 524288 | tf_op jit(solution)/shard_map/all_to_all | solution.py:505
  91.9 63.5 %reduce-scatter.2.cloned.1.call-start = ((), (), s32[]{:S(2)}) async-start(), calls=%async_computation.3 | async-start | bytes 4718592 | tf_op jit(solution)/shard_map/reduce_scatter | solution.py:512
  91.9 25.9 %collective-permute-start.12 = (bf16[544,512]{1,0:T(8,128)(2,1)}, bf16[544,512]{1,0:T(8,128)(2,1)S(1)}, u32[]{:S(2)}, u32[]{:S(2)}) collective-permute-start(bf16[544,512]{1,0:T(8,128)(2,1)} %get-tuple-element.58), channel_id=1, source_target_pairs={{0,3},{1,0},{2,1},{3,2},{4,7},{5,4},{6,5},{7,6},{8,11},{9,8},{10,9... | collective-permute-start | bytes 1671176 | tf_op jit(solution)/shard_map/ppermute | solution.py:470
  95.1 23.6 %collective-permute-start.13 = (bf16[544,512]{1,0:T(8,128)(2,1)}, bf16[544,512]{1,0:T(8,128)(2,1)S(1)}, u32[]{:S(2)}, u32[]{:S(2)}) collective-permute-start(bf16[544,512]{1,0:T(8,128)(2,1)} %get-tuple-element.59), channel_id=1, source_target_pairs={{0,2},{1,3},{2,0},{3,1},{4,6},{5,7},{6,4},{7,5},{8,10},{9,11},{10,... | collective-permute-start | bytes 1671176 | tf_op jit(solution)/shard_map/ppermute | solution.py:470
  96.0 25.0 %collective-permute-start.14 = (bf16[544,512]{1,0:T(8,128)(2,1)}, bf16[544,512]{1,0:T(8,128)(2,1)S(1)}, u32[]{:S(2)}, u32[]{:S(2)}) collective-permute-start(bf16[544,512]{1,0:T(8,128)(2,1)} %get-tuple-element.60), channel_id=1, source_target_pairs={{0,1},{1,2},{2,3},{3,0},{4,5},{5,6},{6,7},{7,4},{8,9},{9,10},{10,1... | collective-permute-start | bytes 1671176 | tf_op jit(solution)/shard_map/ppermute | solution.py:470
  96.8 32.7 %collective-permute-start.18 = (bf16[544,512]{1,0:T(8,128)(2,1)}, bf16[544,512]{1,0:T(8,128)(2,1)}, u32[]{:S(2)}, u32[]{:S(2)}) collective-permute-start(bf16[544,512]{1,0:T(8,128)(2,1)} %get-tuple-element.73), channel_id=1, source_target_pairs={{0,12},{1,13},{2,14},{3,15},{4,0},{5,1},{6,2},{7,3},{8,4},{9,5},{1... | collective-permute-start | bytes 1671176 | tf_op jit(solution)/shard_map/ppermute | solution.py:470
  99.5 30.9 %collective-permute-start.19 = (bf16[544,512]{1,0:T(8,128)(2,1)}, bf16[544,512]{1,0:T(8,128)(2,1)}, u32[]{:S(2)}, u32[]{:S(2)}) collective-permute-start(bf16[544,512]{1,0:T(8,128)(2,1)} %get-tuple-element.74), channel_id=1, source_target_pairs={{0,8},{1,9},{2,10},{3,11},{4,12},{5,13},{6,14},{7,15},{8,0},{9,1},... | collective-permute-start | bytes 1671176 | tf_op jit(solution)/shard_map/ppermute | solution.py:470
  117.9 3.1 %copy-start.17 = (bf16[544,512]{1,0:T(8,128)(2,1)}, bf16[544,512]{1,0:T(8,128)(2,1)S(1)}, u32[]{:S(2)}) copy-start(bf16[544,512]{1,0:T(8,128)(2,1)S(1)} %collective-permute-done.12.refs_5_) | copy-start | bytes 1671172
  117.9 12.6 %collective-permute-start.20 = (bf16[544,512]{1,0:T(8,128)(2,1)}, bf16[544,512]{1,0:T(8,128)(2,1)}, u32[]{:S(2)}, u32[]{:S(2)}) collective-permute-start(bf16[544,512]{1,0:T(8,128)(2,1)} %get-tuple-element.75), channel_id=1, source_target_pairs={{0,4},{1,5},{2,6},{3,7},{4,8},{5,9},{6,10},{7,11},{8,12},{9,13},{1... | collective-permute-start | bytes 1671176 | tf_op jit(solution)/shard_map/ppermute | solution.py:470
  118.8 2.3 %copy-start.18 = (bf16[544,512]{1,0:T(8,128)(2,1)}, bf16[544,512]{1,0:T(8,128)(2,1)S(1)}, u32[]{:S(2)}) copy-start(bf16[544,512]{1,0:T(8,128)(2,1)S(1)} %collective-permute-done.13.refs_6_) | copy-start | bytes 1671172
  121.0 0.8 copy-start.19
  126.4 14.0 %collective-permute-start.15 = (bf16[256,512]{1,0:T(8,128)(2,1)}, bf16[256,512]{1,0:T(8,128)(2,1)}, u32[]{:S(2)}, u32[]{:S(2)}) collective-permute-start(bf16[256,512]{1,0:T(8,128)(2,1)} %get-tuple-element.65), channel_id=1, source_target_pairs={{0,12},{1,13},{2,14},{3,15},{4,0},{5,1},{6,2},{7,3},{8,4},{9,5},{1... | collective-permute-start | bytes 786440 | tf_op jit(solution)/shard_map/ppermute | solution.py:470
  128.7 20.0 %collective-permute-start.16 = (bf16[256,512]{1,0:T(8,128)(2,1)}, bf16[256,512]{1,0:T(8,128)(2,1)}, u32[]{:S(2)}, u32[]{:S(2)}) collective-permute-start(bf16[256,512]{1,0:T(8,128)(2,1)} %get-tuple-element.66), channel_id=1, source_target_pairs={{0,8},{1,9},{2,10},{3,11},{4,12},{5,13},{6,14},{7,15},{8,0},{9,1},... | collective-permute-start | bytes 786440 | tf_op jit(solution)/shard_map/ppermute | solution.py:470
  129.6 19.2 %collective-permute-start.17 = (bf16[256,512]{1,0:T(8,128)(2,1)}, bf16[256,512]{1,0:T(8,128)(2,1)}, u32[]{:S(2)}, u32[]{:S(2)}) collective-permute-start(bf16[256,512]{1,0:T(8,128)(2,1)} %get-tuple-element.67), channel_id=1, source_target_pairs={{0,4},{1,5},{2,6},{3,7},{4,8},{5,9},{6,10},{7,11},{8,12},{9,13},{1... | collective-permute-start | bytes 786440 | tf_op jit(solution)/shard_map/ppermute | solution.py:470
  135.1 13.7 %collective-permute-start.21 = (bf16[256,512]{1,0:T(8,128)(2,1)}, bf16[256,512]{1,0:T(8,128)(2,1)S(1)}, u32[]{:S(2)}, u32[]{:S(2)}) collective-permute-start(bf16[256,512]{1,0:T(8,128)(2,1)} %get-tuple-element.77), channel_id=1, source_target_pairs={{0,3},{1,0},{2,1},{3,2},{4,7},{5,4},{6,5},{7,6},{8,11},{9,8},{10,9... | collective-permute-start | bytes 786440 | tf_op jit(solution)/shard_map/ppermute | solution.py:470
  137.2 11.6 %collective-permute-start.22 = (bf16[256,512]{1,0:T(8,128)(2,1)}, bf16[256,512]{1,0:T(8,128)(2,1)S(1)}, u32[]{:S(2)}, u32[]{:S(2)}) collective-permute-start(bf16[256,512]{1,0:T(8,128)(2,1)} %get-tuple-element.78), channel_id=1, source_target_pairs={{0,2},{1,3},{2,0},{3,1},{4,6},{5,7},{6,4},{7,5},{8,10},{9,11},{10,... | collective-permute-start | bytes 786440 | tf_op jit(solution)/shard_map/ppermute | solution.py:470
  140.4 9.3 %collective-permute-start.23 = (bf16[256,512]{1,0:T(8,128)(2,1)}, bf16[256,512]{1,0:T(8,128)(2,1)S(1)}, u32[]{:S(2)}, u32[]{:S(2)}) collective-permute-start(bf16[256,512]{1,0:T(8,128)(2,1)} %get-tuple-element.79), channel_id=1, source_target_pairs={{0,1},{1,2},{2,3},{3,0},{4,5},{5,6},{6,7},{7,4},{8,9},{9,10},{10,1... | collective-permute-start | bytes 786440 | tf_op jit(solution)/shard_map/ppermute | solution.py:470
  148.7 0.9 copy-start.14
  148.8 0.9 copy-start.15
  149.6 0.7 copy-start.16
Sparse Core Ops, SparseCore 0:
  9.7 34.7 all-gather.1
  117.3 38.0 reduce-scatter.1

commit v7 on v6

--- a/solution.py
+++ b/solution.py
@@ -82,7 +82,7 @@
 
 def mid_kernel(shift, cap, groups, reps, negs, place_ref, *refs):
     sources = (refs[0:SIDE], refs[SIDE : 2 * SIDE])
-    outs, ranks_out = refs[2 * SIDE : 2 * SIDE + 2], refs[2 * SIDE + 2 :]
+    outs, ranks_out = refs[-4:-2], refs[-2:]
     rows, half_width = sources[0][0].shape
     toks = rows - 16
     slots = groups * cap
@@ -121,16 +121,16 @@
         outs[half][groups * SIDE * cap :, :] = codes.astype(BF16)
 
 
-def mid(place, shift, first, second, groups, reps, cap, negs):
+def mid(place, shift, first, second, earlier, groups, reps, cap, negs):
     rows, half_width = first[0].shape
     slots = jax.ShapeDtypeStruct((groups * SIDE * cap + 16, half_width), BF16)
     ranks = jax.ShapeDtypeStruct((SIDE * groups, rows - 16), BF16)
     return call(
         functools.partial(mid_kernel, shift, cap, groups, reps, negs), "mid", 1,
-        [full((rows, half_width))] * (2 * SIDE),
+        [full((rows, half_width))] * (2 * SIDE) + [full(v.shape) for v in earlier],
         [full(slots.shape)] * 2 + [full(ranks.shape)] * 2,
         [slots, slots, ranks, ranks], [], LIGHT,
-    )(place, *first, *second)
+    )(place, *first, *second, *earlier)
 
 
 def inside_kernel(temper, place_ref, p_ref, q_ref, out_ref, top, total):
@@ -490,13 +490,15 @@
         sources.append([block] + [along(block, half, s) for s in range(1, SIDE)])
     gathered = lax.all_gather(passages, "grp", axis=0, tiled=True)
 
-    first, second, ranks_first, ranks_second = [], [], [], []
-    for shift in range(SIDE):
-        one, two, rank_one, rank_two = mid(place, shift, *sources, groups, reps, cap, negs)
-        first.append(along(one, 1, shift) if shift else one)
-        second.append(along(two, 0, shift) if shift else two)
-        ranks_first.append(rank_one)
-        ranks_second.append(rank_two)
+    first, second, ranks_first, ranks_second = ([None] * SIDE for _ in range(4))
+    earlier = []
+    for shift in (3, 1, 2, 0):
+        one, two, ranks_first[shift], ranks_second[shift] = mid(
+            place, shift, *sources, earlier, groups, reps, cap, negs
+        )
+        earlier = [ranks_first[shift]]
+        first[shift] = along(one, 1, shift) if shift else one
+        second[shift] = along(two, 0, shift) if shift else two
 
     within = inside(place, gathered, queries, temper)
     back_first, back_second, hard_scores, codes, part = hard(

time: 163 us -> 159 us (0.975)
  waiting for transfers between devices: 38 us -> 34 us
    all_to_all x1, starting transfers between devices: 7.03 us -> 4.18 us  [shards(): parts = lax.all_to_all(part, 'rep', split_axis=0, concat_axis=0, tiled=True)]
    ppermute x24, waiting for transfers between devices: 31.2 us -> 28.4 us  [along(): return lax.ppermute(x, 'rep', pairs)]
    ppermute x24, starting transfers between devices: 32.3 us -> 34.1 us  [along(): return lax.ppermute(x, 'rep', pairs)]
  transfers between devices with their start and end apart: 27 -> 27, of which waited for: 11 -> 11; matrix products, arithmetic and copies ran while one was open for 2% -> 2% of each run, Pallas kernels for 34% -> 35%
where the time goes in v7:
time: 159 us; the launch traced here: 158 us
  Pallas kernels  64.4 us (41%)
  starting transfers between devices  38.4 us (24%)
  waiting for transfers between devices  34 us (21%)
  between operations  14.2 us (9%)
  local copies, waits for them, and re-layouts  4.58 us (3%)
  other arithmetic  2.04 us (1%)
    ppermute x24, starting transfers between devices, along(): return lax.ppermute(x, 'rep', pairs)  34.1 us
    ppermute x24, waiting for transfers between devices, along(): return lax.ppermute(x, 'rep', pairs)  28.4 us
    pallas_call x4, Pallas kernels, mid(): call(functools.partial(mid_kernel, shift, cap, groups, reps, negs), 'mid'...  17.8 us
    pallas_call x1, Pallas kernels, column(): call(functools.partial(column_kernel, reps, cap, temper), 'column', gathe...  10.5 us
    pallas_call x2, Pallas kernels, reduce(): call(functools.partial(reduce_kernel, half, cap, groups), 'reduce', 1, [f...  9.2 us
    pallas_call x1, Pallas kernels, hard(): call(functools.partial(hard_kernel, reps, cap, temper), 'hard', levels +...  9.03 us
    pallas_call x1, Pallas kernels, inner(): call(functools.partial(inner_kernel, temper), 'inner', 2, [full(log_total...  8.37 us
    pallas_call x1, Pallas kernels, inside(): call(functools.partial(inside_kernel, temper), 'inside', 2, [pl.BlockSpec...  4.95 us
  transfers between devices with their start and end apart: 27, of which 11 were waited for; matrix products, arithmetic and copies ran while one was open for 2% of the time, Pallas kernels for 35%

profile of v7, /device:TPU:0, one launch (start us, length us, event | category | flops | bytes accessed | tf_op | source)
XLA Modules:
  0.0 157.6 jit_solution(10803694535406266429)
XLA Ops:
  7.2 0.7 all-gather.2.cloned.1.call-update
  7.9 0.7 convert_bitcast_fusion
  8.6 1.1 fusion.7
  9.8 3.2 %collective-permute-start.5 = (bf16[272,512]{1,0:T(8,128)(2,1)S(1)}, bf16[272,512]{1,0:T(8,128)(2,1)S(1)}, u32[]{:S(2)}, u32[]{:S(2)}) collective-permute-start(bf16[272,512]{1,0:T(8,128)(2,1)S(1)} %get-tuple-element.83.refs_4_), channel_id=1, source_target_pairs={{0,3},{1,0},{2,1},{3,2},{4,7},{5,4},{6,5},{7,6},{8,11},{9,8},{10,9... | collective-permute-start | bytes 835592 | tf_op jit(solution)/shard_map/ppermute | solution.py:470
  12.9 0.6 collective-permute-start.4
  13.6 1.0 collective-permute-start.3
  14.5 2.8 %collective-permute-start.2 = (bf16[272,512]{1,0:T(8,128)(2,1)S(1)}, bf16[272,512]{1,0:T(8,128)(2,1)S(1)}, u32[]{:S(2)}, u32[]{:S(2)}) collective-permute-start(bf16[272,512]{1,0:T(8,128)(2,1)S(1)} %get-tuple-element.84.refs_0_), channel_id=1, source_target_pairs={{0,12},{1,13},{2,14},{3,15},{4,0},{5,1},{6,2},{7,3},{8,4},{9,5},{1... | collective-permute-start | bytes 835592 | tf_op jit(solution)/shard_map/ppermute | solution.py:470
  17.3 0.8 collective-permute-start.1
  18.1 6.7 %collective-permute-done.5.refs_7_ = bf16[272,512]{1,0:T(8,128)(2,1)S(1)} collective-permute-done((bf16[272,512]{1,0:T(8,128)(2,1)S(1)}, bf16[272,512]{1,0:T(8,128)(2,1)S(1)}, u32[]{:S(2)}, u32[]{:S(2)}) %collective-permute-start.5) | collective-permute-done | bytes 278560 | tf_op jit(solution)/shard_map/ppermute | solution.py:470
  24.8 1.5 collective-permute-start
  26.9 1.6 %collective-permute-done.3.refs_5_ = bf16[272,512]{1,0:T(8,128)(2,1)S(1)} collective-permute-done((bf16[272,512]{1,0:T(8,128)(2,1)S(1)}, bf16[272,512]{1,0:T(8,128)(2,1)S(1)}, u32[]{:S(2)}, u32[]{:S(2)}) %collective-permute-start.3) | collective-permute-done | bytes 278560 | tf_op jit(solution)/shard_map/ppermute | solution.py:470
  28.5 5.3 %collective-permute-done.refs_1_ = bf16[272,512]{1,0:T(8,128)(2,1)S(1)} collective-permute-done((bf16[272,512]{1,0:T(8,128)(2,1)S(1)}, bf16[272,512]{1,0:T(8,128)(2,1)S(1)}, u32[]{:S(2)}, u32[]{:S(2)}) %collective-permute-start) | collective-permute-done | bytes 278560 | tf_op jit(solution)/shard_map/ppermute | solution.py:470
  34.0 0.7 copy-done.10
  34.7 4.5 %mid.4 = (bf16[528,512]{1,0:T(8,128)(2,1)}, bf16[528,512]{1,0:T(8,128)(2,1)}, bf16[32,256]{1,0:T(8,128)(2,1)}, bf16[32,256]{1,0:T(8,128)(2,1)}) custom-call(s32[3]{0:T(128)} %pad_add_fusion.place_ref, bf16[272,512]{1,0:T(8,128)(2,1)} %copy-done.1, bf16[272,512]{1,0:T(8,128)(2,1)} %copy-done.10, bf16[272,512]{1,0:T(8,128)(2,1)} %copy-done.9, ...), custom_call_target="tpu_custom_call" | custom-call | flops 1048576 | bytes 65536 | tf_op jit(solution)/shard_map/mid/pallas_call | solution.py:128
  39.1 3.4 %collective-permute-start.8 = (bf16[528,512]{1,0:T(8,128)(2,1)}, bf16[528,512]{1,0:T(8,128)(2,1)S(1)}, u32[]{:S(2)}, u32[]{:S(2)}) collective-permute-start(bf16[528,512]{1,0:T(8,128)(2,1)} %get-tuple-element.48), channel_id=1, source_target_pairs={{0,3},{1,0},{2,1},{3,2},{4,7},{5,4},{6,5},{7,6},{8,11},{9,8},{10,9... | collective-permute-start | bytes 1622024 | tf_op jit(solution)/shard_map/ppermute | solution.py:470
  42.5 1.6 collective-permute-start.11
  44.1 4.4 %mid.5 = (bf16[528,512]{1,0:T(8,128)(2,1)}, bf16[528,512]{1,0:T(8,128)(2,1)}, bf16[32,256]{1,0:T(8,128)(2,1)}, bf16[32,256]{1,0:T(8,128)(2,1)}) custom-call(s32[3]{0:T(128)} %pad_add_fusion.place_ref, bf16[272,512]{1,0:T(8,128)(2,1)} %copy-done.1, bf16[272,512]{1,0:T(8,128)(2,1)} %copy-done.10, bf16[272,512]{1,0:T(8,128)(2,1)} %copy-done.9, ...), custom_call_target="tpu_custom_call" | custom-call | flops 1048576 | bytes 65536 | tf_op jit(solution)/shard_map/mid/pallas_call | solution.py:128
  49.0 4.4 %mid.6 = (bf16[528,512]{1,0:T(8,128)(2,1)}, bf16[528,512]{1,0:T(8,128)(2,1)}, bf16[32,256]{1,0:T(8,128)(2,1)}, bf16[32,256]{1,0:T(8,128)(2,1)}) custom-call(s32[3]{0:T(128)} %pad_add_fusion.place_ref, bf16[272,512]{1,0:T(8,128)(2,1)} %copy-done.1, bf16[272,512]{1,0:T(8,128)(2,1)} %copy-done.10, bf16[272,512]{1,0:T(8,128)(2,1)} %copy-done.9, ...), custom_call_target="tpu_custom_call" | custom-call | flops 1048576 | bytes 65536 | tf_op jit(solution)/shard_map/mid/pallas_call | solution.py:128
  53.5 1.5 collective-permute-start.7
  55.0 1.9 %collective-permute-start.10 = (bf16[528,512]{1,0:T(8,128)(2,1)}, bf16[528,512]{1,0:T(8,128)(2,1)S(1)}, u32[]{:S(2)}, u32[]{:S(2)}) collective-permute-start(bf16[528,512]{1,0:T(8,128)(2,1)} %get-tuple-element.51), channel_id=1, source_target_pairs={{0,8},{1,9},{2,10},{3,11},{4,12},{5,13},{6,14},{7,15},{8,0},{9,1},... | collective-permute-start | bytes 1622024 | tf_op jit(solution)/shard_map/ppermute | solution.py:470
  56.8 4.5 %mid.7 = (bf16[528,512]{1,0:T(8,128)(2,1)}, bf16[528,512]{1,0:T(8,128)(2,1)}, bf16[32,256]{1,0:T(8,128)(2,1)}, bf16[32,256]{1,0:T(8,128)(2,1)}) custom-call(s32[3]{0:T(128)} %pad_add_fusion.place_ref, bf16[272,512]{1,0:T(8,128)(2,1)} %copy-done.1, bf16[272,512]{1,0:T(8,128)(2,1)} %copy-done.10, bf16[272,512]{1,0:T(8,128)(2,1)} %copy-done.9, ...), custom_call_target="tpu_custom_call" | custom-call | flops 1048576 | bytes 65536 | tf_op jit(solution)/shard_map/mid/pallas_call | solution.py:128
  61.3 5.0 %inside.1.refs_13_ = f32[1,256]{1,0:T(1,128)} custom-call(s32[3]{0:T(128)} %pad_add_fusion.place_ref, bf16[2048,1024]{1,0:T(8,128)(2,1)} %all-gather.2.cloned.1.call-done.p_ref.refs_12_.refs_8_, bf16[256,1024]{1,0:T(8,128)(2,1)} %refs_9_.1), custom_call_target="tpu_custom_call" | custom-call | flops 1048576 | bytes 65536 | tf_op jit(solution)/shard_map/inside/pallas_call | solution.py:158
  66.3 7.0 %collective-permute-done.6.refs_1_.refs_9_ = bf16[528,512]{1,0:T(8,128)(2,1)S(1)} collective-permute-done((bf16[528,512]{1,0:T(8,128)(2,1)}, bf16[528,512]{1,0:T(8,128)(2,1)S(1)}, u32[]{:S(2)}, u32[]{:S(2)}) %collective-permute-start.6) | collective-permute-done | bytes 540704 | tf_op jit(solution)/shard_map/ppermute | solution.py:470
  73.4 0.7 copy-done.3
  74.6 9.0 %hard.1 = (bf16[544,512]{1,0:T(8,128)(2,1)}, bf16[544,512]{1,0:T(8,128)(2,1)}, bf16[544,512]{1,0:T(8,128)(2,1)}, bf16[544,512]{1,0:T(8,128)(2,1)}, bf16[544,512]...) custom-call(s32[3]{0:T(128)} %pad_add_fusion.place_ref, ...), custom_call_target="tpu_custom_call" | custom-call | flops 1048576 | bytes 65536 | tf_op jit(solution)/shard_map/hard/pallas_call | solution.py:286
  83.7 4.2 %all-to-all-start = ((f32[16,16,256]{2,1,0:T(8,128)}), f32[16,16,256]{2,1,0:T(8,128)S(1)}, u32[]{:S(2)}, u32[]{:S(2)}) async-start(f32[16,16,256]{2,1,0:T(8,128)} %get-tuple-element.53), calls=%async_computation | async-start | bytes 524288 | tf_op jit(solution)/shard_map/all_to_all | solution.py:507
  87.9 3.2 %collective-permute-start.12 = (bf16[544,512]{1,0:T(8,128)(2,1)}, bf16[544,512]{1,0:T(8,128)(2,1)S(1)}, u32[]{:S(2)}, u32[]{:S(2)}) collective-permute-start(bf16[544,512]{1,0:T(8,128)(2,1)} %get-tuple-element.58), channel_id=1, source_target_pairs={{0,3},{1,0},{2,1},{3,2},{4,7},{5,4},{6,5},{7,6},{8,11},{9,8},{10,9... | collective-permute-start | bytes 1671176 | tf_op jit(solution)/shard_map/ppermute | solution.py:470
  91.1 0.9 collective-permute-start.13
  92.0 0.9 collective-permute-start.14
  92.8 2.7 %collective-permute-start.18 = (bf16[544,512]{1,0:T(8,128)(2,1)}, bf16[544,512]{1,0:T(8,128)(2,1)}, u32[]{:S(2)}, u32[]{:S(2)}) collective-permute-start(bf16[544,512]{1,0:T(8,128)(2,1)} %get-tuple-element.73), channel_id=1, source_target_pairs={{0,12},{1,13},{2,14},{3,15},{4,0},{5,1},{6,2},{7,3},{8,4},{9,5},{1... | collective-permute-start | bytes 1671176 | tf_op jit(solution)/shard_map/ppermute | solution.py:470
  95.5 0.9 collective-permute-start.19
  96.4 4.4 %all-to-all-done = f32[16,16,256]{2,1,0:T(8,128)S(1)} async-done(((f32[16,16,256]{2,1,0:T(8,128)}), f32[16,16,256]{2,1,0:T(8,128)S(1)}, u32[]{:S(2)}, u32[]{:S(2)}) %all-to-all-start) | async-done | bytes 262176 | tf_op jit(solution)/shard_map/all_to_all | solution.py:507
  101.4 10.5 %column.1 = (bf16[2048,1024]{1,0:T(8,128)(2,1)}, f32[8,128]{1,0:T(8,128)}) custom-call(s32[3]{0:T(128)} %pad_add_fusion.place_ref, s32[16,256]{1,0:T(8,128)} %get-tuple-element.61.code_ref, f32[8,256]{1,0:T(8,128)} %get-tuple-element.62.hs_ref, f32[16,256]{1,0:T(8,128)} %log_add_fusion.lt_ref, bf16[528,512]{1,0:T(8,128)(2,1)} %get-tuple-element.45.refs_0_.refs_8_, ...), custom_call_target="tpu_custom_call" | custom-call | flops 1048576 | bytes 65536 | tf_op jit(solution)/shard_map/column/pallas_call | solution.py:353
  112.0 1.3 collective-permute-done.12.refs_5_
  113.3 0.9 collective-permute-start.20
  114.2 2.2 %collective-permute-done.14.refs_7_ = bf16[544,512]{1,0:T(8,128)(2,1)S(1)} collective-permute-done((bf16[544,512]{1,0:T(8,128)(2,1)}, bf16[544,512]{1,0:T(8,128)(2,1)S(1)}, u32[]{:S(2)}, u32[]{:S(2)}) %collective-permute-start.14) | collective-permute-done | bytes 557088 | tf_op jit(solution)/shard_map/ppermute | solution.py:470
  116.5 0.8 copy-done.19
  117.3 4.6 %reduce.2 = (f32[256,512]{1,0:T(8,128)}, bf16[256,512]{1,0:T(8,128)(2,1)}, bf16[256,512]{1,0:T(8,128)(2,1)}, bf16[256,512]{1,0:T(8,128)(2,1)}) custom-call(s32[3]{0:T(128)} %pad_add_fusion.place_ref, f32[16,256]{1,0:T(8,128)} %log_add_fusion.lt_ref, bf16[32,256]{1,0:T(8,128)(2,1)} %get-tuple-element.56.refs_0_, ...), custom_call_target="tpu_custom_call" | custom-call | flops 549755813888 | bytes 65536 | tf_op jit(solution)/shard_map/reduce/pallas_call | solution.py:435
  121.8 2.3 %collective-permute-start.15 = (bf16[256,512]{1,0:T(8,128)(2,1)}, bf16[256,512]{1,0:T(8,128)(2,1)}, u32[]{:S(2)}, u32[]{:S(2)}) collective-permute-start(bf16[256,512]{1,0:T(8,128)(2,1)} %get-tuple-element.65), channel_id=1, source_target_pairs={{0,12},{1,13},{2,14},{3,15},{4,0},{5,1},{6,2},{7,3},{8,4},{9,5},{1... | collective-permute-start | bytes 786440 | tf_op jit(solution)/shard_map/ppermute | solution.py:470
  124.1 0.9 collective-permute-start.16
  125.0 0.8 collective-permute-start.17
  125.9 4.6 %reduce.3 = (f32[256,512]{1,0:T(8,128)}, bf16[256,512]{1,0:T(8,128)(2,1)}, bf16[256,512]{1,0:T(8,128)(2,1)}, bf16[256,512]{1,0:T(8,128)(2,1)}) custom-call(s32[3]{0:T(128)} %pad_add_fusion.place_ref, f32[16,256]{1,0:T(8,128)} %log_add_fusion.lt_ref, bf16[32,256]{1,0:T(8,128)(2,1)} %get-tuple-element.68.refs_0_, bf16[32,256]{1,0:T(8,128)(2,1)} %get-tuple-element.69.refs_1_, ...), custom_call_target="tpu_custom_call" | custom-call | flops 549755813888 | bytes 65536 | tf_op jit(solution)/shard_map/reduce/pallas_call | solution.py:435
  130.5 2.1 %collective-permute-start.21 = (bf16[256,512]{1,0:T(8,128)(2,1)}, bf16[256,512]{1,0:T(8,128)(2,1)S(1)}, u32[]{:S(2)}, u32[]{:S(2)}) collective-permute-start(bf16[256,512]{1,0:T(8,128)(2,1)} %get-tuple-element.77), channel_id=1, source_target_pairs={{0,3},{1,0},{2,1},{3,2},{4,7},{5,4},{6,5},{7,6},{8,11},{9,8},{10,9... | collective-permute-start | bytes 786440 | tf_op jit(solution)/shard_map/ppermute | solution.py:470
  132.6 3.2 %collective-permute-done.15.refs_1_ = bf16[256,512]{1,0:T(8,128)(2,1)} collective-permute-done((bf16[256,512]{1,0:T(8,128)(2,1)}, bf16[256,512]{1,0:T(8,128)(2,1)}, u32[]{:S(2)}, u32[]{:S(2)}) %collective-permute-start.15) | collective-permute-done | bytes 262176 | tf_op jit(solution)/shard_map/ppermute | solution.py:470
  135.8 8.4 %inner.1 = (f32[256,1024]{1,0:T(8,128)}, f32[1,256]{1,0:T(1,128)}) custom-call(s32[3]{0:T(128)} %pad_add_fusion.place_ref, f32[16,256]{1,0:T(8,128)} %log_add_fusion.lt_ref, bf16[2048,1024]{1,0:T(8,128)(2,1)} %all-gather.2.cloned.1.call-done.p_ref.refs_12_.refs_8_, bf16[256,1024]{1,0:T(8,128)(2,1)} %refs_9_.1), custom_call_target="tpu_custom_call" | custom-call | flops 1048576 | bytes 65536 | tf_op jit(solution)/shard_map/inner/pallas_call | solution.py:389
  144.2 0.9 collective-permute-done.23.refs_7_
  145.1 0.7 copy-done.16
  145.8 4.5 %final.1 = bf16[256,1024]{1,0:T(8,128)(2,1)} custom-call(s32[3]{0:T(128)} %pad_add_fusion.place_ref, f32[256,1024]{1,0:T(8,128)} %get-tuple-element.55.gq_ref, f32[256,512]{1,0:T(8,128)} %get-tuple-element.64.refs_0_, bf16[256,512]{1,0:T(8,128)(2,1)} %collective-permute-done.15.refs_1_, bf16[256,512]{1,0:T(8,128)(2,1)} %collective-permute-done.16.refs_2_, ...), custom_call_target="tpu_custom_call" | custom-call | flops 1048576 | bytes 65536 | tf_op jit(solution)/shard_map/final/pallas_call | solution.py:459
  (67 shorter events, 3.2 us)
Async XLA Ops:
  7.2 54.1 %all-gather.2.cloned.1.call-start = ((), (), s32[]{:S(2)}) async-start(), calls=%async_computation.2 | async-start | bytes 4718592 | tf_op jit(solution)/shard_map/all_gather | solution.py:491
  9.7 24.1 %copy-start = (bf16[272,512]{1,0:T(8,128)(2,1)}, bf16[272,512]{1,0:T(8,128)(2,1)S(1)}, u32[]{:S(2)}) copy-start(bf16[272,512]{1,0:T(8,128)(2,1)S(1)} %get-tuple-element.83.refs_4_) | copy-start | bytes 835588
  9.8 24.1 %copy-start.1 = (bf16[272,512]{1,0:T(8,128)(2,1)}, bf16[272,512]{1,0:T(8,128)(2,1)S(1)}, u32[]{:S(2)}) copy-start(bf16[272,512]{1,0:T(8,128)(2,1)S(1)} %get-tuple-element.84.refs_0_) | copy-start | bytes 835588
  9.8 15.1 %collective-permute-start.5 = (bf16[272,512]{1,0:T(8,128)(2,1)S(1)}, bf16[272,512]{1,0:T(8,128)(2,1)S(1)}, u32[]{:S(2)}, u32[]{:S(2)}) collective-permute-start(bf16[272,512]{1,0:T(8,128)(2,1)S(1)} %get-tuple-element.83.refs_4_), channel_id=1, source_target_pairs={{0,3},{1,0},{2,1},{3,2},{4,7},{5,4},{6,5},{7,6},{8,11},{9,8},{10,9... | collective-permute-start | bytes 835592 | tf_op jit(solution)/shard_map/ppermute | solution.py:470
  12.9 14.0 %collective-permute-start.4 = (bf16[272,512]{1,0:T(8,128)(2,1)S(1)}, bf16[272,512]{1,0:T(8,128)(2,1)S(1)}, u32[]{:S(2)}, u32[]{:S(2)}) collective-permute-start(bf16[272,512]{1,0:T(8,128)(2,1)S(1)} %get-tuple-element.83.refs_4_), channel_id=1, source_target_pairs={{0,2},{1,3},{2,0},{3,1},{4,6},{5,7},{6,4},{7,5},{8,10},{9,11},{10,... | collective-permute-start | bytes 835592 | tf_op jit(solution)/shard_map/ppermute | solution.py:470
  13.6 15.0 %collective-permute-start.3 = (bf16[272,512]{1,0:T(8,128)(2,1)S(1)}, bf16[272,512]{1,0:T(8,128)(2,1)S(1)}, u32[]{:S(2)}, u32[]{:S(2)}) collective-permute-start(bf16[272,512]{1,0:T(8,128)(2,1)S(1)} %get-tuple-element.83.refs_4_), channel_id=1, source_target_pairs={{0,1},{1,2},{2,3},{3,0},{4,5},{5,6},{6,7},{7,4},{8,9},{9,10},{10,1... | collective-permute-start | bytes 835592 | tf_op jit(solution)/shard_map/ppermute | solution.py:470
  14.5 14.0 %collective-permute-start.2 = (bf16[272,512]{1,0:T(8,128)(2,1)S(1)}, bf16[272,512]{1,0:T(8,128)(2,1)S(1)}, u32[]{:S(2)}, u32[]{:S(2)}) collective-permute-start(bf16[272,512]{1,0:T(8,128)(2,1)S(1)} %get-tuple-element.84.refs_0_), channel_id=1, source_target_pairs={{0,12},{1,13},{2,14},{3,15},{4,0},{5,1},{6,2},{7,3},{8,4},{9,5},{1... | collective-permute-start | bytes 835592 | tf_op jit(solution)/shard_map/ppermute | solution.py:470
  17.3 11.2 %collective-permute-start.1 = (bf16[272,512]{1,0:T(8,128)(2,1)S(1)}, bf16[272,512]{1,0:T(8,128)(2,1)S(1)}, u32[]{:S(2)}, u32[]{:S(2)}) collective-permute-start(bf16[272,512]{1,0:T(8,128)(2,1)S(1)} %get-tuple-element.84.refs_0_), channel_id=1, source_target_pairs={{0,8},{1,9},{2,10},{3,11},{4,12},{5,13},{6,14},{7,15},{8,0},{9,1},... | collective-permute-start | bytes 835592 | tf_op jit(solution)/shard_map/ppermute | solution.py:470
  24.8 9.1 %copy-start.5 = (bf16[272,512]{1,0:T(8,128)(2,1)}, bf16[272,512]{1,0:T(8,128)(2,1)S(1)}, u32[]{:S(2)}) copy-start(bf16[272,512]{1,0:T(8,128)(2,1)S(1)} %collective-permute-done.5.refs_7_) | copy-start | bytes 835588
  24.8 9.1 %collective-permute-start = (bf16[272,512]{1,0:T(8,128)(2,1)S(1)}, bf16[272,512]{1,0:T(8,128)(2,1)S(1)}, u32[]{:S(2)}, u32[]{:S(2)}) collective-permute-start(bf16[272,512]{1,0:T(8,128)(2,1)S(1)} %get-tuple-element.84.refs_0_), channel_id=1, source_target_pairs={{0,4},{1,5},{2,6},{3,7},{4,8},{5,9},{6,10},{7,11},{8,12},{9,13},{1... | collective-permute-start | bytes 835592 | tf_op jit(solution)/shard_map/ppermute | solution.py:470
  26.9 7.0 %copy-start.6 = (bf16[272,512]{1,0:T(8,128)(2,1)}, bf16[272,512]{1,0:T(8,128)(2,1)S(1)}, u32[]{:S(2)}) copy-start(bf16[272,512]{1,0:T(8,128)(2,1)S(1)} %collective-permute-done.4.refs_6_) | copy-start | bytes 835588
  28.5 5.4 %copy-start.7 = (bf16[272,512]{1,0:T(8,128)(2,1)}, bf16[272,512]{1,0:T(8,128)(2,1)S(1)}, u32[]{:S(2)}) copy-start(bf16[272,512]{1,0:T(8,128)(2,1)S(1)} %collective-permute-done.3.refs_5_) | copy-start | bytes 835588
  28.5 5.4 %copy-start.8 = (bf16[272,512]{1,0:T(8,128)(2,1)}, bf16[272,512]{1,0:T(8,128)(2,1)S(1)}, u32[]{:S(2)}) copy-start(bf16[272,512]{1,0:T(8,128)(2,1)S(1)} %collective-permute-done.2.refs_3_) | copy-start | bytes 835588
  28.5 5.4 %copy-start.9 = (bf16[272,512]{1,0:T(8,128)(2,1)}, bf16[272,512]{1,0:T(8,128)(2,1)S(1)}, u32[]{:S(2)}) copy-start(bf16[272,512]{1,0:T(8,128)(2,1)S(1)} %collective-permute-done.1.refs_2_) | copy-start | bytes 835588
  33.9 0.7 copy-start.10
  39.1 15.8 %collective-permute-start.8 = (bf16[528,512]{1,0:T(8,128)(2,1)}, bf16[528,512]{1,0:T(8,128)(2,1)S(1)}, u32[]{:S(2)}, u32[]{:S(2)}) collective-permute-start(bf16[528,512]{1,0:T(8,128)(2,1)} %get-tuple-element.48), channel_id=1, source_target_pairs={{0,3},{1,0},{2,1},{3,2},{4,7},{5,4},{6,5},{7,6},{8,11},{9,8},{10,9... | collective-permute-start | bytes 1622024 | tf_op jit(solution)/shard_map/ppermute | solution.py:470
  42.5 23.7 %collective-permute-start.11 = (bf16[528,512]{1,0:T(8,128)(2,1)}, bf16[528,512]{1,0:T(8,128)(2,1)S(1)}, u32[]{:S(2)}, u32[]{:S(2)}) collective-permute-start(bf16[528,512]{1,0:T(8,128)(2,1)} %get-tuple-element.52), channel_id=1, source_target_pairs={{0,12},{1,13},{2,14},{3,15},{4,0},{5,1},{6,2},{7,3},{8,4},{9,5},{1... | collective-permute-start | bytes 1622024 | tf_op jit(solution)/shard_map/ppermute | solution.py:470
  48.5 24.8 %collective-permute-start.6 = (bf16[528,512]{1,0:T(8,128)(2,1)}, bf16[528,512]{1,0:T(8,128)(2,1)S(1)}, u32[]{:S(2)}, u32[]{:S(2)}) collective-permute-start(bf16[528,512]{1,0:T(8,128)(2,1)} %get-tuple-element.46), channel_id=1, source_target_pairs={{0,1},{1,2},{2,3},{3,0},{4,5},{5,6},{6,7},{7,4},{8,9},{9,10},{10,1... | collective-permute-start | bytes 1622024 | tf_op jit(solution)/shard_map/ppermute | solution.py:470
  48.5 24.8 %collective-permute-start.9 = (bf16[528,512]{1,0:T(8,128)(2,1)}, bf16[528,512]{1,0:T(8,128)(2,1)S(1)}, u32[]{:S(2)}, u32[]{:S(2)}) collective-permute-start(bf16[528,512]{1,0:T(8,128)(2,1)} %get-tuple-element.50), channel_id=1, source_target_pairs={{0,4},{1,5},{2,6},{3,7},{4,8},{5,9},{6,10},{7,11},{8,12},{9,13},{1... | collective-permute-start | bytes 1622024 | tf_op jit(solution)/shard_map/ppermute | solution.py:470
  53.5 19.9 %collective-permute-start.7 = (bf16[528,512]{1,0:T(8,128)(2,1)}, bf16[528,512]{1,0:T(8,128)(2,1)S(1)}, u32[]{:S(2)}, u32[]{:S(2)}) collective-permute-start(bf16[528,512]{1,0:T(8,128)(2,1)} %get-tuple-element.47), channel_id=1, source_target_pairs={{0,2},{1,3},{2,0},{3,1},{4,6},{5,7},{6,4},{7,5},{8,10},{9,11},{10,... | collective-permute-start | bytes 1622024 | tf_op jit(solution)/shard_map/ppermute | solution.py:470
  55.0 18.4 %copy-start.2 = (bf16[528,512]{1,0:T(8,128)(2,1)}, bf16[528,512]{1,0:T(8,128)(2,1)S(1)}, u32[]{:S(2)}) copy-start(bf16[528,512]{1,0:T(8,128)(2,1)S(1)} %collective-permute-done.8.refs_3_.refs_11_) | copy-start | bytes 1622020
  55.0 18.4 %collective-permute-start.10 = (bf16[528,512]{1,0:T(8,128)(2,1)}, bf16[528,512]{1,0:T(8,128)(2,1)S(1)}, u32[]{:S(2)}, u32[]{:S(2)}) collective-permute-start(bf16[528,512]{1,0:T(8,128)(2,1)} %get-tuple-element.51), channel_id=1, source_target_pairs={{0,8},{1,9},{2,10},{3,11},{4,12},{5,13},{6,14},{7,15},{8,0},{9,1},... | collective-permute-start | bytes 1622024 | tf_op jit(solution)/shard_map/ppermute | solution.py:470
  66.3 7.1 %copy-start.11 = (bf16[528,512]{1,0:T(8,128)(2,1)}, bf16[528,512]{1,0:T(8,128)(2,1)S(1)}, u32[]{:S(2)}) copy-start(bf16[528,512]{1,0:T(8,128)(2,1)S(1)} %collective-permute-done.11.refs_7_) | copy-start | bytes 1622020
  73.3 0.8 copy-start.3
  73.3 0.9 copy-start.12
  73.4 1.1 copy-start.4
  73.4 1.3 copy-start.13
  83.7 17.0 %all-to-all-start = ((f32[16,16,256]{2,1,0:T(8,128)}), f32[16,16,256]{2,1,0:T(8,128)S(1)}, u32[]{:S(2)}, u32[]{:S(2)}) async-start(f32[16,16,256]{2,1,0:T(8,128)} %get-tuple-element.53), calls=%async_computation | async-start | bytes 524288 | tf_op jit(solution)/shard_map/all_to_all | solution.py:507
  87.9 62.9 %reduce-scatter.2.cloned.1.call-start = ((), (), s32[]{:S(2)}) async-start(), calls=%async_computation.3 | async-start | bytes 4718592 | tf_op jit(solution)/shard_map/reduce_scatter | solution.py:514
  87.9 25.4 %collective-permute-start.12 = (bf16[544,512]{1,0:T(8,128)(2,1)}, bf16[544,512]{1,0:T(8,128)(2,1)S(1)}, u32[]{:S(2)}, u32[]{:S(2)}) collective-permute-start(bf16[544,512]{1,0:T(8,128)(2,1)} %get-tuple-element.58), channel_id=1, source_target_pairs={{0,3},{1,0},{2,1},{3,2},{4,7},{5,4},{6,5},{7,6},{8,11},{9,8},{10,9... | collective-permute-start | bytes 1671176 | tf_op jit(solution)/shard_map/ppermute | solution.py:470
  91.1 23.1 %collective-permute-start.13 = (bf16[544,512]{1,0:T(8,128)(2,1)}, bf16[544,512]{1,0:T(8,128)(2,1)S(1)}, u32[]{:S(2)}, u32[]{:S(2)}) collective-permute-start(bf16[544,512]{1,0:T(8,128)(2,1)} %get-tuple-element.59), channel_id=1, source_target_pairs={{0,2},{1,3},{2,0},{3,1},{4,6},{5,7},{6,4},{7,5},{8,10},{9,11},{10,... | collective-permute-start | bytes 1671176 | tf_op jit(solution)/shard_map/ppermute | solution.py:470
  92.0 24.5 %collective-permute-start.14 = (bf16[544,512]{1,0:T(8,128)(2,1)}, bf16[544,512]{1,0:T(8,128)(2,1)S(1)}, u32[]{:S(2)}, u32[]{:S(2)}) collective-permute-start(bf16[544,512]{1,0:T(8,128)(2,1)} %get-tuple-element.60), channel_id=1, source_target_pairs={{0,1},{1,2},{2,3},{3,0},{4,5},{5,6},{6,7},{7,4},{8,9},{9,10},{10,1... | collective-permute-start | bytes 1671176 | tf_op jit(solution)/shard_map/ppermute | solution.py:470
  92.8 32.2 %collective-permute-start.18 = (bf16[544,512]{1,0:T(8,128)(2,1)}, bf16[544,512]{1,0:T(8,128)(2,1)}, u32[]{:S(2)}, u32[]{:S(2)}) collective-permute-start(bf16[544,512]{1,0:T(8,128)(2,1)} %get-tuple-element.73), channel_id=1, source_target_pairs={{0,12},{1,13},{2,14},{3,15},{4,0},{5,1},{6,2},{7,3},{8,4},{9,5},{1... | collective-permute-start | bytes 1671176 | tf_op jit(solution)/shard_map/ppermute | solution.py:470
  95.5 30.4 %collective-permute-start.19 = (bf16[544,512]{1,0:T(8,128)(2,1)}, bf16[544,512]{1,0:T(8,128)(2,1)}, u32[]{:S(2)}, u32[]{:S(2)}) collective-permute-start(bf16[544,512]{1,0:T(8,128)(2,1)} %get-tuple-element.74), channel_id=1, source_target_pairs={{0,8},{1,9},{2,10},{3,11},{4,12},{5,13},{6,14},{7,15},{8,0},{9,1},... | collective-permute-start | bytes 1671176 | tf_op jit(solution)/shard_map/ppermute | solution.py:470
  113.3 3.1 %copy-start.17 = (bf16[544,512]{1,0:T(8,128)(2,1)}, bf16[544,512]{1,0:T(8,128)(2,1)S(1)}, u32[]{:S(2)}) copy-start(bf16[544,512]{1,0:T(8,128)(2,1)S(1)} %collective-permute-done.12.refs_5_) | copy-start | bytes 1671172
  113.3 12.6 %collective-permute-start.20 = (bf16[544,512]{1,0:T(8,128)(2,1)}, bf16[544,512]{1,0:T(8,128)(2,1)}, u32[]{:S(2)}, u32[]{:S(2)}) collective-permute-start(bf16[544,512]{1,0:T(8,128)(2,1)} %get-tuple-element.75), channel_id=1, source_target_pairs={{0,4},{1,5},{2,6},{3,7},{4,8},{5,9},{6,10},{7,11},{8,12},{9,13},{1... | collective-permute-start | bytes 1671176 | tf_op jit(solution)/shard_map/ppermute | solution.py:470
  114.2 2.3 %copy-start.18 = (bf16[544,512]{1,0:T(8,128)(2,1)}, bf16[544,512]{1,0:T(8,128)(2,1)S(1)}, u32[]{:S(2)}) copy-start(bf16[544,512]{1,0:T(8,128)(2,1)S(1)} %collective-permute-done.13.refs_6_) | copy-start | bytes 1671172
  116.4 0.8 copy-start.19
  121.8 13.9 %collective-permute-start.15 = (bf16[256,512]{1,0:T(8,128)(2,1)}, bf16[256,512]{1,0:T(8,128)(2,1)}, u32[]{:S(2)}, u32[]{:S(2)}) collective-permute-start(bf16[256,512]{1,0:T(8,128)(2,1)} %get-tuple-element.65), channel_id=1, source_target_pairs={{0,12},{1,13},{2,14},{3,15},{4,0},{5,1},{6,2},{7,3},{8,4},{9,5},{1... | collective-permute-start | bytes 786440 | tf_op jit(solution)/shard_map/ppermute | solution.py:470
  124.1 20.0 %collective-permute-start.16 = (bf16[256,512]{1,0:T(8,128)(2,1)}, bf16[256,512]{1,0:T(8,128)(2,1)}, u32[]{:S(2)}, u32[]{:S(2)}) collective-permute-start(bf16[256,512]{1,0:T(8,128)(2,1)} %get-tuple-element.66), channel_id=1, source_target_pairs={{0,8},{1,9},{2,10},{3,11},{4,12},{5,13},{6,14},{7,15},{8,0},{9,1},... | collective-permute-start | bytes 786440 | tf_op jit(solution)/shard_map/ppermute | solution.py:470
  125.0 19.1 %collective-permute-start.17 = (bf16[256,512]{1,0:T(8,128)(2,1)}, bf16[256,512]{1,0:T(8,128)(2,1)}, u32[]{:S(2)}, u32[]{:S(2)}) collective-permute-start(bf16[256,512]{1,0:T(8,128)(2,1)} %get-tuple-element.67), channel_id=1, source_target_pairs={{0,4},{1,5},{2,6},{3,7},{4,8},{5,9},{6,10},{7,11},{8,12},{9,13},{1... | collective-permute-start | bytes 786440 | tf_op jit(solution)/shard_map/ppermute | solution.py:470
  130.5 13.7 %collective-permute-start.21 = (bf16[256,512]{1,0:T(8,128)(2,1)}, bf16[256,512]{1,0:T(8,128)(2,1)S(1)}, u32[]{:S(2)}, u32[]{:S(2)}) collective-permute-start(bf16[256,512]{1,0:T(8,128)(2,1)} %get-tuple-element.77), channel_id=1, source_target_pairs={{0,3},{1,0},{2,1},{3,2},{4,7},{5,4},{6,5},{7,6},{8,11},{9,8},{10,9... | collective-permute-start | bytes 786440 | tf_op jit(solution)/shard_map/ppermute | solution.py:470
  132.6 11.6 %collective-permute-start.22 = (bf16[256,512]{1,0:T(8,128)(2,1)}, bf16[256,512]{1,0:T(8,128)(2,1)S(1)}, u32[]{:S(2)}, u32[]{:S(2)}) collective-permute-start(bf16[256,512]{1,0:T(8,128)(2,1)} %get-tuple-element.78), channel_id=1, source_target_pairs={{0,2},{1,3},{2,0},{3,1},{4,6},{5,7},{6,4},{7,5},{8,10},{9,11},{10,... | collective-permute-start | bytes 786440 | tf_op jit(solution)/shard_map/ppermute | solution.py:470
  135.8 9.3 %collective-permute-start.23 = (bf16[256,512]{1,0:T(8,128)(2,1)}, bf16[256,512]{1,0:T(8,128)(2,1)S(1)}, u32[]{:S(2)}, u32[]{:S(2)}) collective-permute-start(bf16[256,512]{1,0:T(8,128)(2,1)} %get-tuple-element.79), channel_id=1, source_target_pairs={{0,1},{1,2},{2,3},{3,0},{4,5},{5,6},{6,7},{7,4},{8,9},{9,10},{10,1... | collective-permute-start | bytes 786440 | tf_op jit(solution)/shard_map/ppermute | solution.py:470
  144.2 0.9 copy-start.14
  144.2 0.9 copy-start.15
  145.1 0.7 copy-start.16
Sparse Core Ops, SparseCore 0:
  9.7 34.7 all-gather.1
  112.1 38.6 reduce-scatter.1

commit v8 on v7

--- a/solution.py
+++ b/solution.py
@@ -305,10 +305,9 @@
 
 def column_kernel(reps, cap, temper, place_ref, code_ref, hs_ref, lt_ref, *refs):
     first, second = refs[0:4], refs[4:8]
-    p_ref, q_ref, gp_ref, mark_ref, d_ref = refs[8:]
+    p_ref, q_ref, gp_ref, gq_ref, loss_ref, mark_ref, d_ref = refs[8:]
     step = pl.program_id(0)
     toks, width = q_ref.shape
-    half_width = width // 2
     slots = reps * cap
     groups = code_ref.shape[0] // 2
 
@@ -327,22 +326,35 @@
             rows.append(jnp.where(valid, jnp.exp(hs_ref[g : g + 1, :] - log_slot), 0.0))
         d_ref[...] = jnp.concatenate(rows, axis=0)
         mark_ref[...] = jnp.zeros(mark_ref.shape, F32)
+        loss_ref[...] = own_row(lt_ref, rep_of(place_ref[1], place_ref[2]))
 
     queries = q_ref[...]
+    passages = p_ref[...]
     lt_own = own_row(lt_ref, rep_of(place_ref[1], place_ref[2]))
+    scores = temper * mm(passages, queries, NT)
+    row = iota(scores.shape, 0) + CORES * toks * step - toks * place_ref[0]
+    eye = row == iota(scores.shape, 1)
+    d_scores = (jnp.exp(scores - lt_own) - jnp.where(eye, 1.0, 0.0)).astype(BF16)
+    loss_ref[...] -= jnp.sum(jnp.where(eye, scores, 0.0), axis=0, keepdims=True)
     for core in range(CORES):
         group = CORES * step + core
-        here = pl.ds(core * toks, toks)
+        here = slice(core * toks, (core + 1) * toks)
         ids = code_ref[pl.ds(group, 1), :]
         d_hard = d_ref[pl.ds(group, 1), :]
         hot = jnp.where(iota((toks, slots), 0) + 1 == ids, d_hard, 0.0).astype(BF16)
-        scores = temper * mm(p_ref[here, :], queries, NT)
-        eye = (iota((toks, toks), 0) == iota((toks, toks), 1)) & (group == place_ref[0])
-        d_scores = (jnp.exp(scores - lt_own) - jnp.where(eye, 1.0, 0.0)).astype(BF16)
-        both = jnp.concatenate([hot, d_scores], axis=1)
+        both = jnp.concatenate([hot, d_scores[here]], axis=1)
         one, two = asking_rows(first, second, core * SIDE * cap, cap)
         rows = jnp.concatenate([jnp.concatenate([one, two], axis=1), queries], axis=0)
         gp_ref[here, :] = (temper * mm(both, rows)).astype(BF16)
+    new = mm(d_scores, passages, TN)
+
+    @pl.when(step == 0)
+    def _():
+        gq_ref[...] = new
+
+    @pl.when(step > 0)
+    def _():
+        gq_ref[...] += new
 
 
 def column(place, codes, hard_scores, log_total, first, second, gathered, queries, temper, cap):
@@ -355,45 +367,11 @@
         gathered.shape[0] // (CORES * toks),
         [full(codes.shape), full(hard_scores.shape), full(log_total.shape)] + [slots] * 8
         + [block, full((toks, width))],
-        [block, full((8, 128))],
-        [jax.ShapeDtypeStruct(gathered.shape, BF16), jax.ShapeDtypeStruct((8, 128), F32)],
+        [block, full((toks, width)), full((1, toks)), full((8, 128))],
+        [jax.ShapeDtypeStruct(gathered.shape, BF16), jax.ShapeDtypeStruct((toks, width), F32),
+         jax.ShapeDtypeStruct((1, toks), F32), jax.ShapeDtypeStruct((8, 128), F32)],
         [pltpu.VMEM(hard_scores.shape, F32)], LIGHT,
     )(place, codes, hard_scores, log_total, *first, *second, gathered, queries)
-
-
-def inner_kernel(temper, place_ref, lt_ref, p_ref, q_ref, gq_ref, loss_ref):
-    step = pl.program_id(0)
-    toks, width = q_ref.shape
-    lt_own = own_row(lt_ref, rep_of(place_ref[1], place_ref[2]))
-    passages = p_ref[...]
-    scores = temper * mm(passages, q_ref[...], NT)
-    row = iota(scores.shape, 0) + passages.shape[0] * step - toks * place_ref[0]
-    eye = row == iota(scores.shape, 1)
-    d_scores = (jnp.exp(scores - lt_own) - jnp.where(eye, 1.0, 0.0)).astype(BF16)
-    new = mm(d_scores, passages, TN)
-    own = jnp.sum(jnp.where(eye, scores, 0.0), axis=0, keepdims=True)
-
-    @pl.when(step == 0)
-    def _():
-        gq_ref[...] = new
-        loss_ref[...] = lt_own - own
-
-    @pl.when(step > 0)
-    def _():
-        gq_ref[...] += new
-        loss_ref[...] -= own
-
-
-def inner(place, log_total, gathered, queries, temper):
-    toks, width = queries.shape
-    return call(
-        functools.partial(inner_kernel, temper), "inner", 2,
-        [full(log_total.shape), pl.BlockSpec((gathered.shape[0] // 2, width), lambda s, _: (s, 0)),
-         full((toks, width))],
-        [full((toks, width)), full((1, toks))],
-        [jax.ShapeDtypeStruct((toks, width), F32), jax.ShapeDtypeStruct((1, toks), F32)],
-        [], LIGHT,
-    )(place, log_total, gathered, queries)
 
 
 def reduce_kernel(half, cap, groups, place_ref, lt_ref, *refs):
@@ -453,12 +431,11 @@
 
 
 def final(place, within, first, second, temper):
-    rows, width = within.shape
-    wide = pl.BlockSpec((rows // 4, width), lambda s, _: (s, 0))
-    narrow = pl.BlockSpec((rows // 4, width // 2), lambda s, _: (s, 0))
+    shape = within.shape
     return call(
-        functools.partial(final_kernel, temper), "final", 4, [wide] + [narrow] * 8, wide,
-        jax.ShapeDtypeStruct((rows, width), BF16), [], LIGHT,
+        functools.partial(final_kernel, temper), "final", 1,
+        [full(shape)] + [full(first[0].shape)] * 8, full(shape),
+        jax.ShapeDtypeStruct(shape, BF16), [], LIGHT,
     )(place, within, *first, *second)
 
 
@@ -492,7 +469,7 @@
 
     first, second, ranks_first, ranks_second = ([None] * SIDE for _ in range(4))
     earlier = []
-    for shift in (3, 1, 2, 0):
+    for shift in (2, 1, 3, 0):
         one, two, ranks_first[shift], ranks_second[shift] = mid(
             place, shift, *sources, earlier, groups, reps, cap, negs
         )
@@ -508,13 +485,12 @@
     high = jnp.max(parts, axis=0)
     log_total = high + jnp.log(jnp.sum(jnp.exp(parts - high), axis=0))
 
-    partial_sum, mark = column(
+    partial_sum, grad_inner, losses, mark = column(
         place, codes, hard_scores, log_total, first, second, gathered, queries, temper, cap
     )
     grad_passages = lax.psum_scatter(partial_sum, "grp", scatter_dimension=0, tiled=True)
     back_first = [along(v, 1, -s) if s else v for s, v in enumerate(back_first)]
     back_second = [along(v, 0, -s) if s else v for s, v in enumerate(back_second)]
-    grad_inner, losses = inner(place, log_total, gathered, queries, temper)
 
     sums = []
     for half, ranks, rows in ((0, ranks_first, back_first), (1, ranks_second, back_second)):

time: 159 us -> 155 us (0.975)
  Pallas kernels: 64.4 us -> 56.7 us
  waiting for transfers between devices: 34 us -> 36.1 us
    pallas_call x2 -> x1, Pallas kernels: 12.9 us -> 3.76 us  [final(): call(functools.partial(final_kernel, temper), 'final', 1, [full(shape)] +...]
    ppermute x24, waiting for transfers between devices: 28.4 us -> 35.2 us  [along(): return lax.ppermute(x, 'rep', pairs)]
    all_to_all x1, waiting for transfers between devices: 4.36 us -> 0.15 us  [shards(): parts = lax.all_to_all(part, 'rep', split_axis=0, concat_axis=0, tiled=True)]
  transfers between devices with their start and end apart: 27 -> 27, of which waited for: 11 -> 11; matrix products, arithmetic and copies ran while one was open for 2% -> 2% of each run, Pallas kernels for 35% -> 31%
where the time goes in v8:
time: 155 us; the launch traced here: 154 us
  Pallas kernels  56.7 us (37%)
  starting transfers between devices  39.6 us (26%)
  waiting for transfers between devices  36.1 us (23%)
  between operations  14.3 us (9%)
  local copies, waits for them, and re-layouts  4.78 us (3%)
  other arithmetic  2.11 us (1%)
    ppermute x24, waiting for transfers between devices, along(): return lax.ppermute(x, 'rep', pairs)  35.2 us
    ppermute x24, starting transfers between devices, along(): return lax.ppermute(x, 'rep', pairs)  34.1 us
    pallas_call x4, Pallas kernels, mid(): call(functools.partial(mid_kernel, shift, cap, groups, reps, negs), 'mid'...  17.8 us
    pallas_call x1, Pallas kernels, column(): call(functools.partial(column_kernel, reps, cap, temper), 'column', gathe...  12 us
    pallas_call x2, Pallas kernels, reduce(): call(functools.partial(reduce_kernel, half, cap, groups), 'reduce', 1, [f...  9.18 us
    pallas_call x1, Pallas kernels, hard(): call(functools.partial(hard_kernel, reps, cap, temper), 'hard', levels +...  9.03 us
    all_to_all x1, starting transfers between devices, shards(): parts = lax.all_to_all(part, 'rep', split_axis=0, concat_axis=0, tiled=True)  5.39 us
    pallas_call x1, Pallas kernels, inside(): call(functools.partial(inside_kernel, temper), 'inside', 2, [pl.BlockSpec...  4.95 us
  transfers between devices with their start and end apart: 27, of which 11 were waited for; matrix products, arithmetic and copies ran while one was open for 2% of the time, Pallas kernels for 31%

profile of v8, /device:TPU:0, one launch (start us, length us, event | category | flops | bytes accessed | tf_op | source)
XLA Modules:
  0.0 153.5 jit_solution(16281771696053460947)
XLA Ops:
  7.2 0.7 all-gather.2.cloned.1.call-update
  7.9 0.7 convert_bitcast_fusion
  8.6 1.1 fusion.7
  9.8 3.2 %collective-permute-start.5 = (bf16[272,512]{1,0:T(8,128)(2,1)S(1)}, bf16[272,512]{1,0:T(8,128)(2,1)S(1)}, u32[]{:S(2)}, u32[]{:S(2)}) collective-permute-start(bf16[272,512]{1,0:T(8,128)(2,1)S(1)} %get-tuple-element.83.refs_4_), channel_id=1, source_target_pairs={{0,3},{1,0},{2,1},{3,2},{4,7},{5,4},{6,5},{7,6},{8,11},{9,8},{10,9... | collective-permute-start | bytes 835592 | tf_op jit(solution)/shard_map/ppermute | solution.py:447
  12.9 0.6 collective-permute-start.4
  13.6 1.0 collective-permute-start.3
  14.5 2.8 %collective-permute-start.2 = (bf16[272,512]{1,0:T(8,128)(2,1)S(1)}, bf16[272,512]{1,0:T(8,128)(2,1)S(1)}, u32[]{:S(2)}, u32[]{:S(2)}) collective-permute-start(bf16[272,512]{1,0:T(8,128)(2,1)S(1)} %get-tuple-element.84.refs_0_), channel_id=1, source_target_pairs={{0,12},{1,13},{2,14},{3,15},{4,0},{5,1},{6,2},{7,3},{8,4},{9,5},{1... | collective-permute-start | bytes 835592 | tf_op jit(solution)/shard_map/ppermute | solution.py:447
  17.3 0.8 collective-permute-start.1
  18.1 6.7 %collective-permute-done.5.refs_7_ = bf16[272,512]{1,0:T(8,128)(2,1)S(1)} collective-permute-done((bf16[272,512]{1,0:T(8,128)(2,1)S(1)}, bf16[272,512]{1,0:T(8,128)(2,1)S(1)}, u32[]{:S(2)}, u32[]{:S(2)}) %collective-permute-start.5) | collective-permute-done | bytes 278560 | tf_op jit(solution)/shard_map/ppermute | solution.py:447
  24.8 1.5 collective-permute-start
  26.3 0.7 pad_add_fusion.place_ref
  27.0 1.5 %collective-permute-done.3.refs_5_ = bf16[272,512]{1,0:T(8,128)(2,1)S(1)} collective-permute-done((bf16[272,512]{1,0:T(8,128)(2,1)S(1)}, bf16[272,512]{1,0:T(8,128)(2,1)S(1)}, u32[]{:S(2)}, u32[]{:S(2)}) %collective-permute-start.3) | collective-permute-done | bytes 278560 | tf_op jit(solution)/shard_map/ppermute | solution.py:447
  28.5 5.3 %collective-permute-done.refs_1_ = bf16[272,512]{1,0:T(8,128)(2,1)S(1)} collective-permute-done((bf16[272,512]{1,0:T(8,128)(2,1)S(1)}, bf16[272,512]{1,0:T(8,128)(2,1)S(1)}, u32[]{:S(2)}, u32[]{:S(2)}) %collective-permute-start) | collective-permute-done | bytes 278560 | tf_op jit(solution)/shard_map/ppermute | solution.py:447
  34.0 0.7 copy-done.10
  34.7 4.5 %mid.4 = (bf16[528,512]{1,0:T(8,128)(2,1)}, bf16[528,512]{1,0:T(8,128)(2,1)}, bf16[32,256]{1,0:T(8,128)(2,1)}, bf16[32,256]{1,0:T(8,128)(2,1)}) custom-call(s32[3]{0:T(128)} %pad_add_fusion.place_ref, bf16[272,512]{1,0:T(8,128)(2,1)} %copy-done.1, bf16[272,512]{1,0:T(8,128)(2,1)} %copy-done.10, bf16[272,512]{1,0:T(8,128)(2,1)} %copy-done.9, ...), custom_call_target="tpu_custom_call" | custom-call | flops 1048576 | bytes 65536 | tf_op jit(solution)/shard_map/mid/pallas_call | solution.py:128
  39.5 0.8 collective-permute-start.10
  40.3 4.4 %mid.5 = (bf16[528,512]{1,0:T(8,128)(2,1)}, bf16[528,512]{1,0:T(8,128)(2,1)}, bf16[32,256]{1,0:T(8,128)(2,1)}, bf16[32,256]{1,0:T(8,128)(2,1)}) custom-call(s32[3]{0:T(128)} %pad_add_fusion.place_ref, bf16[272,512]{1,0:T(8,128)(2,1)} %copy-done.1, bf16[272,512]{1,0:T(8,128)(2,1)} %copy-done.10, bf16[272,512]{1,0:T(8,128)(2,1)} %copy-done.9, ...), custom_call_target="tpu_custom_call" | custom-call | flops 1048576 | bytes 65536 | tf_op jit(solution)/shard_map/mid/pallas_call | solution.py:128
  44.7 4.9 %collective-permute-start.6 = (bf16[528,512]{1,0:T(8,128)(2,1)}, bf16[528,512]{1,0:T(8,128)(2,1)S(1)}, u32[]{:S(2)}, u32[]{:S(2)}) collective-permute-start(bf16[528,512]{1,0:T(8,128)(2,1)} %get-tuple-element.46), channel_id=1, source_target_pairs={{0,1},{1,2},{2,3},{3,0},{4,5},{5,6},{6,7},{7,4},{8,9},{9,10},{10,1... | collective-permute-start | bytes 1622024 | tf_op jit(solution)/shard_map/ppermute | solution.py:447
  50.2 4.4 %mid.6 = (bf16[528,512]{1,0:T(8,128)(2,1)}, bf16[528,512]{1,0:T(8,128)(2,1)}, bf16[32,256]{1,0:T(8,128)(2,1)}, bf16[32,256]{1,0:T(8,128)(2,1)}) custom-call(s32[3]{0:T(128)} %pad_add_fusion.place_ref, bf16[272,512]{1,0:T(8,128)(2,1)} %copy-done.1, bf16[272,512]{1,0:T(8,128)(2,1)} %copy-done.10, bf16[272,512]{1,0:T(8,128)(2,1)} %copy-done.9, ...), custom_call_target="tpu_custom_call" | custom-call | flops 1048576 | bytes 65536 | tf_op jit(solution)/shard_map/mid/pallas_call | solution.py:128
  54.6 1.4 collective-permute-done.7.refs_2_.refs_10_
  56.1 1.3 collective-permute-start.11
  57.4 4.5 %mid.7 = (bf16[528,512]{1,0:T(8,128)(2,1)}, bf16[528,512]{1,0:T(8,128)(2,1)}, bf16[32,256]{1,0:T(8,128)(2,1)}, bf16[32,256]{1,0:T(8,128)(2,1)}) custom-call(s32[3]{0:T(128)} %pad_add_fusion.place_ref, bf16[272,512]{1,0:T(8,128)(2,1)} %copy-done.1, bf16[272,512]{1,0:T(8,128)(2,1)} %copy-done.10, bf16[272,512]{1,0:T(8,128)(2,1)} %copy-done.9, ...), custom_call_target="tpu_custom_call" | custom-call | flops 1048576 | bytes 65536 | tf_op jit(solution)/shard_map/mid/pallas_call | solution.py:128
  61.8 5.0 %inside.1.refs_13_ = f32[1,256]{1,0:T(1,128)} custom-call(s32[3]{0:T(128)} %pad_add_fusion.place_ref, bf16[2048,1024]{1,0:T(8,128)(2,1)} %all-gather.2.cloned.1.call-done.p_ref.refs_12_.refs_8_, bf16[256,1024]{1,0:T(8,128)(2,1)} %refs_9_.1), custom_call_target="tpu_custom_call" | custom-call | flops 1048576 | bytes 65536 | tf_op jit(solution)/shard_map/inside/pallas_call | solution.py:158
  66.9 0.7 copy-done.11
  68.3 9.0 %hard.1 = (bf16[544,512]{1,0:T(8,128)(2,1)}, bf16[544,512]{1,0:T(8,128)(2,1)}, bf16[544,512]{1,0:T(8,128)(2,1)}, bf16[544,512]{1,0:T(8,128)(2,1)}, bf16[544,512]...) custom-call(s32[3]{0:T(128)} %pad_add_fusion.place_ref, ...), custom_call_target="tpu_custom_call" | custom-call | flops 1048576 | bytes 65536 | tf_op jit(solution)/shard_map/hard/pallas_call | solution.py:286
  77.3 5.4 %all-to-all-start = ((f32[16,16,256]{2,1,0:T(8,128)}), f32[16,16,256]{2,1,0:T(8,128)S(1)}, u32[]{:S(2)}, u32[]{:S(2)}) async-start(f32[16,16,256]{2,1,0:T(8,128)} %get-tuple-element.55), calls=%async_computation | async-start | bytes 524288 | tf_op jit(solution)/shard_map/all_to_all | solution.py:484
  82.8 3.2 %collective-permute-start.12 = (bf16[544,512]{1,0:T(8,128)(2,1)}, bf16[544,512]{1,0:T(8,128)(2,1)S(1)}, u32[]{:S(2)}, u32[]{:S(2)}) collective-permute-start(bf16[544,512]{1,0:T(8,128)(2,1)} %get-tuple-element.60), channel_id=1, source_target_pairs={{0,3},{1,0},{2,1},{3,2},{4,7},{5,4},{6,5},{7,6},{8,11},{9,8},{10,9... | collective-permute-start | bytes 1671176 | tf_op jit(solution)/shard_map/ppermute | solution.py:447
  86.0 0.9 collective-permute-start.13
  86.8 0.9 collective-permute-start.14
  87.7 2.7 %collective-permute-start.18 = (bf16[544,512]{1,0:T(8,128)(2,1)}, bf16[544,512]{1,0:T(8,128)(2,1)}, u32[]{:S(2)}, u32[]{:S(2)}) collective-permute-start(bf16[544,512]{1,0:T(8,128)(2,1)} %get-tuple-element.73), channel_id=1, source_target_pairs={{0,12},{1,13},{2,14},{3,15},{4,0},{5,1},{6,2},{7,3},{8,4},{9,5},{1... | collective-permute-start | bytes 1671176 | tf_op jit(solution)/shard_map/ppermute | solution.py:447
  90.4 0.9 collective-permute-start.19
  92.1 12.0 %column.1 = (bf16[2048,1024]{1,0:T(8,128)(2,1)}, f32[256,1024]{1,0:T(8,128)}, f32[1,256]{1,0:T(1,128)}, f32[8,128]{1,0:T(8,128)}) custom-call(s32[3]{0:T(128)} %pad_add_fusion.place_ref, s32[16,256]{1,0:T(8,128)} %get-tuple-element.53.code_ref, f32[8,256]{1,0:T(8,128)} %get-tuple-element.54.hs_ref, f32[16,256]{1,0:T(8,128)} %log_add_fusion.lt_ref, ...), custom_call_target="tpu_custom_call" | custom-call | flops 1048576 | bytes 65536 | tf_op jit(solution)/shard_map/column/pallas_call | solution.py:365
  104.2 6.5 %collective-permute-done.12.refs_5_ = bf16[544,512]{1,0:T(8,128)(2,1)S(1)} collective-permute-done((bf16[544,512]{1,0:T(8,128)(2,1)}, bf16[544,512]{1,0:T(8,128)(2,1)S(1)}, u32[]{:S(2)}, u32[]{:S(2)}) %collective-permute-start.12) | collective-permute-done | bytes 557088 | tf_op jit(solution)/shard_map/ppermute | solution.py:447
  110.6 1.1 collective-permute-start.20
  111.7 2.0 %collective-permute-done.14.refs_7_ = bf16[544,512]{1,0:T(8,128)(2,1)S(1)} collective-permute-done((bf16[544,512]{1,0:T(8,128)(2,1)}, bf16[544,512]{1,0:T(8,128)(2,1)S(1)}, u32[]{:S(2)}, u32[]{:S(2)}) %collective-permute-start.14) | collective-permute-done | bytes 557088 | tf_op jit(solution)/shard_map/ppermute | solution.py:447
  113.7 0.8 copy-done.19
  114.5 4.6 %reduce.2 = (f32[256,512]{1,0:T(8,128)}, bf16[256,512]{1,0:T(8,128)(2,1)}, bf16[256,512]{1,0:T(8,128)(2,1)}, bf16[256,512]{1,0:T(8,128)(2,1)}) custom-call(s32[3]{0:T(128)} %pad_add_fusion.place_ref, f32[16,256]{1,0:T(8,128)} %log_add_fusion.lt_ref, bf16[32,256]{1,0:T(8,128)(2,1)} %get-tuple-element.58.refs_0_, ...), custom_call_target="tpu_custom_call" | custom-call | flops 549755813888 | bytes 65536 | tf_op jit(solution)/shard_map/reduce/pallas_call | solution.py:413
  119.1 2.0 %collective-permute-start.15 = (bf16[256,512]{1,0:T(8,128)(2,1)}, bf16[256,512]{1,0:T(8,128)(2,1)}, u32[]{:S(2)}, u32[]{:S(2)}) collective-permute-start(bf16[256,512]{1,0:T(8,128)(2,1)} %get-tuple-element.65), channel_id=1, source_target_pairs={{0,12},{1,13},{2,14},{3,15},{4,0},{5,1},{6,2},{7,3},{8,4},{9,5},{1... | collective-permute-start | bytes 786440 | tf_op jit(solution)/shard_map/ppermute | solution.py:447
  121.1 1.0 collective-permute-start.16
  122.1 0.7 collective-permute-start.17
  122.9 4.6 %reduce.3 = (f32[256,512]{1,0:T(8,128)}, bf16[256,512]{1,0:T(8,128)(2,1)}, bf16[256,512]{1,0:T(8,128)(2,1)}, bf16[256,512]{1,0:T(8,128)(2,1)}) custom-call(s32[3]{0:T(128)} %pad_add_fusion.place_ref, f32[16,256]{1,0:T(8,128)} %log_add_fusion.lt_ref, bf16[32,256]{1,0:T(8,128)(2,1)} %get-tuple-element.68.refs_0_, bf16[32,256]{1,0:T(8,128)(2,1)} %get-tuple-element.69.refs_1_, ...), custom_call_target="tpu_custom_call" | custom-call | flops 549755813888 | bytes 65536 | tf_op jit(solution)/shard_map/reduce/pallas_call | solution.py:413
  127.5 3.1 %collective-permute-start.21 = (bf16[256,512]{1,0:T(8,128)(2,1)}, bf16[256,512]{1,0:T(8,128)(2,1)S(1)}, u32[]{:S(2)}, u32[]{:S(2)}) collective-permute-start(bf16[256,512]{1,0:T(8,128)(2,1)} %get-tuple-element.77), channel_id=1, source_target_pairs={{0,3},{1,0},{2,1},{3,2},{4,7},{5,4},{6,5},{7,6},{8,11},{9,8},{10,9... | collective-permute-start | bytes 786440 | tf_op jit(solution)/shard_map/ppermute | solution.py:447
  130.5 2.3 %collective-permute-done.15.refs_1_ = bf16[256,512]{1,0:T(8,128)(2,1)} collective-permute-done((bf16[256,512]{1,0:T(8,128)(2,1)}, bf16[256,512]{1,0:T(8,128)(2,1)}, u32[]{:S(2)}, u32[]{:S(2)}) %collective-permute-start.15) | collective-permute-done | bytes 262176 | tf_op jit(solution)/shard_map/ppermute | solution.py:447
  132.9 3.7 %collective-permute-done.17.refs_3_ = bf16[256,512]{1,0:T(8,128)(2,1)} collective-permute-done((bf16[256,512]{1,0:T(8,128)(2,1)}, bf16[256,512]{1,0:T(8,128)(2,1)}, u32[]{:S(2)}, u32[]{:S(2)}) %collective-permute-start.17) | collective-permute-done | bytes 262176 | tf_op jit(solution)/shard_map/ppermute | solution.py:447
  136.5 3.9 %collective-permute-done.21.refs_5_ = bf16[256,512]{1,0:T(8,128)(2,1)S(1)} collective-permute-done((bf16[256,512]{1,0:T(8,128)(2,1)}, bf16[256,512]{1,0:T(8,128)(2,1)S(1)}, u32[]{:S(2)}, u32[]{:S(2)}) %collective-permute-start.21) | collective-permute-done | bytes 262176 | tf_op jit(solution)/shard_map/ppermute | solution.py:447
  140.4 1.8 %collective-permute-done.23.refs_7_ = bf16[256,512]{1,0:T(8,128)(2,1)S(1)} collective-permute-done((bf16[256,512]{1,0:T(8,128)(2,1)}, bf16[256,512]{1,0:T(8,128)(2,1)S(1)}, u32[]{:S(2)}, u32[]{:S(2)}) %collective-permute-start.23) | collective-permute-done | bytes 262176 | tf_op jit(solution)/shard_map/ppermute | solution.py:447
  142.2 0.7 copy-done.16
  142.9 3.8 %final.1 = bf16[256,1024]{1,0:T(8,128)(2,1)} custom-call(s32[3]{0:T(128)} %pad_add_fusion.place_ref, f32[256,1024]{1,0:T(8,128)} %get-tuple-element.57.gq_ref, f32[256,512]{1,0:T(8,128)} %get-tuple-element.64.refs_0_, bf16[256,512]{1,0:T(8,128)(2,1)} %collective-permute-done.15.refs_1_, bf16[256,512]{1,0:T(8,128)(2,1)} %collective-permute-done.16.refs_2_, ...), custom_call_target="tpu_custom_call" | custom-call | flops 1048576 | bytes 65536 | tf_op jit(solution)/shard_map/final/pallas_call | solution.py:435
  (66 shorter events, 2.7 us)
Async XLA Ops:
  7.2 54.7 %all-gather.2.cloned.1.call-start = ((), (), s32[]{:S(2)}) async-start(), calls=%async_computation.2 | async-start | bytes 4718592 | tf_op jit(solution)/shard_map/all_gather | solution.py:468
  9.7 24.1 %copy-start = (bf16[272,512]{1,0:T(8,128)(2,1)}, bf16[272,512]{1,0:T(8,128)(2,1)S(1)}, u32[]{:S(2)}) copy-start(bf16[272,512]{1,0:T(8,128)(2,1)S(1)} %get-tuple-element.83.refs_4_) | copy-start | bytes 835588
  9.8 24.1 %copy-start.1 = (bf16[272,512]{1,0:T(8,128)(2,1)}, bf16[272,512]{1,0:T(8,128)(2,1)S(1)}, u32[]{:S(2)}) copy-start(bf16[272,512]{1,0:T(8,128)(2,1)S(1)} %get-tuple-element.84.refs_0_) | copy-start | bytes 835588
  9.8 15.1 %collective-permute-start.5 = (bf16[272,512]{1,0:T(8,128)(2,1)S(1)}, bf16[272,512]{1,0:T(8,128)(2,1)S(1)}, u32[]{:S(2)}, u32[]{:S(2)}) collective-permute-start(bf16[272,512]{1,0:T(8,128)(2,1)S(1)} %get-tuple-element.83.refs_4_), channel_id=1, source_target_pairs={{0,3},{1,0},{2,1},{3,2},{4,7},{5,4},{6,5},{7,6},{8,11},{9,8},{10,9... | collective-permute-start | bytes 835592 | tf_op jit(solution)/shard_map/ppermute | solution.py:447
  12.9 14.0 %collective-permute-start.4 = (bf16[272,512]{1,0:T(8,128)(2,1)S(1)}, bf16[272,512]{1,0:T(8,128)(2,1)S(1)}, u32[]{:S(2)}, u32[]{:S(2)}) collective-permute-start(bf16[272,512]{1,0:T(8,128)(2,1)S(1)} %get-tuple-element.83.refs_4_), channel_id=1, source_target_pairs={{0,2},{1,3},{2,0},{3,1},{4,6},{5,7},{6,4},{7,5},{8,10},{9,11},{10,... | collective-permute-start | bytes 835592 | tf_op jit(solution)/shard_map/ppermute | solution.py:447
  13.6 15.0 %collective-permute-start.3 = (bf16[272,512]{1,0:T(8,128)(2,1)S(1)}, bf16[272,512]{1,0:T(8,128)(2,1)S(1)}, u32[]{:S(2)}, u32[]{:S(2)}) collective-permute-start(bf16[272,512]{1,0:T(8,128)(2,1)S(1)} %get-tuple-element.83.refs_4_), channel_id=1, source_target_pairs={{0,1},{1,2},{2,3},{3,0},{4,5},{5,6},{6,7},{7,4},{8,9},{9,10},{10,1... | collective-permute-start | bytes 835592 | tf_op jit(solution)/shard_map/ppermute | solution.py:447
  14.5 14.0 %collective-permute-start.2 = (bf16[272,512]{1,0:T(8,128)(2,1)S(1)}, bf16[272,512]{1,0:T(8,128)(2,1)S(1)}, u32[]{:S(2)}, u32[]{:S(2)}) collective-permute-start(bf16[272,512]{1,0:T(8,128)(2,1)S(1)} %get-tuple-element.84.refs_0_), channel_id=1, source_target_pairs={{0,12},{1,13},{2,14},{3,15},{4,0},{5,1},{6,2},{7,3},{8,4},{9,5},{1... | collective-permute-start | bytes 835592 | tf_op jit(solution)/shard_map/ppermute | solution.py:447
  17.3 11.2 %collective-permute-start.1 = (bf16[272,512]{1,0:T(8,128)(2,1)S(1)}, bf16[272,512]{1,0:T(8,128)(2,1)S(1)}, u32[]{:S(2)}, u32[]{:S(2)}) collective-permute-start(bf16[272,512]{1,0:T(8,128)(2,1)S(1)} %get-tuple-element.84.refs_0_), channel_id=1, source_target_pairs={{0,8},{1,9},{2,10},{3,11},{4,12},{5,13},{6,14},{7,15},{8,0},{9,1},... | collective-permute-start | bytes 835592 | tf_op jit(solution)/shard_map/ppermute | solution.py:447
  24.8 9.1 %copy-start.5 = (bf16[272,512]{1,0:T(8,128)(2,1)}, bf16[272,512]{1,0:T(8,128)(2,1)S(1)}, u32[]{:S(2)}) copy-start(bf16[272,512]{1,0:T(8,128)(2,1)S(1)} %collective-permute-done.5.refs_7_) | copy-start | bytes 835588
  24.8 9.1 %collective-permute-start = (bf16[272,512]{1,0:T(8,128)(2,1)S(1)}, bf16[272,512]{1,0:T(8,128)(2,1)S(1)}, u32[]{:S(2)}, u32[]{:S(2)}) collective-permute-start(bf16[272,512]{1,0:T(8,128)(2,1)S(1)} %get-tuple-element.84.refs_0_), channel_id=1, source_target_pairs={{0,4},{1,5},{2,6},{3,7},{4,8},{5,9},{6,10},{7,11},{8,12},{9,13},{1... | collective-permute-start | bytes 835592 | tf_op jit(solution)/shard_map/ppermute | solution.py:447
  27.0 6.9 %copy-start.6 = (bf16[272,512]{1,0:T(8,128)(2,1)}, bf16[272,512]{1,0:T(8,128)(2,1)S(1)}, u32[]{:S(2)}) copy-start(bf16[272,512]{1,0:T(8,128)(2,1)S(1)} %collective-permute-done.4.refs_6_) | copy-start | bytes 835588
  28.5 5.4 %copy-start.7 = (bf16[272,512]{1,0:T(8,128)(2,1)}, bf16[272,512]{1,0:T(8,128)(2,1)S(1)}, u32[]{:S(2)}) copy-start(bf16[272,512]{1,0:T(8,128)(2,1)S(1)} %collective-permute-done.3.refs_5_) | copy-start | bytes 835588
  28.5 5.4 %copy-start.8 = (bf16[272,512]{1,0:T(8,128)(2,1)}, bf16[272,512]{1,0:T(8,128)(2,1)S(1)}, u32[]{:S(2)}) copy-start(bf16[272,512]{1,0:T(8,128)(2,1)S(1)} %collective-permute-done.2.refs_3_) | copy-start | bytes 835588
  28.5 5.4 %copy-start.9 = (bf16[272,512]{1,0:T(8,128)(2,1)}, bf16[272,512]{1,0:T(8,128)(2,1)S(1)}, u32[]{:S(2)}) copy-start(bf16[272,512]{1,0:T(8,128)(2,1)S(1)} %collective-permute-done.1.refs_2_) | copy-start | bytes 835588
  33.9 0.7 copy-start.10
  39.1 17.0 %collective-permute-start.7 = (bf16[528,512]{1,0:T(8,128)(2,1)}, bf16[528,512]{1,0:T(8,128)(2,1)S(1)}, u32[]{:S(2)}, u32[]{:S(2)}) collective-permute-start(bf16[528,512]{1,0:T(8,128)(2,1)} %get-tuple-element.47), channel_id=1, source_target_pairs={{0,2},{1,3},{2,0},{3,1},{4,6},{5,7},{6,4},{7,5},{8,10},{9,11},{10,... | collective-permute-start | bytes 1622024 | tf_op jit(solution)/shard_map/ppermute | solution.py:447
  39.5 27.3 %collective-permute-start.10 = (bf16[528,512]{1,0:T(8,128)(2,1)}, bf16[528,512]{1,0:T(8,128)(2,1)S(1)}, u32[]{:S(2)}, u32[]{:S(2)}) collective-permute-start(bf16[528,512]{1,0:T(8,128)(2,1)} %get-tuple-element.51), channel_id=1, source_target_pairs={{0,8},{1,9},{2,10},{3,11},{4,12},{5,13},{6,14},{7,15},{8,0},{9,1},... | collective-permute-start | bytes 1622024 | tf_op jit(solution)/shard_map/ppermute | solution.py:447
  44.7 22.0 %collective-permute-start.6 = (bf16[528,512]{1,0:T(8,128)(2,1)}, bf16[528,512]{1,0:T(8,128)(2,1)S(1)}, u32[]{:S(2)}, u32[]{:S(2)}) collective-permute-start(bf16[528,512]{1,0:T(8,128)(2,1)} %get-tuple-element.46), channel_id=1, source_target_pairs={{0,1},{1,2},{2,3},{3,0},{4,5},{5,6},{6,7},{7,4},{8,9},{9,10},{10,1... | collective-permute-start | bytes 1622024 | tf_op jit(solution)/shard_map/ppermute | solution.py:447
  49.6 17.2 %collective-permute-start.9 = (bf16[528,512]{1,0:T(8,128)(2,1)}, bf16[528,512]{1,0:T(8,128)(2,1)S(1)}, u32[]{:S(2)}, u32[]{:S(2)}) collective-permute-start(bf16[528,512]{1,0:T(8,128)(2,1)} %get-tuple-element.50), channel_id=1, source_target_pairs={{0,4},{1,5},{2,6},{3,7},{4,8},{5,9},{6,10},{7,11},{8,12},{9,13},{1... | collective-permute-start | bytes 1622024 | tf_op jit(solution)/shard_map/ppermute | solution.py:447
  54.6 12.2 %collective-permute-start.8 = (bf16[528,512]{1,0:T(8,128)(2,1)}, bf16[528,512]{1,0:T(8,128)(2,1)S(1)}, u32[]{:S(2)}, u32[]{:S(2)}) collective-permute-start(bf16[528,512]{1,0:T(8,128)(2,1)} %get-tuple-element.48), channel_id=1, source_target_pairs={{0,3},{1,0},{2,1},{3,2},{4,7},{5,4},{6,5},{7,6},{8,11},{9,8},{10,9... | collective-permute-start | bytes 1622024 | tf_op jit(solution)/shard_map/ppermute | solution.py:447
  56.1 10.8 %copy-start.2 = (bf16[528,512]{1,0:T(8,128)(2,1)}, bf16[528,512]{1,0:T(8,128)(2,1)S(1)}, u32[]{:S(2)}) copy-start(bf16[528,512]{1,0:T(8,128)(2,1)S(1)} %collective-permute-done.7.refs_2_.refs_10_) | copy-start | bytes 1622020
  56.1 10.8 %collective-permute-start.11 = (bf16[528,512]{1,0:T(8,128)(2,1)}, bf16[528,512]{1,0:T(8,128)(2,1)S(1)}, u32[]{:S(2)}, u32[]{:S(2)}) collective-permute-start(bf16[528,512]{1,0:T(8,128)(2,1)} %get-tuple-element.52), channel_id=1, source_target_pairs={{0,12},{1,13},{2,14},{3,15},{4,0},{5,1},{6,2},{7,3},{8,4},{9,5},{1... | collective-permute-start | bytes 1622024 | tf_op jit(solution)/shard_map/ppermute | solution.py:447
  66.8 0.8 copy-start.11
  66.8 1.0 copy-start.3
  66.8 1.2 copy-start.12
  66.8 1.3 copy-start.4
  66.9 1.4 copy-start.13
  77.3 14.0 %all-to-all-start = ((f32[16,16,256]{2,1,0:T(8,128)}), f32[16,16,256]{2,1,0:T(8,128)S(1)}, u32[]{:S(2)}, u32[]{:S(2)}) async-start(f32[16,16,256]{2,1,0:T(8,128)} %get-tuple-element.55), calls=%async_computation | async-start | bytes 524288 | tf_op jit(solution)/shard_map/all_to_all | solution.py:484
  82.7 63.9 %reduce-scatter.2.cloned.1.call-start = ((), (), s32[]{:S(2)}) async-start(), calls=%async_computation.3 | async-start | bytes 4718592 | tf_op jit(solution)/shard_map/reduce_scatter | solution.py:491
  82.8 27.8 %collective-permute-start.12 = (bf16[544,512]{1,0:T(8,128)(2,1)}, bf16[544,512]{1,0:T(8,128)(2,1)S(1)}, u32[]{:S(2)}, u32[]{:S(2)}) collective-permute-start(bf16[544,512]{1,0:T(8,128)(2,1)} %get-tuple-element.60), channel_id=1, source_target_pairs={{0,3},{1,0},{2,1},{3,2},{4,7},{5,4},{6,5},{7,6},{8,11},{9,8},{10,9... | collective-permute-start | bytes 1671176 | tf_op jit(solution)/shard_map/ppermute | solution.py:447
  86.0 25.7 %collective-permute-start.13 = (bf16[544,512]{1,0:T(8,128)(2,1)}, bf16[544,512]{1,0:T(8,128)(2,1)S(1)}, u32[]{:S(2)}, u32[]{:S(2)}) collective-permute-start(bf16[544,512]{1,0:T(8,128)(2,1)} %get-tuple-element.61), channel_id=1, source_target_pairs={{0,2},{1,3},{2,0},{3,1},{4,6},{5,7},{6,4},{7,5},{8,10},{9,11},{10,... | collective-permute-start | bytes 1671176 | tf_op jit(solution)/shard_map/ppermute | solution.py:447
  86.8 26.9 %collective-permute-start.14 = (bf16[544,512]{1,0:T(8,128)(2,1)}, bf16[544,512]{1,0:T(8,128)(2,1)S(1)}, u32[]{:S(2)}, u32[]{:S(2)}) collective-permute-start(bf16[544,512]{1,0:T(8,128)(2,1)} %get-tuple-element.62), channel_id=1, source_target_pairs={{0,1},{1,2},{2,3},{3,0},{4,5},{5,6},{6,7},{7,4},{8,9},{9,10},{10,1... | collective-permute-start | bytes 1671176 | tf_op jit(solution)/shard_map/ppermute | solution.py:447
  87.7 34.4 %collective-permute-start.18 = (bf16[544,512]{1,0:T(8,128)(2,1)}, bf16[544,512]{1,0:T(8,128)(2,1)}, u32[]{:S(2)}, u32[]{:S(2)}) collective-permute-start(bf16[544,512]{1,0:T(8,128)(2,1)} %get-tuple-element.73), channel_id=1, source_target_pairs={{0,12},{1,13},{2,14},{3,15},{4,0},{5,1},{6,2},{7,3},{8,4},{9,5},{1... | collective-permute-start | bytes 1671176 | tf_op jit(solution)/shard_map/ppermute | solution.py:447
  90.4 32.5 %collective-permute-start.19 = (bf16[544,512]{1,0:T(8,128)(2,1)}, bf16[544,512]{1,0:T(8,128)(2,1)}, u32[]{:S(2)}, u32[]{:S(2)}) collective-permute-start(bf16[544,512]{1,0:T(8,128)(2,1)} %get-tuple-element.74), channel_id=1, source_target_pairs={{0,8},{1,9},{2,10},{3,11},{4,12},{5,13},{6,14},{7,15},{8,0},{9,1},... | collective-permute-start | bytes 1671176 | tf_op jit(solution)/shard_map/ppermute | solution.py:447
  110.6 3.1 %copy-start.17 = (bf16[544,512]{1,0:T(8,128)(2,1)}, bf16[544,512]{1,0:T(8,128)(2,1)S(1)}, u32[]{:S(2)}) copy-start(bf16[544,512]{1,0:T(8,128)(2,1)S(1)} %collective-permute-done.12.refs_5_) | copy-start | bytes 1671172
  110.6 12.3 %collective-permute-start.20 = (bf16[544,512]{1,0:T(8,128)(2,1)}, bf16[544,512]{1,0:T(8,128)(2,1)}, u32[]{:S(2)}, u32[]{:S(2)}) collective-permute-start(bf16[544,512]{1,0:T(8,128)(2,1)} %get-tuple-element.75), channel_id=1, source_target_pairs={{0,4},{1,5},{2,6},{3,7},{4,8},{5,9},{6,10},{7,11},{8,12},{9,13},{1... | collective-permute-start | bytes 1671176 | tf_op jit(solution)/shard_map/ppermute | solution.py:447
  111.7 2.0 %copy-start.18 = (bf16[544,512]{1,0:T(8,128)(2,1)}, bf16[544,512]{1,0:T(8,128)(2,1)S(1)}, u32[]{:S(2)}) copy-start(bf16[544,512]{1,0:T(8,128)(2,1)S(1)} %collective-permute-done.13.refs_6_) | copy-start | bytes 1671172
  113.7 0.8 copy-start.19
  119.1 13.7 %collective-permute-start.15 = (bf16[256,512]{1,0:T(8,128)(2,1)}, bf16[256,512]{1,0:T(8,128)(2,1)}, u32[]{:S(2)}, u32[]{:S(2)}) collective-permute-start(bf16[256,512]{1,0:T(8,128)(2,1)} %get-tuple-element.65), channel_id=1, source_target_pairs={{0,12},{1,13},{2,14},{3,15},{4,0},{5,1},{6,2},{7,3},{8,4},{9,5},{1... | collective-permute-start | bytes 786440 | tf_op jit(solution)/shard_map/ppermute | solution.py:447
  121.1 11.7 %collective-permute-start.16 = (bf16[256,512]{1,0:T(8,128)(2,1)}, bf16[256,512]{1,0:T(8,128)(2,1)}, u32[]{:S(2)}, u32[]{:S(2)}) collective-permute-start(bf16[256,512]{1,0:T(8,128)(2,1)} %get-tuple-element.66), channel_id=1, source_target_pairs={{0,8},{1,9},{2,10},{3,11},{4,12},{5,13},{6,14},{7,15},{8,0},{9,1},... | collective-permute-start | bytes 786440 | tf_op jit(solution)/shard_map/ppermute | solution.py:447
  122.1 14.4 %collective-permute-start.17 = (bf16[256,512]{1,0:T(8,128)(2,1)}, bf16[256,512]{1,0:T(8,128)(2,1)}, u32[]{:S(2)}, u32[]{:S(2)}) collective-permute-start(bf16[256,512]{1,0:T(8,128)(2,1)} %get-tuple-element.67), channel_id=1, source_target_pairs={{0,4},{1,5},{2,6},{3,7},{4,8},{5,9},{6,10},{7,11},{8,12},{9,13},{1... | collective-permute-start | bytes 786440 | tf_op jit(solution)/shard_map/ppermute | solution.py:447
  127.5 12.9 %collective-permute-start.21 = (bf16[256,512]{1,0:T(8,128)(2,1)}, bf16[256,512]{1,0:T(8,128)(2,1)S(1)}, u32[]{:S(2)}, u32[]{:S(2)}) collective-permute-start(bf16[256,512]{1,0:T(8,128)(2,1)} %get-tuple-element.77), channel_id=1, source_target_pairs={{0,3},{1,0},{2,1},{3,2},{4,7},{5,4},{6,5},{7,6},{8,11},{9,8},{10,9... | collective-permute-start | bytes 786440 | tf_op jit(solution)/shard_map/ppermute | solution.py:447
  130.5 9.9 %collective-permute-start.22 = (bf16[256,512]{1,0:T(8,128)(2,1)}, bf16[256,512]{1,0:T(8,128)(2,1)S(1)}, u32[]{:S(2)}, u32[]{:S(2)}) collective-permute-start(bf16[256,512]{1,0:T(8,128)(2,1)} %get-tuple-element.78), channel_id=1, source_target_pairs={{0,2},{1,3},{2,0},{3,1},{4,6},{5,7},{6,4},{7,5},{8,10},{9,11},{10,... | collective-permute-start | bytes 786440 | tf_op jit(solution)/shard_map/ppermute | solution.py:447
  132.8 9.3 %collective-permute-start.23 = (bf16[256,512]{1,0:T(8,128)(2,1)}, bf16[256,512]{1,0:T(8,128)(2,1)S(1)}, u32[]{:S(2)}, u32[]{:S(2)}) collective-permute-start(bf16[256,512]{1,0:T(8,128)(2,1)} %get-tuple-element.79), channel_id=1, source_target_pairs={{0,1},{1,2},{2,3},{3,0},{4,5},{5,6},{6,7},{7,4},{8,9},{9,10},{10,1... | collective-permute-start | bytes 786440 | tf_op jit(solution)/shard_map/ppermute | solution.py:447
  140.4 1.8 %copy-start.14 = (bf16[256,512]{1,0:T(8,128)(2,1)}, bf16[256,512]{1,0:T(8,128)(2,1)S(1)}, u32[]{:S(2)}) copy-start(bf16[256,512]{1,0:T(8,128)(2,1)S(1)} %collective-permute-done.21.refs_5_) | copy-start | bytes 786436
  140.4 1.8 %copy-start.15 = (bf16[256,512]{1,0:T(8,128)(2,1)}, bf16[256,512]{1,0:T(8,128)(2,1)S(1)}, u32[]{:S(2)}) copy-start(bf16[256,512]{1,0:T(8,128)(2,1)S(1)} %collective-permute-done.22.refs_6_) | copy-start | bytes 786436
  142.2 0.7 copy-start.16
Sparse Core Ops, SparseCore 0:
  9.7 34.7 all-gather.1
  104.3 40.0 reduce-scatter.1

commit v9 on v8

--- a/solution.py
+++ b/solution.py
@@ -15,7 +15,7 @@
 NT = (((1,), (1,)), ((), ()))
 TN = (((0,), (0,)), ((), ()))
 NN = (((1,), (0,)), ((), ()))
-VMEM_LIMIT = 60 * 1024 * 1024
+VMEM_LIMIT = 63 * 1024 * 1024
 
 
 def mm(a, b, dims=NN):
@@ -54,6 +54,7 @@
     )
 
 
+ANY = pl.BlockSpec(memory_space=pl.ANY)
 LIGHT, MIDDLE, HEAVY = 1 << 20, 1 << 20, 1 << 39
 SIDE = 4
 CORES = 2
@@ -420,23 +421,31 @@
 
 
 def final_kernel(temper, place_ref, gq_ref, *refs):
-    out_ref = refs[8]
-    half_width = out_ref.shape[1] // 2
-    for half in range(2):
-        lanes = slice(half * half_width, (half + 1) * half_width)
-        total = gq_ref[:, lanes]
-        for ref in refs[4 * half : 4 * half + 4]:
-            total = total + ref[...].astype(F32)
-        out_ref[:, lanes] = (temper * total).astype(BF16)
-
-
-def final(place, within, first, second, temper):
-    shape = within.shape
-    return call(
-        functools.partial(final_kernel, temper), "final", 1,
-        [full(shape)] + [full(first[0].shape)] * 8, full(shape),
-        jax.ShapeDtypeStruct(shape, BF16), [], LIGHT,
-    )(place, within, *first, *second)
+    total = gq_ref[...]
+    for ref in refs[0:SIDE]:
+        total = total + ref[...].astype(F32)
+    refs[-1][...] = (temper * total).astype(BF16)
+
+
+def final(place, within, parts, half, temper, made=None):
+    rows, half_width = parts[0].shape
+    lanes = pl.BlockSpec((rows, half_width), lambda *_: (0, half))
+    more = [] if made is None else [made]
+    return pl.pallas_call(
+        functools.partial(final_kernel, temper),
+        grid_spec=pltpu.PrefetchScalarGridSpec(
+            num_scalar_prefetch=1, grid=(1,),
+            in_specs=[lanes] + [full((rows, half_width))] * SIDE + [ANY] * len(more),
+            out_specs=lanes, scratch_shapes=[],
+        ),
+        out_shape=jax.ShapeDtypeStruct(within.shape, BF16),
+        compiler_params=pltpu.CompilerParams(
+            dimension_semantics=("arbitrary",), vmem_limit_bytes=VMEM_LIMIT
+        ),
+        input_output_aliases={2 + SIDE: 0} if more else {},
+        cost_estimate=pl.CostEstimate(flops=LIGHT, bytes_accessed=1 << 16, transcendentals=0),
+        name="final",
+    )(place, within, *parts, *more)
 
 
 def along(x, half, shift):
@@ -496,7 +505,8 @@
     for half, ranks, rows in ((0, ranks_first, back_first), (1, ranks_second, back_second)):
         made = reduce(place, half, log_total, ranks, rows, mark, groups, cap)
         sums.append([along(v, half, -s) if s else v for s, v in enumerate(made)])
-    grad_queries = final(place, grad_inner, *sums, temper)
+    grad_queries = final(place, grad_inner, sums[0], 0, temper)
+    grad_queries = final(place, grad_inner, sums[1], 1, temper, grad_queries)
     return (losses.reshape(toks), grad_queries, grad_passages)
 
 

time: 155 us -> 155 us (level)
  waiting for transfers between devices: 36.1 us -> 29.3 us
  starting transfers between devices: 39.6 us -> 45.9 us
  Pallas kernels: 56.7 us -> 59.2 us
    ppermute x24, waiting for transfers between devices: 35.2 us -> 28.6 us  [along(): return lax.ppermute(x, 'rep', pairs)]
    ppermute x24, starting transfers between devices: 34.1 us -> 39.7 us  [along(): return lax.ppermute(x, 'rep', pairs)]
    pallas_call x1 -> x2, Pallas kernels: 3.76 us -> 5.92 us  [final(): pl.pallas_call(functools.partial(final_kernel, temper), grid_spec=pltpu.P...]
    unnamed x40 -> x24, local copies, waits for them, and re-layouts: 3.71 us -> 2.27 us
  transfers between devices with their start and end apart: 27 -> 27, of which waited for: 11 -> 10; matrix products, arithmetic and copies ran while one was open for 2% -> 2% of each run, Pallas kernels for 31% -> 33%
where the time goes in v9:
time: 155 us; the launch traced here: 154 us
  Pallas kernels  59.2 us (38%)
  starting transfers between devices  45.9 us (30%)
  waiting for transfers between devices  29.3 us (19%)
  between operations  14.2 us (9%)
  local copies, waits for them, and re-layouts  3.34 us (2%)
  other arithmetic  2.09 us (1%)
    ppermute x24, starting transfers between devices, along(): return lax.ppermute(x, 'rep', pairs)  39.7 us
    ppermute x24, waiting for transfers between devices, along(): return lax.ppermute(x, 'rep', pairs)  28.6 us
    pallas_call x4, Pallas kernels, mid(): call(functools.partial(mid_kernel, shift, cap, groups, reps, negs), 'mid'...  17.9 us
    pallas_call x1, Pallas kernels, column(): call(functools.partial(column_kernel, reps, cap, temper), 'column', gathe...  12.1 us
    pallas_call x2, Pallas kernels, reduce(): call(functools.partial(reduce_kernel, half, cap, groups), 'reduce', 1, [f...  9.29 us
    pallas_call x1, Pallas kernels, hard(): call(functools.partial(hard_kernel, reps, cap, temper), 'hard', levels +...  9.04 us
    all_to_all x1, starting transfers between devices, shards(): parts = lax.all_to_all(part, 'rep', split_axis=0, concat_axis=0, tiled=True)  6.1 us
    pallas_call x2, Pallas kernels, final(): pl.pallas_call(functools.partial(final_kernel, temper), grid_spec=pltpu.P...  5.92 us
  transfers between devices with their start and end apart: 27, of which 10 were waited for; matrix products, arithmetic and copies ran while one was open for 2% of the time, Pallas kernels for 33%

profile of v9, /device:TPU:0, one launch (start us, length us, event | category | flops | bytes accessed | tf_op | source)
XLA Modules:
  0.0 154.0 jit_solution(11909313095549718289)
XLA Ops:
  7.2 0.7 all-gather.2.cloned.1.call-update
  7.9 0.7 convert_bitcast_fusion
  8.6 1.1 fusion.7
  9.8 3.2 %collective-permute-start.5 = (bf16[272,512]{1,0:T(8,128)(2,1)S(1)}, bf16[272,512]{1,0:T(8,128)(2,1)S(1)}, u32[]{:S(2)}, u32[]{:S(2)}) collective-permute-start(bf16[272,512]{1,0:T(8,128)(2,1)S(1)} %get-tuple-element.83.refs_4_), channel_id=1, source_target_pairs={{0,3},{1,0},{2,1},{3,2},{4,7},{5,4},{6,5},{7,6},{8,11},{9,8},{10,9... | collective-permute-start | bytes 835592 | tf_op jit(solution)/shard_map/ppermute | solution.py:456
  13.6 1.0 collective-permute-start.3
  14.5 2.8 %collective-permute-start.2 = (bf16[272,512]{1,0:T(8,128)(2,1)S(1)}, bf16[272,512]{1,0:T(8,128)(2,1)S(1)}, u32[]{:S(2)}, u32[]{:S(2)}) collective-permute-start(bf16[272,512]{1,0:T(8,128)(2,1)S(1)} %get-tuple-element.84.refs_0_), channel_id=1, source_target_pairs={{0,12},{1,13},{2,14},{3,15},{4,0},{5,1},{6,2},{7,3},{8,4},{9,5},{1... | collective-permute-start | bytes 835592 | tf_op jit(solution)/shard_map/ppermute | solution.py:456
  17.3 0.8 collective-permute-start.1
  18.1 6.7 %collective-permute-done.5.refs_7_ = bf16[272,512]{1,0:T(8,128)(2,1)S(1)} collective-permute-done((bf16[272,512]{1,0:T(8,128)(2,1)S(1)}, bf16[272,512]{1,0:T(8,128)(2,1)S(1)}, u32[]{:S(2)}, u32[]{:S(2)}) %collective-permute-start.5) | collective-permute-done | bytes 278560 | tf_op jit(solution)/shard_map/ppermute | solution.py:456
  24.8 1.5 collective-permute-start
  26.3 0.6 pad_add_fusion.place_ref
  27.0 1.6 %collective-permute-done.3.refs_5_ = bf16[272,512]{1,0:T(8,128)(2,1)S(1)} collective-permute-done((bf16[272,512]{1,0:T(8,128)(2,1)S(1)}, bf16[272,512]{1,0:T(8,128)(2,1)S(1)}, u32[]{:S(2)}, u32[]{:S(2)}) %collective-permute-start.3) | collective-permute-done | bytes 278560 | tf_op jit(solution)/shard_map/ppermute | solution.py:456
  28.5 0.7 copy-done.5
  29.4 0.7 copy-done.7
  30.1 3.9 %collective-permute-done.refs_1_ = bf16[272,512]{1,0:T(8,128)(2,1)} collective-permute-done((bf16[272,512]{1,0:T(8,128)(2,1)S(1)}, bf16[272,512]{1,0:T(8,128)(2,1)}, u32[]{:S(2)}, u32[]{:S(2)}) %collective-permute-start) | collective-permute-done | bytes 278560 | tf_op jit(solution)/shard_map/ppermute | solution.py:456
  34.0 4.5 %mid.4 = (bf16[528,512]{1,0:T(8,128)(2,1)}, bf16[528,512]{1,0:T(8,128)(2,1)}, bf16[32,256]{1,0:T(8,128)(2,1)}, bf16[32,256]{1,0:T(8,128)(2,1)}) custom-call(s32[3]{0:T(128)} %pad_add_fusion.place_ref, bf16[272,512]{1,0:T(8,128)(2,1)} %copy-done.1, bf16[272,512]{1,0:T(8,128)(2,1)} %collective-permute-done.refs_1_, bf16[272,512]{1,0:T(8,128)(2,1)} %copy-done.7, ...), custom_call_target="tpu_custom_call" | custom-call | flops 1048576 | bytes 65536 | tf_op jit(solution)/shard_map/mid/pallas_call | solution.py:129
  38.9 0.7 collective-permute-start.10
  39.7 4.5 %mid.5 = (bf16[528,512]{1,0:T(8,128)(2,1)}, bf16[528,512]{1,0:T(8,128)(2,1)}, bf16[32,256]{1,0:T(8,128)(2,1)}, bf16[32,256]{1,0:T(8,128)(2,1)}) custom-call(s32[3]{0:T(128)} %pad_add_fusion.place_ref, bf16[272,512]{1,0:T(8,128)(2,1)} %copy-done.1, bf16[272,512]{1,0:T(8,128)(2,1)} %collective-permute-done.refs_1_, bf16[272,512]{1,0:T(8,128)(2,1)} %copy-done.7, ...), custom_call_target="tpu_custom_call" | custom-call | flops 1048576 | bytes 65536 | tf_op jit(solution)/shard_map/mid/pallas_call | solution.py:129
  44.2 4.8 %collective-permute-start.6 = (bf16[528,512]{1,0:T(8,128)(2,1)}, bf16[528,512]{1,0:T(8,128)(2,1)}, u32[]{:S(2)}, u32[]{:S(2)}) collective-permute-start(bf16[528,512]{1,0:T(8,128)(2,1)} %get-tuple-element.46), channel_id=1, source_target_pairs={{0,1},{1,2},{2,3},{3,0},{4,5},{5,6},{6,7},{7,4},{8,9},{9,10},{10,1... | collective-permute-start | bytes 1622024 | tf_op jit(solution)/shard_map/ppermute | solution.py:456
  49.0 0.6 collective-permute-start.9
  49.6 4.4 %mid.6 = (bf16[528,512]{1,0:T(8,128)(2,1)}, bf16[528,512]{1,0:T(8,128)(2,1)}, bf16[32,256]{1,0:T(8,128)(2,1)}, bf16[32,256]{1,0:T(8,128)(2,1)}) custom-call(s32[3]{0:T(128)} %pad_add_fusion.place_ref, bf16[272,512]{1,0:T(8,128)(2,1)} %copy-done.1, bf16[272,512]{1,0:T(8,128)(2,1)} %collective-permute-done.refs_1_, bf16[272,512]{1,0:T(8,128)(2,1)} %copy-done.7, ...), custom_call_target="tpu_custom_call" | custom-call | flops 1048576 | bytes 65536 | tf_op jit(solution)/shard_map/mid/pallas_call | solution.py:129
  54.0 1.5 collective-permute-done.7.refs_2_.refs_10_
  55.5 1.2 collective-permute-start.11
  56.7 4.4 %mid.7 = (bf16[528,512]{1,0:T(8,128)(2,1)}, bf16[528,512]{1,0:T(8,128)(2,1)}, bf16[32,256]{1,0:T(8,128)(2,1)}, bf16[32,256]{1,0:T(8,128)(2,1)}) custom-call(s32[3]{0:T(128)} %pad_add_fusion.place_ref, bf16[272,512]{1,0:T(8,128)(2,1)} %copy-done.1, bf16[272,512]{1,0:T(8,128)(2,1)} %collective-permute-done.refs_1_, bf16[272,512]{1,0:T(8,128)(2,1)} %copy-done.7, ...), custom_call_target="tpu_custom_call" | custom-call | flops 1048576 | bytes 65536 | tf_op jit(solution)/shard_map/mid/pallas_call | solution.py:129
  61.2 5.0 %inside.1.refs_13_ = f32[1,256]{1,0:T(1,128)} custom-call(s32[3]{0:T(128)} %pad_add_fusion.place_ref, bf16[2048,1024]{1,0:T(8,128)(2,1)} %all-gather.2.cloned.1.call-done.p_ref.refs_12_.refs_8_, bf16[256,1024]{1,0:T(8,128)(2,1)} %refs_9_.1), custom_call_target="tpu_custom_call" | custom-call | flops 1048576 | bytes 65536 | tf_op jit(solution)/shard_map/inside/pallas_call | solution.py:159
  66.2 9.0 %hard.1 = (bf16[544,512]{1,0:T(8,128)(2,1)}, bf16[544,512]{1,0:T(8,128)(2,1)}, bf16[544,512]{1,0:T(8,128)(2,1)}, bf16[544,512]{1,0:T(8,128)(2,1)}, bf16[544,512]...) custom-call(s32[3]{0:T(128)} %pad_add_fusion.place_ref, ...), custom_call_target="tpu_custom_call" | custom-call | flops 1048576 | bytes 65536 | tf_op jit(solution)/shard_map/hard/pallas_call | solution.py:287
  75.2 6.1 %all-to-all-start = ((f32[16,16,256]{2,1,0:T(8,128)}), f32[16,16,256]{2,1,0:T(8,128)S(1)}, u32[]{:S(2)}, u32[]{:S(2)}) async-start(f32[16,16,256]{2,1,0:T(8,128)} %get-tuple-element.55), calls=%async_computation | async-start | bytes 524288 | tf_op jit(solution)/shard_map/all_to_all | solution.py:493
  81.4 3.4 %collective-permute-start.18 = (bf16[544,512]{1,0:T(8,128)(2,1)}, bf16[544,512]{1,0:T(8,128)(2,1)S(1)}, u32[]{:S(2)}, u32[]{:S(2)}) collective-permute-start(bf16[544,512]{1,0:T(8,128)(2,1)} %get-tuple-element.73), channel_id=1, source_target_pairs={{0,3},{1,0},{2,1},{3,2},{4,7},{5,4},{6,5},{7,6},{8,11},{9,8},{10,9... | collective-permute-start | bytes 1671176 | tf_op jit(solution)/shard_map/ppermute | solution.py:456
  84.8 0.9 collective-permute-start.19
  85.6 0.9 collective-permute-start.20
  86.5 2.7 %collective-permute-start.12 = (bf16[544,512]{1,0:T(8,128)(2,1)}, bf16[544,512]{1,0:T(8,128)(2,1)}, u32[]{:S(2)}, u32[]{:S(2)}) collective-permute-start(bf16[544,512]{1,0:T(8,128)(2,1)} %get-tuple-element.63), channel_id=1, source_target_pairs={{0,12},{1,13},{2,14},{3,15},{4,0},{5,1},{6,2},{7,3},{8,4},{9,5},{1... | collective-permute-start | bytes 1671176 | tf_op jit(solution)/shard_map/ppermute | solution.py:456
  89.2 0.9 collective-permute-start.13
  90.7 12.1 %column.1 = (bf16[2048,1024]{1,0:T(8,128)(2,1)}, f32[256,1024]{1,0:T(8,128)}, f32[1,256]{1,0:T(1,128)}, f32[8,128]{1,0:T(8,128)}) custom-call(s32[3]{0:T(128)} %pad_add_fusion.place_ref, s32[16,256]{1,0:T(8,128)} %get-tuple-element.53.code_ref, f32[8,256]{1,0:T(8,128)} %get-tuple-element.54.hs_ref, f32[16,256]{1,0:T(8,128)} %log_add_fusion.lt_ref, ...), custom_call_target="tpu_custom_call" | custom-call | flops 1048576 | bytes 65536 | tf_op jit(solution)/shard_map/column/pallas_call | solution.py:366
  102.8 6.0 %collective-permute-done.18.refs_5_ = bf16[544,512]{1,0:T(8,128)(2,1)S(1)} collective-permute-done((bf16[544,512]{1,0:T(8,128)(2,1)}, bf16[544,512]{1,0:T(8,128)(2,1)S(1)}, u32[]{:S(2)}, u32[]{:S(2)}) %collective-permute-start.18) | collective-permute-done | bytes 557088 | tf_op jit(solution)/shard_map/ppermute | solution.py:456
  108.9 1.1 collective-permute-start.14
  110.0 2.1 %collective-permute-done.20.refs_7_ = bf16[544,512]{1,0:T(8,128)(2,1)} collective-permute-done((bf16[544,512]{1,0:T(8,128)(2,1)}, bf16[544,512]{1,0:T(8,128)(2,1)}, u32[]{:S(2)}, u32[]{:S(2)}) %collective-permute-start.20) | collective-permute-done | bytes 557088 | tf_op jit(solution)/shard_map/ppermute | solution.py:456
  112.1 4.7 %reduce.3 = (f32[256,512]{1,0:T(8,128)}, bf16[256,512]{1,0:T(8,128)(2,1)}, bf16[256,512]{1,0:T(8,128)(2,1)}, bf16[256,512]{1,0:T(8,128)(2,1)}) custom-call(s32[3]{0:T(128)} %pad_add_fusion.place_ref, f32[16,256]{1,0:T(8,128)} %log_add_fusion.lt_ref, bf16[32,256]{1,0:T(8,128)(2,1)} %get-tuple-element.71.refs_0_, ...), custom_call_target="tpu_custom_call" | custom-call | flops 549755813888 | bytes 65536 | tf_op jit(solution)/shard_map/reduce/pallas_call | solution.py:414
  116.8 2.5 %collective-permute-start.21 = (bf16[256,512]{1,0:T(8,128)(2,1)}, bf16[256,512]{1,0:T(8,128)(2,1)}, u32[]{:S(2)}, u32[]{:S(2)}) collective-permute-start(bf16[256,512]{1,0:T(8,128)(2,1)} %get-tuple-element.77), channel_id=1, source_target_pairs={{0,12},{1,13},{2,14},{3,15},{4,0},{5,1},{6,2},{7,3},{8,4},{9,5},{1... | collective-permute-start | bytes 786440 | tf_op jit(solution)/shard_map/ppermute | solution.py:456
  119.3 0.8 collective-permute-start.22
  120.2 0.8 collective-permute-start.23
  121.0 4.6 %reduce.2 = (f32[256,512]{1,0:T(8,128)}, bf16[256,512]{1,0:T(8,128)(2,1)}, bf16[256,512]{1,0:T(8,128)(2,1)}, bf16[256,512]{1,0:T(8,128)(2,1)}) custom-call(s32[3]{0:T(128)} %pad_add_fusion.place_ref, f32[16,256]{1,0:T(8,128)} %log_add_fusion.lt_ref, bf16[32,256]{1,0:T(8,128)(2,1)} %get-tuple-element.58.refs_0_, bf16[32,256]{1,0:T(8,128)(2,1)} %get-tuple-element.59.refs_1_, ...), custom_call_target="tpu_custom_call" | custom-call | flops 549755813888 | bytes 65536 | tf_op jit(solution)/shard_map/reduce/pallas_call | solution.py:414
  125.6 7.3 %collective-permute-start.15 = (bf16[256,512]{1,0:T(8,128)(2,1)}, bf16[256,512]{1,0:T(8,128)(2,1)S(1)}, u32[]{:S(2)}, u32[]{:S(2)}) collective-permute-start(bf16[256,512]{1,0:T(8,128)(2,1)} %get-tuple-element.68), channel_id=1, source_target_pairs={{0,3},{1,0},{2,1},{3,2},{4,7},{5,4},{6,5},{7,6},{8,11},{9,8},{10,9... | collective-permute-start | bytes 786440 | tf_op jit(solution)/shard_map/ppermute | solution.py:456
  132.9 0.9 collective-permute-start.17
  133.8 0.8 collective-permute-done.23.refs_3_
  134.6 3.0 %final.2.refs_4_ = bf16[256,1024]{1,0:T(8,128)(2,1)} custom-call(s32[3]{0:T(128)} %pad_add_fusion.place_ref, f32[256,1024]{1,0:T(8,128)} %get-tuple-element.57.gq_ref, f32[256,512]{1,0:T(8,128)} %get-tuple-element.76.refs_0_, bf16[256,512]{1,0:T(8,128)(2,1)} %collective-permute-done.21.refs_1_, bf16[256,512]{1,0:T(8,128)(2,1)} %collective-permute-done.22.refs_2_, ...), custom_call_target="tpu_custom_call" | custom-call | flops 1048576 | bytes 65536 | tf_op jit(solution)/shard_map/final/pallas_call | solution.py:434
  137.6 3.0 %collective-permute-done.15.refs_1_ = bf16[256,512]{1,0:T(8,128)(2,1)S(1)} collective-permute-done((bf16[256,512]{1,0:T(8,128)(2,1)}, bf16[256,512]{1,0:T(8,128)(2,1)S(1)}, u32[]{:S(2)}, u32[]{:S(2)}) %collective-permute-start.15) | collective-permute-done | bytes 262176 | tf_op jit(solution)/shard_map/ppermute | solution.py:456
  141.1 2.4 %collective-permute-done.17.refs_3_ = bf16[256,512]{1,0:T(8,128)(2,1)S(1)} collective-permute-done((bf16[256,512]{1,0:T(8,128)(2,1)}, bf16[256,512]{1,0:T(8,128)(2,1)S(1)}, u32[]{:S(2)}, u32[]{:S(2)}) %collective-permute-start.17) | collective-permute-done | bytes 262176 | tf_op jit(solution)/shard_map/ppermute | solution.py:456
  143.5 0.7 copy-done.10
  144.2 2.9 %final.3 = bf16[256,1024]{1,0:T(8,128)(2,1)} custom-call(s32[3]{0:T(128)} %pad_add_fusion.place_ref, f32[256,1024]{1,0:T(8,128)} %get-tuple-element.57.gq_ref, f32[256,512]{1,0:T(8,128)} %get-tuple-element.67.refs_0_, bf16[256,512]{1,0:T(8,128)(2,1)} %copy-done.8, bf16[256,512]{1,0:T(8,128)(2,1)} %copy-done.9, ...), custom_call_target="tpu_custom_call", output_to_operand_aliasing={{}: (6, {})} | custom-call | flops 1048576 | bytes 65536 | tf_op jit(solution)/shard_map/final/pallas_call | solution.py:434
  (51 shorter events, 2.6 us)
Async XLA Ops:
  7.2 54.0 %all-gather.2.cloned.1.call-start = ((), (), s32[]{:S(2)}) async-start(), calls=%async_computation.2 | async-start | bytes 4718592 | tf_op jit(solution)/shard_map/all_gather | solution.py:477
  9.7 24.3 %copy-start = (bf16[272,512]{1,0:T(8,128)(2,1)}, bf16[272,512]{1,0:T(8,128)(2,1)S(1)}, u32[]{:S(2)}) copy-start(bf16[272,512]{1,0:T(8,128)(2,1)S(1)} %get-tuple-element.83.refs_4_) | copy-start | bytes 835588
  9.8 24.2 %copy-start.1 = (bf16[272,512]{1,0:T(8,128)(2,1)}, bf16[272,512]{1,0:T(8,128)(2,1)S(1)}, u32[]{:S(2)}) copy-start(bf16[272,512]{1,0:T(8,128)(2,1)S(1)} %get-tuple-element.84.refs_0_) | copy-start | bytes 835588
  9.8 15.1 %collective-permute-start.5 = (bf16[272,512]{1,0:T(8,128)(2,1)S(1)}, bf16[272,512]{1,0:T(8,128)(2,1)S(1)}, u32[]{:S(2)}, u32[]{:S(2)}) collective-permute-start(bf16[272,512]{1,0:T(8,128)(2,1)S(1)} %get-tuple-element.83.refs_4_), channel_id=1, source_target_pairs={{0,3},{1,0},{2,1},{3,2},{4,7},{5,4},{6,5},{7,6},{8,11},{9,8},{10,9... | collective-permute-start | bytes 835592 | tf_op jit(solution)/shard_map/ppermute | solution.py:456
  12.9 14.0 %collective-permute-start.4 = (bf16[272,512]{1,0:T(8,128)(2,1)S(1)}, bf16[272,512]{1,0:T(8,128)(2,1)S(1)}, u32[]{:S(2)}, u32[]{:S(2)}) collective-permute-start(bf16[272,512]{1,0:T(8,128)(2,1)S(1)} %get-tuple-element.83.refs_4_), channel_id=1, source_target_pairs={{0,2},{1,3},{2,0},{3,1},{4,6},{5,7},{6,4},{7,5},{8,10},{9,11},{10,... | collective-permute-start | bytes 835592 | tf_op jit(solution)/shard_map/ppermute | solution.py:456
  13.6 15.0 %collective-permute-start.3 = (bf16[272,512]{1,0:T(8,128)(2,1)S(1)}, bf16[272,512]{1,0:T(8,128)(2,1)S(1)}, u32[]{:S(2)}, u32[]{:S(2)}) collective-permute-start(bf16[272,512]{1,0:T(8,128)(2,1)S(1)} %get-tuple-element.83.refs_4_), channel_id=1, source_target_pairs={{0,1},{1,2},{2,3},{3,0},{4,5},{5,6},{6,7},{7,4},{8,9},{9,10},{10,1... | collective-permute-start | bytes 835592 | tf_op jit(solution)/shard_map/ppermute | solution.py:456
  14.5 14.0 %collective-permute-start.2 = (bf16[272,512]{1,0:T(8,128)(2,1)S(1)}, bf16[272,512]{1,0:T(8,128)(2,1)S(1)}, u32[]{:S(2)}, u32[]{:S(2)}) collective-permute-start(bf16[272,512]{1,0:T(8,128)(2,1)S(1)} %get-tuple-element.84.refs_0_), channel_id=1, source_target_pairs={{0,12},{1,13},{2,14},{3,15},{4,0},{5,1},{6,2},{7,3},{8,4},{9,5},{1... | collective-permute-start | bytes 835592 | tf_op jit(solution)/shard_map/ppermute | solution.py:456
  17.3 11.2 %collective-permute-start.1 = (bf16[272,512]{1,0:T(8,128)(2,1)S(1)}, bf16[272,512]{1,0:T(8,128)(2,1)S(1)}, u32[]{:S(2)}, u32[]{:S(2)}) collective-permute-start(bf16[272,512]{1,0:T(8,128)(2,1)S(1)} %get-tuple-element.84.refs_0_), channel_id=1, source_target_pairs={{0,8},{1,9},{2,10},{3,11},{4,12},{5,13},{6,14},{7,15},{8,0},{9,1},... | collective-permute-start | bytes 835592 | tf_op jit(solution)/shard_map/ppermute | solution.py:456
  24.8 9.2 %copy-start.3 = (bf16[272,512]{1,0:T(8,128)(2,1)}, bf16[272,512]{1,0:T(8,128)(2,1)S(1)}, u32[]{:S(2)}) copy-start(bf16[272,512]{1,0:T(8,128)(2,1)S(1)} %collective-permute-done.5.refs_7_) | copy-start | bytes 835588
  24.8 9.2 %collective-permute-start = (bf16[272,512]{1,0:T(8,128)(2,1)S(1)}, bf16[272,512]{1,0:T(8,128)(2,1)}, u32[]{:S(2)}, u32[]{:S(2)}) collective-permute-start(bf16[272,512]{1,0:T(8,128)(2,1)S(1)} %get-tuple-element.84.refs_0_), channel_id=1, source_target_pairs={{0,4},{1,5},{2,6},{3,7},{4,8},{5,9},{6,10},{7,11},{8,12},{9,13},{1... | collective-permute-start | bytes 835592 | tf_op jit(solution)/shard_map/ppermute | solution.py:456
  27.0 1.6 %copy-start.4 = (bf16[272,512]{1,0:T(8,128)(2,1)}, bf16[272,512]{1,0:T(8,128)(2,1)S(1)}, u32[]{:S(2)}) copy-start(bf16[272,512]{1,0:T(8,128)(2,1)S(1)} %collective-permute-done.4.refs_6_) | copy-start | bytes 835588
  28.5 0.7 copy-start.5
  28.5 0.8 copy-start.6
  29.4 0.7 copy-start.7
  38.5 17.0 %collective-permute-start.7 = (bf16[528,512]{1,0:T(8,128)(2,1)}, bf16[528,512]{1,0:T(8,128)(2,1)S(1)}, u32[]{:S(2)}, u32[]{:S(2)}) collective-permute-start(bf16[528,512]{1,0:T(8,128)(2,1)} %get-tuple-element.47), channel_id=1, source_target_pairs={{0,2},{1,3},{2,0},{3,1},{4,6},{5,7},{6,4},{7,5},{8,10},{9,11},{10,... | collective-permute-start | bytes 1622024 | tf_op jit(solution)/shard_map/ppermute | solution.py:456
  38.9 27.2 %collective-permute-start.10 = (bf16[528,512]{1,0:T(8,128)(2,1)}, bf16[528,512]{1,0:T(8,128)(2,1)}, u32[]{:S(2)}, u32[]{:S(2)}) collective-permute-start(bf16[528,512]{1,0:T(8,128)(2,1)} %get-tuple-element.51), channel_id=1, source_target_pairs={{0,8},{1,9},{2,10},{3,11},{4,12},{5,13},{6,14},{7,15},{8,0},{9,1},... | collective-permute-start | bytes 1622024 | tf_op jit(solution)/shard_map/ppermute | solution.py:456
  44.2 22.0 %collective-permute-start.6 = (bf16[528,512]{1,0:T(8,128)(2,1)}, bf16[528,512]{1,0:T(8,128)(2,1)}, u32[]{:S(2)}, u32[]{:S(2)}) collective-permute-start(bf16[528,512]{1,0:T(8,128)(2,1)} %get-tuple-element.46), channel_id=1, source_target_pairs={{0,1},{1,2},{2,3},{3,0},{4,5},{5,6},{6,7},{7,4},{8,9},{9,10},{10,1... | collective-permute-start | bytes 1622024 | tf_op jit(solution)/shard_map/ppermute | solution.py:456
  49.0 17.2 %collective-permute-start.9 = (bf16[528,512]{1,0:T(8,128)(2,1)}, bf16[528,512]{1,0:T(8,128)(2,1)}, u32[]{:S(2)}, u32[]{:S(2)}) collective-permute-start(bf16[528,512]{1,0:T(8,128)(2,1)} %get-tuple-element.50), channel_id=1, source_target_pairs={{0,4},{1,5},{2,6},{3,7},{4,8},{5,9},{6,10},{7,11},{8,12},{9,13},{1... | collective-permute-start | bytes 1622024 | tf_op jit(solution)/shard_map/ppermute | solution.py:456
  54.0 12.1 %collective-permute-start.8 = (bf16[528,512]{1,0:T(8,128)(2,1)}, bf16[528,512]{1,0:T(8,128)(2,1)}, u32[]{:S(2)}, u32[]{:S(2)}) collective-permute-start(bf16[528,512]{1,0:T(8,128)(2,1)} %get-tuple-element.48), channel_id=1, source_target_pairs={{0,3},{1,0},{2,1},{3,2},{4,7},{5,4},{6,5},{7,6},{8,11},{9,8},{10,9... | collective-permute-start | bytes 1622024 | tf_op jit(solution)/shard_map/ppermute | solution.py:456
  55.5 10.7 %copy-start.2 = (bf16[528,512]{1,0:T(8,128)(2,1)}, bf16[528,512]{1,0:T(8,128)(2,1)S(1)}, u32[]{:S(2)}) copy-start(bf16[528,512]{1,0:T(8,128)(2,1)S(1)} %collective-permute-done.7.refs_2_.refs_10_) | copy-start | bytes 1622020
  55.5 10.7 %collective-permute-start.11 = (bf16[528,512]{1,0:T(8,128)(2,1)}, bf16[528,512]{1,0:T(8,128)(2,1)}, u32[]{:S(2)}, u32[]{:S(2)}) collective-permute-start(bf16[528,512]{1,0:T(8,128)(2,1)} %get-tuple-element.52), channel_id=1, source_target_pairs={{0,12},{1,13},{2,14},{3,15},{4,0},{5,1},{6,2},{7,3},{8,4},{9,5},{1... | collective-permute-start | bytes 1622024 | tf_op jit(solution)/shard_map/ppermute | solution.py:456
  75.2 14.8 %all-to-all-start = ((f32[16,16,256]{2,1,0:T(8,128)}), f32[16,16,256]{2,1,0:T(8,128)S(1)}, u32[]{:S(2)}, u32[]{:S(2)}) async-start(f32[16,16,256]{2,1,0:T(8,128)} %get-tuple-element.55), calls=%async_computation | async-start | bytes 524288 | tf_op jit(solution)/shard_map/all_to_all | solution.py:493
  81.3 65.8 %reduce-scatter.2.cloned.1.call-start = ((), (), s32[]{:S(2)}) async-start(), calls=%async_computation.3 | async-start | bytes 4718592 | tf_op jit(solution)/shard_map/reduce_scatter | solution.py:500
  81.4 27.5 %collective-permute-start.18 = (bf16[544,512]{1,0:T(8,128)(2,1)}, bf16[544,512]{1,0:T(8,128)(2,1)S(1)}, u32[]{:S(2)}, u32[]{:S(2)}) collective-permute-start(bf16[544,512]{1,0:T(8,128)(2,1)} %get-tuple-element.73), channel_id=1, source_target_pairs={{0,3},{1,0},{2,1},{3,2},{4,7},{5,4},{6,5},{7,6},{8,11},{9,8},{10,9... | collective-permute-start | bytes 1671176 | tf_op jit(solution)/shard_map/ppermute | solution.py:456
  84.8 25.3 %collective-permute-start.19 = (bf16[544,512]{1,0:T(8,128)(2,1)}, bf16[544,512]{1,0:T(8,128)(2,1)}, u32[]{:S(2)}, u32[]{:S(2)}) collective-permute-start(bf16[544,512]{1,0:T(8,128)(2,1)} %get-tuple-element.74), channel_id=1, source_target_pairs={{0,2},{1,3},{2,0},{3,1},{4,6},{5,7},{6,4},{7,5},{8,10},{9,11},{10,... | collective-permute-start | bytes 1671176 | tf_op jit(solution)/shard_map/ppermute | solution.py:456
  85.6 26.5 %collective-permute-start.20 = (bf16[544,512]{1,0:T(8,128)(2,1)}, bf16[544,512]{1,0:T(8,128)(2,1)}, u32[]{:S(2)}, u32[]{:S(2)}) collective-permute-start(bf16[544,512]{1,0:T(8,128)(2,1)} %get-tuple-element.75), channel_id=1, source_target_pairs={{0,1},{1,2},{2,3},{3,0},{4,5},{5,6},{6,7},{7,4},{8,9},{9,10},{10,1... | collective-permute-start | bytes 1671176 | tf_op jit(solution)/shard_map/ppermute | solution.py:456
  86.5 33.7 %collective-permute-start.12 = (bf16[544,512]{1,0:T(8,128)(2,1)}, bf16[544,512]{1,0:T(8,128)(2,1)}, u32[]{:S(2)}, u32[]{:S(2)}) collective-permute-start(bf16[544,512]{1,0:T(8,128)(2,1)} %get-tuple-element.63), channel_id=1, source_target_pairs={{0,12},{1,13},{2,14},{3,15},{4,0},{5,1},{6,2},{7,3},{8,4},{9,5},{1... | collective-permute-start | bytes 1671176 | tf_op jit(solution)/shard_map/ppermute | solution.py:456
  89.2 31.8 %collective-permute-start.13 = (bf16[544,512]{1,0:T(8,128)(2,1)}, bf16[544,512]{1,0:T(8,128)(2,1)}, u32[]{:S(2)}, u32[]{:S(2)}) collective-permute-start(bf16[544,512]{1,0:T(8,128)(2,1)} %get-tuple-element.64), channel_id=1, source_target_pairs={{0,8},{1,9},{2,10},{3,11},{4,12},{5,13},{6,14},{7,15},{8,0},{9,1},... | collective-permute-start | bytes 1671176 | tf_op jit(solution)/shard_map/ppermute | solution.py:456
  108.9 3.3 %copy-start.11 = (bf16[544,512]{1,0:T(8,128)(2,1)}, bf16[544,512]{1,0:T(8,128)(2,1)S(1)}, u32[]{:S(2)}) copy-start(bf16[544,512]{1,0:T(8,128)(2,1)S(1)} %collective-permute-done.18.refs_5_) | copy-start | bytes 1671172
  108.9 12.1 %collective-permute-start.14 = (bf16[544,512]{1,0:T(8,128)(2,1)}, bf16[544,512]{1,0:T(8,128)(2,1)}, u32[]{:S(2)}, u32[]{:S(2)}) collective-permute-start(bf16[544,512]{1,0:T(8,128)(2,1)} %get-tuple-element.65), channel_id=1, source_target_pairs={{0,4},{1,5},{2,6},{3,7},{4,8},{5,9},{6,10},{7,11},{8,12},{9,13},{1... | collective-permute-start | bytes 1671176 | tf_op jit(solution)/shard_map/ppermute | solution.py:456
  116.8 16.0 %collective-permute-start.21 = (bf16[256,512]{1,0:T(8,128)(2,1)}, bf16[256,512]{1,0:T(8,128)(2,1)}, u32[]{:S(2)}, u32[]{:S(2)}) collective-permute-start(bf16[256,512]{1,0:T(8,128)(2,1)} %get-tuple-element.77), channel_id=1, source_target_pairs={{0,12},{1,13},{2,14},{3,15},{4,0},{5,1},{6,2},{7,3},{8,4},{9,5},{1... | collective-permute-start | bytes 786440 | tf_op jit(solution)/shard_map/ppermute | solution.py:456
  119.3 14.5 %collective-permute-start.22 = (bf16[256,512]{1,0:T(8,128)(2,1)}, bf16[256,512]{1,0:T(8,128)(2,1)}, u32[]{:S(2)}, u32[]{:S(2)}) collective-permute-start(bf16[256,512]{1,0:T(8,128)(2,1)} %get-tuple-element.78), channel_id=1, source_target_pairs={{0,8},{1,9},{2,10},{3,11},{4,12},{5,13},{6,14},{7,15},{8,0},{9,1},... | collective-permute-start | bytes 786440 | tf_op jit(solution)/shard_map/ppermute | solution.py:456
  120.2 14.4 %collective-permute-start.23 = (bf16[256,512]{1,0:T(8,128)(2,1)}, bf16[256,512]{1,0:T(8,128)(2,1)}, u32[]{:S(2)}, u32[]{:S(2)}) collective-permute-start(bf16[256,512]{1,0:T(8,128)(2,1)} %get-tuple-element.79), channel_id=1, source_target_pairs={{0,4},{1,5},{2,6},{3,7},{4,8},{5,9},{6,10},{7,11},{8,12},{9,13},{1... | collective-permute-start | bytes 786440 | tf_op jit(solution)/shard_map/ppermute | solution.py:456
  125.6 14.9 %collective-permute-start.15 = (bf16[256,512]{1,0:T(8,128)(2,1)}, bf16[256,512]{1,0:T(8,128)(2,1)S(1)}, u32[]{:S(2)}, u32[]{:S(2)}) collective-permute-start(bf16[256,512]{1,0:T(8,128)(2,1)} %get-tuple-element.68), channel_id=1, source_target_pairs={{0,3},{1,0},{2,1},{3,2},{4,7},{5,4},{6,5},{7,6},{8,11},{9,8},{10,9... | collective-permute-start | bytes 786440 | tf_op jit(solution)/shard_map/ppermute | solution.py:456
  132.9 8.2 %collective-permute-start.16 = (bf16[256,512]{1,0:T(8,128)(2,1)}, bf16[256,512]{1,0:T(8,128)(2,1)S(1)}, u32[]{:S(2)}, u32[]{:S(2)}) collective-permute-start(bf16[256,512]{1,0:T(8,128)(2,1)} %get-tuple-element.69), channel_id=1, source_target_pairs={{0,2},{1,3},{2,0},{3,1},{4,6},{5,7},{6,4},{7,5},{8,10},{9,11},{10,... | collective-permute-start | bytes 786440 | tf_op jit(solution)/shard_map/ppermute | solution.py:456
  132.9 10.6 %collective-permute-start.17 = (bf16[256,512]{1,0:T(8,128)(2,1)}, bf16[256,512]{1,0:T(8,128)(2,1)S(1)}, u32[]{:S(2)}, u32[]{:S(2)}) collective-permute-start(bf16[256,512]{1,0:T(8,128)(2,1)} %get-tuple-element.70), channel_id=1, source_target_pairs={{0,1},{1,2},{2,3},{3,0},{4,5},{5,6},{6,7},{7,4},{8,9},{9,10},{10,1... | collective-permute-start | bytes 786440 | tf_op jit(solution)/shard_map/ppermute | solution.py:456
  140.5 3.0 %copy-start.8 = (bf16[256,512]{1,0:T(8,128)(2,1)}, bf16[256,512]{1,0:T(8,128)(2,1)S(1)}, u32[]{:S(2)}) copy-start(bf16[256,512]{1,0:T(8,128)(2,1)S(1)} %collective-permute-done.15.refs_1_) | copy-start | bytes 786436
  141.1 2.4 %copy-start.9 = (bf16[256,512]{1,0:T(8,128)(2,1)}, bf16[256,512]{1,0:T(8,128)(2,1)S(1)}, u32[]{:S(2)}) copy-start(bf16[256,512]{1,0:T(8,128)(2,1)S(1)} %collective-permute-done.16.refs_2_) | copy-start | bytes 786436
  143.5 0.7 copy-start.10
Sparse Core Ops, SparseCore 0:
  9.7 34.7 all-gather.1
  103.0 40.1 reduce-scatter.1

commit v10 on v9

--- a/solution.py
+++ b/solution.py
@@ -134,7 +134,7 @@
     )(place, *first, *second, *earlier)
 
 
-def inside_kernel(temper, place_ref, p_ref, q_ref, out_ref, top, total):
+def inside_kernel(temper, place_ref, p_ref, q_ref, out_ref, scores_ref, top, total):
     step = pl.program_id(0)
 
     @pl.when(step == 0)
@@ -143,6 +143,7 @@
         total[...] = jnp.zeros(total.shape, F32)
 
     scores = temper * mm(p_ref[...], q_ref[...], NT)
+    scores_ref[...] = scores
     high = jnp.maximum(top[...], jnp.max(scores, axis=0, keepdims=True))
     total[...] = total[...] * jnp.exp(top[...] - high) + jnp.sum(
         jnp.exp(scores - high), axis=0, keepdims=True
@@ -159,7 +160,9 @@
     return call(
         functools.partial(inside_kernel, temper), "inside", 2,
         [pl.BlockSpec((gathered.shape[0] // 2, width), lambda s, _: (s, 0)), full((toks, width))],
-        full((1, toks)), jax.ShapeDtypeStruct((1, toks), F32),
+        [full((1, toks)), pl.BlockSpec((gathered.shape[0] // 2, toks), lambda s, _: (s, 0))],
+        [jax.ShapeDtypeStruct((1, toks), F32),
+         jax.ShapeDtypeStruct((gathered.shape[0], toks), F32)],
         [pltpu.VMEM((1, toks), F32), pltpu.VMEM((1, toks), F32)], MIDDLE,
     )(place, gathered, queries)
 
@@ -306,7 +309,7 @@
 
 def column_kernel(reps, cap, temper, place_ref, code_ref, hs_ref, lt_ref, *refs):
     first, second = refs[0:4], refs[4:8]
-    p_ref, q_ref, gp_ref, gq_ref, loss_ref, mark_ref, d_ref = refs[8:]
+    p_ref, q_ref, scores_ref, gp_ref, gq_ref, loss_ref, mark_ref, d_ref = refs[8:]
     step = pl.program_id(0)
     toks, width = q_ref.shape
     slots = reps * cap
@@ -332,7 +335,7 @@
     queries = q_ref[...]
     passages = p_ref[...]
     lt_own = own_row(lt_ref, rep_of(place_ref[1], place_ref[2]))
-    scores = temper * mm(passages, queries, NT)
+    scores = scores_ref[...]
     row = iota(scores.shape, 0) + CORES * toks * step - toks * place_ref[0]
     eye = row == iota(scores.shape, 1)
     d_scores = (jnp.exp(scores - lt_own) - jnp.where(eye, 1.0, 0.0)).astype(BF16)
@@ -358,7 +361,8 @@
         gq_ref[...] += new
 
 
-def column(place, codes, hard_scores, log_total, first, second, gathered, queries, temper, cap):
+def column(place, codes, hard_scores, log_total, first, second, gathered, queries, scores, temper,
+           cap):
     reps = log_total.shape[0]
     toks, width = queries.shape
     slots = pl.BlockSpec((CORES * SIDE * cap, width // 2), lambda s, _: (s, 0))
@@ -367,12 +371,13 @@
         functools.partial(column_kernel, reps, cap, temper), "column",
         gathered.shape[0] // (CORES * toks),
         [full(codes.shape), full(hard_scores.shape), full(log_total.shape)] + [slots] * 8
-        + [block, full((toks, width))],
+        + [block, full((toks, width)),
+           pl.BlockSpec((CORES * toks, toks), lambda s, _: (s, 0))],
         [block, full((toks, width)), full((1, toks)), full((8, 128))],
         [jax.ShapeDtypeStruct(gathered.shape, BF16), jax.ShapeDtypeStruct((toks, width), F32),
          jax.ShapeDtypeStruct((1, toks), F32), jax.ShapeDtypeStruct((8, 128), F32)],
         [pltpu.VMEM(hard_scores.shape, F32)], LIGHT,
-    )(place, codes, hard_scores, log_total, *first, *second, gathered, queries)
+    )(place, codes, hard_scores, log_total, *first, *second, gathered, queries, scores)
 
 
 def reduce_kernel(half, cap, groups, place_ref, lt_ref, *refs):
@@ -486,7 +491,7 @@
         first[shift] = along(one, 1, shift) if shift else one
         second[shift] = along(two, 0, shift) if shift else two
 
-    within = inside(place, gathered, queries, temper)
+    within, scores = inside(place, gathered, queries, temper)
     back_first, back_second, hard_scores, codes, part = hard(
         place, first, second, gathered, within, temper, reps, cap
     )
@@ -495,7 +500,7 @@
     log_total = high + jnp.log(jnp.sum(jnp.exp(parts - high), axis=0))
 
     partial_sum, grad_inner, losses, mark = column(
-        place, codes, hard_scores, log_total, first, second, gathered, queries, temper, cap
+        place, codes, hard_scores, log_total, first, second, gathered, queries, scores, temper, cap
     )
     grad_passages = lax.psum_scatter(partial_sum, "grp", scatter_dimension=0, tiled=True)
     back_first = [along(v, 1, -s) if s else v for s, v in enumerate(back_first)]

time: 155 us -> 155 us (level)
  waiting for transfers between devices: 29.3 us -> 31.3 us
  Pallas kernels: 59.2 us -> 57.3 us
    ppermute x24, waiting for transfers between devices: 28.6 us -> 30.6 us  [along(): return lax.ppermute(x, 'rep', pairs)]
    pallas_call x1, Pallas kernels: 12.1 us -> 10 us  [column(): call(functools.partial(column_kernel, reps, cap, temper), 'column', gathe...]
  transfers between devices with their start and end apart: 27 -> 27, of which waited for: 10 -> 10; matrix products, arithmetic and copies ran while one was open for 2% -> 2% of each run, Pallas kernels for 33% -> 31%
where the time goes in v10:
time: 155 us; the launch traced here: 154 us
  Pallas kernels  57.3 us (37%)
  starting transfers between devices  45.6 us (29%)
  waiting for transfers between devices  31.3 us (20%)
  between operations  14.2 us (9%)
  local copies, waits for them, and re-layouts  3.31 us (2%)
  other arithmetic  2.1 us (1%)
    ppermute x24, starting transfers between devices, along(): return lax.ppermute(x, 'rep', pairs)  39.8 us
    ppermute x24, waiting for transfers between devices, along(): return lax.ppermute(x, 'rep', pairs)  30.6 us
    pallas_call x4, Pallas kernels, mid(): call(functools.partial(mid_kernel, shift, cap, groups, reps, negs), 'mid'...  17.9 us
    pallas_call x1, Pallas kernels, column(): call(functools.partial(column_kernel, reps, cap, temper), 'column', gathe...  10 us
    pallas_call x2, Pallas kernels, reduce(): call(functools.partial(reduce_kernel, half, cap, groups), 'reduce', 1, [f...  9.11 us
    pallas_call x1, Pallas kernels, hard(): call(functools.partial(hard_kernel, reps, cap, temper), 'hard', levels +...  9.04 us
    pallas_call x2, Pallas kernels, final(): pl.pallas_call(functools.partial(final_kernel, temper), grid_spec=pltpu.P...  5.91 us
    all_to_all x1, starting transfers between devices, shards(): parts = lax.all_to_all(part, 'rep', split_axis=0, concat_axis=0, tiled=True)  5.79 us
  transfers between devices with their start and end apart: 27, of which 10 were waited for; matrix products, arithmetic and copies ran while one was open for 2% of the time, Pallas kernels for 31%

profile of v10, /device:TPU:0, one launch (start us, length us, event | category | flops | bytes accessed | tf_op | source)
XLA Modules:
  0.0 153.8 jit_solution(8272993584308977156)
XLA Ops:
  7.2 0.7 all-gather.2.cloned.1.call-update
  7.9 0.7 convert_bitcast_fusion
  8.6 1.1 fusion.7
  9.8 3.2 %collective-permute-start.5 = (bf16[272,512]{1,0:T(8,128)(2,1)S(1)}, bf16[272,512]{1,0:T(8,128)(2,1)S(1)}, u32[]{:S(2)}, u32[]{:S(2)}) collective-permute-start(bf16[272,512]{1,0:T(8,128)(2,1)S(1)} %get-tuple-element.87.refs_4_), channel_id=1, source_target_pairs={{0,3},{1,0},{2,1},{3,2},{4,7},{5,4},{6,5},{7,6},{8,11},{9,8},{10,9... | collective-permute-start | bytes 835592 | tf_op jit(solution)/shard_map/ppermute | solution.py:461
  13.6 1.0 collective-permute-start.3
  14.5 2.8 %collective-permute-start.2 = (bf16[272,512]{1,0:T(8,128)(2,1)S(1)}, bf16[272,512]{1,0:T(8,128)(2,1)S(1)}, u32[]{:S(2)}, u32[]{:S(2)}) collective-permute-start(bf16[272,512]{1,0:T(8,128)(2,1)S(1)} %get-tuple-element.88.refs_0_), channel_id=1, source_target_pairs={{0,12},{1,13},{2,14},{3,15},{4,0},{5,1},{6,2},{7,3},{8,4},{9,5},{1... | collective-permute-start | bytes 835592 | tf_op jit(solution)/shard_map/ppermute | solution.py:461
  17.3 0.8 collective-permute-start.1
  18.1 6.7 %collective-permute-done.5.refs_7_ = bf16[272,512]{1,0:T(8,128)(2,1)S(1)} collective-permute-done((bf16[272,512]{1,0:T(8,128)(2,1)S(1)}, bf16[272,512]{1,0:T(8,128)(2,1)S(1)}, u32[]{:S(2)}, u32[]{:S(2)}) %collective-permute-start.5) | collective-permute-done | bytes 278560 | tf_op jit(solution)/shard_map/ppermute | solution.py:461
  24.8 1.5 collective-permute-start
  26.3 0.7 pad_add_fusion.place_ref
  27.0 1.6 %collective-permute-done.3.refs_5_ = bf16[272,512]{1,0:T(8,128)(2,1)S(1)} collective-permute-done((bf16[272,512]{1,0:T(8,128)(2,1)S(1)}, bf16[272,512]{1,0:T(8,128)(2,1)S(1)}, u32[]{:S(2)}, u32[]{:S(2)}) %collective-permute-start.3) | collective-permute-done | bytes 278560 | tf_op jit(solution)/shard_map/ppermute | solution.py:461
  28.5 0.7 copy-done.5
  29.4 0.7 copy-done.7
  30.1 3.9 %collective-permute-done.refs_1_ = bf16[272,512]{1,0:T(8,128)(2,1)} collective-permute-done((bf16[272,512]{1,0:T(8,128)(2,1)S(1)}, bf16[272,512]{1,0:T(8,128)(2,1)}, u32[]{:S(2)}, u32[]{:S(2)}) %collective-permute-start) | collective-permute-done | bytes 278560 | tf_op jit(solution)/shard_map/ppermute | solution.py:461
  34.0 4.5 %mid.4 = (bf16[528,512]{1,0:T(8,128)(2,1)}, bf16[528,512]{1,0:T(8,128)(2,1)}, bf16[32,256]{1,0:T(8,128)(2,1)}, bf16[32,256]{1,0:T(8,128)(2,1)}) custom-call(s32[3]{0:T(128)} %pad_add_fusion.place_ref, bf16[272,512]{1,0:T(8,128)(2,1)} %copy-done.1, bf16[272,512]{1,0:T(8,128)(2,1)} %collective-permute-done.refs_1_, bf16[272,512]{1,0:T(8,128)(2,1)} %copy-done.7, ...), custom_call_target="tpu_custom_call" | custom-call | flops 1048576 | bytes 65536 | tf_op jit(solution)/shard_map/mid/pallas_call | solution.py:129
  38.9 0.7 collective-permute-start.10
  39.6 4.5 %mid.5 = (bf16[528,512]{1,0:T(8,128)(2,1)}, bf16[528,512]{1,0:T(8,128)(2,1)}, bf16[32,256]{1,0:T(8,128)(2,1)}, bf16[32,256]{1,0:T(8,128)(2,1)}) custom-call(s32[3]{0:T(128)} %pad_add_fusion.place_ref, bf16[272,512]{1,0:T(8,128)(2,1)} %copy-done.1, bf16[272,512]{1,0:T(8,128)(2,1)} %collective-permute-done.refs_1_, bf16[272,512]{1,0:T(8,128)(2,1)} %copy-done.7, ...), custom_call_target="tpu_custom_call" | custom-call | flops 1048576 | bytes 65536 | tf_op jit(solution)/shard_map/mid/pallas_call | solution.py:129
  44.1 4.8 %collective-permute-start.6 = (bf16[528,512]{1,0:T(8,128)(2,1)}, bf16[528,512]{1,0:T(8,128)(2,1)}, u32[]{:S(2)}, u32[]{:S(2)}) collective-permute-start(bf16[528,512]{1,0:T(8,128)(2,1)} %get-tuple-element.48), channel_id=1, source_target_pairs={{0,1},{1,2},{2,3},{3,0},{4,5},{5,6},{6,7},{7,4},{8,9},{9,10},{10,1... | collective-permute-start | bytes 1622024 | tf_op jit(solution)/shard_map/ppermute | solution.py:461
  48.9 0.6 collective-permute-start.9
  49.6 4.4 %mid.6 = (bf16[528,512]{1,0:T(8,128)(2,1)}, bf16[528,512]{1,0:T(8,128)(2,1)}, bf16[32,256]{1,0:T(8,128)(2,1)}, bf16[32,256]{1,0:T(8,128)(2,1)}) custom-call(s32[3]{0:T(128)} %pad_add_fusion.place_ref, bf16[272,512]{1,0:T(8,128)(2,1)} %copy-done.1, bf16[272,512]{1,0:T(8,128)(2,1)} %collective-permute-done.refs_1_, bf16[272,512]{1,0:T(8,128)(2,1)} %copy-done.7, ...), custom_call_target="tpu_custom_call" | custom-call | flops 1048576 | bytes 65536 | tf_op jit(solution)/shard_map/mid/pallas_call | solution.py:129
  54.0 1.5 collective-permute-done.7.refs_2_.refs_10_
  55.5 1.2 collective-permute-start.11
  56.7 4.4 %mid.7 = (bf16[528,512]{1,0:T(8,128)(2,1)}, bf16[528,512]{1,0:T(8,128)(2,1)}, bf16[32,256]{1,0:T(8,128)(2,1)}, bf16[32,256]{1,0:T(8,128)(2,1)}) custom-call(s32[3]{0:T(128)} %pad_add_fusion.place_ref, bf16[272,512]{1,0:T(8,128)(2,1)} %copy-done.1, bf16[272,512]{1,0:T(8,128)(2,1)} %collective-permute-done.refs_1_, bf16[272,512]{1,0:T(8,128)(2,1)} %copy-done.7, ...), custom_call_target="tpu_custom_call" | custom-call | flops 1048576 | bytes 65536 | tf_op jit(solution)/shard_map/mid/pallas_call | solution.py:129
  61.2 5.3 %inside.1 = (f32[1,256]{1,0:T(1,128)}, f32[2048,256]{1,0:T(8,128)}) custom-call(s32[3]{0:T(128)} %pad_add_fusion.place_ref, bf16[2048,1024]{1,0:T(8,128)(2,1)} %all-gather.2.cloned.1.call-done.p_ref.refs_12_.refs_8_, bf16[256,1024]{1,0:T(8,128)(2,1)} %refs_9_.1), custom_call_target="tpu_custom_call" | custom-call | flops 1048576 | bytes 65536 | tf_op jit(solution)/shard_map/inside/pallas_call | solution.py:160
  66.5 9.0 %hard.1 = (bf16[544,512]{1,0:T(8,128)(2,1)}, bf16[544,512]{1,0:T(8,128)(2,1)}, bf16[544,512]{1,0:T(8,128)(2,1)}, bf16[544,512]{1,0:T(8,128)(2,1)}, bf16[544,512]...) custom-call(s32[3]{0:T(128)} %pad_add_fusion.place_ref, ...), custom_call_target="tpu_custom_call" | custom-call | flops 1048576 | bytes 65536 | tf_op jit(solution)/shard_map/hard/pallas_call | solution.py:290
  75.5 5.8 %all-to-all-start = ((f32[16,16,256]{2,1,0:T(8,128)}), f32[16,16,256]{2,1,0:T(8,128)S(1)}, u32[]{:S(2)}, u32[]{:S(2)}) async-start(f32[16,16,256]{2,1,0:T(8,128)} %get-tuple-element.58), calls=%async_computation | async-start | bytes 524288 | tf_op jit(solution)/shard_map/all_to_all | solution.py:498
  81.4 3.4 %collective-permute-start.18 = (bf16[544,512]{1,0:T(8,128)(2,1)}, bf16[544,512]{1,0:T(8,128)(2,1)S(1)}, u32[]{:S(2)}, u32[]{:S(2)}) collective-permute-start(bf16[544,512]{1,0:T(8,128)(2,1)} %get-tuple-element.77), channel_id=1, source_target_pairs={{0,3},{1,0},{2,1},{3,2},{4,7},{5,4},{6,5},{7,6},{8,11},{9,8},{10,9... | collective-permute-start | bytes 1671176 | tf_op jit(solution)/shard_map/ppermute | solution.py:461
  84.8 0.9 collective-permute-start.19
  85.6 0.9 collective-permute-start.20
  86.5 2.7 %collective-permute-start.12 = (bf16[544,512]{1,0:T(8,128)(2,1)}, bf16[544,512]{1,0:T(8,128)(2,1)}, u32[]{:S(2)}, u32[]{:S(2)}) collective-permute-start(bf16[544,512]{1,0:T(8,128)(2,1)} %get-tuple-element.67), channel_id=1, source_target_pairs={{0,12},{1,13},{2,14},{3,15},{4,0},{5,1},{6,2},{7,3},{8,4},{9,5},{1... | collective-permute-start | bytes 1671176 | tf_op jit(solution)/shard_map/ppermute | solution.py:461
  89.2 0.9 collective-permute-start.13
  90.7 10.0 %column.1 = (bf16[2048,1024]{1,0:T(8,128)(2,1)}, f32[256,1024]{1,0:T(8,128)}, f32[1,256]{1,0:T(1,128)}, f32[8,128]{1,0:T(8,128)}) custom-call(s32[3]{0:T(128)} %pad_add_fusion.place_ref, s32[16,256]{1,0:T(8,128)} %get-tuple-element.56.code_ref, f32[8,256]{1,0:T(8,128)} %get-tuple-element.57.hs_ref, f32[16,256]{1,0:T(8,128)} %log_add_fusion.lt_ref, ...), custom_call_target="tpu_custom_call" | custom-call | flops 1048576 | bytes 65536 | tf_op jit(solution)/shard_map/column/pallas_call | solution.py:370
  100.8 8.1 %collective-permute-done.18.refs_5_ = bf16[544,512]{1,0:T(8,128)(2,1)S(1)} collective-permute-done((bf16[544,512]{1,0:T(8,128)(2,1)}, bf16[544,512]{1,0:T(8,128)(2,1)S(1)}, u32[]{:S(2)}, u32[]{:S(2)}) %collective-permute-start.18) | collective-permute-done | bytes 557088 | tf_op jit(solution)/shard_map/ppermute | solution.py:461
  108.9 1.1 collective-permute-start.14
  110.0 2.1 %collective-permute-done.20.refs_7_ = bf16[544,512]{1,0:T(8,128)(2,1)} collective-permute-done((bf16[544,512]{1,0:T(8,128)(2,1)}, bf16[544,512]{1,0:T(8,128)(2,1)}, u32[]{:S(2)}, u32[]{:S(2)}) %collective-permute-start.20) | collective-permute-done | bytes 557088 | tf_op jit(solution)/shard_map/ppermute | solution.py:461
  112.1 4.6 %reduce.3 = (f32[256,512]{1,0:T(8,128)}, bf16[256,512]{1,0:T(8,128)(2,1)}, bf16[256,512]{1,0:T(8,128)(2,1)}, bf16[256,512]{1,0:T(8,128)(2,1)}) custom-call(s32[3]{0:T(128)} %pad_add_fusion.place_ref, f32[16,256]{1,0:T(8,128)} %log_add_fusion.lt_ref, bf16[32,256]{1,0:T(8,128)(2,1)} %get-tuple-element.75.refs_0_, ...), custom_call_target="tpu_custom_call" | custom-call | flops 549755813888 | bytes 65536 | tf_op jit(solution)/shard_map/reduce/pallas_call | solution.py:419
  116.7 2.3 %collective-permute-start.21 = (bf16[256,512]{1,0:T(8,128)(2,1)}, bf16[256,512]{1,0:T(8,128)(2,1)}, u32[]{:S(2)}, u32[]{:S(2)}) collective-permute-start(bf16[256,512]{1,0:T(8,128)(2,1)} %get-tuple-element.81), channel_id=1, source_target_pairs={{0,12},{1,13},{2,14},{3,15},{4,0},{5,1},{6,2},{7,3},{8,4},{9,5},{1... | collective-permute-start | bytes 786440 | tf_op jit(solution)/shard_map/ppermute | solution.py:461
  119.0 0.9 collective-permute-start.22
  119.8 0.8 collective-permute-start.23
  120.6 4.6 %reduce.2 = (f32[256,512]{1,0:T(8,128)}, bf16[256,512]{1,0:T(8,128)(2,1)}, bf16[256,512]{1,0:T(8,128)(2,1)}, bf16[256,512]{1,0:T(8,128)(2,1)}) custom-call(s32[3]{0:T(128)} %pad_add_fusion.place_ref, f32[16,256]{1,0:T(8,128)} %log_add_fusion.lt_ref, bf16[32,256]{1,0:T(8,128)(2,1)} %get-tuple-element.62.refs_0_, bf16[32,256]{1,0:T(8,128)(2,1)} %get-tuple-element.63.refs_1_, ...), custom_call_target="tpu_custom_call" | custom-call | flops 549755813888 | bytes 65536 | tf_op jit(solution)/shard_map/reduce/pallas_call | solution.py:419
  125.2 7.6 %collective-permute-start.15 = (bf16[256,512]{1,0:T(8,128)(2,1)}, bf16[256,512]{1,0:T(8,128)(2,1)S(1)}, u32[]{:S(2)}, u32[]{:S(2)}) collective-permute-start(bf16[256,512]{1,0:T(8,128)(2,1)} %get-tuple-element.72), channel_id=1, source_target_pairs={{0,3},{1,0},{2,1},{3,2},{4,7},{5,4},{6,5},{7,6},{8,11},{9,8},{10,9... | collective-permute-start | bytes 786440 | tf_op jit(solution)/shard_map/ppermute | solution.py:461
  132.7 0.9 collective-permute-start.17
  134.2 3.0 %final.2.refs_4_ = bf16[256,1024]{1,0:T(8,128)(2,1)} custom-call(s32[3]{0:T(128)} %pad_add_fusion.place_ref, f32[256,1024]{1,0:T(8,128)} %get-tuple-element.61.gq_ref, f32[256,512]{1,0:T(8,128)} %get-tuple-element.80.refs_0_, bf16[256,512]{1,0:T(8,128)(2,1)} %collective-permute-done.21.refs_1_, bf16[256,512]{1,0:T(8,128)(2,1)} %collective-permute-done.22.refs_2_, ...), custom_call_target="tpu_custom_call" | custom-call | flops 1048576 | bytes 65536 | tf_op jit(solution)/shard_map/final/pallas_call | solution.py:439
  137.2 2.9 %collective-permute-done.15.refs_1_ = bf16[256,512]{1,0:T(8,128)(2,1)S(1)} collective-permute-done((bf16[256,512]{1,0:T(8,128)(2,1)}, bf16[256,512]{1,0:T(8,128)(2,1)S(1)}, u32[]{:S(2)}, u32[]{:S(2)}) %collective-permute-start.15) | collective-permute-done | bytes 262176 | tf_op jit(solution)/shard_map/ppermute | solution.py:461
  140.1 0.8 collective-permute-done.16.refs_2_
  140.9 2.4 %collective-permute-done.17.refs_3_ = bf16[256,512]{1,0:T(8,128)(2,1)S(1)} collective-permute-done((bf16[256,512]{1,0:T(8,128)(2,1)}, bf16[256,512]{1,0:T(8,128)(2,1)S(1)}, u32[]{:S(2)}, u32[]{:S(2)}) %collective-permute-start.17) | collective-permute-done | bytes 262176 | tf_op jit(solution)/shard_map/ppermute | solution.py:461
  143.4 0.7 copy-done.10
  144.1 2.9 %final.3 = bf16[256,1024]{1,0:T(8,128)(2,1)} custom-call(s32[3]{0:T(128)} %pad_add_fusion.place_ref, f32[256,1024]{1,0:T(8,128)} %get-tuple-element.61.gq_ref, f32[256,512]{1,0:T(8,128)} %get-tuple-element.71.refs_0_, bf16[256,512]{1,0:T(8,128)(2,1)} %copy-done.8, bf16[256,512]{1,0:T(8,128)(2,1)} %copy-done.9, ...), custom_call_target="tpu_custom_call", output_to_operand_aliasing={{}: (6, {})} | custom-call | flops 1048576 | bytes 65536 | tf_op jit(solution)/shard_map/final/pallas_call | solution.py:439
  (51 shorter events, 2.6 us)
Async XLA Ops:
  7.2 54.0 %all-gather.2.cloned.1.call-start = ((), (), s32[]{:S(2)}) async-start(), calls=%async_computation.2 | async-start | bytes 4718592 | tf_op jit(solution)/shard_map/all_gather | solution.py:482
  9.7 24.3 %copy-start = (bf16[272,512]{1,0:T(8,128)(2,1)}, bf16[272,512]{1,0:T(8,128)(2,1)S(1)}, u32[]{:S(2)}) copy-start(bf16[272,512]{1,0:T(8,128)(2,1)S(1)} %get-tuple-element.87.refs_4_) | copy-start | bytes 835588
  9.8 24.2 %copy-start.1 = (bf16[272,512]{1,0:T(8,128)(2,1)}, bf16[272,512]{1,0:T(8,128)(2,1)S(1)}, u32[]{:S(2)}) copy-start(bf16[272,512]{1,0:T(8,128)(2,1)S(1)} %get-tuple-element.88.refs_0_) | copy-start | bytes 835588
  9.8 15.1 %collective-permute-start.5 = (bf16[272,512]{1,0:T(8,128)(2,1)S(1)}, bf16[272,512]{1,0:T(8,128)(2,1)S(1)}, u32[]{:S(2)}, u32[]{:S(2)}) collective-permute-start(bf16[272,512]{1,0:T(8,128)(2,1)S(1)} %get-tuple-element.87.refs_4_), channel_id=1, source_target_pairs={{0,3},{1,0},{2,1},{3,2},{4,7},{5,4},{6,5},{7,6},{8,11},{9,8},{10,9... | collective-permute-start | bytes 835592 | tf_op jit(solution)/shard_map/ppermute | solution.py:461
  12.9 14.0 %collective-permute-start.4 = (bf16[272,512]{1,0:T(8,128)(2,1)S(1)}, bf16[272,512]{1,0:T(8,128)(2,1)S(1)}, u32[]{:S(2)}, u32[]{:S(2)}) collective-permute-start(bf16[272,512]{1,0:T(8,128)(2,1)S(1)} %get-tuple-element.87.refs_4_), channel_id=1, source_target_pairs={{0,2},{1,3},{2,0},{3,1},{4,6},{5,7},{6,4},{7,5},{8,10},{9,11},{10,... | collective-permute-start | bytes 835592 | tf_op jit(solution)/shard_map/ppermute | solution.py:461
  13.6 15.0 %collective-permute-start.3 = (bf16[272,512]{1,0:T(8,128)(2,1)S(1)}, bf16[272,512]{1,0:T(8,128)(2,1)S(1)}, u32[]{:S(2)}, u32[]{:S(2)}) collective-permute-start(bf16[272,512]{1,0:T(8,128)(2,1)S(1)} %get-tuple-element.87.refs_4_), channel_id=1, source_target_pairs={{0,1},{1,2},{2,3},{3,0},{4,5},{5,6},{6,7},{7,4},{8,9},{9,10},{10,1... | collective-permute-start | bytes 835592 | tf_op jit(solution)/shard_map/ppermute | solution.py:461
  14.5 14.0 %collective-permute-start.2 = (bf16[272,512]{1,0:T(8,128)(2,1)S(1)}, bf16[272,512]{1,0:T(8,128)(2,1)S(1)}, u32[]{:S(2)}, u32[]{:S(2)}) collective-permute-start(bf16[272,512]{1,0:T(8,128)(2,1)S(1)} %get-tuple-element.88.refs_0_), channel_id=1, source_target_pairs={{0,12},{1,13},{2,14},{3,15},{4,0},{5,1},{6,2},{7,3},{8,4},{9,5},{1... | collective-permute-start | bytes 835592 | tf_op jit(solution)/shard_map/ppermute | solution.py:461
  17.3 11.2 %collective-permute-start.1 = (bf16[272,512]{1,0:T(8,128)(2,1)S(1)}, bf16[272,512]{1,0:T(8,128)(2,1)S(1)}, u32[]{:S(2)}, u32[]{:S(2)}) collective-permute-start(bf16[272,512]{1,0:T(8,128)(2,1)S(1)} %get-tuple-element.88.refs_0_), channel_id=1, source_target_pairs={{0,8},{1,9},{2,10},{3,11},{4,12},{5,13},{6,14},{7,15},{8,0},{9,1},... | collective-permute-start | bytes 835592 | tf_op jit(solution)/shard_map/ppermute | solution.py:461
  24.8 9.2 %copy-start.3 = (bf16[272,512]{1,0:T(8,128)(2,1)}, bf16[272,512]{1,0:T(8,128)(2,1)S(1)}, u32[]{:S(2)}) copy-start(bf16[272,512]{1,0:T(8,128)(2,1)S(1)} %collective-permute-done.5.refs_7_) | copy-start | bytes 835588
  24.8 9.2 %collective-permute-start = (bf16[272,512]{1,0:T(8,128)(2,1)S(1)}, bf16[272,512]{1,0:T(8,128)(2,1)}, u32[]{:S(2)}, u32[]{:S(2)}) collective-permute-start(bf16[272,512]{1,0:T(8,128)(2,1)S(1)} %get-tuple-element.88.refs_0_), channel_id=1, source_target_pairs={{0,4},{1,5},{2,6},{3,7},{4,8},{5,9},{6,10},{7,11},{8,12},{9,13},{1... | collective-permute-start | bytes 835592 | tf_op jit(solution)/shard_map/ppermute | solution.py:461
  27.0 1.6 %copy-start.4 = (bf16[272,512]{1,0:T(8,128)(2,1)}, bf16[272,512]{1,0:T(8,128)(2,1)S(1)}, u32[]{:S(2)}) copy-start(bf16[272,512]{1,0:T(8,128)(2,1)S(1)} %collective-permute-done.4.refs_6_) | copy-start | bytes 835588
  28.5 0.7 copy-start.5
  28.5 0.8 copy-start.6
  29.3 0.7 copy-start.7
  38.5 17.0 %collective-permute-start.7 = (bf16[528,512]{1,0:T(8,128)(2,1)}, bf16[528,512]{1,0:T(8,128)(2,1)S(1)}, u32[]{:S(2)}, u32[]{:S(2)}) collective-permute-start(bf16[528,512]{1,0:T(8,128)(2,1)} %get-tuple-element.49), channel_id=1, source_target_pairs={{0,2},{1,3},{2,0},{3,1},{4,6},{5,7},{6,4},{7,5},{8,10},{9,11},{10,... | collective-permute-start | bytes 1622024 | tf_op jit(solution)/shard_map/ppermute | solution.py:461
  38.9 27.5 %collective-permute-start.10 = (bf16[528,512]{1,0:T(8,128)(2,1)}, bf16[528,512]{1,0:T(8,128)(2,1)}, u32[]{:S(2)}, u32[]{:S(2)}) collective-permute-start(bf16[528,512]{1,0:T(8,128)(2,1)} %get-tuple-element.53), channel_id=1, source_target_pairs={{0,8},{1,9},{2,10},{3,11},{4,12},{5,13},{6,14},{7,15},{8,0},{9,1},... | collective-permute-start | bytes 1622024 | tf_op jit(solution)/shard_map/ppermute | solution.py:461
  44.1 22.3 %collective-permute-start.6 = (bf16[528,512]{1,0:T(8,128)(2,1)}, bf16[528,512]{1,0:T(8,128)(2,1)}, u32[]{:S(2)}, u32[]{:S(2)}) collective-permute-start(bf16[528,512]{1,0:T(8,128)(2,1)} %get-tuple-element.48), channel_id=1, source_target_pairs={{0,1},{1,2},{2,3},{3,0},{4,5},{5,6},{6,7},{7,4},{8,9},{9,10},{10,1... | collective-permute-start | bytes 1622024 | tf_op jit(solution)/shard_map/ppermute | solution.py:461
  48.9 17.5 %collective-permute-start.9 = (bf16[528,512]{1,0:T(8,128)(2,1)}, bf16[528,512]{1,0:T(8,128)(2,1)}, u32[]{:S(2)}, u32[]{:S(2)}) collective-permute-start(bf16[528,512]{1,0:T(8,128)(2,1)} %get-tuple-element.52), channel_id=1, source_target_pairs={{0,4},{1,5},{2,6},{3,7},{4,8},{5,9},{6,10},{7,11},{8,12},{9,13},{1... | collective-permute-start | bytes 1622024 | tf_op jit(solution)/shard_map/ppermute | solution.py:461
  54.0 12.4 %collective-permute-start.8 = (bf16[528,512]{1,0:T(8,128)(2,1)}, bf16[528,512]{1,0:T(8,128)(2,1)}, u32[]{:S(2)}, u32[]{:S(2)}) collective-permute-start(bf16[528,512]{1,0:T(8,128)(2,1)} %get-tuple-element.50), channel_id=1, source_target_pairs={{0,3},{1,0},{2,1},{3,2},{4,7},{5,4},{6,5},{7,6},{8,11},{9,8},{10,9... | collective-permute-start | bytes 1622024 | tf_op jit(solution)/shard_map/ppermute | solution.py:461
  55.5 11.0 %copy-start.2 = (bf16[528,512]{1,0:T(8,128)(2,1)}, bf16[528,512]{1,0:T(8,128)(2,1)S(1)}, u32[]{:S(2)}) copy-start(bf16[528,512]{1,0:T(8,128)(2,1)S(1)} %collective-permute-done.7.refs_2_.refs_10_) | copy-start | bytes 1622020
  55.5 11.0 %collective-permute-start.11 = (bf16[528,512]{1,0:T(8,128)(2,1)}, bf16[528,512]{1,0:T(8,128)(2,1)}, u32[]{:S(2)}, u32[]{:S(2)}) collective-permute-start(bf16[528,512]{1,0:T(8,128)(2,1)} %get-tuple-element.54), channel_id=1, source_target_pairs={{0,12},{1,13},{2,14},{3,15},{4,0},{5,1},{6,2},{7,3},{8,4},{9,5},{1... | collective-permute-start | bytes 1622024 | tf_op jit(solution)/shard_map/ppermute | solution.py:461
  75.5 14.5 %all-to-all-start = ((f32[16,16,256]{2,1,0:T(8,128)}), f32[16,16,256]{2,1,0:T(8,128)S(1)}, u32[]{:S(2)}, u32[]{:S(2)}) async-start(f32[16,16,256]{2,1,0:T(8,128)} %get-tuple-element.58), calls=%async_computation | async-start | bytes 524288 | tf_op jit(solution)/shard_map/all_to_all | solution.py:498
  81.3 65.7 %reduce-scatter.2.cloned.1.call-start = ((), (), s32[]{:S(2)}) async-start(), calls=%async_computation.3 | async-start | bytes 4718592 | tf_op jit(solution)/shard_map/reduce_scatter | solution.py:505
  81.4 27.5 %collective-permute-start.18 = (bf16[544,512]{1,0:T(8,128)(2,1)}, bf16[544,512]{1,0:T(8,128)(2,1)S(1)}, u32[]{:S(2)}, u32[]{:S(2)}) collective-permute-start(bf16[544,512]{1,0:T(8,128)(2,1)} %get-tuple-element.77), channel_id=1, source_target_pairs={{0,3},{1,0},{2,1},{3,2},{4,7},{5,4},{6,5},{7,6},{8,11},{9,8},{10,9... | collective-permute-start | bytes 1671176 | tf_op jit(solution)/shard_map/ppermute | solution.py:461
  84.8 25.3 %collective-permute-start.19 = (bf16[544,512]{1,0:T(8,128)(2,1)}, bf16[544,512]{1,0:T(8,128)(2,1)}, u32[]{:S(2)}, u32[]{:S(2)}) collective-permute-start(bf16[544,512]{1,0:T(8,128)(2,1)} %get-tuple-element.78), channel_id=1, source_target_pairs={{0,2},{1,3},{2,0},{3,1},{4,6},{5,7},{6,4},{7,5},{8,10},{9,11},{10,... | collective-permute-start | bytes 1671176 | tf_op jit(solution)/shard_map/ppermute | solution.py:461
  85.6 26.5 %collective-permute-start.20 = (bf16[544,512]{1,0:T(8,128)(2,1)}, bf16[544,512]{1,0:T(8,128)(2,1)}, u32[]{:S(2)}, u32[]{:S(2)}) collective-permute-start(bf16[544,512]{1,0:T(8,128)(2,1)} %get-tuple-element.79), channel_id=1, source_target_pairs={{0,1},{1,2},{2,3},{3,0},{4,5},{5,6},{6,7},{7,4},{8,9},{9,10},{10,1... | collective-permute-start | bytes 1671176 | tf_op jit(solution)/shard_map/ppermute | solution.py:461
  86.5 33.4 %collective-permute-start.12 = (bf16[544,512]{1,0:T(8,128)(2,1)}, bf16[544,512]{1,0:T(8,128)(2,1)}, u32[]{:S(2)}, u32[]{:S(2)}) collective-permute-start(bf16[544,512]{1,0:T(8,128)(2,1)} %get-tuple-element.67), channel_id=1, source_target_pairs={{0,12},{1,13},{2,14},{3,15},{4,0},{5,1},{6,2},{7,3},{8,4},{9,5},{1... | collective-permute-start | bytes 1671176 | tf_op jit(solution)/shard_map/ppermute | solution.py:461
  89.2 31.5 %collective-permute-start.13 = (bf16[544,512]{1,0:T(8,128)(2,1)}, bf16[544,512]{1,0:T(8,128)(2,1)}, u32[]{:S(2)}, u32[]{:S(2)}) collective-permute-start(bf16[544,512]{1,0:T(8,128)(2,1)} %get-tuple-element.68), channel_id=1, source_target_pairs={{0,8},{1,9},{2,10},{3,11},{4,12},{5,13},{6,14},{7,15},{8,0},{9,1},... | collective-permute-start | bytes 1671176 | tf_op jit(solution)/shard_map/ppermute | solution.py:461
  108.9 3.3 %copy-start.11 = (bf16[544,512]{1,0:T(8,128)(2,1)}, bf16[544,512]{1,0:T(8,128)(2,1)S(1)}, u32[]{:S(2)}) copy-start(bf16[544,512]{1,0:T(8,128)(2,1)S(1)} %collective-permute-done.18.refs_5_) | copy-start | bytes 1671172
  108.9 11.8 %collective-permute-start.14 = (bf16[544,512]{1,0:T(8,128)(2,1)}, bf16[544,512]{1,0:T(8,128)(2,1)}, u32[]{:S(2)}, u32[]{:S(2)}) collective-permute-start(bf16[544,512]{1,0:T(8,128)(2,1)} %get-tuple-element.69), channel_id=1, source_target_pairs={{0,4},{1,5},{2,6},{3,7},{4,8},{5,9},{6,10},{7,11},{8,12},{9,13},{1... | collective-permute-start | bytes 1671176 | tf_op jit(solution)/shard_map/ppermute | solution.py:461
  116.7 16.1 %collective-permute-start.21 = (bf16[256,512]{1,0:T(8,128)(2,1)}, bf16[256,512]{1,0:T(8,128)(2,1)}, u32[]{:S(2)}, u32[]{:S(2)}) collective-permute-start(bf16[256,512]{1,0:T(8,128)(2,1)} %get-tuple-element.81), channel_id=1, source_target_pairs={{0,12},{1,13},{2,14},{3,15},{4,0},{5,1},{6,2},{7,3},{8,4},{9,5},{1... | collective-permute-start | bytes 786440 | tf_op jit(solution)/shard_map/ppermute | solution.py:461
  119.0 14.7 %collective-permute-start.22 = (bf16[256,512]{1,0:T(8,128)(2,1)}, bf16[256,512]{1,0:T(8,128)(2,1)}, u32[]{:S(2)}, u32[]{:S(2)}) collective-permute-start(bf16[256,512]{1,0:T(8,128)(2,1)} %get-tuple-element.82), channel_id=1, source_target_pairs={{0,8},{1,9},{2,10},{3,11},{4,12},{5,13},{6,14},{7,15},{8,0},{9,1},... | collective-permute-start | bytes 786440 | tf_op jit(solution)/shard_map/ppermute | solution.py:461
  119.8 14.4 %collective-permute-start.23 = (bf16[256,512]{1,0:T(8,128)(2,1)}, bf16[256,512]{1,0:T(8,128)(2,1)}, u32[]{:S(2)}, u32[]{:S(2)}) collective-permute-start(bf16[256,512]{1,0:T(8,128)(2,1)} %get-tuple-element.83), channel_id=1, source_target_pairs={{0,4},{1,5},{2,6},{3,7},{4,8},{5,9},{6,10},{7,11},{8,12},{9,13},{1... | collective-permute-start | bytes 786440 | tf_op jit(solution)/shard_map/ppermute | solution.py:461
  125.2 15.0 %collective-permute-start.15 = (bf16[256,512]{1,0:T(8,128)(2,1)}, bf16[256,512]{1,0:T(8,128)(2,1)S(1)}, u32[]{:S(2)}, u32[]{:S(2)}) collective-permute-start(bf16[256,512]{1,0:T(8,128)(2,1)} %get-tuple-element.72), channel_id=1, source_target_pairs={{0,3},{1,0},{2,1},{3,2},{4,7},{5,4},{6,5},{7,6},{8,11},{9,8},{10,9... | collective-permute-start | bytes 786440 | tf_op jit(solution)/shard_map/ppermute | solution.py:461
  132.7 8.2 %collective-permute-start.16 = (bf16[256,512]{1,0:T(8,128)(2,1)}, bf16[256,512]{1,0:T(8,128)(2,1)S(1)}, u32[]{:S(2)}, u32[]{:S(2)}) collective-permute-start(bf16[256,512]{1,0:T(8,128)(2,1)} %get-tuple-element.73), channel_id=1, source_target_pairs={{0,2},{1,3},{2,0},{3,1},{4,6},{5,7},{6,4},{7,5},{8,10},{9,11},{10,... | collective-permute-start | bytes 786440 | tf_op jit(solution)/shard_map/ppermute | solution.py:461
  132.7 10.6 %collective-permute-start.17 = (bf16[256,512]{1,0:T(8,128)(2,1)}, bf16[256,512]{1,0:T(8,128)(2,1)S(1)}, u32[]{:S(2)}, u32[]{:S(2)}) collective-permute-start(bf16[256,512]{1,0:T(8,128)(2,1)} %get-tuple-element.74), channel_id=1, source_target_pairs={{0,1},{1,2},{2,3},{3,0},{4,5},{5,6},{6,7},{7,4},{8,9},{9,10},{10,1... | collective-permute-start | bytes 786440 | tf_op jit(solution)/shard_map/ppermute | solution.py:461
  140.1 3.2 %copy-start.8 = (bf16[256,512]{1,0:T(8,128)(2,1)}, bf16[256,512]{1,0:T(8,128)(2,1)S(1)}, u32[]{:S(2)}) copy-start(bf16[256,512]{1,0:T(8,128)(2,1)S(1)} %collective-permute-done.15.refs_1_) | copy-start | bytes 786436
  140.9 2.4 %copy-start.9 = (bf16[256,512]{1,0:T(8,128)(2,1)}, bf16[256,512]{1,0:T(8,128)(2,1)S(1)}, u32[]{:S(2)}) copy-start(bf16[256,512]{1,0:T(8,128)(2,1)S(1)} %collective-permute-done.16.refs_2_) | copy-start | bytes 786436
  143.3 0.7 copy-start.10
Sparse Core Ops, SparseCore 0:
  9.7 34.7 all-gather.1
  100.9 40.3 reduce-scatter.1

commit v11 on v10

--- a/solution.py
+++ b/solution.py
@@ -381,35 +381,39 @@
 
 
 def reduce_kernel(half, cap, groups, place_ref, lt_ref, *refs):
-    ranks, rows, outs = refs[0:4], refs[4:8], refs[9:13]
+    ranks, rows, outs, weight_ref = refs[0:4], refs[4:8], refs[9:13], refs[13]
     toks = lt_ref.shape[1]
     slots = groups * cap
     reps = lt_ref.shape[0]
-    shape = (SIDE * slots, 4 * groups)
-    group = iota(shape, 0) // cap % groups
-    parts = (iota(shape, 1) % groups == group) & (iota(shape, 1) < 3 * groups)
-    parts = parts.astype(BF16)
-    log_rows = jnp.concatenate(
-        [jnp.broadcast_to(own_row(lt_ref, source_of(place_ref, half, s)), (slots, toks))
-         for s in range(SIDE)], axis=0
-    )
-    weights = []
-    for line in range(SIDE):
-        scores = mm(parts, rows[line][slots * SIDE :, : reps * cap])
-        slot, lane = iota(scores.shape, 0), iota(scores.shape, 1)
-        s = slot // slots
-        block = s * SIDE + line if half == 0 else line * SIDE + s
-        hs = jnp.sum(
-            jnp.where(lane == block * cap + slot % cap, scores, 0.0), axis=1, keepdims=True
+    @pl.when(pl.program_id(0) == 0)
+    def _():
+        shape = (SIDE * slots, 4 * groups)
+        group = iota(shape, 0) // cap % groups
+        parts = (iota(shape, 1) % groups == group) & (iota(shape, 1) < 3 * groups)
+        parts = parts.astype(BF16)
+        log_rows = jnp.concatenate(
+            [jnp.broadcast_to(own_row(lt_ref, source_of(place_ref, half, s)), (slots, toks))
+             for s in range(SIDE)], axis=0
         )
-        _, hit = hits_of(ranks[line][...], groups, cap)
-        weights.append(jnp.where(hit, jnp.exp(hs - log_rows), 0.0).astype(BF16))
+        for line in range(SIDE):
+            scores = mm(parts, rows[line][slots * SIDE :, : reps * cap])
+            slot, lane = iota(scores.shape, 0), iota(scores.shape, 1)
+            s = slot // slots
+            block = s * SIDE + line if half == 0 else line * SIDE + s
+            hs = jnp.sum(
+                jnp.where(lane == block * cap + slot % cap, scores, 0.0), axis=1, keepdims=True
+            )
+            _, hit = hits_of(ranks[line][...], groups, cap)
+            weight_ref[line] = jnp.where(hit, jnp.exp(hs - log_rows), 0.0).astype(BF16)
+
     for s in range(SIDE):
         values = [
             rows[line][(g * SIDE + s) * cap : (g * SIDE + s + 1) * cap, :]
             for line in range(SIDE) for g in range(groups)
         ]
-        weight = jnp.concatenate([w[s * slots : (s + 1) * slots] for w in weights], axis=0)
+        weight = jnp.concatenate(
+            [weight_ref[line, s * slots : (s + 1) * slots, :] for line in range(SIDE)], axis=0
+        )
         outs[s][...] = mm(weight, jnp.concatenate(values, axis=0), TN).astype(outs[s].dtype)
 
 
@@ -417,11 +421,12 @@
     toks = log_total.shape[1]
     shape = (toks, rows[0].shape[1])
     return call(
-        functools.partial(reduce_kernel, half, cap, groups), "reduce", 1,
-        [full(log_total.shape)] + [full(ranks[0].shape)] * 4 + [full(rows[0].shape)] * 4
+        functools.partial(reduce_kernel, half, cap, groups), "reduce", 2,
+        [full(log_total.shape)] + [full(ranks[0].shape)] * 4 + [pl.BlockSpec((rows[0].shape[0], shape[1] // 2), lambda s, _: (0, s))] * 4
         + [full(mark.shape)],
-        [full(shape)] * 4,
-        [jax.ShapeDtypeStruct(shape, F32)] + [jax.ShapeDtypeStruct(shape, BF16)] * 3, [], HEAVY,
+        [pl.BlockSpec((toks, shape[1] // 2), lambda s, _: (0, s))] * 4,
+        [jax.ShapeDtypeStruct(shape, F32)] + [jax.ShapeDtypeStruct(shape, BF16)] * 3,
+        [pltpu.VMEM((SIDE, SIDE * groups * cap, toks), BF16)], HEAVY,
     )(place, log_total, *ranks, *rows, mark)
 
 

time: 155 us -> 154 us (level)
  transfers between devices with their start and end apart: 27 -> 27, of which waited for: 10 -> 10; matrix products, arithmetic and copies ran while one was open for 2% -> 2% of each run, Pallas kernels for 31% -> 32%
where the time goes in v11:
time: 154 us
  Pallas kernels  57.5 us (37%)
  starting transfers between devices  45.3 us (29%)
  waiting for transfers between devices  31.3 us (20%)
  between operations  14.2 us (9%)
  local copies, waits for them, and re-layouts  3.31 us (2%)
  other arithmetic  2.1 us (1%)
    ppermute x24, starting transfers between devices, along(): return lax.ppermute(x, 'rep', pairs)  39.5 us
    ppermute x24, waiting for transfers between devices, along(): return lax.ppermute(x, 'rep', pairs)  30.5 us
    pallas_call x4, Pallas kernels, mid(): call(functools.partial(mid_kernel, shift, cap, groups, reps, negs), 'mid'...  17.9 us
    pallas_call x1, Pallas kernels, column(): call(functools.partial(column_kernel, reps, cap, temper), 'column', gathe...  10 us
    pallas_call x2, Pallas kernels, reduce(): call(functools.partial(reduce_kernel, half, cap, groups), 'reduce', 2, [f...  9.3 us
    pallas_call x1, Pallas kernels, hard(): call(functools.partial(hard_kernel, reps, cap, temper), 'hard', levels +...  9.04 us
    pallas_call x2, Pallas kernels, final(): pl.pallas_call(functools.partial(final_kernel, temper), grid_spec=pltpu.P...  5.92 us
    all_to_all x1, starting transfers between devices, shards(): parts = lax.all_to_all(part, 'rep', split_axis=0, concat_axis=0, tiled=True)  5.79 us
  transfers between devices with their start and end apart: 27, of which 10 were waited for; matrix products, arithmetic and copies ran while one was open for 2% of the time, Pallas kernels for 32%

profile of v11, /device:TPU:0, one launch (start us, length us, event | category | flops | bytes accessed | tf_op | source)
XLA Modules:
  0.0 153.7 jit_solution(2381056138521754530)
XLA Ops:
  7.2 0.7 all-gather.2.cloned.1.call-update
  7.9 0.7 convert_bitcast_fusion
  8.6 1.1 fusion.7
  9.8 3.2 %collective-permute-start.5 = (bf16[272,512]{1,0:T(8,128)(2,1)S(1)}, bf16[272,512]{1,0:T(8,128)(2,1)S(1)}, u32[]{:S(2)}, u32[]{:S(2)}) collective-permute-start(bf16[272,512]{1,0:T(8,128)(2,1)S(1)} %get-tuple-element.87.refs_4_), channel_id=1, source_target_pairs={{0,3},{1,0},{2,1},{3,2},{4,7},{5,4},{6,5},{7,6},{8,11},{9,8},{10,9... | collective-permute-start | bytes 835592 | tf_op jit(solution)/shard_map/ppermute | solution.py:466
  13.6 1.0 collective-permute-start.3
  14.5 2.8 %collective-permute-start.2 = (bf16[272,512]{1,0:T(8,128)(2,1)S(1)}, bf16[272,512]{1,0:T(8,128)(2,1)S(1)}, u32[]{:S(2)}, u32[]{:S(2)}) collective-permute-start(bf16[272,512]{1,0:T(8,128)(2,1)S(1)} %get-tuple-element.88.refs_0_), channel_id=1, source_target_pairs={{0,12},{1,13},{2,14},{3,15},{4,0},{5,1},{6,2},{7,3},{8,4},{9,5},{1... | collective-permute-start | bytes 835592 | tf_op jit(solution)/shard_map/ppermute | solution.py:466
  17.3 0.8 collective-permute-start.1
  18.1 6.7 %collective-permute-done.5.refs_7_ = bf16[272,512]{1,0:T(8,128)(2,1)S(1)} collective-permute-done((bf16[272,512]{1,0:T(8,128)(2,1)S(1)}, bf16[272,512]{1,0:T(8,128)(2,1)S(1)}, u32[]{:S(2)}, u32[]{:S(2)}) %collective-permute-start.5) | collective-permute-done | bytes 278560 | tf_op jit(solution)/shard_map/ppermute | solution.py:466
  24.8 1.5 collective-permute-start
  26.3 0.7 pad_add_fusion.place_ref
  27.0 1.6 %collective-permute-done.3.refs_5_ = bf16[272,512]{1,0:T(8,128)(2,1)S(1)} collective-permute-done((bf16[272,512]{1,0:T(8,128)(2,1)S(1)}, bf16[272,512]{1,0:T(8,128)(2,1)S(1)}, u32[]{:S(2)}, u32[]{:S(2)}) %collective-permute-start.3) | collective-permute-done | bytes 278560 | tf_op jit(solution)/shard_map/ppermute | solution.py:466
  28.5 0.7 copy-done.5
  29.4 0.7 copy-done.7
  30.1 3.9 %collective-permute-done.refs_1_ = bf16[272,512]{1,0:T(8,128)(2,1)} collective-permute-done((bf16[272,512]{1,0:T(8,128)(2,1)S(1)}, bf16[272,512]{1,0:T(8,128)(2,1)}, u32[]{:S(2)}, u32[]{:S(2)}) %collective-permute-start) | collective-permute-done | bytes 278560 | tf_op jit(solution)/shard_map/ppermute | solution.py:466
  34.0 4.5 %mid.4 = (bf16[528,512]{1,0:T(8,128)(2,1)}, bf16[528,512]{1,0:T(8,128)(2,1)}, bf16[32,256]{1,0:T(8,128)(2,1)}, bf16[32,256]{1,0:T(8,128)(2,1)}) custom-call(s32[3]{0:T(128)} %pad_add_fusion.place_ref, bf16[272,512]{1,0:T(8,128)(2,1)} %copy-done.1, bf16[272,512]{1,0:T(8,128)(2,1)} %collective-permute-done.refs_1_, bf16[272,512]{1,0:T(8,128)(2,1)} %copy-done.7, ...), custom_call_target="tpu_custom_call" | custom-call | flops 1048576 | bytes 65536 | tf_op jit(solution)/shard_map/mid/pallas_call | solution.py:129
  38.9 0.7 collective-permute-start.10
  39.6 4.5 %mid.5 = (bf16[528,512]{1,0:T(8,128)(2,1)}, bf16[528,512]{1,0:T(8,128)(2,1)}, bf16[32,256]{1,0:T(8,128)(2,1)}, bf16[32,256]{1,0:T(8,128)(2,1)}) custom-call(s32[3]{0:T(128)} %pad_add_fusion.place_ref, bf16[272,512]{1,0:T(8,128)(2,1)} %copy-done.1, bf16[272,512]{1,0:T(8,128)(2,1)} %collective-permute-done.refs_1_, bf16[272,512]{1,0:T(8,128)(2,1)} %copy-done.7, ...), custom_call_target="tpu_custom_call" | custom-call | flops 1048576 | bytes 65536 | tf_op jit(solution)/shard_map/mid/pallas_call | solution.py:129
  44.1 4.8 %collective-permute-start.6 = (bf16[528,512]{1,0:T(8,128)(2,1)}, bf16[528,512]{1,0:T(8,128)(2,1)}, u32[]{:S(2)}, u32[]{:S(2)}) collective-permute-start(bf16[528,512]{1,0:T(8,128)(2,1)} %get-tuple-element.48), channel_id=1, source_target_pairs={{0,1},{1,2},{2,3},{3,0},{4,5},{5,6},{6,7},{7,4},{8,9},{9,10},{10,1... | collective-permute-start | bytes 1622024 | tf_op jit(solution)/shard_map/ppermute | solution.py:466
  48.9 0.6 collective-permute-start.9
  49.6 4.4 %mid.6 = (bf16[528,512]{1,0:T(8,128)(2,1)}, bf16[528,512]{1,0:T(8,128)(2,1)}, bf16[32,256]{1,0:T(8,128)(2,1)}, bf16[32,256]{1,0:T(8,128)(2,1)}) custom-call(s32[3]{0:T(128)} %pad_add_fusion.place_ref, bf16[272,512]{1,0:T(8,128)(2,1)} %copy-done.1, bf16[272,512]{1,0:T(8,128)(2,1)} %collective-permute-done.refs_1_, bf16[272,512]{1,0:T(8,128)(2,1)} %copy-done.7, ...), custom_call_target="tpu_custom_call" | custom-call | flops 1048576 | bytes 65536 | tf_op jit(solution)/shard_map/mid/pallas_call | solution.py:129
  54.0 1.5 collective-permute-done.7.refs_2_.refs_10_
  55.5 1.2 collective-permute-start.11
  56.7 4.4 %mid.7 = (bf16[528,512]{1,0:T(8,128)(2,1)}, bf16[528,512]{1,0:T(8,128)(2,1)}, bf16[32,256]{1,0:T(8,128)(2,1)}, bf16[32,256]{1,0:T(8,128)(2,1)}) custom-call(s32[3]{0:T(128)} %pad_add_fusion.place_ref, bf16[272,512]{1,0:T(8,128)(2,1)} %copy-done.1, bf16[272,512]{1,0:T(8,128)(2,1)} %collective-permute-done.refs_1_, bf16[272,512]{1,0:T(8,128)(2,1)} %copy-done.7, ...), custom_call_target="tpu_custom_call" | custom-call | flops 1048576 | bytes 65536 | tf_op jit(solution)/shard_map/mid/pallas_call | solution.py:129
  61.2 5.3 %inside.1 = (f32[1,256]{1,0:T(1,128)}, f32[2048,256]{1,0:T(8,128)}) custom-call(s32[3]{0:T(128)} %pad_add_fusion.place_ref, bf16[2048,1024]{1,0:T(8,128)(2,1)} %all-gather.2.cloned.1.call-done.p_ref.refs_12_.refs_8_, bf16[256,1024]{1,0:T(8,128)(2,1)} %refs_9_.1), custom_call_target="tpu_custom_call" | custom-call | flops 1048576 | bytes 65536 | tf_op jit(solution)/shard_map/inside/pallas_call | solution.py:160
  66.5 9.0 %hard.1 = (bf16[544,512]{1,0:T(8,128)(2,1)}, bf16[544,512]{1,0:T(8,128)(2,1)}, bf16[544,512]{1,0:T(8,128)(2,1)}, bf16[544,512]{1,0:T(8,128)(2,1)}, bf16[544,512]...) custom-call(s32[3]{0:T(128)} %pad_add_fusion.place_ref, ...), custom_call_target="tpu_custom_call" | custom-call | flops 1048576 | bytes 65536 | tf_op jit(solution)/shard_map/hard/pallas_call | solution.py:290
  75.5 5.8 %all-to-all-start = ((f32[16,16,256]{2,1,0:T(8,128)}), f32[16,16,256]{2,1,0:T(8,128)S(1)}, u32[]{:S(2)}, u32[]{:S(2)}) async-start(f32[16,16,256]{2,1,0:T(8,128)} %get-tuple-element.58), calls=%async_computation | async-start | bytes 524288 | tf_op jit(solution)/shard_map/all_to_all | solution.py:503
  81.4 3.4 %collective-permute-start.18 = (bf16[544,512]{1,0:T(8,128)(2,1)}, bf16[544,512]{1,0:T(8,128)(2,1)S(1)}, u32[]{:S(2)}, u32[]{:S(2)}) collective-permute-start(bf16[544,512]{1,0:T(8,128)(2,1)} %get-tuple-element.77), channel_id=1, source_target_pairs={{0,3},{1,0},{2,1},{3,2},{4,7},{5,4},{6,5},{7,6},{8,11},{9,8},{10,9... | collective-permute-start | bytes 1671176 | tf_op jit(solution)/shard_map/ppermute | solution.py:466
  84.8 0.9 collective-permute-start.19
  85.6 0.9 collective-permute-start.20
  86.5 2.7 %collective-permute-start.12 = (bf16[544,512]{1,0:T(8,128)(2,1)}, bf16[544,512]{1,0:T(8,128)(2,1)}, u32[]{:S(2)}, u32[]{:S(2)}) collective-permute-start(bf16[544,512]{1,0:T(8,128)(2,1)} %get-tuple-element.67), channel_id=1, source_target_pairs={{0,12},{1,13},{2,14},{3,15},{4,0},{5,1},{6,2},{7,3},{8,4},{9,5},{1... | collective-permute-start | bytes 1671176 | tf_op jit(solution)/shard_map/ppermute | solution.py:466
  89.2 0.9 collective-permute-start.13
  90.7 10.0 %column.1 = (bf16[2048,1024]{1,0:T(8,128)(2,1)}, f32[256,1024]{1,0:T(8,128)}, f32[1,256]{1,0:T(1,128)}, f32[8,128]{1,0:T(8,128)}) custom-call(s32[3]{0:T(128)} %pad_add_fusion.place_ref, s32[16,256]{1,0:T(8,128)} %get-tuple-element.56.code_ref, f32[8,256]{1,0:T(8,128)} %get-tuple-element.57.hs_ref, f32[16,256]{1,0:T(8,128)} %log_add_fusion.lt_ref, ...), custom_call_target="tpu_custom_call" | custom-call | flops 1048576 | bytes 65536 | tf_op jit(solution)/shard_map/column/pallas_call | solution.py:370
  100.8 8.1 %collective-permute-done.18.refs_5_ = bf16[544,512]{1,0:T(8,128)(2,1)S(1)} collective-permute-done((bf16[544,512]{1,0:T(8,128)(2,1)}, bf16[544,512]{1,0:T(8,128)(2,1)S(1)}, u32[]{:S(2)}, u32[]{:S(2)}) %collective-permute-start.18) | collective-permute-done | bytes 557088 | tf_op jit(solution)/shard_map/ppermute | solution.py:466
  108.9 1.1 collective-permute-start.14
  110.0 2.1 %collective-permute-done.20.refs_7_ = bf16[544,512]{1,0:T(8,128)(2,1)} collective-permute-done((bf16[544,512]{1,0:T(8,128)(2,1)}, bf16[544,512]{1,0:T(8,128)(2,1)}, u32[]{:S(2)}, u32[]{:S(2)}) %collective-permute-start.20) | collective-permute-done | bytes 557088 | tf_op jit(solution)/shard_map/ppermute | solution.py:466
  112.1 4.6 %reduce.3 = (f32[256,512]{1,0:T(8,128)}, bf16[256,512]{1,0:T(8,128)(2,1)}, bf16[256,512]{1,0:T(8,128)(2,1)}, bf16[256,512]{1,0:T(8,128)(2,1)}) custom-call(s32[3]{0:T(128)} %pad_add_fusion.place_ref, f32[16,256]{1,0:T(8,128)} %log_add_fusion.lt_ref, bf16[32,256]{1,0:T(8,128)(2,1)} %get-tuple-element.75.refs_0_, ...), custom_call_target="tpu_custom_call" | custom-call | flops 549755813888 | bytes 65536 | tf_op jit(solution)/shard_map/reduce/pallas_call | solution.py:423
  116.8 2.3 %collective-permute-start.21 = (bf16[256,512]{1,0:T(8,128)(2,1)}, bf16[256,512]{1,0:T(8,128)(2,1)}, u32[]{:S(2)}, u32[]{:S(2)}) collective-permute-start(bf16[256,512]{1,0:T(8,128)(2,1)} %get-tuple-element.81), channel_id=1, source_target_pairs={{0,12},{1,13},{2,14},{3,15},{4,0},{5,1},{6,2},{7,3},{8,4},{9,5},{1... | collective-permute-start | bytes 786440 | tf_op jit(solution)/shard_map/ppermute | solution.py:466
  119.1 0.9 collective-permute-start.22
  120.0 0.8 collective-permute-start.23
  120.8 4.7 %reduce.2 = (f32[256,512]{1,0:T(8,128)}, bf16[256,512]{1,0:T(8,128)(2,1)}, bf16[256,512]{1,0:T(8,128)(2,1)}, bf16[256,512]{1,0:T(8,128)(2,1)}) custom-call(s32[3]{0:T(128)} %pad_add_fusion.place_ref, f32[16,256]{1,0:T(8,128)} %log_add_fusion.lt_ref, bf16[32,256]{1,0:T(8,128)(2,1)} %get-tuple-element.62.refs_0_, bf16[32,256]{1,0:T(8,128)(2,1)} %get-tuple-element.63.refs_1_, ...), custom_call_target="tpu_custom_call" | custom-call | flops 549755813888 | bytes 65536 | tf_op jit(solution)/shard_map/reduce/pallas_call | solution.py:423
  125.4 7.1 %collective-permute-start.15 = (bf16[256,512]{1,0:T(8,128)(2,1)}, bf16[256,512]{1,0:T(8,128)(2,1)S(1)}, u32[]{:S(2)}, u32[]{:S(2)}) collective-permute-start(bf16[256,512]{1,0:T(8,128)(2,1)} %get-tuple-element.72), channel_id=1, source_target_pairs={{0,3},{1,0},{2,1},{3,2},{4,7},{5,4},{6,5},{7,6},{8,11},{9,8},{10,9... | collective-permute-start | bytes 786440 | tf_op jit(solution)/shard_map/ppermute | solution.py:466
  132.6 0.9 collective-permute-start.17
  133.5 0.8 collective-permute-done.23.refs_3_
  134.3 3.0 %final.2.refs_4_ = bf16[256,1024]{1,0:T(8,128)(2,1)} custom-call(s32[3]{0:T(128)} %pad_add_fusion.place_ref, f32[256,1024]{1,0:T(8,128)} %get-tuple-element.61.gq_ref, f32[256,512]{1,0:T(8,128)} %get-tuple-element.80.refs_0_, bf16[256,512]{1,0:T(8,128)(2,1)} %collective-permute-done.21.refs_1_, bf16[256,512]{1,0:T(8,128)(2,1)} %collective-permute-done.22.refs_2_, ...), custom_call_target="tpu_custom_call" | custom-call | flops 1048576 | bytes 65536 | tf_op jit(solution)/shard_map/final/pallas_call | solution.py:444
  137.3 3.1 %collective-permute-done.15.refs_1_ = bf16[256,512]{1,0:T(8,128)(2,1)S(1)} collective-permute-done((bf16[256,512]{1,0:T(8,128)(2,1)}, bf16[256,512]{1,0:T(8,128)(2,1)S(1)}, u32[]{:S(2)}, u32[]{:S(2)}) %collective-permute-start.15) | collective-permute-done | bytes 262176 | tf_op jit(solution)/shard_map/ppermute | solution.py:466
  140.8 2.4 %collective-permute-done.17.refs_3_ = bf16[256,512]{1,0:T(8,128)(2,1)S(1)} collective-permute-done((bf16[256,512]{1,0:T(8,128)(2,1)}, bf16[256,512]{1,0:T(8,128)(2,1)S(1)}, u32[]{:S(2)}, u32[]{:S(2)}) %collective-permute-start.17) | collective-permute-done | bytes 262176 | tf_op jit(solution)/shard_map/ppermute | solution.py:466
  143.2 0.7 copy-done.10
  143.9 2.9 %final.3 = bf16[256,1024]{1,0:T(8,128)(2,1)} custom-call(s32[3]{0:T(128)} %pad_add_fusion.place_ref, f32[256,1024]{1,0:T(8,128)} %get-tuple-element.61.gq_ref, f32[256,512]{1,0:T(8,128)} %get-tuple-element.71.refs_0_, bf16[256,512]{1,0:T(8,128)(2,1)} %copy-done.8, bf16[256,512]{1,0:T(8,128)(2,1)} %copy-done.9, ...), custom_call_target="tpu_custom_call", output_to_operand_aliasing={{}: (6, {})} | custom-call | flops 1048576 | bytes 65536 | tf_op jit(solution)/shard_map/final/pallas_call | solution.py:444
  (51 shorter events, 2.4 us)
Async XLA Ops:
  7.2 54.0 %all-gather.2.cloned.1.call-start = ((), (), s32[]{:S(2)}) async-start(), calls=%async_computation.2 | async-start | bytes 4718592 | tf_op jit(solution)/shard_map/all_gather | solution.py:487
  9.7 24.3 %copy-start = (bf16[272,512]{1,0:T(8,128)(2,1)}, bf16[272,512]{1,0:T(8,128)(2,1)S(1)}, u32[]{:S(2)}) copy-start(bf16[272,512]{1,0:T(8,128)(2,1)S(1)} %get-tuple-element.87.refs_4_) | copy-start | bytes 835588
  9.8 24.2 %copy-start.1 = (bf16[272,512]{1,0:T(8,128)(2,1)}, bf16[272,512]{1,0:T(8,128)(2,1)S(1)}, u32[]{:S(2)}) copy-start(bf16[272,512]{1,0:T(8,128)(2,1)S(1)} %get-tuple-element.88.refs_0_) | copy-start | bytes 835588
  9.8 15.1 %collective-permute-start.5 = (bf16[272,512]{1,0:T(8,128)(2,1)S(1)}, bf16[272,512]{1,0:T(8,128)(2,1)S(1)}, u32[]{:S(2)}, u32[]{:S(2)}) collective-permute-start(bf16[272,512]{1,0:T(8,128)(2,1)S(1)} %get-tuple-element.87.refs_4_), channel_id=1, source_target_pairs={{0,3},{1,0},{2,1},{3,2},{4,7},{5,4},{6,5},{7,6},{8,11},{9,8},{10,9... | collective-permute-start | bytes 835592 | tf_op jit(solution)/shard_map/ppermute | solution.py:466
  12.9 14.0 %collective-permute-start.4 = (bf16[272,512]{1,0:T(8,128)(2,1)S(1)}, bf16[272,512]{1,0:T(8,128)(2,1)S(1)}, u32[]{:S(2)}, u32[]{:S(2)}) collective-permute-start(bf16[272,512]{1,0:T(8,128)(2,1)S(1)} %get-tuple-element.87.refs_4_), channel_id=1, source_target_pairs={{0,2},{1,3},{2,0},{3,1},{4,6},{5,7},{6,4},{7,5},{8,10},{9,11},{10,... | collective-permute-start | bytes 835592 | tf_op jit(solution)/shard_map/ppermute | solution.py:466
  13.6 15.0 %collective-permute-start.3 = (bf16[272,512]{1,0:T(8,128)(2,1)S(1)}, bf16[272,512]{1,0:T(8,128)(2,1)S(1)}, u32[]{:S(2)}, u32[]{:S(2)}) collective-permute-start(bf16[272,512]{1,0:T(8,128)(2,1)S(1)} %get-tuple-element.87.refs_4_), channel_id=1, source_target_pairs={{0,1},{1,2},{2,3},{3,0},{4,5},{5,6},{6,7},{7,4},{8,9},{9,10},{10,1... | collective-permute-start | bytes 835592 | tf_op jit(solution)/shard_map/ppermute | solution.py:466
  14.5 14.0 %collective-permute-start.2 = (bf16[272,512]{1,0:T(8,128)(2,1)S(1)}, bf16[272,512]{1,0:T(8,128)(2,1)S(1)}, u32[]{:S(2)}, u32[]{:S(2)}) collective-permute-start(bf16[272,512]{1,0:T(8,128)(2,1)S(1)} %get-tuple-element.88.refs_0_), channel_id=1, source_target_pairs={{0,12},{1,13},{2,14},{3,15},{4,0},{5,1},{6,2},{7,3},{8,4},{9,5},{1... | collective-permute-start | bytes 835592 | tf_op jit(solution)/shard_map/ppermute | solution.py:466
  17.3 11.2 %collective-permute-start.1 = (bf16[272,512]{1,0:T(8,128)(2,1)S(1)}, bf16[272,512]{1,0:T(8,128)(2,1)S(1)}, u32[]{:S(2)}, u32[]{:S(2)}) collective-permute-start(bf16[272,512]{1,0:T(8,128)(2,1)S(1)} %get-tuple-element.88.refs_0_), channel_id=1, source_target_pairs={{0,8},{1,9},{2,10},{3,11},{4,12},{5,13},{6,14},{7,15},{8,0},{9,1},... | collective-permute-start | bytes 835592 | tf_op jit(solution)/shard_map/ppermute | solution.py:466
  24.8 9.2 %copy-start.3 = (bf16[272,512]{1,0:T(8,128)(2,1)}, bf16[272,512]{1,0:T(8,128)(2,1)S(1)}, u32[]{:S(2)}) copy-start(bf16[272,512]{1,0:T(8,128)(2,1)S(1)} %collective-permute-done.5.refs_7_) | copy-start | bytes 835588
  24.8 9.2 %collective-permute-start = (bf16[272,512]{1,0:T(8,128)(2,1)S(1)}, bf16[272,512]{1,0:T(8,128)(2,1)}, u32[]{:S(2)}, u32[]{:S(2)}) collective-permute-start(bf16[272,512]{1,0:T(8,128)(2,1)S(1)} %get-tuple-element.88.refs_0_), channel_id=1, source_target_pairs={{0,4},{1,5},{2,6},{3,7},{4,8},{5,9},{6,10},{7,11},{8,12},{9,13},{1... | collective-permute-start | bytes 835592 | tf_op jit(solution)/shard_map/ppermute | solution.py:466
  27.0 1.6 %copy-start.4 = (bf16[272,512]{1,0:T(8,128)(2,1)}, bf16[272,512]{1,0:T(8,128)(2,1)S(1)}, u32[]{:S(2)}) copy-start(bf16[272,512]{1,0:T(8,128)(2,1)S(1)} %collective-permute-done.4.refs_6_) | copy-start | bytes 835588
  28.5 0.7 copy-start.5
  28.5 0.8 copy-start.6
  29.3 0.7 copy-start.7
  38.5 17.0 %collective-permute-start.7 = (bf16[528,512]{1,0:T(8,128)(2,1)}, bf16[528,512]{1,0:T(8,128)(2,1)S(1)}, u32[]{:S(2)}, u32[]{:S(2)}) collective-permute-start(bf16[528,512]{1,0:T(8,128)(2,1)} %get-tuple-element.49), channel_id=1, source_target_pairs={{0,2},{1,3},{2,0},{3,1},{4,6},{5,7},{6,4},{7,5},{8,10},{9,11},{10,... | collective-permute-start | bytes 1622024 | tf_op jit(solution)/shard_map/ppermute | solution.py:466
  38.9 27.5 %collective-permute-start.10 = (bf16[528,512]{1,0:T(8,128)(2,1)}, bf16[528,512]{1,0:T(8,128)(2,1)}, u32[]{:S(2)}, u32[]{:S(2)}) collective-permute-start(bf16[528,512]{1,0:T(8,128)(2,1)} %get-tuple-element.53), channel_id=1, source_target_pairs={{0,8},{1,9},{2,10},{3,11},{4,12},{5,13},{6,14},{7,15},{8,0},{9,1},... | collective-permute-start | bytes 1622024 | tf_op jit(solution)/shard_map/ppermute | solution.py:466
  44.1 22.3 %collective-permute-start.6 = (bf16[528,512]{1,0:T(8,128)(2,1)}, bf16[528,512]{1,0:T(8,128)(2,1)}, u32[]{:S(2)}, u32[]{:S(2)}) collective-permute-start(bf16[528,512]{1,0:T(8,128)(2,1)} %get-tuple-element.48), channel_id=1, source_target_pairs={{0,1},{1,2},{2,3},{3,0},{4,5},{5,6},{6,7},{7,4},{8,9},{9,10},{10,1... | collective-permute-start | bytes 1622024 | tf_op jit(solution)/shard_map/ppermute | solution.py:466
  48.9 17.5 %collective-permute-start.9 = (bf16[528,512]{1,0:T(8,128)(2,1)}, bf16[528,512]{1,0:T(8,128)(2,1)}, u32[]{:S(2)}, u32[]{:S(2)}) collective-permute-start(bf16[528,512]{1,0:T(8,128)(2,1)} %get-tuple-element.52), channel_id=1, source_target_pairs={{0,4},{1,5},{2,6},{3,7},{4,8},{5,9},{6,10},{7,11},{8,12},{9,13},{1... | collective-permute-start | bytes 1622024 | tf_op jit(solution)/shard_map/ppermute | solution.py:466
  54.0 12.4 %collective-permute-start.8 = (bf16[528,512]{1,0:T(8,128)(2,1)}, bf16[528,512]{1,0:T(8,128)(2,1)}, u32[]{:S(2)}, u32[]{:S(2)}) collective-permute-start(bf16[528,512]{1,0:T(8,128)(2,1)} %get-tuple-element.50), channel_id=1, source_target_pairs={{0,3},{1,0},{2,1},{3,2},{4,7},{5,4},{6,5},{7,6},{8,11},{9,8},{10,9... | collective-permute-start | bytes 1622024 | tf_op jit(solution)/shard_map/ppermute | solution.py:466
  55.5 11.0 %copy-start.2 = (bf16[528,512]{1,0:T(8,128)(2,1)}, bf16[528,512]{1,0:T(8,128)(2,1)S(1)}, u32[]{:S(2)}) copy-start(bf16[528,512]{1,0:T(8,128)(2,1)S(1)} %collective-permute-done.7.refs_2_.refs_10_) | copy-start | bytes 1622020
  55.5 11.0 %collective-permute-start.11 = (bf16[528,512]{1,0:T(8,128)(2,1)}, bf16[528,512]{1,0:T(8,128)(2,1)}, u32[]{:S(2)}, u32[]{:S(2)}) collective-permute-start(bf16[528,512]{1,0:T(8,128)(2,1)} %get-tuple-element.54), channel_id=1, source_target_pairs={{0,12},{1,13},{2,14},{3,15},{4,0},{5,1},{6,2},{7,3},{8,4},{9,5},{1... | collective-permute-start | bytes 1622024 | tf_op jit(solution)/shard_map/ppermute | solution.py:466
  75.5 14.5 %all-to-all-start = ((f32[16,16,256]{2,1,0:T(8,128)}), f32[16,16,256]{2,1,0:T(8,128)S(1)}, u32[]{:S(2)}, u32[]{:S(2)}) async-start(f32[16,16,256]{2,1,0:T(8,128)} %get-tuple-element.58), calls=%async_computation | async-start | bytes 524288 | tf_op jit(solution)/shard_map/all_to_all | solution.py:503
  81.3 65.5 %reduce-scatter.2.cloned.1.call-start = ((), (), s32[]{:S(2)}) async-start(), calls=%async_computation.3 | async-start | bytes 4718592 | tf_op jit(solution)/shard_map/reduce_scatter | solution.py:510
  81.4 27.5 %collective-permute-start.18 = (bf16[544,512]{1,0:T(8,128)(2,1)}, bf16[544,512]{1,0:T(8,128)(2,1)S(1)}, u32[]{:S(2)}, u32[]{:S(2)}) collective-permute-start(bf16[544,512]{1,0:T(8,128)(2,1)} %get-tuple-element.77), channel_id=1, source_target_pairs={{0,3},{1,0},{2,1},{3,2},{4,7},{5,4},{6,5},{7,6},{8,11},{9,8},{10,9... | collective-permute-start | bytes 1671176 | tf_op jit(solution)/shard_map/ppermute | solution.py:466
  84.8 25.3 %collective-permute-start.19 = (bf16[544,512]{1,0:T(8,128)(2,1)}, bf16[544,512]{1,0:T(8,128)(2,1)}, u32[]{:S(2)}, u32[]{:S(2)}) collective-permute-start(bf16[544,512]{1,0:T(8,128)(2,1)} %get-tuple-element.78), channel_id=1, source_target_pairs={{0,2},{1,3},{2,0},{3,1},{4,6},{5,7},{6,4},{7,5},{8,10},{9,11},{10,... | collective-permute-start | bytes 1671176 | tf_op jit(solution)/shard_map/ppermute | solution.py:466
  85.6 26.5 %collective-permute-start.20 = (bf16[544,512]{1,0:T(8,128)(2,1)}, bf16[544,512]{1,0:T(8,128)(2,1)}, u32[]{:S(2)}, u32[]{:S(2)}) collective-permute-start(bf16[544,512]{1,0:T(8,128)(2,1)} %get-tuple-element.79), channel_id=1, source_target_pairs={{0,1},{1,2},{2,3},{3,0},{4,5},{5,6},{6,7},{7,4},{8,9},{9,10},{10,1... | collective-permute-start | bytes 1671176 | tf_op jit(solution)/shard_map/ppermute | solution.py:466
  86.5 33.5 %collective-permute-start.12 = (bf16[544,512]{1,0:T(8,128)(2,1)}, bf16[544,512]{1,0:T(8,128)(2,1)}, u32[]{:S(2)}, u32[]{:S(2)}) collective-permute-start(bf16[544,512]{1,0:T(8,128)(2,1)} %get-tuple-element.67), channel_id=1, source_target_pairs={{0,12},{1,13},{2,14},{3,15},{4,0},{5,1},{6,2},{7,3},{8,4},{9,5},{1... | collective-permute-start | bytes 1671176 | tf_op jit(solution)/shard_map/ppermute | solution.py:466
  89.2 31.6 %collective-permute-start.13 = (bf16[544,512]{1,0:T(8,128)(2,1)}, bf16[544,512]{1,0:T(8,128)(2,1)}, u32[]{:S(2)}, u32[]{:S(2)}) collective-permute-start(bf16[544,512]{1,0:T(8,128)(2,1)} %get-tuple-element.68), channel_id=1, source_target_pairs={{0,8},{1,9},{2,10},{3,11},{4,12},{5,13},{6,14},{7,15},{8,0},{9,1},... | collective-permute-start | bytes 1671176 | tf_op jit(solution)/shard_map/ppermute | solution.py:466
  108.9 3.3 %copy-start.11 = (bf16[544,512]{1,0:T(8,128)(2,1)}, bf16[544,512]{1,0:T(8,128)(2,1)S(1)}, u32[]{:S(2)}) copy-start(bf16[544,512]{1,0:T(8,128)(2,1)S(1)} %collective-permute-done.18.refs_5_) | copy-start | bytes 1671172
  108.9 11.9 %collective-permute-start.14 = (bf16[544,512]{1,0:T(8,128)(2,1)}, bf16[544,512]{1,0:T(8,128)(2,1)}, u32[]{:S(2)}, u32[]{:S(2)}) collective-permute-start(bf16[544,512]{1,0:T(8,128)(2,1)} %get-tuple-element.69), channel_id=1, source_target_pairs={{0,4},{1,5},{2,6},{3,7},{4,8},{5,9},{6,10},{7,11},{8,12},{9,13},{1... | collective-permute-start | bytes 1671176 | tf_op jit(solution)/shard_map/ppermute | solution.py:466
  116.8 15.8 %collective-permute-start.21 = (bf16[256,512]{1,0:T(8,128)(2,1)}, bf16[256,512]{1,0:T(8,128)(2,1)}, u32[]{:S(2)}, u32[]{:S(2)}) collective-permute-start(bf16[256,512]{1,0:T(8,128)(2,1)} %get-tuple-element.81), channel_id=1, source_target_pairs={{0,12},{1,13},{2,14},{3,15},{4,0},{5,1},{6,2},{7,3},{8,4},{9,5},{1... | collective-permute-start | bytes 786440 | tf_op jit(solution)/shard_map/ppermute | solution.py:466
  119.1 14.4 %collective-permute-start.22 = (bf16[256,512]{1,0:T(8,128)(2,1)}, bf16[256,512]{1,0:T(8,128)(2,1)}, u32[]{:S(2)}, u32[]{:S(2)}) collective-permute-start(bf16[256,512]{1,0:T(8,128)(2,1)} %get-tuple-element.82), channel_id=1, source_target_pairs={{0,8},{1,9},{2,10},{3,11},{4,12},{5,13},{6,14},{7,15},{8,0},{9,1},... | collective-permute-start | bytes 786440 | tf_op jit(solution)/shard_map/ppermute | solution.py:466
  120.0 14.4 %collective-permute-start.23 = (bf16[256,512]{1,0:T(8,128)(2,1)}, bf16[256,512]{1,0:T(8,128)(2,1)}, u32[]{:S(2)}, u32[]{:S(2)}) collective-permute-start(bf16[256,512]{1,0:T(8,128)(2,1)} %get-tuple-element.83), channel_id=1, source_target_pairs={{0,4},{1,5},{2,6},{3,7},{4,8},{5,9},{6,10},{7,11},{8,12},{9,13},{1... | collective-permute-start | bytes 786440 | tf_op jit(solution)/shard_map/ppermute | solution.py:466
  125.4 15.0 %collective-permute-start.15 = (bf16[256,512]{1,0:T(8,128)(2,1)}, bf16[256,512]{1,0:T(8,128)(2,1)S(1)}, u32[]{:S(2)}, u32[]{:S(2)}) collective-permute-start(bf16[256,512]{1,0:T(8,128)(2,1)} %get-tuple-element.72), channel_id=1, source_target_pairs={{0,3},{1,0},{2,1},{3,2},{4,7},{5,4},{6,5},{7,6},{8,11},{9,8},{10,9... | collective-permute-start | bytes 786440 | tf_op jit(solution)/shard_map/ppermute | solution.py:466
  132.6 8.2 %collective-permute-start.16 = (bf16[256,512]{1,0:T(8,128)(2,1)}, bf16[256,512]{1,0:T(8,128)(2,1)S(1)}, u32[]{:S(2)}, u32[]{:S(2)}) collective-permute-start(bf16[256,512]{1,0:T(8,128)(2,1)} %get-tuple-element.73), channel_id=1, source_target_pairs={{0,2},{1,3},{2,0},{3,1},{4,6},{5,7},{6,4},{7,5},{8,10},{9,11},{10,... | collective-permute-start | bytes 786440 | tf_op jit(solution)/shard_map/ppermute | solution.py:466
  132.6 10.6 %collective-permute-start.17 = (bf16[256,512]{1,0:T(8,128)(2,1)}, bf16[256,512]{1,0:T(8,128)(2,1)S(1)}, u32[]{:S(2)}, u32[]{:S(2)}) collective-permute-start(bf16[256,512]{1,0:T(8,128)(2,1)} %get-tuple-element.74), channel_id=1, source_target_pairs={{0,1},{1,2},{2,3},{3,0},{4,5},{5,6},{6,7},{7,4},{8,9},{9,10},{10,1... | collective-permute-start | bytes 786440 | tf_op jit(solution)/shard_map/ppermute | solution.py:466
  140.4 2.8 %copy-start.8 = (bf16[256,512]{1,0:T(8,128)(2,1)}, bf16[256,512]{1,0:T(8,128)(2,1)S(1)}, u32[]{:S(2)}) copy-start(bf16[256,512]{1,0:T(8,128)(2,1)S(1)} %collective-permute-done.15.refs_1_) | copy-start | bytes 786436
  140.8 2.4 %copy-start.9 = (bf16[256,512]{1,0:T(8,128)(2,1)}, bf16[256,512]{1,0:T(8,128)(2,1)S(1)}, u32[]{:S(2)}) copy-start(bf16[256,512]{1,0:T(8,128)(2,1)S(1)} %collective-permute-done.16.refs_2_) | copy-start | bytes 786436
  143.2 0.7 copy-start.10
Sparse Core Ops, SparseCore 0:
  9.7 34.7 all-gather.1
  100.9 40.3 reduce-scatter.1
